TPU v7x, 256 devices: a whole 4x4x8 slice. The times are simulated.
256 devices in a mesh: seq: 32 (over y, z_hi, core), blk: 8 (over z_lo, x).
Axes of the slice: x: 4, y: 4, z: 8 (z_hi: 4, z_lo: 2; z = z_hi * 2 + z_lo), core: 2. Of those that a mesh axis runs over, the one named last changes fastest.
Arguments:
- query_vectors: bfloat16 [12288, 4096], P(('seq', 'blk')), may hold values from -120 to 120
- key_vectors: bfloat16 [12288, 4096], P(('seq', 'blk')), may hold values from -9 to 9
- value_vectors: bfloat16 [12288, 4096], P(('seq', 'blk')), may hold values from -6 to 6
- weight_head: bfloat16 [4096, 64], replicated, may hold values from -0.5 to 0.5
- noisy_latent: float32 [4, 128, 96, 16], P(None, 'seq', 'blk'), may hold values from -6 to 6
- noise_level: float32 [1], replicated, may hold values from 0.5 to 1
- latent_mean: float32 [16], replicated, may hold values from -3 to 3
- latent_scale: float32 [16], replicated, may hold values from 0.5 to 2
- cache_in: bfloat16 [2, 128, 96, 16], P(None, 'seq', 'blk'), may hold values from -6 to 6
- weight_in: bfloat16 [3, 3, 3, 16, 384], replicated, may hold values from -0.3125 to 0.3125
- bias_in: float32 [384], replicated, may hold values from -3 to 3
- norm_gain: float32 [384], replicated, may hold values from 0.5 to 1.5
- cache_mid: bfloat16 [2, 128, 96, 384], P(None, 'seq', 'blk'), may hold values from -6 to 6
- weight_mid: bfloat16 [3, 3, 3, 384, 384], replicated, may hold values from -0.0625 to 0.0625
- bias_mid: float32 [384], replicated, may hold values from -3 to 3
Outputs:
- denoised: float32 [4, 128, 96, 16], P(None, 'seq', 'blk')
- features: bfloat16 [4, 128, 96, 384], P(None, 'seq', 'blk')
All inputs are finite; a program needn't handle non-finite values.
Results may differ from a plain program's by a relative error of at most 0.011.
Values may be sent and summed in bfloat16 or wider, within the bound.
No kernel may reach another device: no remote copies, remote signals or barrier semaphores. Data moves between devices by JAX's collectives and lax.ppermute only.
A program may use at most 128 MiB of HBM per device.

v0:
```python
import math

import jax
import jax.numpy as jnp
from jax import lax
from jax.sharding import PartitionSpec as P

HEAD_DIM = 128
HEAD_DEV = 1
LAT = 16
F = 4
TR = 2


EPSILON = 1e-06


def with_halo(cells, sides, width):
    for axis, dim in sides:
        count = lax.axis_size(axis)
        ends = count - 1
        head = lax.slice_in_dim(cells, 0, width, axis=dim)
        tail = lax.slice_in_dim(cells, cells.shape[dim] - width, cells.shape[dim], axis=dim)
        cells = jnp.concatenate(
            [
                lax.ppermute(tail, axis, [(i, (i + 1) % count) for i in range(ends)]),
                cells,
                lax.ppermute(head, axis, [((i + 1) % count, i) for i in range(ends)]),
            ],
            axis=dim,
        )
    return cells


def block_update(query_heads, scaling):

    def update(state_now, block_pair):
        top_prev, totals_prev, running_prev = state_now
        key_block, value_block = block_pair
        scores = (
            jnp.einsum("qhd,khd->qhk", query_heads, key_block, preferred_element_type=jnp.float32)
            * scaling
        )
        highest = jnp.maximum(top_prev, jnp.max(scores, axis=-1))
        fading = jnp.exp(top_prev - highest)
        expd = jnp.exp(scores - highest[..., None])
        totals = totals_prev * fading + jnp.sum(expd, axis=-1)
        mixed = jnp.einsum(
            "qhk,khd->qhd",
            expd.astype(jnp.bfloat16),
            value_block,
            preferred_element_type=jnp.float32,
        )
        running = running_prev * fading[..., None] + mixed
        return ((highest, totals, running), None)

    return update


def key_folding(query_heads, heads_here, state_now, shard_piece):
    update = block_update(query_heads, 1.0 / math.sqrt(HEAD_DIM))
    key_rows, value_rows = shard_piece
    row_count = key_rows.shape[0]
    block_rows = math.gcd(row_count, 2048)
    block_count = row_count // block_rows
    key_blocks = key_rows.reshape(block_count, block_rows, heads_here, HEAD_DIM)
    value_blocks = value_rows.reshape(block_count, block_rows, heads_here, HEAD_DIM)
    state_now, unused = lax.scan(update, state_now, (key_blocks, value_blocks))
    return state_now


def start_state(query_heads, heads_here):
    state_shape = (query_heads.shape[0], heads_here)
    return (
        jnp.full(state_shape, -1e30, jnp.float32),
        jnp.zeros(state_shape, jnp.float32),
        jnp.zeros(state_shape + (HEAD_DIM,), jnp.float32),
    )


def finish(state_now):
    highest, totals, running = state_now
    attended = (running / totals[..., None]).astype(jnp.bfloat16)
    return attended.reshape(attended.shape[0], -1)


def causal_conv(frames, cache, weight, bias_row):
    stacked = jnp.concatenate([cache, frames], axis=0)
    padded = with_halo(stacked, (("seq", 1), ("blk", 2)), 1)
    frame_count, row_count, col_count = (frames.shape[0], frames.shape[1], frames.shape[2])
    tap_list = [
        padded[
            shift_t : shift_t + frame_count,
            shift_h : shift_h + row_count,
            shift_w : shift_w + col_count,
        ]
        for shift_t in range(3)
        for shift_h in range(3)
        for shift_w in range(3)
    ]
    gathered = jnp.concatenate(tap_list, axis=-1).reshape(frame_count * row_count * col_count, -1)
    flat_weight = weight.reshape(-1, weight.shape[-1])
    result = jnp.dot(gathered, flat_weight, preferred_element_type=jnp.float32) + bias_row
    return result.reshape(frame_count, row_count, col_count, -1)


def relay_tiles(velocity):
    band_count = F * TR // lax.axis_size("blk")
    band_rows = velocity.reshape(band_count, -1, velocity.shape[1])
    tile_rows = lax.all_to_all(band_rows, "blk", split_axis=1, concat_axis=0, tiled=True)
    return tile_rows.reshape(F, TR, -1, 2, 2, LAT)


def shards(
    query_vectors,
    key_vectors,
    value_vectors,
    weight_head,
    noisy_latent,
    noise_level,
    latent_mean,
    latent_scale,
    cache_in,
    weight_in,
    bias_in,
    norm_gain,
    cache_mid,
    weight_mid,
    bias_mid,
):
    heads_total = HEAD_DEV * lax.axis_size("seq")
    moved_query, moved_key, moved_value = (
        lax.all_to_all(query_vectors, "blk", split_axis=1, concat_axis=0, tiled=True),
        lax.all_to_all(key_vectors, "blk", split_axis=1, concat_axis=0, tiled=True),
        lax.all_to_all(value_vectors, "blk", split_axis=1, concat_axis=0, tiled=True),
    )
    heads_here = heads_total // lax.axis_size("blk")
    query_heads = moved_query.reshape(moved_query.shape[0], heads_here, HEAD_DIM)
    state_now = key_folding(
        query_heads,
        heads_here,
        start_state(query_heads, heads_here),
        (
            lax.all_gather(moved_key, "seq", axis=0, tiled=True),
            lax.all_gather(moved_value, "seq", axis=0, tiled=True),
        ),
    )
    attended = finish(state_now)
    returned = lax.all_to_all(attended, "blk", split_axis=0, concat_axis=1, tiled=True)
    velocity = jnp.dot(returned, weight_head, preferred_element_type=jnp.float32)
    patch_grid = relay_tiles(velocity)
    columns = patch_grid.shape[2]
    patch_grid = patch_grid.transpose(0, 1, 3, 2, 4, 5).reshape(F, 2 * TR, 2 * columns, LAT)
    denoised = noisy_latent - noise_level[0] * patch_grid
    latent = (denoised * latent_scale + latent_mean).astype(jnp.bfloat16)
    first_conv = causal_conv(latent, cache_in, weight_in, bias_in)
    power = jnp.mean(first_conv * first_conv, axis=-1, keepdims=True)
    active = jax.nn.silu(first_conv * lax.rsqrt(power + EPSILON) * norm_gain).astype(jnp.bfloat16)
    features = (first_conv + causal_conv(active, cache_mid, weight_mid, bias_mid)).astype(
        jnp.bfloat16
    )
    return (denoised, features)


def solution(mesh):
    in_specs = (
        P(("seq", "blk"), None),
        P(("seq", "blk"), None),
        P(("seq", "blk"), None),
        P(),
        P(None, "seq", "blk", None),
        P(),
        P(),
        P(),
        P(None, "seq", "blk", None),
        P(),
        P(),
        P(),
        P(None, "seq", "blk", None),
        P(),
        P(),
    )
    out_specs = (P(None, "seq", "blk", None), P(None, "seq", "blk", None))
    return jax.shard_map(shards, mesh=mesh, in_specs=in_specs, out_specs=out_specs, check_vma=False)
```

profile of v0, /device:TPU:1, one launch (start us, length us, event | category | flops | bytes accessed | tf_op | source)
XLA Modules:
  0.0 519.6 jit_solution(11030282618832788773)
XLA Ops:
  8.3 13.5 %all_to_all.82 = bf16[48,8,512]{2,0,1:T(8,128)(2,1)} all-to-all(bf16[48,8,512]{2,0,1:T(8,128)(2,1)S(1)} %bitcast.90), channel_id=1, replica_groups=mesh['seq'=32,'blk'=8] {'blk'}, dimensions={1} | all-to-all | bytes 786432 | tf_op jit(solution)/shard_map/all_to_all | solution.py:134
  22.9 9.9 %all_to_all.83 = bf16[48,8,512]{2,0,1:T(8,128)(2,1)} all-to-all(bf16[48,8,512]{2,0,1:T(8,128)(2,1)S(1)} %bitcast.91), channel_id=1, replica_groups=mesh['seq'=32,'blk'=8] {'blk'}, dimensions={1} | all-to-all | bytes 786432 | tf_op jit(solution)/shard_map/all_to_all | solution.py:135
  38.2 13.3 %all-to-all-done.1 = bf16[48,8,512]{2,0,1:T(8,128)(2,1)S(1)} async-done(((bf16[48,8,512]{2,0,1:T(8,128)(2,1)}), bf16[48,8,512]{2,0,1:T(8,128)(2,1)S(1)}, u32[]{:S(2)}, u32[]{:S(2)}) %all-to-all-start.1) | async-done | bytes 393248 | tf_op jit(solution)/shard_map/all_to_all | solution.py:133
  51.6 67.0 %all-gather.3.cloned.1.call-done = bf16[12288,512]{1,0:T(8,128)(2,1)} async-done(((bf16[384,512]{1,0:T(8,128)(2,1)}), bf16[12288,512]{1,0:T(8,128)(2,1)}) %all-gather.3.cloned.1.call-update) | async-done | bytes 12582928 | tf_op jit(solution)/shard_map/all_gather | solution.py:144
  118.6 18.2 %reshape.84 = bf16[6,2048,4,128]{3,2,1,0:T(4,128)(2,1)} reshape(bf16[12288,512]{1,0:T(8,128)(2,1)} %all-gather.3.cloned.1.call-done) | data formatting | bytes 25165824 | tf_op jit(solution)/shard_map/reshape | solution.py:66
  136.8 81.6 %all-gather.5.cloned.1.call-done = bf16[12288,512]{1,0:T(8,128)(2,1)} async-done(((bf16[384,512]{1,0:T(8,128)(2,1)}), bf16[12288,512]{1,0:T(8,128)(2,1)}) %all-gather.5.cloned.1.call-update) | async-done | bytes 12582928 | tf_op jit(solution)/shard_map/all_gather | solution.py:145
  218.3 18.2 %reshape.86 = bf16[6,2048,4,128]{3,2,1,0:T(4,128)(2,1)} reshape(bf16[12288,512]{1,0:T(8,128)(2,1)} %all-gather.5.cloned.1.call-done) | data formatting | bytes 25165824 | tf_op jit(solution)/shard_map/reshape | solution.py:67
  236.5 168.4 %while.15 = (s32[]{:T(128)}, f32[384,4]{0,1:T(4,128)S(1)}, f32[384,4]{0,1:T(4,128)S(1)}, f32[384,4,128]{0,2,1:T(8,128)}, bf16[6,2048,4,128]{3,2,1,0:T(4,128)(2,1...) while((s32[]{:T(128)}, f32[384,4]{0,1:T(4,128)S(1)}, ...), condition=%wide.region_3.4_spmd.clone, body=%wide.region_0.3_spmd.clone.sunk | while | flops 1636376064 | bytes 56590440 | solution.py:68
  246.9 6.6 %fusion.50 = f32[384,4]{0,1:T(4,128)S(1)} fusion(f32[4,2048,384]{2,1,0:T(8,128)} %get-tuple-element.222, f32[384,4]{0,1:T(4,128)S(1)} %select_maximum_fusion.2), kind=kLoop, calls=%fused_computation.4.clone.1 | loop fusion | flops 9435648 | bytes 12595200 | tf_op jit(solution)/shard_map/while/body/eval_jaxpr/reduce_sum | solution.py:47
  256.5 8.0 %fusion.52 = f32[384,4,128]{0,2,1:T(8,128)} fusion(f32[4,2048,384]{2,1,0:T(8,128)} %get-tuple-element.222, f32[384,4]{0,1:T(4,128)S(1)} %select_maximum_fusion.2, bf16[1,2048,4,128]{1,3,2,0:T(8,128)(2,1)S(1)} %copy.80, f32[384,4,128]{0,2,1:T(8,128)} %get-tuple-element.238, f32[384,4]{0,1:T(4,128)S(1)} %get-tuple-element.225, pred[]{:T(512)S(6)} %compare.3), kind=kOutput, calls=%fused_computation.12.clone.1 | convolution fusion | flops 815333376 | bytes 16265217 | tf_op jit(solution)/shard_map/while/body/eval_jaxpr/qhk,khd->qhd/dot_general | solution.py:48
  274.8 6.6 %fusion.50 = f32[384,4]{0,1:T(4,128)S(1)} fusion(f32[4,2048,384]{2,1,0:T(8,128)} %get-tuple-element.222, f32[384,4]{0,1:T(4,128)S(1)} %select_maximum_fusion.2), kind=kLoop, calls=%fused_computation.4.clone.1 | loop fusion | flops 9435648 | bytes 12595200 | tf_op jit(solution)/shard_map/while/body/eval_jaxpr/reduce_sum | solution.py:47
  284.4 8.1 %fusion.52 = f32[384,4,128]{0,2,1:T(8,128)} fusion(f32[4,2048,384]{2,1,0:T(8,128)} %get-tuple-element.222, f32[384,4]{0,1:T(4,128)S(1)} %select_maximum_fusion.2, bf16[1,2048,4,128]{1,3,2,0:T(8,128)(2,1)S(1)} %copy.80, f32[384,4,128]{0,2,1:T(8,128)} %get-tuple-element.238, f32[384,4]{0,1:T(4,128)S(1)} %get-tuple-element.225, pred[]{:T(512)S(6)} %compare.3), kind=kOutput, calls=%fused_computation.12.clone.1 | convolution fusion | flops 815333376 | bytes 16265217 | tf_op jit(solution)/shard_map/while/body/eval_jaxpr/qhk,khd->qhd/dot_general | solution.py:48
  302.9 6.6 %fusion.50 = f32[384,4]{0,1:T(4,128)S(1)} fusion(f32[4,2048,384]{2,1,0:T(8,128)} %get-tuple-element.222, f32[384,4]{0,1:T(4,128)S(1)} %select_maximum_fusion.2), kind=kLoop, calls=%fused_computation.4.clone.1 | loop fusion | flops 9435648 | bytes 12595200 | tf_op jit(solution)/shard_map/while/body/eval_jaxpr/reduce_sum | solution.py:47
  312.5 8.1 %fusion.52 = f32[384,4,128]{0,2,1:T(8,128)} fusion(f32[4,2048,384]{2,1,0:T(8,128)} %get-tuple-element.222, f32[384,4]{0,1:T(4,128)S(1)} %select_maximum_fusion.2, bf16[1,2048,4,128]{1,3,2,0:T(8,128)(2,1)S(1)} %copy.80, f32[384,4,128]{0,2,1:T(8,128)} %get-tuple-element.238, f32[384,4]{0,1:T(4,128)S(1)} %get-tuple-element.225, pred[]{:T(512)S(6)} %compare.3), kind=kOutput, calls=%fused_computation.12.clone.1 | convolution fusion | flops 815333376 | bytes 16265217 | tf_op jit(solution)/shard_map/while/body/eval_jaxpr/qhk,khd->qhd/dot_general | solution.py:48
  331.0 6.6 %fusion.50 = f32[384,4]{0,1:T(4,128)S(1)} fusion(f32[4,2048,384]{2,1,0:T(8,128)} %get-tuple-element.222, f32[384,4]{0,1:T(4,128)S(1)} %select_maximum_fusion.2), kind=kLoop, calls=%fused_computation.4.clone.1 | loop fusion | flops 9435648 | bytes 12595200 | tf_op jit(solution)/shard_map/while/body/eval_jaxpr/reduce_sum | solution.py:47
  340.6 8.1 %fusion.52 = f32[384,4,128]{0,2,1:T(8,128)} fusion(f32[4,2048,384]{2,1,0:T(8,128)} %get-tuple-element.222, f32[384,4]{0,1:T(4,128)S(1)} %select_maximum_fusion.2, bf16[1,2048,4,128]{1,3,2,0:T(8,128)(2,1)S(1)} %copy.80, f32[384,4,128]{0,2,1:T(8,128)} %get-tuple-element.238, f32[384,4]{0,1:T(4,128)S(1)} %get-tuple-element.225, pred[]{:T(512)S(6)} %compare.3), kind=kOutput, calls=%fused_computation.12.clone.1 | convolution fusion | flops 815333376 | bytes 16265217 | tf_op jit(solution)/shard_map/while/body/eval_jaxpr/qhk,khd->qhd/dot_general | solution.py:48
  352.7 6.4 %bitcast_reduce_fusion.2 = (f32[384,4]{0,1:T(4,128)S(1)}, f32[4,2048,384]{2,1,0:T(8,128)}) fusion(bf16[384,4,128]{2,0,1:T(8,128)(2,1)S(1)} %get-tuple-element.249, bf16[1,2048,4,128]{3,2,1,0:T(4,128)(2,1)S(1)} %get-tuple-element.220), kind=kOutput, calls=%fused_computation.1.clone.1 | convolution fusion | flops 811596288 | bytes 15079424 | tf_op jit(solution)/shard_map/while/body/eval_jaxpr/qhd,khd->qhk/dot_general | solution.py:41
  359.1 6.6 %fusion.50 = f32[384,4]{0,1:T(4,128)S(1)} fusion(f32[4,2048,384]{2,1,0:T(8,128)} %get-tuple-element.222, f32[384,4]{0,1:T(4,128)S(1)} %select_maximum_fusion.2), kind=kLoop, calls=%fused_computation.4.clone.1 | loop fusion | flops 9435648 | bytes 12595200 | tf_op jit(solution)/shard_map/while/body/eval_jaxpr/reduce_sum | solution.py:47
  368.7 8.1 %fusion.52 = f32[384,4,128]{0,2,1:T(8,128)} fusion(f32[4,2048,384]{2,1,0:T(8,128)} %get-tuple-element.222, f32[384,4]{0,1:T(4,128)S(1)} %select_maximum_fusion.2, bf16[1,2048,4,128]{1,3,2,0:T(8,128)(2,1)S(1)} %copy.80, f32[384,4,128]{0,2,1:T(8,128)} %get-tuple-element.238, f32[384,4]{0,1:T(4,128)S(1)} %get-tuple-element.225, pred[]{:T(512)S(6)} %compare.3), kind=kOutput, calls=%fused_computation.12.clone.1 | convolution fusion | flops 815333376 | bytes 16265217 | tf_op jit(solution)/shard_map/while/body/eval_jaxpr/qhk,khd->qhd/dot_general | solution.py:48
  387.2 6.6 %fusion.50 = f32[384,4]{0,1:T(4,128)S(1)} fusion(f32[4,2048,384]{2,1,0:T(8,128)} %get-tuple-element.222, f32[384,4]{0,1:T(4,128)S(1)} %select_maximum_fusion.2), kind=kLoop, calls=%fused_computation.4.clone.1 | loop fusion | flops 9435648 | bytes 12595200 | tf_op jit(solution)/shard_map/while/body/eval_jaxpr/reduce_sum | solution.py:47
  396.8 8.1 %fusion.52 = f32[384,4,128]{0,2,1:T(8,128)} fusion(f32[4,2048,384]{2,1,0:T(8,128)} %get-tuple-element.222, f32[384,4]{0,1:T(4,128)S(1)} %select_maximum_fusion.2, bf16[1,2048,4,128]{1,3,2,0:T(8,128)(2,1)S(1)} %copy.80, f32[384,4,128]{0,2,1:T(8,128)} %get-tuple-element.238, f32[384,4]{0,1:T(4,128)S(1)} %get-tuple-element.225, pred[]{:T(512)S(6)} %compare.3), kind=kOutput, calls=%fused_computation.12.clone.1 | convolution fusion | flops 815333376 | bytes 16265217 | tf_op jit(solution)/shard_map/while/body/eval_jaxpr/qhk,khd->qhd/dot_general | solution.py:48
  406.6 18.7 %all_to_all.84 = bf16[8,48,512]{2,1,0:T(8,128)(2,1)S(1)} all-to-all(bf16[8,48,512]{2,1,0:T(8,128)(2,1)S(1)} %all_to_all.72), channel_id=1, replica_groups=mesh['seq'=32,'blk'=8] {'blk'}, dimensions={0} | all-to-all | bytes 786432 | tf_op jit(solution)/shard_map/all_to_all | solution.py:149
  498.1 7.1 %reshape.91 = bf16[192,10368]{1,0:T(8,128)(2,1)} reshape(bf16[4,4,12,10368]{3,2,1,0:T(8,128)(2,1)} %slice_dynamic-update-slice_fusion) | data formatting | bytes 7962624 | tf_op jit(solution)/shard_map/reshape | solution.py:101
  505.2 6.7 %convolution_add_fusion.1 = f32[192,384]{1,0:T(8,128)S(1)} fusion(bf16[192,10368]{1,0:T(8,128)(2,1)} %reshape.91, bf16[10368,384]{1,0:T(8,128)(2,1)} %bitcast.99, f32[384]{0:T(512)S(1)} %copy-done.9), kind=kOutput, calls=%fused_computation.22 | convolution fusion | flops 1528897536 | bytes 12240384 | tf_op jit(solution)/shard_map/dot_general | solution.py:103
  (150 shorter events, 155.7 us)
Async XLA Ops:
  7.2 418.2 %copy-start = (bf16[4096,64]{0,1:T(8,128)(2,1)S(1)}, bf16[4096,64]{0,1:T(8,128)(2,1)}, u32[]{:S(2)}) copy-start(bf16[4096,64]{0,1:T(8,128)(2,1)} %param.20) | copy-start | bytes 1572868
  7.2 111.4 %all-gather.3.cloned.1.call-start = ((), (), s32[]{:S(2)}) async-start(), calls=%async_computation.5 | async-start | bytes 12976128 | tf_op jit(solution)/shard_map/all_gather | solution.py:144
  21.8 196.5 %all-gather.5.cloned.1.call-start = ((), (), s32[]{:S(2)}) async-start(), calls=%async_computation.6 | async-start | bytes 12976128 | tf_op jit(solution)/shard_map/all_gather | solution.py:145
  34.7 16.8 %all-to-all-start.1 = ((bf16[48,8,512]{2,0,1:T(8,128)(2,1)}), bf16[48,8,512]{2,0,1:T(8,128)(2,1)S(1)}, u32[]{:S(2)}, u32[]{:S(2)}) async-start(bf16[48,8,512]{2,0,1:T(8,128)(2,1)} %bitcast.68), calls=%async_computation.1 | async-start | bytes 786432 | tf_op jit(solution)/shard_map/all_to_all | solution.py:133
  404.9 26.8 %copy-start.4 = (bf16[2,4,12,384]{3,1,2,0:T(4,128)(2,1)S(1)}, bf16[2,4,12,384]{3,1,2,0:T(4,128)(2,1)}, u32[]{:S(2)}) copy-start(bf16[2,4,12,384]{3,1,2,0:T(4,128)(2,1)} %param.29) | copy-start | bytes 221188
  404.9 32.2 %copy-start.3 = (f32[4,4,12,16]{3,1,2,0:T(4,128)S(1)}, f32[4,4,12,16]{3,1,2,0:T(4,128)}, u32[]{:S(2)}) copy-start(f32[4,4,12,16]{3,1,2,0:T(4,128)} %param.21) | copy-start | bytes 36868
  404.9 32.2 %copy-start.7 = (f32[16]{0:T(128)S(1)}, f32[16]{0:T(128)}, u32[]{:S(2)}) copy-start(f32[16]{0:T(128)} %param.23) | copy-start | bytes 196
  404.9 32.2 %copy-start.8 = (f32[16]{0:T(128)S(1)}, f32[16]{0:T(128)}, u32[]{:S(2)}) copy-start(f32[16]{0:T(128)} %param.24) | copy-start | bytes 196
  404.9 32.9 %copy-start.1 = (bf16[2,4,12,16]{3,1,2,0:T(4,128)(2,1)S(1)}, bf16[2,4,12,16]{3,1,2,0:T(4,128)(2,1)}, u32[]{:S(2)}) copy-start(bf16[2,4,12,16]{3,1,2,0:T(4,128)(2,1)} %param.25) | copy-start | bytes 9220
  406.4 53.1 %copy-start.2 = (bf16[3,3,3,16,384]{4,3,2,1,0:T(8,128)(2,1)S(1)}, bf16[3,3,3,16,384]{4,3,2,1,0:T(8,128)(2,1)}, u32[]{:S(2)}) copy-start(bf16[3,3,3,16,384]{4,3,2,1,0:T(8,128)(2,1)} %param.26) | copy-start | bytes 995332
  406.5 53.1 %copy-start.6 = (f32[384]{0:T(512)S(1)}, f32[384]{0:T(512)}, u32[]{:S(2)}) copy-start(f32[384]{0:T(512)} %param.27) | copy-start | bytes 4612
  425.3 34.8 %copy-start.5 = (f32[384]{0:T(512)S(1)}, f32[384]{0:T(512)}, u32[]{:S(2)}) copy-start(f32[384]{0:T(512)} %param.28) | copy-start | bytes 4612
  427.7 8.3 %all-to-all-start.4 = ((f32[8,1,384]{2,1,0:T(1,128)}), f32[8,1,384]{2,1,0:T(1,128)S(1)}, u32[]{:S(2)}, u32[]{:S(2)}) async-start(f32[8,1,384]{2,1,0:T(1,128)} %reshape.101), calls=%async_computation.4 | async-start | bytes 24576 | tf_op jit(solution)/shard_map/all_to_all | solution.py:110
  437.9 7.9 %collective-permute-start = (bf16[6,1,12,16]{3,1,2,0:T(2,128)(2,1)S(1)}, bf16[6,1,12,16]{3,1,2,0:T(2,128)(2,1)S(1)}, u32[]{:S(2)}, u32[]{:S(2)}) collective-permute-start(bf16[6,1,12,16]{3,1,2,0:T(2,128)(2,1)S(1)} %get-tuple-element.155), channel_id=1, source_target_pairs={{0,8},{8,16},{16,24},{24,32},{32,40},{40,48},{48,56},{56,64},{64,7... | collective-permute-start | bytes 6920 | tf_op jit(solution)/shard_map/ppermute | solution.py:26
  443.8 6.6 %collective-permute-start.1 = (bf16[6,1,12,16]{3,1,2,0:T(2,128)(2,1)S(1)}, bf16[6,1,12,16]{3,1,2,0:T(2,128)(2,1)S(1)}, u32[]{:S(2)}, u32[]{:S(2)}) collective-permute-start(bf16[6,1,12,16]{3,1,2,0:T(2,128)(2,1)S(1)} %get-tuple-element.156), channel_id=1, source_target_pairs={{8,0},{16,8},{24,16},{32,24},{40,32},{48,40},{56,48},{64,56},{72,6... | collective-permute-start | bytes 6920 | tf_op jit(solution)/shard_map/ppermute | solution.py:28
  450.4 4.0 collective-permute-start.2
  452.6 4.4 collective-permute-start.3
  460.3 5.1 collective-permute-start.4
  463.5 6.6 %collective-permute-start.5 = (bf16[6,1,12,384]{3,2,1,0:T(8,128)(2,1)S(1)}, bf16[6,1,12,384]{3,2,1,0:T(8,128)(2,1)S(1)}, u32[]{:S(2)}, u32[]{:S(2)}) collective-permute-start(bf16[6,1,12,384]{3,2,1,0:T(8,128)(2,1)S(1)} %get-tuple-element.122), channel_id=1, source_target_pairs={{8,0},{16,8},{24,16},{32,24},{40,32},{48,40},{56,48},{64,56},{72,6... | collective-permute-start | bytes 165896 | tf_op jit(solution)/shard_map/ppermute | solution.py:28
  470.2 4.1 collective-permute-start.6
  472.9 4.9 collective-permute-start.7
  495.9 9.3 %copy-start.9 = (f32[384]{0:T(512)S(1)}, f32[384]{0:T(512)}, u32[]{:S(2)}) copy-start(f32[384]{0:T(512)} %param.31) | copy-start | bytes 4612
Sparse Core Ops, SparseCore 0:
  22.0 96.5 all-gather.2
  121.1 97.1 all-gather.4
where the time goes:
time: 528 us; the launch traced here: 520 us
  waiting for transfers between devices  181 us (34%)
  local copies, waits for them, and re-layouts  112 us (21%)
  matrix products  94.2 us (18%)
  other arithmetic  47.1 us (9%)
  blocking collectives  42.1 us (8%)
  starting transfers between devices  27.5 us (5%)
  between operations  15.2 us (3%)
    all_gather x1, waiting for transfers between devices, shards(): lax.all_gather(moved_value, 'seq', axis=0, tiled=True)  81.6 us
    all_gather x1, waiting for transfers between devices, shards(): lax.all_gather(moved_key, 'seq', axis=0, tiled=True)  67 us
    dot_general x6, matrix products, update(): jnp.einsum('qhk,khd->qhd', expd.astype(jnp.bfloat16), value_block, prefer...  48.4 us
    dynamic_slice x12, local copies, waits for them, and re-layouts, key_folding(): state_now, unused = lax.scan(update, state_now, (key_blocks, value_blocks))  41.6 us
    reduce_sum x6, other arithmetic, update(): totals = totals_prev * fading + jnp.sum(expd, axis=-1)  39.7 us
    dot_general x6, matrix products, update(): jnp.einsum('qhd,khd->qhk', query_heads, key_block, preferred_element_type...  38.5 us
    unnamed x49, local copies, waits for them, and re-layouts  19 us
    all_to_all x1, blocking collectives, shards(): lax.all_to_all(attended, 'blk', split_axis=0, concat_axis=1, tiled=True)  18.7 us
  transfers between devices with their start and end apart: 12, of which 8 were waited for; matrix products, arithmetic and copies ran while one was open for 4% of the time, Pallas kernels for 0%

commit v1 on v0

v1 whole, which is shorter than its diff:
```python
import functools
import math

import jax
import jax.numpy as jnp
from jax import lax
from jax.experimental import pallas as pl
from jax.experimental.pallas import tpu as pltpu
from jax.sharding import Mesh
from jax.sharding import PartitionSpec as P

HEAD_DIM = 128
LAT = 16
C1 = 384
F = 4
EPSILON = 1e-06

SEQ = ("y", "zh", "core")
BLK = ("zl", "x")
HEAD = ("y", "zh", "zl")
SHARD = SEQ + BLK

TILE = 512
SUB = 256
CHUNK = 768
NT = (((1,), (1,)), ((), ()))


def lane_max(s):
    t = s[:, :128]
    for j in range(1, s.shape[1] // 128):
        t = jnp.maximum(t, s[:, j * 128 : (j + 1) * 128])
    return jnp.max(t, axis=1, keepdims=True)


def flash_kernel(first, last, n_kv, half, *refs):
    qo_ref, qx_ref = refs[:2]
    kv_refs = refs[2 : 2 + n_kv]
    refs = refs[2 + n_kv :]
    if not first:
        st_ref, refs = refs[0], refs[1:]
    if last:
        w_ref, own_ref, oth_ref = refs
    else:
        (so_ref,) = refs
    i = pl.program_id(0)
    scale = math.log2(math.e) / math.sqrt(HEAD_DIM)
    qf = jnp.where(i < half, qo_ref[...], qx_ref[...]).astype(jnp.float32) * scale
    q_hi = qf.astype(jnp.bfloat16)
    q_lo = (qf - q_hi.astype(jnp.float32)).astype(jnp.bfloat16)
    q = jnp.concatenate([q_hi, q_lo], axis=1)
    subs = TILE // SUB
    tops, accs = [], []
    for r in range(subs):
        if first:
            tops.append(jnp.full((SUB, 128), -1e30, jnp.float32))
            accs.append(jnp.zeros((SUB, 256), jnp.float32))
        else:
            st = st_ref[pl.ds(r * SUB, SUB), :]
            acc_l = st[:, 128:]
            lane = lax.broadcasted_iota(jnp.int32, (SUB, 128), 1)
            total = jnp.max(jnp.where(lane < 64, acc_l, -1e30), axis=1, keepdims=True)
            top = jnp.max(jnp.where(lane < 64, -1e30, acc_l), axis=1, keepdims=True)
            tops.append(jnp.broadcast_to(top, (SUB, 128)))
            accs.append(
                jnp.concatenate([st[:, :128], jnp.broadcast_to(total, (SUB, 128))], axis=1)
            )
    items = [
        (r, b, c)
        for b in range(n_kv)
        for c in range(kv_refs[b].shape[0] // CHUNK)
        for r in range(subs)
    ]
    ones = jnp.ones((CHUNK, 128), jnp.bfloat16)

    def score(item):
        r, b, c = item
        k = kv_refs[b][pl.ds(c * CHUNK, CHUNK), :128]
        return lax.dot_general(
            q[r * SUB : (r + 1) * SUB],
            jnp.concatenate([k, k], axis=1),
            NT,
            preferred_element_type=jnp.float32,
        )

    s = score(items[0])
    for n, (r, b, c) in enumerate(items):
        following = score(items[n + 1]) if n + 1 < len(items) else None
        top = jnp.maximum(tops[r], lane_max(s))
        p = jnp.exp2(s - top[:, :1]).astype(jnp.bfloat16)
        fade = jnp.exp2(tops[r] - top)
        v = jnp.concatenate([kv_refs[b][pl.ds(c * CHUNK, CHUNK), 128:], ones], axis=1)
        accs[r] = accs[r] * jnp.concatenate([fade, fade], axis=1) + jnp.dot(
            p, v, preferred_element_type=jnp.float32
        )
        tops[r] = top
        s = following
    lane = lax.broadcasted_iota(jnp.int32, (SUB, 128), 1)
    outs = []
    for r in range(subs):
        if last:
            total = accs[r][:, 128:]
            mixed = (accs[r][:, :128] / total).astype(jnp.bfloat16)
            u = jnp.dot(mixed, w_ref[...], preferred_element_type=jnp.float32)
            outs.append(jnp.where(lane < 64, u, tops[r] + jnp.log2(total)))
        else:
            so_ref[pl.ds(r * SUB, SUB), :] = jnp.concatenate(
                [accs[r][:, :128], jnp.where(lane < 64, accs[r][:, 128:], tops[r])], axis=1
            )
    if last:

        @pl.when(i < half)
        def _():
            for r in range(subs):
                own_ref[pl.ds(r * SUB, SUB), :] = outs[r]

        @pl.when(i >= half)
        def _():
            for r in range(subs):
                oth_ref[pl.ds(r * SUB, SUB), :] = outs[r]


def flash(q_own, q_oth, kvs, state=None, weight=None):
    first, last = state is None, weight is not None
    rows = q_own.shape[0]
    half = rows // TILE
    keys = sum(kv.shape[0] for kv in kvs)

    def lower(i):
        return (jnp.minimum(i, half - 1), 0)

    def upper(i):
        return (jnp.maximum(i - half, 0), 0)

    in_specs = [pl.BlockSpec((TILE, 128), lower), pl.BlockSpec((TILE, 128), upper)]
    in_specs += [pl.BlockSpec(kv.shape, lambda i: (0, 0)) for kv in kvs]
    args = [q_own, q_oth, *kvs]
    if not first:
        in_specs.append(pl.BlockSpec((TILE, 256), lambda i: (i, 0)))
        args.append(state)
    if last:
        in_specs.append(pl.BlockSpec(weight.shape, lambda i: (0, 0)))
        args.append(weight)
        out_specs = [pl.BlockSpec((TILE, 128), lower), pl.BlockSpec((TILE, 128), upper)]
        out_shape = [jax.ShapeDtypeStruct((rows, 128), jnp.float32)] * 2
    else:
        out_specs = pl.BlockSpec((TILE, 256), lambda i: (i, 0))
        out_shape = jax.ShapeDtypeStruct((2 * rows, 256), jnp.float32)
    return pl.pallas_call(
        functools.partial(flash_kernel, first, last, len(kvs), half),
        grid=(2 * half,),
        in_specs=in_specs,
        out_specs=out_specs,
        out_shape=out_shape,
        compiler_params=pltpu.CompilerParams(vmem_limit_bytes=40 << 20),
        cost_estimate=pl.CostEstimate(
            flops=2 * rows * keys * 512 * 2,
            bytes_accessed=rows * 4096,
            transcendentals=2 * rows * keys,
        ),
    )(*args)


def conv_kernel(x_ref, w_ref, base_ref, out_ref, acc_ref):
    step = pl.program_id(0)
    t, u = step // 3, step % 3

    @pl.when(step == 0)
    def _():
        acc_ref[...] = base_ref[...]

    total = acc_ref[...]
    for v in range(3):
        rows = x_ref[v, pl.ds(t, 4), pl.ds(u, 4)].reshape(256, C1)
        total = total + jnp.dot(
            rows, w_ref[0, pl.ds(v * C1, C1), :], preferred_element_type=jnp.float32
        )
    acc_ref[...] = total

    @pl.when(step == 8)
    def _():
        out_ref[...] = total.astype(jnp.bfloat16)


def conv_mid(shifted, weight, base):
    return pl.pallas_call(
        conv_kernel,
        grid=(9,),
        in_specs=[
            pl.BlockSpec(shifted.shape, lambda i: (0, 0, 0, 0, 0)),
            pl.BlockSpec((1, 3 * C1, C1), lambda i: (i, 0, 0)),
            pl.BlockSpec((256, C1), lambda i: (0, 0)),
        ],
        out_specs=pl.BlockSpec((256, C1), lambda i: (0, 0)),
        out_shape=jax.ShapeDtypeStruct((256, C1), jnp.bfloat16),
        scratch_shapes=[pltpu.VMEM((256, C1), jnp.float32)],
        compiler_params=pltpu.CompilerParams(vmem_limit_bytes=32 << 20),
        cost_estimate=pl.CostEstimate(
            flops=2 * 256 * 27 * C1 * C1, bytes_accessed=10 << 20, transcendentals=0
        ),
    )(shifted, weight.reshape(9, 3 * C1, C1), base)


def along(axis, step):
    count = lax.axis_size(axis)
    return [(i, i + step) for i in range(count) if 0 <= i + step < count]


def with_halo(cells, sides, width):
    for axis, dim in sides:
        head = lax.slice_in_dim(cells, 0, width, axis=dim)
        tail = lax.slice_in_dim(cells, cells.shape[dim] - width, cells.shape[dim], axis=dim)
        cells = jnp.concatenate(
            [
                lax.ppermute(tail, axis, along(axis, 1)),
                cells,
                lax.ppermute(head, axis, along(axis, -1)),
            ],
            axis=dim,
        )
    return cells


def attention(query_vectors, key_vectors, value_vectors, weight_head):
    tokens = query_vectors.shape[0]
    heads = lax.axis_size(HEAD)
    packed = jnp.concatenate(
        [
            a.reshape(tokens, heads, HEAD_DIM)
            for a in (query_vectors, key_vectors, value_vectors)
        ],
        axis=2,
    ).transpose(1, 0, 2)
    moved = lax.all_to_all(packed, HEAD, split_axis=0, concat_axis=0, tiled=True)
    moved = moved.reshape(heads * tokens, 3 * HEAD_DIM)
    q_own, kv = moved[:, :128], moved[:, 128:]
    swap = [(0, 1), (1, 0)]
    right = [(i, (i + 1) % 4) for i in range(4)]
    left = [((i + 1) % 4, i) for i in range(4)]
    q_oth = lax.ppermute(q_own, "core", swap)
    mid = kv.shape[0] // 2
    a, b = kv[:mid], kv[mid:]
    left_a = lax.ppermute(a, "x", right)
    right_b = lax.ppermute(b, "x", left)
    state = flash(q_own, q_oth, [kv])
    left_b = lax.ppermute(b, "x", right)
    right_a = lax.ppermute(a, "x", left)
    state = flash(q_own, q_oth, [left_a, right_b], state)
    far_a = lax.ppermute(left_a, "x", right)
    far_b = lax.ppermute(right_b, "x", left)
    state = flash(q_own, q_oth, [left_b, right_a], state)
    head = lax.axis_index(HEAD)
    weight = lax.dynamic_slice_in_dim(weight_head, head * HEAD_DIM, HEAD_DIM, axis=0)
    weight = jnp.pad(weight, ((0, 0), (0, 64)))
    own, oth = flash(q_own, q_oth, [far_a, far_b], state, weight)
    oth = lax.ppermute(oth, "core", swap)
    share = 1.0 / (1.0 + jnp.exp2(oth[:, 64:] - own[:, 64:]))
    partial = own[:, :64] * share + oth[:, :64] * (1.0 - share)
    partial = partial.astype(jnp.bfloat16).reshape(heads, tokens, 64)
    parts = lax.all_to_all(partial, HEAD, split_axis=0, concat_axis=0, tiled=True)
    return jnp.sum(parts.astype(jnp.float32), axis=0)


def shards(
    query_vectors,
    key_vectors,
    value_vectors,
    weight_head,
    noisy_latent,
    noise_level,
    latent_mean,
    latent_scale,
    cache_in,
    weight_in,
    bias_in,
    norm_gain,
    cache_mid,
    weight_mid,
    bias_mid,
):
    sides = ((SEQ, 1), (BLK, 2))
    noisy = with_halo(noisy_latent, sides, 2)
    cache_first = with_halo(cache_in, sides, 2)
    cache_second = with_halo(cache_mid, sides, 1)

    velocity = attention(query_vectors, key_vectors, value_vectors, weight_head)

    tiles = lax.axis_size(BLK)
    cols = velocity.shape[0] // tiles
    wide = jnp.pad(velocity, ((1, 1), (0, 0)))
    pieces = jnp.stack([wide[k * cols : k * cols + cols + 2] for k in range(tiles)])
    patch = lax.all_to_all(pieces, BLK, split_axis=0, concat_axis=0, tiled=True)
    patch = patch.reshape(F, 2, cols + 2, 64)
    patch = jnp.concatenate(
        [
            lax.ppermute(patch[:, 1:], SEQ, along(SEQ, 1)),
            patch,
            lax.ppermute(patch[:, :1], SEQ, along(SEQ, -1)),
        ],
        axis=1,
    )
    grid = patch.reshape(F, 4, cols + 2, 2, 2, LAT).transpose(0, 1, 3, 2, 4, 5)
    grid = grid.reshape(F, 8, 2 * cols + 4, LAT)
    rows, width = noisy_latent.shape[1], noisy_latent.shape[2]
    denoised = noisy - noise_level[0] * grid
    row_at = lax.axis_index(SEQ) * rows - 2 + jnp.arange(rows + 4)
    col_at = lax.axis_index(BLK) * width - 2 + jnp.arange(width + 4)
    row_ok = (row_at >= 0) & (row_at < lax.axis_size(SEQ) * rows)
    col_ok = (col_at >= 0) & (col_at < tiles * width)
    inside = row_ok[:, None, None] & col_ok[None, :, None]
    latent = jnp.where(inside, denoised * latent_scale + latent_mean, 0.0).astype(jnp.bfloat16)

    stacked = jnp.concatenate([cache_first, latent], axis=0)
    taps = [
        stacked[t : t + F, u : u + rows + 2, v : v + width + 2]
        for t in range(3)
        for u in range(3)
        for v in range(3)
    ]
    gathered = jnp.concatenate(taps, axis=-1).reshape(F * (rows + 2) * (width + 2), -1)
    first = jnp.dot(
        gathered, weight_in.reshape(-1, C1), preferred_element_type=jnp.float32
    )
    first = (first + bias_in).reshape(F, rows + 2, width + 2, C1)
    power = jnp.mean(first * first, axis=-1, keepdims=True)
    active = jax.nn.silu(first * lax.rsqrt(power + EPSILON) * norm_gain)
    active = jnp.where(inside[1:-1, 1:-1], active, 0.0).astype(jnp.bfloat16)
    padded = jnp.concatenate([cache_second, active], axis=0)
    padded = jnp.pad(padded, ((0, 0), (0, 0), (0, 4), (0, 0)))
    shifted = jnp.stack([padded[:, :, v : v + 16] for v in range(3)])
    base = first[:, 1:-1, 1:-1] + bias_mid
    base = jnp.pad(base, ((0, 0), (0, 0), (0, 4), (0, 0))).reshape(256, C1)
    features = conv_mid(shifted, weight_mid, base)
    features = features.reshape(F, rows, 16, C1)[:, :, :width]
    return (denoised[:, 2:-2, 2:-2], features)


def solution(mesh):
    inner = Mesh(mesh.devices.reshape(4, 4, 2, 2, 4), SHARD)
    tokens, tile = P(SHARD, None), P(None, SEQ, BLK, None)
    in_specs = (
        tokens,
        tokens,
        tokens,
        P(),
        tile,
        P(),
        P(),
        P(),
        tile,
        P(),
        P(),
        P(),
        tile,
        P(),
        P(),
    )
    return jax.shard_map(
        shards, mesh=inner, in_specs=in_specs, out_specs=(tile, tile), check_vma=False
    )
```

time: 528 us -> 175 us (0.33)
  the two profiles are of different devices: /device:TPU:1 before, /device:TPU:40 now
where the time goes in v1:
time: 175 us; the launch traced here: 174 us
  starting transfers between devices  84.6 us (48%)
  Pallas kernels  36 us (21%)
  waiting for transfers between devices  29.9 us (17%)
  local copies, waits for them, and re-layouts  15.2 us (9%)
  other arithmetic  4.37 us (2%)
  between operations  2.16 us (1%)
    ppermute x6, starting transfers between devices, with_halo(): lax.ppermute(head, axis, along(axis, -1))  35 us
    pallas_call x4, Pallas kernels, flash(): pl.pallas_call(functools.partial(flash_kernel, first, last, len(kvs), hal...  31.3 us
    ppermute x6, starting transfers between devices, with_halo(): lax.ppermute(tail, axis, along(axis, 1))  12.5 us
    all_to_all x1, starting transfers between devices, attention(): lax.all_to_all(packed, HEAD, split_axis=0, concat_axis=0, tiled=True)  11.4 us
    ppermute x6, waiting for transfers between devices, with_halo(): lax.ppermute(tail, axis, along(axis, 1))  10.3 us
    all_to_all x1, waiting for transfers between devices, attention(): lax.all_to_all(partial, HEAD, split_axis=0, concat_axis=0, tiled=True)  8.18 us
    unnamed x50, local copies, waits for them, and re-layouts  7.33 us
    ppermute x1, starting transfers between devices, shards(): lax.ppermute(patch[:, :1], SEQ, along(SEQ, -1))  6.65 us
  transfers between devices with their start and end apart: 25, of which 7 were waited for; matrix products, arithmetic and copies ran while one was open for 6% of the time, Pallas kernels for 18%

profile of v1, /device:TPU:40, one launch (start us, length us, event | category | flops | bytes accessed | tf_op | source)
XLA Modules:
  0.0 173.6 jit_solution(6501881920967744133)
XLA Ops:
  4.2 11.4 %all-to-all-start = ((bf16[32,48,384]{2,1,0:T(8,128)(2,1)}), bf16[32,48,384]{2,1,0:T(8,128)(2,1)S(1)}, u32[]{:S(2)}, u32[]{:S(2)}) async-start(bf16[32,48,384]{2,1,0:T(8,128)(2,1)} %maximum_bitcast_fusion), calls=%async_computation | async-start | bytes 2359296 | tf_op jit(solution)/shard_map/all_to_all | solution.py:234
  17.6 6.7 %collective-permute-start.1 = (f32[4,2,12,16]{3,2,1,0:T(8,128)S(1)}, f32[4,2,12,16]{3,2,1,0:T(8,128)S(1)}, u32[]{:S(2)}, u32[]{:S(2)}) collective-permute-start(f32[4,2,12,16]{3,2,1,0:T(8,128)S(1)} %copy.66), channel_id=1, source_target_pairs={{8,0},{16,8},{24,16},{32,24},{40,32},{48,40},{56,48},{64,56},{72,6... | collective-permute-start | bytes 18440 | tf_op jit(solution)/shard_map/ppermute | solution.py:217
  26.3 6.7 %collective-permute-start.19 = (bf16[2,2,12,16]{3,2,1,0:T(8,128)(2,1)S(1)}, bf16[2,2,12,16]{3,2,1,0:T(8,128)(2,1)S(1)}, u32[]{:S(2)}, u32[]{:S(2)}) collective-permute-start(bf16[2,2,12,16]{3,2,1,0:T(8,128)(2,1)S(1)} %copy.68), channel_id=1, source_target_pairs={{8,0},{16,8},{24,16},{32,24},{40,32},{48,40},{56,48},{64,56},{72,6... | collective-permute-start | bytes 4616 | tf_op jit(solution)/shard_map/ppermute | solution.py:217
  34.1 10.2 %collective-permute-done.18 = bf16[2,2,12,16]{3,2,1,0:T(8,128)(2,1)S(1)} collective-permute-done((bf16[2,2,12,16]{3,2,1,0:T(8,128)(2,1)S(1)}, bf16[2,2,12,16]{3,2,1,0:T(8,128)(2,1)S(1)}, u32[]{:S(2)}, u32[]{:S(2)}) %collective-permute-start.18) | collective-permute-done | bytes 1568 | tf_op jit(solution)/shard_map/ppermute | solution.py:215
  44.4 2.4 %all-to-all-done = bf16[32,48,384]{2,1,0:T(8,128)(2,1)S(1)} async-done(((bf16[32,48,384]{2,1,0:T(8,128)(2,1)}), bf16[32,48,384]{2,1,0:T(8,128)(2,1)S(1)}, u32[]{:S(2)}, u32[]{:S(2)}) %all-to-all-start) | async-done | bytes 1179680 | tf_op jit(solution)/shard_map/all_to_all | solution.py:234
  48.7 2.8 %collective-permute-start.7 = (bf16[768,256]{1,0:T(8,128)(2,1)S(1)}, bf16[768,256]{1,0:T(8,128)(2,1)S(1)}, u32[]{:S(2)}, u32[]{:S(2)}) collective-permute-start(bf16[768,256]{1,0:T(8,128)(2,1)S(1)} %get-tuple-element.10), channel_id=1, source_target_pairs={{1,0},{2,1},{3,2},{0,3},{5,4},{6,5},{7,6},{4,7},{9,8},{10,9},{11,1... | collective-permute-start | bytes 1179656 | tf_op jit(solution)/shard_map/ppermute | solution.py:244
  51.4 7.6 %shard_map.158.refs_4_ = f32[3072,256]{1,0:T(8,128)S(1)} custom-call(bf16[1536,128]{1,0:T(8,128)(2,1)S(1)} %slice.271.refs_0_, bf16[1536,128]{1,0:T(8,128)(2,1)S(1)} %collective-permute-done.4.refs_1_, bf16[1536,256]{1,0:T(8,128)(2,1)S(1)} %slice.274.refs_2_), custom_call_target="tpu_custom_call" | custom-call | flops 4831838208 | bytes 6291456 | tf_op jit(solution)/shard_map/pallas_call | solution.py:149
  61.9 7.6 %shard_map.159.refs_4_ = f32[3072,256]{1,0:T(8,128)S(1)} custom-call(bf16[1536,128]{1,0:T(8,128)(2,1)S(1)} %slice.271.refs_0_, bf16[1536,128]{1,0:T(8,128)(2,1)S(1)} %collective-permute-done.4.refs_1_, bf16[768,256]{1,0:T(8,128)(2,1)S(1)} %collective-permute-done.5.refs_2_, bf16[768,256]{1,0:T(8,128)(2,1)S(1)} %collective-permute-done.7.refs_3_, ...), custom_call_target="tpu_custom_call" | custom-call | flops 4831838208 | bytes 6291456 | tf_op jit(solution)/shard_map/pallas_call | solution.py:149
  70.9 2.2 %collective-permute-done.9.refs_2_ = bf16[768,256]{1,0:T(8,128)(2,1)S(1)} collective-permute-done((bf16[768,256]{1,0:T(8,128)(2,1)S(1)}, bf16[768,256]{1,0:T(8,128)(2,1)S(1)}, u32[]{:S(2)}, u32[]{:S(2)}) %collective-permute-start.9) | collective-permute-done | bytes 393248 | tf_op jit(solution)/shard_map/ppermute | solution.py:246
  74.1 7.6 %shard_map.160.refs_4_ = f32[3072,256]{1,0:T(8,128)S(1)} custom-call(bf16[1536,128]{1,0:T(8,128)(2,1)S(1)} %slice.271.refs_0_, bf16[1536,128]{1,0:T(8,128)(2,1)S(1)} %collective-permute-done.4.refs_1_, bf16[768,256]{1,0:T(8,128)(2,1)S(1)} %collective-permute-done.9.refs_2_, bf16[768,256]{1,0:T(8,128)(2,1)S(1)} %collective-permute-done.10.refs_3_, ...), custom_call_target="tpu_custom_call" | custom-call | flops 4831838208 | bytes 6291456 | tf_op jit(solution)/shard_map/pallas_call | solution.py:149
  83.6 6.7 %collective-permute-start.15 = (bf16[2,1,12,384]{3,2,1,0:T(8,128)(2,1)S(1)}, bf16[2,1,12,384]{3,2,1,0:T(8,128)(2,1)S(1)}, u32[]{:S(2)}, u32[]{:S(2)}) collective-permute-start(bf16[2,1,12,384]{3,2,1,0:T(8,128)(2,1)S(1)} %copy.70), channel_id=1, source_target_pairs={{8,0},{16,8},{24,16},{32,24},{40,32},{48,40},{56,48},{64,56},{72,6... | collective-permute-start | bytes 55304 | tf_op jit(solution)/shard_map/ppermute | solution.py:217
  90.3 8.6 %shard_map.161 = (f32[1536,128]{1,0:T(8,128)S(1)}, f32[1536,128]{1,0:T(8,128)S(1)}) custom-call(bf16[1536,128]{1,0:T(8,128)(2,1)S(1)} %slice.271.refs_0_, bf16[1536,128]{1,0:T(8,128)(2,1)S(1)} %collective-permute-done.4.refs_1_, bf16[768,256]{1,0:T(8,128)(2,1)S(1)} %collective-permute-done.6.refs_2_, bf16[768,256]{1,0:T(8,128)(2,1)S(1)} %collective-permute-done.8.refs_3_, ...), custom_call_target="tpu_custom_call" | custom-call | flops 4831838208 | bytes 6291456 | tf_op jit(solution)/shard_map/pallas_call | solution.py:149
  99.2 2.9 %collective-permute-start.20 = (bf16[2,8,2,16]{3,2,1,0:T(2,128)(2,1)S(1)}, bf16[2,8,2,16]{3,2,1,0:T(2,128)(2,1)S(1)}, u32[]{:S(2)}, u32[]{:S(2)}) collective-permute-start(bf16[2,8,2,16]{3,2,1,0:T(2,128)(2,1)S(1)} %get-tuple-element.50), channel_id=1, source_target_pairs={{0,1},{1,2},{2,3},{3,4},{4,5},{5,6},{6,7},{8,9},{9,10},{10,11},{11... | collective-permute-start | bytes 3080 | tf_op jit(solution)/shard_map/ppermute | solution.py:215
  102.2 5.0 %collective-permute-start.21 = (bf16[2,8,2,16]{3,2,1,0:T(2,128)(2,1)S(1)}, bf16[2,8,2,16]{3,2,1,0:T(2,128)(2,1)S(1)}, u32[]{:S(2)}, u32[]{:S(2)}) collective-permute-start(bf16[2,8,2,16]{3,2,1,0:T(2,128)(2,1)S(1)} %get-tuple-element.51), channel_id=1, source_target_pairs={{1,0},{2,1},{3,2},{4,3},{5,4},{6,5},{7,6},{9,8},{10,9},{11,10},{12... | collective-permute-start | bytes 3080 | tf_op jit(solution)/shard_map/ppermute | solution.py:217
  108.7 5.3 %all-to-all-start.1 = ((bf16[32,2,1536]{2,1,0:T(2,128)(2,1)}), bf16[32,2,1536]{2,1,0:T(2,128)(2,1)S(1)}, u32[]{:S(2)}, u32[]{:S(2)}) async-start(bf16[32,2,1536]{2,1,0:T(2,128)(2,1)} %reshape.154), calls=%async_computation.1 | async-start | bytes 393216 | tf_op jit(solution)/shard_map/all_to_all | solution.py:260
  116.0 8.2 %all-to-all-done.1 = bf16[32,2,1536]{2,1,0:T(2,128)(2,1)S(1)} async-done(((bf16[32,2,1536]{2,1,0:T(2,128)(2,1)}), bf16[32,2,1536]{2,1,0:T(2,128)(2,1)S(1)}, u32[]{:S(2)}, u32[]{:S(2)}) %all-to-all-start.1) | async-done | bytes 196640 | tf_op jit(solution)/shard_map/all_to_all | solution.py:260
  125.4 3.8 %all-to-all-start.2 = ((f32[8,1,512]{2,1,0:T(1,128)}), f32[8,1,512]{2,1,0:T(1,128)S(1)}, u32[]{:S(2)}, u32[]{:S(2)}) async-start(f32[8,1,512]{2,1,0:T(1,128)} %reshape.156), calls=%async_computation.2 | async-start | bytes 32768 | tf_op jit(solution)/shard_map/all_to_all | solution.py:292
  129.2 4.8 %all-to-all-done.2 = f32[8,1,512]{2,1,0:T(1,128)S(1)} async-done(((f32[8,1,512]{2,1,0:T(1,128)}), f32[8,1,512]{2,1,0:T(1,128)S(1)}, u32[]{:S(2)}, u32[]{:S(2)}) %all-to-all-start.2) | async-done | bytes 16416 | tf_op jit(solution)/shard_map/all_to_all | solution.py:292
  137.2 6.7 %collective-permute-start.13 = (f32[4,1,8,64]{3,2,1,0:T(8,128)S(1)}, f32[4,1,8,64]{3,2,1,0:T(8,128)S(1)}, u32[]{:S(2)}, u32[]{:S(2)}) collective-permute-start(f32[4,1,8,64]{3,2,1,0:T(8,128)S(1)} %get-tuple-element.53), channel_id=1, source_target_pairs={{8,0},{16,8},{24,16},{32,24},{40,32},{48,40},{56,48},{64,56},{72,6... | collective-permute-start | bytes 24584 | tf_op jit(solution)/shard_map/ppermute | solution.py:298
  144.0 4.0 %collective-permute-start.3 = (f32[4,8,2,16]{3,2,1,0:T(2,128)S(1)}, f32[4,8,2,16]{3,2,1,0:T(2,128)S(1)}, u32[]{:S(2)}, u32[]{:S(2)}) collective-permute-start(f32[4,8,2,16]{3,2,1,0:T(2,128)S(1)} %get-tuple-element.16), channel_id=1, source_target_pairs={{1,0},{2,1},{3,2},{4,3},{5,4},{6,5},{7,6},{9,8},{10,9},{11,10},{12... | collective-permute-start | bytes 12296 | tf_op jit(solution)/shard_map/ppermute | solution.py:217
  150.4 6.0 %collective-permute-start.17 = (bf16[2,6,1,384]{3,2,1,0:T(2,128)(2,1)S(1)}, bf16[2,6,1,384]{3,2,1,0:T(2,128)(2,1)}, u32[]{:S(2)}, u32[]{:S(2)}) collective-permute-start(bf16[2,6,1,384]{3,2,1,0:T(2,128)(2,1)S(1)} %get-tuple-element.36), channel_id=1, source_target_pairs={{1,0},{2,1},{3,2},{4,3},{5,4},{6,5},{7,6},{9,8},{10,9},{11,10},{12... | collective-permute-start | bytes 27656 | tf_op jit(solution)/shard_map/ppermute | solution.py:217
  157.8 2.4 %concatenate.52 = bf16[4,6,14,432]{3,2,1,0:T(8,128)(2,1)S(1)} concatenate(bf16[4,6,14,16]{3,2,1,0:T(8,128)(2,1)S(1)} %get-tuple-element.34, bf16[4,6,14,16]{3,2,1,0:T(8,128)(2,1)S(1)} %get-tuple-element.33, bf16[4,6,14,16]{3,2,1,0:T(8,128)(2,1)S(1)} %get-tuple-element.32, bf16[4,6,14,16]{3,2,1,0:T(8,128)(2,1)S(1)} %get-tuple-element.31, ...), dimensions={3} | concatenate | bytes 580608 | tf_op jit(solution)/shard_map/concatenate | solution.py:320
  164.2 3.3 %copy-done.1 = bf16[3,3,3,384,384]{4,3,2,1,0:T(8,128)(2,1)S(1)} copy-done((bf16[3,3,3,384,384]{4,3,2,1,0:T(8,128)(2,1)S(1)}, bf16[3,3,3,384,384]{4,3,2,1,0:T(8,128)(2,1)}, u32[]{:S(2)}) %copy-start.1) | copy-done | bytes 7962648
  167.4 4.8 %shard_map.162 = bf16[256,384]{1,0:T(8,128)(2,1)S(1)} custom-call(bf16[3,6,6,16,384]{4,3,2,1,0:T(8,128)(2,1)S(1)} %pad_maximum_fusion.x_ref, bf16[9,1152,384]{2,1,0:T(8,128)(2,1)S(1)} %bitcast.78, f32[256,384]{1,0:T(8,128)S(1)} %bitcast.79), custom_call_target="tpu_custom_call" | custom-call | flops 2038431744 | bytes 10485760 | tf_op jit(solution)/shard_map/pallas_call | solution.py:186
  (131 shorter events, 34.2 us)
Async XLA Ops:
  4.2 42.6 %all-to-all-start = ((bf16[32,48,384]{2,1,0:T(8,128)(2,1)}), bf16[32,48,384]{2,1,0:T(8,128)(2,1)S(1)}, u32[]{:S(2)}, u32[]{:S(2)}) async-start(bf16[32,48,384]{2,1,0:T(8,128)(2,1)} %maximum_bitcast_fusion), calls=%async_computation | async-start | bytes 2359296 | tf_op jit(solution)/shard_map/all_to_all | solution.py:234
  15.7 83.5 %collective-permute-start = (f32[4,2,12,16]{3,2,1,0:T(8,128)S(1)}, f32[4,2,12,16]{3,2,1,0:T(8,128)S(1)}, u32[]{:S(2)}, u32[]{:S(2)}) collective-permute-start(f32[4,2,12,16]{3,2,1,0:T(8,128)S(1)} %copy.65), channel_id=1, source_target_pairs={{0,8},{8,16},{16,24},{24,32},{32,40},{40,48},{48,56},{56,64},{64,7... | collective-permute-start | bytes 18440 | tf_op jit(solution)/shard_map/ppermute | solution.py:215
  17.6 84.5 %collective-permute-start.1 = (f32[4,2,12,16]{3,2,1,0:T(8,128)S(1)}, f32[4,2,12,16]{3,2,1,0:T(8,128)S(1)}, u32[]{:S(2)}, u32[]{:S(2)}) collective-permute-start(f32[4,2,12,16]{3,2,1,0:T(8,128)S(1)} %copy.66), channel_id=1, source_target_pairs={{8,0},{16,8},{24,16},{32,24},{40,32},{48,40},{56,48},{64,56},{72,6... | collective-permute-start | bytes 18440 | tf_op jit(solution)/shard_map/ppermute | solution.py:217
  24.3 20.0 %collective-permute-start.18 = (bf16[2,2,12,16]{3,2,1,0:T(8,128)(2,1)S(1)}, bf16[2,2,12,16]{3,2,1,0:T(8,128)(2,1)S(1)}, u32[]{:S(2)}, u32[]{:S(2)}) collective-permute-start(bf16[2,2,12,16]{3,2,1,0:T(8,128)(2,1)S(1)} %copy.67), channel_id=1, source_target_pairs={{0,8},{8,16},{16,24},{24,32},{32,40},{40,48},{48,56},{56,64},{64,7... | collective-permute-start | bytes 4616 | tf_op jit(solution)/shard_map/ppermute | solution.py:215
  26.3 72.6 %collective-permute-start.19 = (bf16[2,2,12,16]{3,2,1,0:T(8,128)(2,1)S(1)}, bf16[2,2,12,16]{3,2,1,0:T(8,128)(2,1)S(1)}, u32[]{:S(2)}, u32[]{:S(2)}) collective-permute-start(bf16[2,2,12,16]{3,2,1,0:T(8,128)(2,1)S(1)} %copy.68), channel_id=1, source_target_pairs={{8,0},{16,8},{24,16},{32,24},{40,32},{48,40},{56,48},{64,56},{72,6... | collective-permute-start | bytes 4616 | tf_op jit(solution)/shard_map/ppermute | solution.py:217
  47.1 12.8 %collective-permute-start.5 = (bf16[768,256]{1,0:T(8,128)(2,1)S(1)}, bf16[768,256]{1,0:T(8,128)(2,1)S(1)}, u32[]{:S(2)}, u32[]{:S(2)}) collective-permute-start(bf16[768,256]{1,0:T(8,128)(2,1)S(1)} %get-tuple-element.11), channel_id=1, source_target_pairs={{0,1},{1,2},{2,3},{3,0},{4,5},{5,6},{6,7},{7,4},{8,9},{9,10},{10,1... | collective-permute-start | bytes 1179656 | tf_op jit(solution)/shard_map/ppermute | solution.py:243
  48.7 12.8 %collective-permute-start.7 = (bf16[768,256]{1,0:T(8,128)(2,1)S(1)}, bf16[768,256]{1,0:T(8,128)(2,1)S(1)}, u32[]{:S(2)}, u32[]{:S(2)}) collective-permute-start(bf16[768,256]{1,0:T(8,128)(2,1)S(1)} %get-tuple-element.10), channel_id=1, source_target_pairs={{1,0},{2,1},{3,2},{0,3},{5,4},{6,5},{7,6},{4,7},{9,8},{10,9},{11,1... | collective-permute-start | bytes 1179656 | tf_op jit(solution)/shard_map/ppermute | solution.py:244
  59.9 10.7 %collective-permute-start.10 = (bf16[768,256]{1,0:T(8,128)(2,1)S(1)}, bf16[768,256]{1,0:T(8,128)(2,1)S(1)}, u32[]{:S(2)}, u32[]{:S(2)}) collective-permute-start(bf16[768,256]{1,0:T(8,128)(2,1)S(1)} %get-tuple-element.11), channel_id=1, source_target_pairs={{1,0},{2,1},{3,2},{0,3},{5,4},{6,5},{7,6},{4,7},{9,8},{10,9},{11,1... | collective-permute-start | bytes 1179656 | tf_op jit(solution)/shard_map/ppermute | solution.py:247
  61.4 11.7 %collective-permute-start.9 = (bf16[768,256]{1,0:T(8,128)(2,1)S(1)}, bf16[768,256]{1,0:T(8,128)(2,1)S(1)}, u32[]{:S(2)}, u32[]{:S(2)}) collective-permute-start(bf16[768,256]{1,0:T(8,128)(2,1)S(1)} %get-tuple-element.10), channel_id=1, source_target_pairs={{0,1},{1,2},{2,3},{3,0},{4,5},{5,6},{6,7},{7,4},{8,9},{9,10},{10,1... | collective-permute-start | bytes 1179656 | tf_op jit(solution)/shard_map/ppermute | solution.py:246
  70.6 11.1 %collective-permute-start.6 = (bf16[768,256]{1,0:T(8,128)(2,1)S(1)}, bf16[768,256]{1,0:T(8,128)(2,1)S(1)}, u32[]{:S(2)}, u32[]{:S(2)}) collective-permute-start(bf16[768,256]{1,0:T(8,128)(2,1)S(1)} %collective-permute-done.5.refs_2_), channel_id=1, source_target_pairs={{0,1},{1,2},{2,3},{3,0},{4,5},{5,6},{6,7},{7,4},{8,9},{9,10},{10,1... | collective-permute-start | bytes 1179656 | tf_op jit(solution)/shard_map/ppermute | solution.py:249
  73.1 10.5 %collective-permute-start.8 = (bf16[768,256]{1,0:T(8,128)(2,1)S(1)}, bf16[768,256]{1,0:T(8,128)(2,1)S(1)}, u32[]{:S(2)}, u32[]{:S(2)}) collective-permute-start(bf16[768,256]{1,0:T(8,128)(2,1)S(1)} %collective-permute-done.7.refs_3_), channel_id=1, source_target_pairs={{1,0},{2,1},{3,2},{0,3},{5,4},{6,5},{7,6},{4,7},{9,8},{10,9},{11,1... | collective-permute-start | bytes 1179656 | tf_op jit(solution)/shard_map/ppermute | solution.py:250
  81.7 34.2 %collective-permute-start.14 = (bf16[2,1,12,384]{3,2,1,0:T(8,128)(2,1)S(1)}, bf16[2,1,12,384]{3,2,1,0:T(8,128)(2,1)S(1)}, u32[]{:S(2)}, u32[]{:S(2)}) collective-permute-start(bf16[2,1,12,384]{3,2,1,0:T(8,128)(2,1)S(1)} %copy.69), channel_id=1, source_target_pairs={{0,8},{8,16},{16,24},{24,32},{32,40},{40,48},{48,56},{56,64},{64,7... | collective-permute-start | bytes 55304 | tf_op jit(solution)/shard_map/ppermute | solution.py:215
  83.6 45.5 %collective-permute-start.15 = (bf16[2,1,12,384]{3,2,1,0:T(8,128)(2,1)S(1)}, bf16[2,1,12,384]{3,2,1,0:T(8,128)(2,1)S(1)}, u32[]{:S(2)}, u32[]{:S(2)}) collective-permute-start(bf16[2,1,12,384]{3,2,1,0:T(8,128)(2,1)S(1)} %copy.70), channel_id=1, source_target_pairs={{8,0},{16,8},{24,16},{32,24},{40,32},{48,40},{56,48},{64,56},{72,6... | collective-permute-start | bytes 55304 | tf_op jit(solution)/shard_map/ppermute | solution.py:217
  98.9 8.4 %collective-permute-start.11 = (f32[1536,128]{1,0:T(8,128)S(1)}, f32[1536,128]{1,0:T(8,128)S(1)}, u32[]{:S(2)}, u32[]{:S(2)}) collective-permute-start(f32[1536,128]{1,0:T(8,128)S(1)} %get-tuple-element.5), channel_id=1, source_target_pairs={{0,8},{8,0},{1,9},{9,1},{2,10},{10,2},{3,11},{11,3},{4,12},{12,4},... | collective-permute-start | bytes 2359304 | tf_op jit(solution)/shard_map/ppermute | solution.py:256
  99.2 58.2 %collective-permute-start.20 = (bf16[2,8,2,16]{3,2,1,0:T(2,128)(2,1)S(1)}, bf16[2,8,2,16]{3,2,1,0:T(2,128)(2,1)S(1)}, u32[]{:S(2)}, u32[]{:S(2)}) collective-permute-start(bf16[2,8,2,16]{3,2,1,0:T(2,128)(2,1)S(1)} %get-tuple-element.50), channel_id=1, source_target_pairs={{0,1},{1,2},{2,3},{3,4},{4,5},{5,6},{6,7},{8,9},{9,10},{10,11},{11... | collective-permute-start | bytes 3080 | tf_op jit(solution)/shard_map/ppermute | solution.py:215
  102.2 55.3 %collective-permute-start.21 = (bf16[2,8,2,16]{3,2,1,0:T(2,128)(2,1)S(1)}, bf16[2,8,2,16]{3,2,1,0:T(2,128)(2,1)S(1)}, u32[]{:S(2)}, u32[]{:S(2)}) collective-permute-start(bf16[2,8,2,16]{3,2,1,0:T(2,128)(2,1)S(1)} %get-tuple-element.51), channel_id=1, source_target_pairs={{1,0},{2,1},{3,2},{4,3},{5,4},{6,5},{7,6},{9,8},{10,9},{11,10},{12... | collective-permute-start | bytes 3080 | tf_op jit(solution)/shard_map/ppermute | solution.py:217
  108.7 15.5 %all-to-all-start.1 = ((bf16[32,2,1536]{2,1,0:T(2,128)(2,1)}), bf16[32,2,1536]{2,1,0:T(2,128)(2,1)S(1)}, u32[]{:S(2)}, u32[]{:S(2)}) async-start(bf16[32,2,1536]{2,1,0:T(2,128)(2,1)} %reshape.154), calls=%async_computation.1 | async-start | bytes 393216 | tf_op jit(solution)/shard_map/all_to_all | solution.py:260
  114.0 36.4 %collective-permute-start.2 = (f32[4,8,2,16]{3,2,1,0:T(2,128)S(1)}, f32[4,8,2,16]{3,2,1,0:T(2,128)S(1)}, u32[]{:S(2)}, u32[]{:S(2)}) collective-permute-start(f32[4,8,2,16]{3,2,1,0:T(2,128)S(1)} %get-tuple-element.15), channel_id=1, source_target_pairs={{0,1},{1,2},{2,3},{3,4},{4,5},{5,6},{6,7},{8,9},{9,10},{10,11},{11... | collective-permute-start | bytes 12296 | tf_op jit(solution)/shard_map/ppermute | solution.py:215
  125.4 8.6 %all-to-all-start.2 = ((f32[8,1,512]{2,1,0:T(1,128)}), f32[8,1,512]{2,1,0:T(1,128)S(1)}, u32[]{:S(2)}, u32[]{:S(2)}) async-start(f32[8,1,512]{2,1,0:T(1,128)} %reshape.156), calls=%async_computation.2 | async-start | bytes 32768 | tf_op jit(solution)/shard_map/all_to_all | solution.py:292
  135.2 8.8 %collective-permute-start.12 = (f32[4,1,8,64]{3,2,1,0:T(8,128)S(1)}, f32[4,1,8,64]{3,2,1,0:T(8,128)S(1)}, u32[]{:S(2)}, u32[]{:S(2)}) collective-permute-start(f32[4,1,8,64]{3,2,1,0:T(8,128)S(1)} %get-tuple-element.52), channel_id=1, source_target_pairs={{0,8},{8,16},{16,24},{24,32},{32,40},{40,48},{48,56},{56,64},{64,7... | collective-permute-start | bytes 24584 | tf_op jit(solution)/shard_map/ppermute | solution.py:296
  137.2 10.9 %collective-permute-start.13 = (f32[4,1,8,64]{3,2,1,0:T(8,128)S(1)}, f32[4,1,8,64]{3,2,1,0:T(8,128)S(1)}, u32[]{:S(2)}, u32[]{:S(2)}) collective-permute-start(f32[4,1,8,64]{3,2,1,0:T(8,128)S(1)} %get-tuple-element.53), channel_id=1, source_target_pairs={{8,0},{16,8},{24,16},{32,24},{40,32},{48,40},{56,48},{64,56},{72,6... | collective-permute-start | bytes 24584 | tf_op jit(solution)/shard_map/ppermute | solution.py:298
  144.0 12.5 %collective-permute-start.3 = (f32[4,8,2,16]{3,2,1,0:T(2,128)S(1)}, f32[4,8,2,16]{3,2,1,0:T(2,128)S(1)}, u32[]{:S(2)}, u32[]{:S(2)}) collective-permute-start(f32[4,8,2,16]{3,2,1,0:T(2,128)S(1)} %get-tuple-element.16), channel_id=1, source_target_pairs={{1,0},{2,1},{3,2},{4,3},{5,4},{6,5},{7,6},{9,8},{10,9},{11,10},{12... | collective-permute-start | bytes 12296 | tf_op jit(solution)/shard_map/ppermute | solution.py:217
  148.1 14.1 %collective-permute-start.16 = (bf16[2,6,1,384]{3,2,1,0:T(2,128)(2,1)S(1)}, bf16[2,6,1,384]{3,2,1,0:T(2,128)(2,1)}, u32[]{:S(2)}, u32[]{:S(2)}) collective-permute-start(bf16[2,6,1,384]{3,2,1,0:T(2,128)(2,1)S(1)} %get-tuple-element.35), channel_id=1, source_target_pairs={{0,1},{1,2},{2,3},{3,4},{4,5},{5,6},{6,7},{8,9},{9,10},{10,11},{11... | collective-permute-start | bytes 27656 | tf_op jit(solution)/shard_map/ppermute | solution.py:215
  150.4 11.8 %collective-permute-start.17 = (bf16[2,6,1,384]{3,2,1,0:T(2,128)(2,1)S(1)}, bf16[2,6,1,384]{3,2,1,0:T(2,128)(2,1)}, u32[]{:S(2)}, u32[]{:S(2)}) collective-permute-start(bf16[2,6,1,384]{3,2,1,0:T(2,128)(2,1)S(1)} %get-tuple-element.36), channel_id=1, source_target_pairs={{1,0},{2,1},{3,2},{4,3},{5,4},{6,5},{7,6},{9,8},{10,9},{11,10},{12... | collective-permute-start | bytes 27656 | tf_op jit(solution)/shard_map/ppermute | solution.py:217
  (13 other events, 214.3 us)

commit v2 on v1

--- a/solution.py
+++ b/solution.py
@@ -17,7 +17,7 @@
 
 SEQ = ("y", "zh", "core")
 BLK = ("zl", "x")
-HEAD = ("y", "zh", "zl")
+HEAD = ("y", "zl", "x")
 SHARD = SEQ + BLK
 
 TILE = 512
@@ -132,8 +132,11 @@
     def upper(i):
         return (jnp.maximum(i - half, 0), 0)
 
-    in_specs = [pl.BlockSpec((TILE, 128), lower), pl.BlockSpec((TILE, 128), upper)]
-    in_specs += [pl.BlockSpec(kv.shape, lambda i: (0, 0)) for kv in kvs]
+    in_specs = [
+        pl.BlockSpec((TILE, 128), lambda i: (jnp.minimum(i, half - 1), 2)),
+        pl.BlockSpec((TILE, 128), upper),
+    ]
+    in_specs += [pl.BlockSpec((kv.shape[0], 256), lambda i: (0, 0)) for kv in kvs]
     args = [q_own, q_oth, *kvs]
     if not first:
         in_specs.append(pl.BlockSpec((TILE, 256), lambda i: (i, 0)))
@@ -206,59 +209,136 @@
     return [(i, i + step) for i in range(count) if 0 <= i + step < count]
 
 
-def with_halo(cells, sides, width):
-    for axis, dim in sides:
-        head = lax.slice_in_dim(cells, 0, width, axis=dim)
-        tail = lax.slice_in_dim(cells, cells.shape[dim] - width, cells.shape[dim], axis=dim)
-        cells = jnp.concatenate(
-            [
-                lax.ppermute(tail, axis, along(axis, 1)),
-                cells,
-                lax.ppermute(head, axis, along(axis, -1)),
-            ],
-            axis=dim,
+def swap_edges(parts, axis, dims, widths):
+    def cut(tail):
+        flat = []
+        for part, dim, width in zip(parts, dims, widths):
+            size = part.shape[dim]
+            start = size - width if tail else 0
+            flat.append(lax.slice_in_dim(part, start, start + width, axis=dim).reshape(-1))
+        return jnp.concatenate(flat).reshape(-1, 128)
+
+    before = lax.ppermute(cut(True), axis, along(axis, 1)).reshape(-1)
+    after = lax.ppermute(cut(False), axis, along(axis, -1)).reshape(-1)
+    wider, at = [], 0
+    for part, dim, width in zip(parts, dims, widths):
+        shape = list(part.shape)
+        shape[dim] = width
+        size = math.prod(shape)
+        wider.append(
+            jnp.concatenate(
+                [
+                    before[at : at + size].reshape(shape),
+                    part,
+                    after[at : at + size].reshape(shape),
+                ],
+                axis=dim,
+            )
         )
-    return cells
-
-
-def attention(query_vectors, key_vectors, value_vectors, weight_head):
-    tokens = query_vectors.shape[0]
-    heads = lax.axis_size(HEAD)
-    packed = jnp.concatenate(
-        [
-            a.reshape(tokens, heads, HEAD_DIM)
-            for a in (query_vectors, key_vectors, value_vectors)
+        at += size
+    return wider
+
+
+def input_halos(noisy, cache_in, cache_mid):
+    both = jnp.concatenate([cache_in.astype(jnp.float32), noisy], axis=0)
+    parts = [both, cache_mid.astype(jnp.float32)]
+    parts = swap_edges(parts, SEQ, (1, 1), (2, 1))
+    both, cache_mid = swap_edges(parts, BLK, (2, 2), (2, 1))
+    return both[2:], both[:2].astype(jnp.bfloat16), cache_mid.astype(jnp.bfloat16)
+
+
+def pack_kernel(q_ref, k_ref, v_ref, out_ref):
+    for h in range(out_ref.shape[0]):
+        lanes = pl.ds(h * HEAD_DIM, HEAD_DIM)
+        out_ref[h, :, 0:128] = k_ref[:, lanes]
+        out_ref[h, :, 128:256] = v_ref[:, lanes]
+        out_ref[h, :, 256:384] = q_ref[:, lanes]
+
+
+def pack(query_vectors, key_vectors, value_vectors):
+    tokens, width = query_vectors.shape
+    heads = width // HEAD_DIM
+    block = pl.BlockSpec((tokens, width // 4), lambda i: (0, i))
+    return pl.pallas_call(
+        pack_kernel,
+        grid=(4,),
+        in_specs=[block] * 3,
+        out_specs=pl.BlockSpec((heads // 4, tokens, 3 * HEAD_DIM), lambda i: (i, 0, 0)),
+        out_shape=jax.ShapeDtypeStruct((heads, tokens, 3 * HEAD_DIM), jnp.bfloat16),
+    )(query_vectors, key_vectors, value_vectors)
+
+
+def merge_kernel(own_ref, oth_ref, out_ref, vel_ref, piece_ref):
+    own, oth = own_ref[...], oth_ref[...]
+    gap = pltpu.roll(oth - own, 64, axis=1)
+    share = 1.0 / (1.0 + jnp.exp2(gap))
+    vel = own * share + oth * (1.0 - share)
+    lane = lax.broadcasted_iota(jnp.int32, vel.shape, 1)
+    vel_ref[...] = jnp.where(lane < 64, vel, pltpu.roll(vel, 64, axis=1))
+    low = lax.broadcasted_iota(jnp.int32, (16, 128), 1) < 64
+    zero = jnp.zeros((16, 128), jnp.float32)
+
+    def column(r, at):
+        if at < 0 or at >= 48:
+            return zero
+        return vel_ref[pl.ds(r * 48 + at, 16, stride=96), :]
+
+    for b in range(8):
+        for r in range(2):
+            for c in range(4):
+                at = 6 * b - 1 + c
+                both = jnp.where(low, column(r, at), column(r, at + 4))
+                for y in range(4):
+                    piece_ref[y, b, pl.ds(r * 16 + c * 4, 4), :] = both[y * 4 : y * 4 + 4]
+    out_ref[...] = piece_ref[...].astype(jnp.bfloat16)
+
+
+def merge(own, oth):
+    rows = own.shape[0]
+    whole = pl.BlockSpec((rows, 128), lambda: (0, 0))
+    shape = (4, 8, 32, 128)
+    return pl.pallas_call(
+        merge_kernel,
+        in_specs=[whole, whole],
+        out_specs=pl.BlockSpec(shape, lambda: (0, 0, 0, 0)),
+        out_shape=jax.ShapeDtypeStruct(shape, jnp.bfloat16),
+        scratch_shapes=[
+            pltpu.VMEM((rows, 128), jnp.float32),
+            pltpu.VMEM(shape, jnp.float32),
         ],
-        axis=2,
-    ).transpose(1, 0, 2)
+        compiler_params=pltpu.CompilerParams(vmem_limit_bytes=24 << 20),
+    )(own, oth)
+
+
+def attention(query_vectors, key_vectors, value_vectors, weight_head, work):
+    packed = pack(query_vectors, key_vectors, value_vectors)
+    heads, tokens = packed.shape[:2]
     moved = lax.all_to_all(packed, HEAD, split_axis=0, concat_axis=0, tiled=True)
     moved = moved.reshape(heads * tokens, 3 * HEAD_DIM)
-    q_own, kv = moved[:, :128], moved[:, 128:]
     swap = [(0, 1), (1, 0)]
     right = [(i, (i + 1) % 4) for i in range(4)]
     left = [((i + 1) % 4, i) for i in range(4)]
-    q_oth = lax.ppermute(q_own, "core", swap)
-    mid = kv.shape[0] // 2
-    a, b = kv[:mid], kv[mid:]
-    left_a = lax.ppermute(a, "x", right)
-    right_b = lax.ppermute(b, "x", left)
-    state = flash(q_own, q_oth, [kv])
-    left_b = lax.ppermute(b, "x", right)
-    right_a = lax.ppermute(a, "x", left)
-    state = flash(q_own, q_oth, [left_a, right_b], state)
-    far_a = lax.ppermute(left_a, "x", right)
-    far_b = lax.ppermute(right_b, "x", left)
-    state = flash(q_own, q_oth, [left_b, right_a], state)
+    mid = moved.shape[0] // 2
+    a, b = moved[:mid, :256], moved[mid:, :256]
+    left_a = lax.ppermute(a, "zh", right)
+    right_b = lax.ppermute(b, "zh", left)
+    q_oth = lax.ppermute(moved[:, 256:], "core", swap)
+    state = flash(moved, q_oth, [moved])
+    left_b = lax.ppermute(b, "zh", right)
+    right_a = lax.ppermute(a, "zh", left)
+    state = flash(moved, q_oth, [left_a, right_b], state)
+    far_a = lax.ppermute(left_a, "zh", right)
+    far_b = lax.ppermute(right_b, "zh", left)
+    state = flash(moved, q_oth, [left_b, right_a], state)
+    state, work = lax.optimization_barrier((state, work))
     head = lax.axis_index(HEAD)
     weight = lax.dynamic_slice_in_dim(weight_head, head * HEAD_DIM, HEAD_DIM, axis=0)
     weight = jnp.pad(weight, ((0, 0), (0, 64)))
-    own, oth = flash(q_own, q_oth, [far_a, far_b], state, weight)
+    own, oth = flash(moved, q_oth, [far_a, far_b], state, weight)
     oth = lax.ppermute(oth, "core", swap)
-    share = 1.0 / (1.0 + jnp.exp2(oth[:, 64:] - own[:, 64:]))
-    partial = own[:, :64] * share + oth[:, :64] * (1.0 - share)
-    partial = partial.astype(jnp.bfloat16).reshape(heads, tokens, 64)
+    partial = merge(own, oth).reshape(heads, 32, 128)
     parts = lax.all_to_all(partial, HEAD, split_axis=0, concat_axis=0, tiled=True)
-    return jnp.sum(parts.astype(jnp.float32), axis=0)
+    return jnp.sum(parts.astype(jnp.float32), axis=0), work
 
 
 def shards(
@@ -278,27 +358,16 @@
     weight_mid,
     bias_mid,
 ):
-    sides = ((SEQ, 1), (BLK, 2))
-    noisy = with_halo(noisy_latent, sides, 2)
-    cache_first = with_halo(cache_in, sides, 2)
-    cache_second = with_halo(cache_mid, sides, 1)
-
-    velocity = attention(query_vectors, key_vectors, value_vectors, weight_head)
-
-    tiles = lax.axis_size(BLK)
-    cols = velocity.shape[0] // tiles
-    wide = jnp.pad(velocity, ((1, 1), (0, 0)))
-    pieces = jnp.stack([wide[k * cols : k * cols + cols + 2] for k in range(tiles)])
-    patch = lax.all_to_all(pieces, BLK, split_axis=0, concat_axis=0, tiled=True)
-    patch = patch.reshape(F, 2, cols + 2, 64)
-    patch = jnp.concatenate(
-        [
-            lax.ppermute(patch[:, 1:], SEQ, along(SEQ, 1)),
-            patch,
-            lax.ppermute(patch[:, :1], SEQ, along(SEQ, -1)),
-        ],
-        axis=1,
-    )
+    work = input_halos(noisy_latent, cache_in, cache_mid)
+    mine, work = attention(query_vectors, key_vectors, value_vectors, weight_head, work)
+    noisy, cache_first, cache_second = work
+
+    above = lax.ppermute(mine[16:], SEQ, along(SEQ, 1))
+    below = lax.ppermute(mine[:16], SEQ, along(SEQ, -1))
+    patch = jnp.concatenate([above, mine, below], axis=0)
+    patch = patch.reshape(4, 4, F, 2, 64)
+    patch = patch.transpose(2, 0, 3, 1, 4).reshape(F, 4, 8, 64)
+    tiles, cols = lax.axis_size(BLK), 6
     grid = patch.reshape(F, 4, cols + 2, 2, 2, LAT).transpose(0, 1, 3, 2, 4, 5)
     grid = grid.reshape(F, 8, 2 * cols + 4, LAT)
     rows, width = noisy_latent.shape[1], noisy_latent.shape[2]

time: 175 us -> 175 us (level)
  the two profiles are of different devices: /device:TPU:40 before, /device:TPU:1 now
where the time goes in v2:
time: 175 us; the launch traced here: 172 us
  starting transfers between devices  87.5 us (50%)
  Pallas kernels  42 us (24%)
  waiting for transfers between devices  23.6 us (13%)
  local copies, waits for them, and re-layouts  14 us (8%)
  between operations  1.98 us (1%)
    all_to_all x1, starting transfers between devices, attention(): lax.all_to_all(partial, HEAD, split_axis=0, concat_axis=0, tiled=True)  43.2 us
    pallas_call x4, Pallas kernels, flash(): pl.pallas_call(functools.partial(flash_kernel, first, last, len(kvs), hal...  31.8 us
    all_to_all x1, starting transfers between devices, attention(): lax.all_to_all(packed, HEAD, split_axis=0, concat_axis=0, tiled=True)  9.37 us
    ppermute x2, starting transfers between devices, swap_edges(): before = lax.ppermute(cut(True), axis, along(axis, 1)).reshape(-1)  8.33 us
    all_to_all x1, waiting for transfers between devices, attention(): lax.all_to_all(partial, HEAD, split_axis=0, concat_axis=0, tiled=True)  7.84 us
    unnamed x30, local copies, waits for them, and re-layouts  6.95 us
    ppermute x2, waiting for transfers between devices, swap_edges(): before = lax.ppermute(cut(True), axis, along(axis, 1)).reshape(-1)  5.52 us
    ppermute x1, waiting for transfers between devices, attention(): right_b = lax.ppermute(b, 'zh', left)  5.37 us
  transfers between devices with their start and end apart: 16, of which 7 were waited for; matrix products, arithmetic and copies ran while one was open for 2% of the time, Pallas kernels for 13%

profile of v2, /device:TPU:1, one launch (start us, length us, event | category | flops | bytes accessed | tf_op | source)
XLA Modules:
  0.0 172.1 jit_solution(9190681145778169175)
XLA Ops:
  0.6 3.6 %shard_map.158 = bf16[32,48,384]{2,1,0:T(8,128)(2,1)} custom-call(bf16[48,4096]{1,0:T(8,128)(2,1)} %q_ref.1, bf16[48,4096]{1,0:T(8,128)(2,1)} %k_ref.1, bf16[48,4096]{1,0:T(8,128)(2,1)} %v_ref.1), custom_call_target="tpu_custom_call" | custom-call | tf_op jit(solution)/shard_map/pallas_call | solution.py:262
  4.3 9.4 %all-to-all-start = ((bf16[32,48,384]{2,1,0:T(8,128)(2,1)}), bf16[32,48,384]{2,1,0:T(8,128)(2,1)S(1)}, u32[]{:S(2)}, u32[]{:S(2)}) async-start(bf16[32,48,384]{2,1,0:T(8,128)(2,1)} %shard_map.158), calls=%async_computation | async-start | bytes 2359296 | tf_op jit(solution)/shard_map/all_to_all | solution.py:316
  13.9 2.9 %collective-permute-start.6 = (f32[90,128]{1,0:T(8,128)S(1)}, f32[90,128]{1,0:T(8,128)S(1)}, u32[]{:S(2)}, u32[]{:S(2)}) collective-permute-start(f32[90,128]{1,0:T(8,128)S(1)} %maximum_bitcast_fusion.1), channel_id=1, source_target_pairs={{8,0},{16,8},{24,16},{32,24},{40,32},{48,40},{56,48},{64,56},{72,6... | collective-permute-start | bytes 138248 | tf_op jit(solution)/shard_map/ppermute | solution.py:222
  16.9 4.8 %collective-permute-start.5 = (f32[90,128]{1,0:T(8,128)S(1)}, f32[90,128]{1,0:T(8,128)S(1)}, u32[]{:S(2)}, u32[]{:S(2)}) collective-permute-start(f32[90,128]{1,0:T(8,128)S(1)} %maximum_bitcast_fusion), channel_id=1, source_target_pairs={{0,8},{8,16},{16,24},{24,32},{32,40},{40,48},{48,56},{56,64},{64,7... | collective-permute-start | bytes 138248 | tf_op jit(solution)/shard_map/ppermute | solution.py:221
  21.9 4.8 %collective-permute-done.5 = f32[90,128]{1,0:T(8,128)S(1)} collective-permute-done((f32[90,128]{1,0:T(8,128)S(1)}, f32[90,128]{1,0:T(8,128)S(1)}, u32[]{:S(2)}, u32[]{:S(2)}) %collective-permute-start.5) | collective-permute-done | bytes 46112 | tf_op jit(solution)/shard_map/ppermute | solution.py:221
  28.7 2.4 %all-to-all-done = bf16[32,48,384]{2,1,0:T(8,128)(2,1)S(1)} async-done(((bf16[32,48,384]{2,1,0:T(8,128)(2,1)}), bf16[32,48,384]{2,1,0:T(8,128)(2,1)S(1)}, u32[]{:S(2)}, u32[]{:S(2)}) %all-to-all-start) | async-done | bytes 1179680 | tf_op jit(solution)/shard_map/all_to_all | solution.py:316
  34.6 3.0 %collective-permute-start.3 = (bf16[768,256]{1,0:T(8,128)(2,1)}, bf16[768,256]{1,0:T(8,128)(2,1)S(1)}, u32[]{:S(2)}, u32[]{:S(2)}) collective-permute-start(bf16[768,256]{1,0:T(8,128)(2,1)} %get-tuple-element.20), channel_id=1, source_target_pairs={{0,16},{16,32},{32,48},{48,0},{1,17},{17,33},{33,49},{49,1},{2,18}... | collective-permute-start | bytes 1179656 | tf_op jit(solution)/shard_map/ppermute | solution.py:323
  37.6 3.5 %collective-permute-start.7 = (f32[48,128]{1,0:T(8,128)S(1)}, f32[48,128]{1,0:T(8,128)S(1)}, u32[]{:S(2)}, u32[]{:S(2)}) collective-permute-start(f32[48,128]{1,0:T(8,128)S(1)} %maximum_bitcast_fusion.2), channel_id=1, source_target_pairs={{0,1},{1,2},{2,3},{3,4},{4,5},{5,6},{6,7},{8,9},{9,10},{10,11},{11... | collective-permute-start | bytes 73736 | tf_op jit(solution)/shard_map/ppermute | solution.py:221
  43.2 2.2 %collective-permute-start.2 = (bf16[768,256]{1,0:T(8,128)(2,1)}, bf16[768,256]{1,0:T(8,128)(2,1)S(1)}, u32[]{:S(2)}, u32[]{:S(2)}) collective-permute-start(bf16[768,256]{1,0:T(8,128)(2,1)} %get-tuple-element.20), channel_id=1, source_target_pairs={{16,0},{32,16},{48,32},{0,48},{17,1},{33,17},{49,33},{1,49},{18,2}... | collective-permute-start | bytes 1179656 | tf_op jit(solution)/shard_map/ppermute | solution.py:328
  46.7 2.3 %collective-permute-start.4 = (bf16[768,256]{1,0:T(8,128)(2,1)}, bf16[768,256]{1,0:T(8,128)(2,1)S(1)}, u32[]{:S(2)}, u32[]{:S(2)}) collective-permute-start(bf16[768,256]{1,0:T(8,128)(2,1)} %get-tuple-element.21), channel_id=1, source_target_pairs={{16,0},{32,16},{48,32},{0,48},{17,1},{33,17},{49,33},{1,49},{18,2}... | collective-permute-start | bytes 1179656 | tf_op jit(solution)/shard_map/ppermute | solution.py:324
  50.4 7.8 %shard_map.159.refs_4_ = f32[3072,256]{1,0:T(8,128)S(1)} custom-call(bf16[1536,384]{1,0:T(8,128)(2,1)S(1)} %bitcast.35, bf16[1536,128]{1,0:T(8,128)(2,1)S(1)} %collective-permute-done.refs_1_, bf16[1536,384]{1,0:T(8,128)(2,1)S(1)} %bitcast.36), custom_call_target="tpu_custom_call" | custom-call | flops 4831838208 | bytes 6291456 | tf_op jit(solution)/shard_map/pallas_call | solution.py:152
  58.2 5.4 %collective-permute-done.4.refs_3_ = bf16[768,256]{1,0:T(8,128)(2,1)S(1)} collective-permute-done((bf16[768,256]{1,0:T(8,128)(2,1)}, bf16[768,256]{1,0:T(8,128)(2,1)S(1)}, u32[]{:S(2)}, u32[]{:S(2)}) %collective-permute-start.4) | collective-permute-done | bytes 393248 | tf_op jit(solution)/shard_map/ppermute | solution.py:324
  63.6 2.4 %collective-permute-start.10 = (bf16[768,256]{1,0:T(8,128)(2,1)S(1)}, bf16[768,256]{1,0:T(8,128)(2,1)S(1)}, u32[]{:S(2)}, u32[]{:S(2)}) collective-permute-start(bf16[768,256]{1,0:T(8,128)(2,1)S(1)} %collective-permute-done.4.refs_3_), channel_id=1, source_target_pairs={{16,0},{32,16},{48,32},{0,48},{17,1},{33,17},{49,33},{1,49},{18,2}... | collective-permute-start | bytes 1179656 | tf_op jit(solution)/shard_map/ppermute | solution.py:331
  66.0 7.7 %shard_map.160.refs_4_ = f32[3072,256]{1,0:T(8,128)S(1)} custom-call(bf16[1536,384]{1,0:T(8,128)(2,1)S(1)} %bitcast.37, bf16[1536,128]{1,0:T(8,128)(2,1)S(1)} %collective-permute-done.refs_1_, bf16[768,256]{1,0:T(8,128)(2,1)S(1)} %collective-permute-done.3.refs_2_, bf16[768,256]{1,0:T(8,128)(2,1)S(1)} %collective-permute-done.4.refs_3_, ...), custom_call_target="tpu_custom_call" | custom-call | flops 4831838208 | bytes 6291456 | tf_op jit(solution)/shard_map/pallas_call | solution.py:152
  73.7 7.7 %shard_map.161.refs_4_ = f32[3072,256]{1,0:T(8,128)S(1)} custom-call(bf16[1536,384]{1,0:T(8,128)(2,1)S(1)} %bitcast.38, bf16[1536,128]{1,0:T(8,128)(2,1)S(1)} %collective-permute-done.refs_1_, bf16[768,256]{1,0:T(8,128)(2,1)S(1)} %collective-permute-done.1.refs_2_, bf16[768,256]{1,0:T(8,128)(2,1)S(1)} %collective-permute-done.2.refs_3_, ...), custom_call_target="tpu_custom_call" | custom-call | flops 4831838208 | bytes 6291456 | tf_op jit(solution)/shard_map/pallas_call | solution.py:152
  82.4 8.7 %shard_map.162 = (f32[1536,128]{1,0:T(8,128)S(1)}, f32[1536,128]{1,0:T(8,128)S(1)}) custom-call(bf16[1536,384]{1,0:T(8,128)(2,1)S(1)} %bitcast.39, bf16[1536,128]{1,0:T(8,128)(2,1)S(1)} %copy-done.3, bf16[768,256]{1,0:T(8,128)(2,1)S(1)} %collective-permute-done.9.refs_2_, bf16[768,256]{1,0:T(8,128)(2,1)S(1)} %collective-permute-done.10.refs_3_, ...), custom_call_target="tpu_custom_call" | custom-call | flops 4831838208 | bytes 6291456 | tf_op jit(solution)/shard_map/pallas_call | solution.py:152
  91.1 2.1 %collective-permute-start.11 = (f32[1536,128]{1,0:T(8,128)S(1)}, f32[1536,128]{1,0:T(8,128)S(1)}, u32[]{:S(2)}, u32[]{:S(2)}) collective-permute-start(f32[1536,128]{1,0:T(8,128)S(1)} %get-tuple-element.11), channel_id=1, source_target_pairs={{0,8},{8,0},{1,9},{9,1},{2,10},{10,2},{3,11},{11,3},{4,12},{12,4},... | collective-permute-start | bytes 2359304 | tf_op jit(solution)/shard_map/ppermute | solution.py:338
  97.0 43.2 %all-to-all-start.1 = ((bf16[32,32,128]{2,1,0:T(8,128)(2,1)}), bf16[32,32,128]{2,1,0:T(8,128)(2,1)S(1)}, u32[]{:S(2)}, u32[]{:S(2)}) async-start(bf16[32,32,128]{2,1,0:T(8,128)(2,1)} %bitcast.8), calls=%async_computation.1 | async-start | bytes 524288 | tf_op jit(solution)/shard_map/all_to_all | solution.py:340
  140.3 7.8 %all-to-all-done.1 = bf16[32,32,128]{2,1,0:T(8,128)(2,1)S(1)} async-done(((bf16[32,32,128]{2,1,0:T(8,128)(2,1)}), bf16[32,32,128]{2,1,0:T(8,128)(2,1)S(1)}, u32[]{:S(2)}, u32[]{:S(2)}) %all-to-all-start.1) | async-done | bytes 262176 | tf_op jit(solution)/shard_map/all_to_all | solution.py:340
  148.2 4.0 %collective-permute-start.13 = (f32[16,128]{1,0:T(8,128)S(1)}, f32[16,128]{1,0:T(8,128)S(1)}, u32[]{:S(2)}, u32[]{:S(2)}) collective-permute-start(f32[16,128]{1,0:T(8,128)S(1)} %get-tuple-element.59), channel_id=1, source_target_pairs={{8,0},{16,8},{24,16},{32,24},{40,32},{48,40},{56,48},{64,56},{72,6... | collective-permute-start | bytes 24584 | tf_op jit(solution)/shard_map/ppermute | solution.py:366
  152.2 2.5 %collective-permute-start.12 = (f32[16,128]{1,0:T(8,128)S(1)}, f32[16,128]{1,0:T(8,128)S(1)}, u32[]{:S(2)}, u32[]{:S(2)}) collective-permute-start(f32[16,128]{1,0:T(8,128)S(1)} %get-tuple-element.58), channel_id=1, source_target_pairs={{0,8},{8,16},{16,24},{24,32},{32,40},{40,48},{48,56},{56,64},{64,7... | collective-permute-start | bytes 24584 | tf_op jit(solution)/shard_map/ppermute | solution.py:365
  157.9 2.3 %concatenate.51 = bf16[4,6,14,432]{3,2,1,0:T(8,128)(2,1)S(1)} concatenate(bf16[4,6,14,16]{3,2,1,0:T(8,128)(2,1)S(1)} %get-tuple-element.28, bf16[4,6,14,16]{3,2,1,0:T(8,128)(2,1)S(1)} %get-tuple-element.29, bf16[4,6,14,16]{3,2,1,0:T(8,128)(2,1)S(1)} %get-tuple-element.30, bf16[4,6,14,16]{3,2,1,0:T(8,128)(2,1)S(1)} %get-tuple-element.31, ...), dimensions={3} | concatenate | bytes 580608 | tf_op jit(solution)/shard_map/concatenate | solution.py:389
  163.4 3.3 %copy-done.1 = bf16[3,3,3,384,384]{4,3,2,1,0:T(8,128)(2,1)S(1)} copy-done((bf16[3,3,3,384,384]{4,3,2,1,0:T(8,128)(2,1)S(1)}, bf16[3,3,3,384,384]{4,3,2,1,0:T(8,128)(2,1)}, u32[]{:S(2)}) %copy-start.1) | copy-done | bytes 7962648
  166.6 4.8 %shard_map.164 = bf16[256,384]{1,0:T(8,128)(2,1)S(1)} custom-call(bf16[3,6,6,16,384]{4,3,2,1,0:T(8,128)(2,1)S(1)} %pad_maximum_fusion.x_ref, bf16[9,1152,384]{2,1,0:T(8,128)(2,1)S(1)} %bitcast.32, f32[256,384]{1,0:T(8,128)S(1)} %bitcast.40), custom_call_target="tpu_custom_call" | custom-call | flops 2038431744 | bytes 10485760 | tf_op jit(solution)/shard_map/pallas_call | solution.py:189
  (119 shorter events, 21.7 us)
Async XLA Ops:
  0.6 21.1 %copy-start = (bf16[4096,64]{0,1:T(8,128)(2,1)S(1)}, bf16[4096,64]{0,1:T(8,128)(2,1)}, u32[]{:S(2)}) copy-start(bf16[4096,64]{0,1:T(8,128)(2,1)} %param.18) | copy-start | bytes 1572868
  4.2 9.4 %copy-start.6 = (bf16[2,4,12,384]{3,1,2,0:T(4,128)(2,1)S(1)}, bf16[2,4,12,384]{3,1,2,0:T(4,128)(2,1)}, u32[]{:S(2)}) copy-start(bf16[2,4,12,384]{3,1,2,0:T(4,128)(2,1)} %param.27) | copy-start | bytes 221188
  4.2 9.4 %copy-start.5 = (f32[4,4,12,16]{3,1,2,0:T(4,128)S(1)}, f32[4,4,12,16]{3,1,2,0:T(4,128)}, u32[]{:S(2)}) copy-start(f32[4,4,12,16]{3,1,2,0:T(4,128)} %param.19) | copy-start | bytes 36868
  4.3 9.5 %copy-start.7 = (bf16[2,4,12,16]{3,1,2,0:T(4,128)(2,1)S(1)}, bf16[2,4,12,16]{3,1,2,0:T(4,128)(2,1)}, u32[]{:S(2)}) copy-start(bf16[2,4,12,16]{3,1,2,0:T(4,128)(2,1)} %param.23) | copy-start | bytes 9220
  4.3 26.8 %all-to-all-start = ((bf16[32,48,384]{2,1,0:T(8,128)(2,1)}), bf16[32,48,384]{2,1,0:T(8,128)(2,1)S(1)}, u32[]{:S(2)}, u32[]{:S(2)}) async-start(bf16[32,48,384]{2,1,0:T(8,128)(2,1)} %shard_map.158), calls=%async_computation | async-start | bytes 2359296 | tf_op jit(solution)/shard_map/all_to_all | solution.py:316
  13.9 8.0 %collective-permute-start.6 = (f32[90,128]{1,0:T(8,128)S(1)}, f32[90,128]{1,0:T(8,128)S(1)}, u32[]{:S(2)}, u32[]{:S(2)}) collective-permute-start(f32[90,128]{1,0:T(8,128)S(1)} %maximum_bitcast_fusion.1), channel_id=1, source_target_pairs={{8,0},{16,8},{24,16},{32,24},{40,32},{48,40},{56,48},{64,56},{72,6... | collective-permute-start | bytes 138248 | tf_op jit(solution)/shard_map/ppermute | solution.py:222
  16.9 9.8 %collective-permute-start.5 = (f32[90,128]{1,0:T(8,128)S(1)}, f32[90,128]{1,0:T(8,128)S(1)}, u32[]{:S(2)}, u32[]{:S(2)}) collective-permute-start(f32[90,128]{1,0:T(8,128)S(1)} %maximum_bitcast_fusion), channel_id=1, source_target_pairs={{0,8},{8,16},{16,24},{24,32},{32,40},{40,48},{48,56},{56,64},{64,7... | collective-permute-start | bytes 138248 | tf_op jit(solution)/shard_map/ppermute | solution.py:221
  27.2 14.0 %collective-permute-start.8 = (f32[48,128]{1,0:T(8,128)S(1)}, f32[48,128]{1,0:T(8,128)S(1)}, u32[]{:S(2)}, u32[]{:S(2)}) collective-permute-start(f32[48,128]{1,0:T(8,128)S(1)} %maximum_bitcast_fusion.3), channel_id=1, source_target_pairs={{1,0},{2,1},{3,2},{4,3},{5,4},{6,5},{7,6},{9,8},{10,9},{11,10},{12... | collective-permute-start | bytes 73736 | tf_op jit(solution)/shard_map/ppermute | solution.py:222
  32.8 17.6 %collective-permute-start = (bf16[1536,128]{1,0:T(8,128)(2,1)}, bf16[1536,128]{1,0:T(8,128)(2,1)S(1)}, u32[]{:S(2)}, u32[]{:S(2)}) collective-permute-start(bf16[1536,128]{1,0:T(8,128)(2,1)} %slice.242), channel_id=1, source_target_pairs={{0,8},{8,0},{1,9},{9,1},{2,10},{10,2},{3,11},{11,3},{4,12},{12,4},... | collective-permute-start | bytes 1179656 | tf_op jit(solution)/shard_map/ppermute | solution.py:325
  34.6 15.0 %collective-permute-start.3 = (bf16[768,256]{1,0:T(8,128)(2,1)}, bf16[768,256]{1,0:T(8,128)(2,1)S(1)}, u32[]{:S(2)}, u32[]{:S(2)}) collective-permute-start(bf16[768,256]{1,0:T(8,128)(2,1)} %get-tuple-element.20), channel_id=1, source_target_pairs={{0,16},{16,32},{32,48},{48,0},{1,17},{17,33},{33,49},{49,1},{2,18}... | collective-permute-start | bytes 1179656 | tf_op jit(solution)/shard_map/ppermute | solution.py:323
  37.6 4.5 %collective-permute-start.7 = (f32[48,128]{1,0:T(8,128)S(1)}, f32[48,128]{1,0:T(8,128)S(1)}, u32[]{:S(2)}, u32[]{:S(2)}) collective-permute-start(f32[48,128]{1,0:T(8,128)S(1)} %maximum_bitcast_fusion.2), channel_id=1, source_target_pairs={{0,1},{1,2},{2,3},{3,4},{4,5},{5,6},{6,7},{8,9},{9,10},{10,11},{11... | collective-permute-start | bytes 73736 | tf_op jit(solution)/shard_map/ppermute | solution.py:221
  43.2 30.4 %collective-permute-start.2 = (bf16[768,256]{1,0:T(8,128)(2,1)}, bf16[768,256]{1,0:T(8,128)(2,1)S(1)}, u32[]{:S(2)}, u32[]{:S(2)}) collective-permute-start(bf16[768,256]{1,0:T(8,128)(2,1)} %get-tuple-element.20), channel_id=1, source_target_pairs={{16,0},{32,16},{48,32},{0,48},{17,1},{33,17},{49,33},{1,49},{18,2}... | collective-permute-start | bytes 1179656 | tf_op jit(solution)/shard_map/ppermute | solution.py:328
  45.5 28.2 %collective-permute-start.1 = (bf16[768,256]{1,0:T(8,128)(2,1)}, bf16[768,256]{1,0:T(8,128)(2,1)S(1)}, u32[]{:S(2)}, u32[]{:S(2)}) collective-permute-start(bf16[768,256]{1,0:T(8,128)(2,1)} %get-tuple-element.21), channel_id=1, source_target_pairs={{0,16},{16,32},{32,48},{48,0},{1,17},{17,33},{33,49},{49,1},{2,18}... | collective-permute-start | bytes 1179656 | tf_op jit(solution)/shard_map/ppermute | solution.py:327
  46.7 16.9 %collective-permute-start.4 = (bf16[768,256]{1,0:T(8,128)(2,1)}, bf16[768,256]{1,0:T(8,128)(2,1)S(1)}, u32[]{:S(2)}, u32[]{:S(2)}) collective-permute-start(bf16[768,256]{1,0:T(8,128)(2,1)} %get-tuple-element.21), channel_id=1, source_target_pairs={{16,0},{32,16},{48,32},{0,48},{17,1},{33,17},{49,33},{1,49},{18,2}... | collective-permute-start | bytes 1179656 | tf_op jit(solution)/shard_map/ppermute | solution.py:324
  49.6 31.8 %collective-permute-start.9 = (bf16[768,256]{1,0:T(8,128)(2,1)S(1)}, bf16[768,256]{1,0:T(8,128)(2,1)S(1)}, u32[]{:S(2)}, u32[]{:S(2)}) collective-permute-start(bf16[768,256]{1,0:T(8,128)(2,1)S(1)} %collective-permute-done.3.refs_2_), channel_id=1, source_target_pairs={{0,16},{16,32},{32,48},{48,0},{1,17},{17,33},{33,49},{49,1},{2,18}... | collective-permute-start | bytes 1179656 | tf_op jit(solution)/shard_map/ppermute | solution.py:330
  50.4 23.3 %copy-start.2 = (bf16[1536,128]{1,0:T(8,128)(2,1)}, bf16[1536,128]{1,0:T(8,128)(2,1)S(1)}, u32[]{:S(2)}) copy-start(bf16[1536,128]{1,0:T(8,128)(2,1)S(1)} %collective-permute-done.refs_1_) | copy-start | bytes 1179652
  63.6 17.8 %collective-permute-start.10 = (bf16[768,256]{1,0:T(8,128)(2,1)S(1)}, bf16[768,256]{1,0:T(8,128)(2,1)S(1)}, u32[]{:S(2)}, u32[]{:S(2)}) collective-permute-start(bf16[768,256]{1,0:T(8,128)(2,1)S(1)} %collective-permute-done.4.refs_3_), channel_id=1, source_target_pairs={{16,0},{32,16},{48,32},{0,48},{17,1},{33,17},{49,33},{1,49},{18,2}... | collective-permute-start | bytes 1179656 | tf_op jit(solution)/shard_map/ppermute | solution.py:331
  91.1 4.0 %collective-permute-start.11 = (f32[1536,128]{1,0:T(8,128)S(1)}, f32[1536,128]{1,0:T(8,128)S(1)}, u32[]{:S(2)}, u32[]{:S(2)}) collective-permute-start(f32[1536,128]{1,0:T(8,128)S(1)} %get-tuple-element.11), channel_id=1, source_target_pairs={{0,8},{8,0},{1,9},{9,1},{2,10},{10,2},{3,11},{11,3},{4,12},{12,4},... | collective-permute-start | bytes 2359304 | tf_op jit(solution)/shard_map/ppermute | solution.py:338
  97.0 59.0 %slice-start = ((f32[6,8,16,16]{3,2,1,0:T(8,128)}), f32[4,8,16,16]{3,2,1,0:T(8,128)S(1)}, s32[]{:S(2)}) async-start(f32[6,8,16,16]{3,2,1,0:T(8,128)} %copy-done.4), calls=%async_computation.2 | async-start | bytes 524288 | tf_op jit(solution)/shard_map/slice | solution.py:247
  97.0 59.0 %copy-start.11 = (f32[16]{0:T(128)S(1)}, f32[16]{0:T(128)}, u32[]{:S(2)}) copy-start(f32[16]{0:T(128)} %param.21) | copy-start | bytes 196
  97.0 59.0 %copy-start.12 = (f32[16]{0:T(128)S(1)}, f32[16]{0:T(128)}, u32[]{:S(2)}) copy-start(f32[16]{0:T(128)} %param.22) | copy-start | bytes 196
  97.0 51.2 %all-to-all-start.1 = ((bf16[32,32,128]{2,1,0:T(8,128)(2,1)}), bf16[32,32,128]{2,1,0:T(8,128)(2,1)S(1)}, u32[]{:S(2)}, u32[]{:S(2)}) async-start(bf16[32,32,128]{2,1,0:T(8,128)(2,1)} %bitcast.8), calls=%async_computation.1 | async-start | bytes 524288 | tf_op jit(solution)/shard_map/all_to_all | solution.py:340
  148.2 7.2 %collective-permute-start.13 = (f32[16,128]{1,0:T(8,128)S(1)}, f32[16,128]{1,0:T(8,128)S(1)}, u32[]{:S(2)}, u32[]{:S(2)}) collective-permute-start(f32[16,128]{1,0:T(8,128)S(1)} %get-tuple-element.59), channel_id=1, source_target_pairs={{8,0},{16,8},{24,16},{32,24},{40,32},{48,40},{56,48},{64,56},{72,6... | collective-permute-start | bytes 24584 | tf_op jit(solution)/shard_map/ppermute | solution.py:366
  152.2 3.3 %collective-permute-start.12 = (f32[16,128]{1,0:T(8,128)S(1)}, f32[16,128]{1,0:T(8,128)S(1)}, u32[]{:S(2)}, u32[]{:S(2)}) collective-permute-start(f32[16,128]{1,0:T(8,128)S(1)} %get-tuple-element.58), channel_id=1, source_target_pairs={{0,8},{8,16},{16,24},{24,32},{32,40},{40,48},{48,56},{56,64},{64,7... | collective-permute-start | bytes 24584 | tf_op jit(solution)/shard_map/ppermute | solution.py:365
  (6 other events, 9.8 us)

commit v3 on v2

--- a/solution.py
+++ b/solution.py
@@ -17,7 +17,7 @@
 
 SEQ = ("y", "zh", "core")
 BLK = ("zl", "x")
-HEAD = ("y", "zl", "x")
+HEAD = ("zh", "zl", "x")
 SHARD = SEQ + BLK
 
 TILE = 512
@@ -164,44 +164,133 @@
     )(*args)
 
 
-def conv_kernel(x_ref, w_ref, base_ref, out_ref, acc_ref):
-    step = pl.program_id(0)
-    t, u = step // 3, step % 3
-
-    @pl.when(step == 0)
-    def _():
-        acc_ref[...] = base_ref[...]
-
-    total = acc_ref[...]
+def tail_kernel(
+    above_ref,
+    mine_ref,
+    below_ref,
+    noisy_ref,
+    cache_ref,
+    affine_ref,
+    token_ok_ref,
+    cell_ok_ref,
+    w1_ref,
+    b1_ref,
+    gain_ref,
+    mid_ref,
+    w2_ref,
+    b2_ref,
+    den_ref,
+    out_ref,
+    w2_buf,
+    sems,
+    vel,
+    lat,
+    first,
+    act,
+    wide,
+):
+    for tap in range(9):
+        pltpu.make_async_copy(w2_ref.at[tap], w2_buf.at[tap], sems.at[tap]).start()
+    for at, rows in enumerate(
+        (above_ref[...], mine_ref[0:16, :], mine_ref[16:32, :], below_ref[...])
+    ):
+        turned = pltpu.roll(rows, 64, axis=1)
+        for f in range(F):
+            vel[f, at, 0:4, :] = rows[f * 4 : f * 4 + 4]
+            vel[f, at, 4:8, :] = turned[f * 4 : f * 4 + 4]
+    level, scale, mean = affine_ref[0:1, :], affine_ref[1:2, :], affine_ref[2:3, :]
+    denoised = noisy_ref[...] - level * vel[:, :, :, 0:64]
+    den_ref[...] = denoised
+    latent = jnp.where(token_ok_ref[...] > 0, denoised * scale + mean, 0.0)
+    lat[...] = jnp.zeros(lat.shape, jnp.float32)
+    lat[0:2, :, 0:8, 0:64] = cache_ref[...]
+    lat[2:6, :, 0:8, 0:64] = latent.astype(jnp.bfloat16).astype(jnp.float32)
+    here = lat[:, :, 0:8, :].reshape(192, 128)
+    right = pltpu.roll(lat[:, :, 1:9, :].reshape(192, 128), 64, axis=1)
+    lane = lax.broadcasted_iota(jnp.int32, (192, 128), 1)
+    pair = jnp.where(lane < 64, here, right).reshape(6, 4, 8, 128)
+    lower = jnp.concatenate([pair[:, 1:4], pair[:, 3:4]], axis=1)
+    window = jnp.concatenate([pair, lower], axis=3).reshape(192, 256).astype(jnp.bfloat16)
+    parts = C1 // 128
+    for k in range(parts):
+        act[k, 0:2, :, 0:14, :] = mid_ref[:, :, :, pl.ds(k * 128, 128)]
+    gain = gain_ref[...]
+    for p in range(2):
+        for q in range(2):
+            lanes = pl.ds((2 * p + q) * C1, C1)
+            value = b1_ref[...]
+            for t in range(3):
+                value = value + jnp.dot(
+                    window[t * 32 : t * 32 + 128],
+                    w1_ref[t, :, lanes],
+                    preferred_element_type=jnp.float32,
+                )
+            power = jnp.mean(value * value, axis=1, keepdims=True)
+            normed = value * lax.rsqrt(power + EPSILON) * gain
+            active = (normed / (1.0 + jnp.exp(-normed))).reshape(F, 32, C1)
+            active = active * cell_ok_ref[2 * p + q, :, 0:1]
+            value = value.reshape(F, 4, 8, C1)
+            active = active.reshape(F, 4, 8, C1)
+            for r in range(3):
+                cols = pl.ds(q, 8, stride=2)
+                for k in range(parts):
+                    part = slice(k * 128, k * 128 + 128)
+                    for f in range(F):
+                        first[k, f, 2 * r + p, cols, :] = value[f, r, :, part]
+                        act[k, f + 2, 2 * r + p, cols, :] = active[f, r, :, part]
     for v in range(3):
-        rows = x_ref[v, pl.ds(t, 4), pl.ds(u, 4)].reshape(256, C1)
-        total = total + jnp.dot(
-            rows, w_ref[0, pl.ds(v * C1, C1), :], preferred_element_type=jnp.float32
-        )
-    acc_ref[...] = total
-
-    @pl.when(step == 8)
-    def _():
-        out_ref[...] = total.astype(jnp.bfloat16)
-
-
-def conv_mid(shifted, weight, base):
+        for k in range(parts):
+            wide[:, :, :, pl.ds(v * C1 + k * 128, 128)] = act[k, :, :, pl.ds(v, 16), :].astype(
+                jnp.bfloat16
+            )
+    middle = [first[k, :, 1:5, pl.ds(1, 16), :].reshape(256, 128) for k in range(parts)]
+    total = jnp.concatenate(middle, axis=1) + b2_ref[...]
+    for tap in range(9):
+        t, u = divmod(tap, 3)
+        pltpu.make_async_copy(w2_ref.at[tap], w2_buf.at[tap], sems.at[tap]).wait()
+        rows = wide[t : t + 4, u : u + 4].reshape(256, 3 * C1)
+        total = total + jnp.dot(rows, w2_buf[tap], preferred_element_type=jnp.float32)
+    out_ref[...] = total.reshape(F, 4, 16, C1)[:, :, 0:12].astype(jnp.bfloat16)
+
+
+def tail(*args):
+    specs = [pl.BlockSpec(memory_space=pltpu.VMEM)] * len(args)
+    specs[12] = pl.BlockSpec(memory_space=pl.ANY)
     return pl.pallas_call(
-        conv_kernel,
-        grid=(9,),
-        in_specs=[
-            pl.BlockSpec(shifted.shape, lambda i: (0, 0, 0, 0, 0)),
-            pl.BlockSpec((1, 3 * C1, C1), lambda i: (i, 0, 0)),
-            pl.BlockSpec((256, C1), lambda i: (0, 0)),
+        tail_kernel,
+        in_specs=specs,
+        out_specs=[pl.BlockSpec(memory_space=pltpu.VMEM)] * 2,
+        out_shape=[
+            jax.ShapeDtypeStruct((F, 4, 8, 64), jnp.float32),
+            jax.ShapeDtypeStruct((F, 4, 12, C1), jnp.bfloat16),
         ],
-        out_specs=pl.BlockSpec((256, C1), lambda i: (0, 0)),
-        out_shape=jax.ShapeDtypeStruct((256, C1), jnp.bfloat16),
-        scratch_shapes=[pltpu.VMEM((256, C1), jnp.float32)],
+        scratch_shapes=[
+            pltpu.VMEM((9, 3 * C1, C1), jnp.bfloat16),
+            pltpu.SemaphoreType.DMA((9,)),
+            pltpu.VMEM((F, 4, 8, 128), jnp.float32),
+            pltpu.VMEM((6, 4, 16, 128), jnp.float32),
+            pltpu.VMEM((C1 // 128, F, 6, 24, 128), jnp.float32),
+            pltpu.VMEM((C1 // 128, 6, 6, 24, 128), jnp.float32),
+            pltpu.VMEM((6, 6, 16, 3 * C1), jnp.bfloat16),
+        ],
         compiler_params=pltpu.CompilerParams(vmem_limit_bytes=32 << 20),
-        cost_estimate=pl.CostEstimate(
-            flops=2 * 256 * 27 * C1 * C1, bytes_accessed=10 << 20, transcendentals=0
-        ),
-    )(shifted, weight.reshape(9, 3 * C1, C1), base)
+    )(*args)
+
+
+def window_weights(weight):
+    cells = [
+        jnp.pad(weight, ((0, 0), (p, 1 - p), (q, 1 - q), (0, 0), (0, 0)))
+        for p in range(2)
+        for q in range(2)
+    ]
+    joined = jnp.stack(cells, axis=4).reshape(3, 2, 2, 2, 2, LAT, 4, C1)
+    return joined.transpose(0, 1, 3, 2, 4, 5, 6, 7).reshape(3, 16 * LAT, 4 * C1)
+
+
+def by_token(cells):
+    frames = cells.shape[0]
+    split = cells.reshape(frames, 4, 2, 8, 2, LAT).transpose(0, 1, 3, 2, 4, 5)
+    return split.reshape(frames, 4, 8, 4 * LAT)
 
 
 def along(axis, step):
@@ -244,7 +333,8 @@
     parts = [both, cache_mid.astype(jnp.float32)]
     parts = swap_edges(parts, SEQ, (1, 1), (2, 1))
     both, cache_mid = swap_edges(parts, BLK, (2, 2), (2, 1))
-    return both[2:], both[:2].astype(jnp.bfloat16), cache_mid.astype(jnp.bfloat16)
+    both = by_token(both)
+    return both[2:], both[:2], cache_mid
 
 
 def pack_kernel(q_ref, k_ref, v_ref, out_ref):
@@ -258,12 +348,12 @@
 def pack(query_vectors, key_vectors, value_vectors):
     tokens, width = query_vectors.shape
     heads = width // HEAD_DIM
-    block = pl.BlockSpec((tokens, width // 4), lambda i: (0, i))
+    block = pl.BlockSpec((tokens, width // 2), lambda i: (0, i))
     return pl.pallas_call(
         pack_kernel,
-        grid=(4,),
+        grid=(2,),
         in_specs=[block] * 3,
-        out_specs=pl.BlockSpec((heads // 4, tokens, 3 * HEAD_DIM), lambda i: (i, 0, 0)),
+        out_specs=pl.BlockSpec((heads // 2, tokens, 3 * HEAD_DIM), lambda i: (i, 0, 0)),
         out_shape=jax.ShapeDtypeStruct((heads, tokens, 3 * HEAD_DIM), jnp.bfloat16),
     )(query_vectors, key_vectors, value_vectors)
 
@@ -289,7 +379,7 @@
                 at = 6 * b - 1 + c
                 both = jnp.where(low, column(r, at), column(r, at + 4))
                 for y in range(4):
-                    piece_ref[y, b, pl.ds(r * 16 + c * 4, 4), :] = both[y * 4 : y * 4 + 4]
+                    piece_ref[y, b, pl.ds(r * 16 + c, 4, stride=4), :] = both[y * 4 : y * 4 + 4]
     out_ref[...] = piece_ref[...].astype(jnp.bfloat16)
 
 
@@ -314,23 +404,23 @@
     packed = pack(query_vectors, key_vectors, value_vectors)
     heads, tokens = packed.shape[:2]
     moved = lax.all_to_all(packed, HEAD, split_axis=0, concat_axis=0, tiled=True)
+    moved, work = lax.optimization_barrier((moved, work))
     moved = moved.reshape(heads * tokens, 3 * HEAD_DIM)
     swap = [(0, 1), (1, 0)]
     right = [(i, (i + 1) % 4) for i in range(4)]
     left = [((i + 1) % 4, i) for i in range(4)]
     mid = moved.shape[0] // 2
     a, b = moved[:mid, :256], moved[mid:, :256]
-    left_a = lax.ppermute(a, "zh", right)
-    right_b = lax.ppermute(b, "zh", left)
+    left_a = lax.ppermute(a, "y", right)
+    right_b = lax.ppermute(b, "y", left)
     q_oth = lax.ppermute(moved[:, 256:], "core", swap)
     state = flash(moved, q_oth, [moved])
-    left_b = lax.ppermute(b, "zh", right)
-    right_a = lax.ppermute(a, "zh", left)
+    left_b = lax.ppermute(b, "y", right)
+    right_a = lax.ppermute(a, "y", left)
     state = flash(moved, q_oth, [left_a, right_b], state)
-    far_a = lax.ppermute(left_a, "zh", right)
-    far_b = lax.ppermute(right_b, "zh", left)
+    far_a = lax.ppermute(left_a, "y", right)
+    far_b = lax.ppermute(right_b, "y", left)
     state = flash(moved, q_oth, [left_b, right_a], state)
-    state, work = lax.optimization_barrier((state, work))
     head = lax.axis_index(HEAD)
     weight = lax.dynamic_slice_in_dim(weight_head, head * HEAD_DIM, HEAD_DIM, axis=0)
     weight = jnp.pad(weight, ((0, 0), (0, 64)))
@@ -358,50 +448,48 @@
     weight_mid,
     bias_mid,
 ):
-    work = input_halos(noisy_latent, cache_in, cache_mid)
+    row, col = lax.axis_index(SEQ), lax.axis_index(BLK)
+    last_row, last_col = lax.axis_size(SEQ) - 1, lax.axis_size(BLK) - 1
+    row_ok, col_ok = inside(8, row, last_row), inside(16, col, last_col)
+    token_ok = (row_ok[::2, None] & col_ok[None, ::2]).astype(jnp.float32)
+    token_ok = jnp.broadcast_to(token_ok[:, :, None], (4, 8, 4 * LAT))
+    cell_ok = inside(8, row, last_row)[1:7, None] & jnp.pad(col_ok[1:15], (0, 2))[None, :]
+    cell_ok = cell_ok.reshape(3, 2, 8, 2).transpose(1, 3, 0, 2).astype(jnp.float32)
+    cell_ok = jnp.pad(cell_ok, ((0, 0), (0, 0), (0, 1), (0, 0))).reshape(4, 32, 1)
+    cell_ok = jnp.broadcast_to(cell_ok, (4, 32, 128))
+    level = jnp.broadcast_to(noise_level, (4 * LAT,))
+    affine = jnp.stack([level, jnp.tile(latent_scale, 4), jnp.tile(latent_mean, 4)])
+
+    halos = input_halos(noisy_latent, cache_in, cache_mid)
+    work = (*halos, token_ok, cell_ok, affine, window_weights(weight_in))
     mine, work = attention(query_vectors, key_vectors, value_vectors, weight_head, work)
-    noisy, cache_first, cache_second = work
+    noisy, cache_first, cache_second, token_ok, cell_ok, affine, weight_first = work
 
     above = lax.ppermute(mine[16:], SEQ, along(SEQ, 1))
     below = lax.ppermute(mine[:16], SEQ, along(SEQ, -1))
-    patch = jnp.concatenate([above, mine, below], axis=0)
-    patch = patch.reshape(4, 4, F, 2, 64)
-    patch = patch.transpose(2, 0, 3, 1, 4).reshape(F, 4, 8, 64)
-    tiles, cols = lax.axis_size(BLK), 6
-    grid = patch.reshape(F, 4, cols + 2, 2, 2, LAT).transpose(0, 1, 3, 2, 4, 5)
-    grid = grid.reshape(F, 8, 2 * cols + 4, LAT)
-    rows, width = noisy_latent.shape[1], noisy_latent.shape[2]
-    denoised = noisy - noise_level[0] * grid
-    row_at = lax.axis_index(SEQ) * rows - 2 + jnp.arange(rows + 4)
-    col_at = lax.axis_index(BLK) * width - 2 + jnp.arange(width + 4)
-    row_ok = (row_at >= 0) & (row_at < lax.axis_size(SEQ) * rows)
-    col_ok = (col_at >= 0) & (col_at < tiles * width)
-    inside = row_ok[:, None, None] & col_ok[None, :, None]
-    latent = jnp.where(inside, denoised * latent_scale + latent_mean, 0.0).astype(jnp.bfloat16)
-
-    stacked = jnp.concatenate([cache_first, latent], axis=0)
-    taps = [
-        stacked[t : t + F, u : u + rows + 2, v : v + width + 2]
-        for t in range(3)
-        for u in range(3)
-        for v in range(3)
-    ]
-    gathered = jnp.concatenate(taps, axis=-1).reshape(F * (rows + 2) * (width + 2), -1)
-    first = jnp.dot(
-        gathered, weight_in.reshape(-1, C1), preferred_element_type=jnp.float32
+    denoised, features = tail(
+        above,
+        mine,
+        below,
+        noisy,
+        cache_first,
+        affine,
+        token_ok,
+        cell_ok,
+        weight_first,
+        bias_in.reshape(1, C1),
+        norm_gain.reshape(1, C1),
+        cache_second,
+        weight_mid.reshape(9, 3 * C1, C1),
+        bias_mid.reshape(1, C1),
     )
-    first = (first + bias_in).reshape(F, rows + 2, width + 2, C1)
-    power = jnp.mean(first * first, axis=-1, keepdims=True)
-    active = jax.nn.silu(first * lax.rsqrt(power + EPSILON) * norm_gain)
-    active = jnp.where(inside[1:-1, 1:-1], active, 0.0).astype(jnp.bfloat16)
-    padded = jnp.concatenate([cache_second, active], axis=0)
-    padded = jnp.pad(padded, ((0, 0), (0, 0), (0, 4), (0, 0)))
-    shifted = jnp.stack([padded[:, :, v : v + 16] for v in range(3)])
-    base = first[:, 1:-1, 1:-1] + bias_mid
-    base = jnp.pad(base, ((0, 0), (0, 0), (0, 4), (0, 0))).reshape(256, C1)
-    features = conv_mid(shifted, weight_mid, base)
-    features = features.reshape(F, rows, 16, C1)[:, :, :width]
-    return (denoised[:, 2:-2, 2:-2], features)
+    denoised = denoised[:, 1:3, 1:7].reshape(F, 2, 6, 2, 2, LAT).transpose(0, 1, 3, 2, 4, 5)
+    return denoised.reshape(F, 4, 12, LAT), features
+
+
+def inside(count, index, last):
+    at = jnp.arange(count)
+    return ((at >= 2) | (index > 0)) & ((at < count - 2) | (index < last))
 
 
 def solution(mesh):

time: 175 us -> 168 us (0.960); the launches traced: 172 us -> 167 us
  starting transfers between devices: 87.5 us -> 37.9 us
  blocking collectives: 0 us -> 21.3 us
  other arithmetic: 1.55 us -> 14 us
  local copies, waits for them, and re-layouts: 14 us -> 25.9 us
  Pallas kernels: 42 us -> 46.5 us
  waiting for transfers between devices: 23.6 us -> 19.6 us
    all_to_all x1 -> x0, starting transfers between devices: 43.2 us -> none  [attention(): lax.all_to_all(partial, HEAD, split_axis=0, concat_axis=0, tiled=True)]
    all_to_all x0 -> x1, blocking collectives: none -> 21.3 us  [attention(): lax.all_to_all(partial, HEAD, split_axis=0, concat_axis=0, tiled=True)]
    all_to_all x1 -> x0, waiting for transfers between devices: 7.84 us -> none  [attention(): lax.all_to_all(partial, HEAD, split_axis=0, concat_axis=0, tiled=True)]
    transpose x0 -> x1, other arithmetic: none -> 7.59 us  [window_weights(): return joined.transpose(0, 1, 3, 2, 4, 5, 6, 7).reshape(3, 16 * LAT, 4 * C1)]
    ppermute x2, waiting for transfers between devices: 0.01 us -> 7.33 us  [swap_edges(): after = lax.ppermute(cut(False), axis, along(axis, -1)).reshape(-1)]
    another operation x1 -> x9, local copies, waits for them, and re-layouts: 0.27 us -> 7.07 us  [the longest x4 6.89 us: window_weights(): joined = jnp.stack(cells, axis=4).reshape(3, 2, 2, 2, 2, LAT, 4, C1)]
    ppermute x2, waiting for transfers between devices: 5.52 us -> 0.01 us  [swap_edges(): before = lax.ppermute(cut(True), axis, along(axis, 1)).reshape(-1)]
    ppermute x6, starting transfers between devices: 12 us -> 7.31 us  [the longest x1 2.65 us: attention(): far_b = lax.ppermute(right_b, 'y', left)]
  transfers between devices with their start and end apart: 16 -> 15, of which waited for: 7 -> 5; matrix products, arithmetic and copies ran while one was open for 2% -> 19% of each run, Pallas kernels for 13% -> 17%
where the time goes in v3:
time: 168 us; the launch traced here: 167 us
  Pallas kernels  46.5 us (28%)
  starting transfers between devices  37.9 us (23%)
  local copies, waits for them, and re-layouts  25.9 us (15%)
  blocking collectives  21.3 us (13%)
  waiting for transfers between devices  19.6 us (12%)
  other arithmetic  14 us (8%)
  between operations  1.99 us (1%)
    pallas_call x4, Pallas kernels, flash(): pl.pallas_call(functools.partial(flash_kernel, first, last, len(kvs), hal...  36.3 us
    all_to_all x1, blocking collectives, attention(): lax.all_to_all(partial, HEAD, split_axis=0, concat_axis=0, tiled=True)  21.3 us
    all_to_all x1, starting transfers between devices, attention(): lax.all_to_all(packed, HEAD, split_axis=0, concat_axis=0, tiled=True)  9.35 us
    ppermute x2, starting transfers between devices, swap_edges(): before = lax.ppermute(cut(True), axis, along(axis, 1)).reshape(-1)  9.2 us
    transpose x1, other arithmetic, window_weights(): return joined.transpose(0, 1, 3, 2, 4, 5, 6, 7).reshape(3, 16 * LAT, 4 * C1)  7.59 us
    ppermute x2, waiting for transfers between devices, swap_edges(): after = lax.ppermute(cut(False), axis, along(axis, -1)).reshape(-1)  7.33 us
    another operation x4, local copies, waits for them, and re-layouts, window_weights(): joined = jnp.stack(cells, axis=4).reshape(3, 2, 2, 2, 2, LAT, 4, C1)  6.89 us
    pallas_call x1, Pallas kernels, tail(): pl.pallas_call(tail_kernel, in_specs=specs, out_specs=[pl.BlockSpec(memor...  6.75 us
  transfers between devices with their start and end apart: 15, of which 5 were waited for; matrix products, arithmetic and copies ran while one was open for 19% of the time, Pallas kernels for 17%

profile of v3, /device:TPU:1, one launch (start us, length us, event | category | flops | bytes accessed | tf_op | source)
XLA Modules:
  0.0 167.2 jit_solution(4700703326324009442)
XLA Ops:
  3.6 6.4 %collective-permute-start = (f32[90,128]{1,0:T(8,128)S(1)}, f32[90,128]{1,0:T(8,128)S(1)}, u32[]{:S(2)}, u32[]{:S(2)}) collective-permute-start(f32[90,128]{1,0:T(8,128)S(1)} %maximum_bitcast_fusion.1), channel_id=1, source_target_pairs={{0,8},{8,16},{16,24},{24,32},{32,40},{40,48},{48,56},{56,64},{64,7... | collective-permute-start | bytes 138248 | tf_op jit(solution)/shard_map/ppermute | solution.py:310
  10.0 2.3 %shard_map.161 = bf16[32,48,384]{2,1,0:T(8,128)(2,1)} custom-call(bf16[48,4096]{1,0:T(8,128)(2,1)} %q_ref.1, bf16[48,4096]{1,0:T(8,128)(2,1)} %k_ref.1, bf16[48,4096]{1,0:T(8,128)(2,1)} %v_ref.1), custom_call_target="tpu_custom_call" | custom-call | tf_op jit(solution)/shard_map/pallas_call | solution.py:352
  12.3 9.4 %all-to-all-start = ((bf16[32,48,384]{2,1,0:T(8,128)(2,1)}), bf16[32,48,384]{2,1,0:T(8,128)(2,1)}, u32[]{:S(2)}, u32[]{:S(2)}) async-start(bf16[32,48,384]{2,1,0:T(8,128)(2,1)} %shard_map.161), calls=%async_computation | async-start | bytes 2359296 | tf_op jit(solution)/shard_map/all_to_all | solution.py:406
  22.4 1.9 %collective-permute-start.1 = (f32[90,128]{1,0:T(8,128)}, f32[90,128]{1,0:T(8,128)S(1)}, u32[]{:S(2)}, u32[]{:S(2)}) collective-permute-start(f32[90,128]{1,0:T(8,128)} %maximum_bitcast_fusion.2), channel_id=1, source_target_pairs={{8,0},{16,8},{24,16},{32,24},{40,32},{48,40},{56,48},{64,56},{72,6... | collective-permute-start | bytes 138248 | tf_op jit(solution)/shard_map/ppermute | solution.py:311
  27.9 2.2 %copy.65 = bf16[3,2,2,2,2,16,1,384]{7,6,5,4,2,3,1,0:T(2,128)(2,1)} copy(bf16[3,2,2,2,2,16,1,384]{7,5,4,3,2,1,0,6:T(8,128)(2,1)S(1)} %bitcast.35) | data formatting | bytes 1179648 | tf_op jit(solution)/shard_map/stack | solution.py:286
  30.1 2.2 %copy.66 = bf16[3,2,2,2,2,16,1,384]{7,6,5,4,2,3,1,0:T(2,128)(2,1)} copy(bf16[3,2,2,2,2,16,1,384]{7,5,4,3,2,1,0,6:T(8,128)(2,1)S(1)} %bitcast.34) | data formatting | bytes 1179648 | tf_op jit(solution)/shard_map/stack | solution.py:286
  33.4 7.6 %maximum_bitcast_fusion = bf16[3,2,2,2,2,16,4,384]{7,6,5,4,3,2,1,0:T(4,128)(2,1)} fusion(bf16[3,2,2,2,2,16,1,384]{7,6,5,4,2,3,1,0:T(2,128)(2,1)} %copy.66, bf16[3,2,2,2,2,16,1,384]{7,6,5,4,2,3,1,0:T(2,128)(2,1)} %copy.65, bf16[3,2,2,2,2,16,1,384]{7,6,5,4,2,3,1,0:T(2,128)(2,1)S(1)} %copy.64, bf16[3,2,2,2,2,16,1,384]{7,6,5,4,2,3,1,0:T(2,128)(2,1)S(1)} %copy.63), kind=kLoop, calls=%fused_computation | loop fusion | flops 9437184 | bytes 4718592 | tf_op jit(solution)/shard_map/transpose | solution.py:287
  42.4 7.3 %collective-permute-done.1 = f32[90,128]{1,0:T(8,128)S(1)} collective-permute-done((f32[90,128]{1,0:T(8,128)}, f32[90,128]{1,0:T(8,128)S(1)}, u32[]{:S(2)}, u32[]{:S(2)}) %collective-permute-start.1) | collective-permute-done | bytes 46112 | tf_op jit(solution)/shard_map/ppermute | solution.py:311
  52.5 2.8 %collective-permute-start.2 = (f32[48,128]{1,0:T(8,128)S(1)}, f32[48,128]{1,0:T(8,128)S(1)}, u32[]{:S(2)}, u32[]{:S(2)}) collective-permute-start(f32[48,128]{1,0:T(8,128)S(1)} %maximum_bitcast_fusion.3), channel_id=1, source_target_pairs={{0,1},{1,2},{2,3},{3,4},{4,5},{5,6},{6,7},{8,9},{9,10},{10,11},{11... | collective-permute-start | bytes 73736 | tf_op jit(solution)/shard_map/ppermute | solution.py:310
  56.8 4.0 %reshape.195.w1_ref = bf16[3,256,1536]{2,1,0:T(8,128)(2,1)S(1)} reshape(bf16[3,2,2,2,2,16,4,384]{7,6,5,4,3,2,1,0:T(4,128)(2,1)} %maximum_bitcast_fusion) | data formatting | bytes 4718592 | tf_op jit(solution)/shard_map/reshape | solution.py:287
  67.3 2.1 %fusion.2 = (bf16[768,256]{1,0:T(8,128)(2,1)}, bf16[768,256]{1,0:T(8,128)(2,1)}) fusion(bf16[1536,384]{1,0:T(8,128)(2,1)} %bitcast.16.refs_0_.refs_2_), kind=kLoop, calls=%fused_computation.29 | loop fusion | bytes 1572864 | tf_op jit(solution)/shard_map/slice | solution.py:413
  75.8 3.4 %collective-permute-done.5.refs_2_ = bf16[768,256]{1,0:T(8,128)(2,1)} collective-permute-done((bf16[768,256]{1,0:T(8,128)(2,1)}, bf16[768,256]{1,0:T(8,128)(2,1)}, u32[]{:S(2)}, u32[]{:S(2)}) %collective-permute-start.5) | collective-permute-done | bytes 393248 | tf_op jit(solution)/shard_map/ppermute | solution.py:414
  79.4 9.0 %shard_map.162.refs_4_ = f32[3072,256]{1,0:T(8,128)S(1)} custom-call(bf16[1536,384]{1,0:T(8,128)(2,1)} %bitcast.16.refs_0_.refs_2_, bf16[1536,128]{1,0:T(8,128)(2,1)} %collective-permute-done.4.refs_1_, bf16[1536,384]{1,0:T(8,128)(2,1)} %bitcast.16.refs_0_.refs_2_), custom_call_target="tpu_custom_call" | custom-call | flops 4831838208 | bytes 6291456 | tf_op jit(solution)/shard_map/pallas_call | solution.py:152
  88.4 3.3 %collective-permute-done.7.refs_3_ = bf16[768,256]{1,0:T(8,128)(2,1)S(1)} collective-permute-done((bf16[768,256]{1,0:T(8,128)(2,1)}, bf16[768,256]{1,0:T(8,128)(2,1)S(1)}, u32[]{:S(2)}, u32[]{:S(2)}) %collective-permute-start.7) | collective-permute-done | bytes 393248 | tf_op jit(solution)/shard_map/ppermute | solution.py:415
  91.7 2.7 %collective-permute-start.8 = (bf16[768,256]{1,0:T(8,128)(2,1)S(1)}, bf16[768,256]{1,0:T(8,128)(2,1)S(1)}, u32[]{:S(2)}, u32[]{:S(2)}) collective-permute-start(bf16[768,256]{1,0:T(8,128)(2,1)S(1)} %collective-permute-done.7.refs_3_), channel_id=1, source_target_pairs={{64,0},{128,64},{192,128},{0,192},{65,1},{129,65},{193,129},{1,193... | collective-permute-start | bytes 1179656 | tf_op jit(solution)/shard_map/ppermute | solution.py:422
  94.4 8.8 %shard_map.163.refs_4_ = f32[3072,256]{1,0:T(8,128)S(1)} custom-call(bf16[1536,384]{1,0:T(8,128)(2,1)} %bitcast.16.refs_0_.refs_2_, bf16[1536,128]{1,0:T(8,128)(2,1)} %collective-permute-done.4.refs_1_, bf16[768,256]{1,0:T(8,128)(2,1)} %collective-permute-done.5.refs_2_, bf16[768,256]{1,0:T(8,128)(2,1)S(1)} %collective-permute-done.7.refs_3_, ...), custom_call_target="tpu_custom_call" | custom-call | flops 4831838208 | bytes 6291456 | tf_op jit(solution)/shard_map/pallas_call | solution.py:152
  103.2 8.8 %shard_map.164.refs_4_ = f32[3072,256]{1,0:T(8,128)S(1)} custom-call(bf16[1536,384]{1,0:T(8,128)(2,1)} %bitcast.16.refs_0_.refs_2_, bf16[1536,128]{1,0:T(8,128)(2,1)} %collective-permute-done.4.refs_1_, bf16[768,256]{1,0:T(8,128)(2,1)S(1)} %collective-permute-done.9.refs_2_, bf16[768,256]{1,0:T(8,128)(2,1)S(1)} %collective-permute-done.10.refs_3_, ...), custom_call_target="tpu_custom_call" | custom-call | flops 4831838208 | bytes 6291456 | tf_op jit(solution)/shard_map/pallas_call | solution.py:152
  112.0 9.8 %shard_map.165 = (f32[1536,128]{1,0:T(8,128)S(1)}, f32[1536,128]{1,0:T(8,128)S(1)}) custom-call(bf16[1536,384]{1,0:T(8,128)(2,1)} %bitcast.16.refs_0_.refs_2_, bf16[1536,128]{1,0:T(8,128)(2,1)} %collective-permute-done.4.refs_1_, bf16[768,256]{1,0:T(8,128)(2,1)S(1)} %collective-permute-done.6.refs_2_, bf16[768,256]{1,0:T(8,128)(2,1)S(1)} %collective-permute-done.8.refs_3_, ...), custom_call_target="tpu_custom_call" | custom-call | flops 4831838208 | bytes 6291456 | tf_op jit(solution)/shard_map/pallas_call | solution.py:152
  123.6 1.9 %collective-permute-done.11.oth_ref = f32[1536,128]{1,0:T(8,128)S(1)} collective-permute-done((f32[1536,128]{1,0:T(8,128)S(1)}, f32[1536,128]{1,0:T(8,128)S(1)}, u32[]{:S(2)}, u32[]{:S(2)}) %collective-permute-start.11) | collective-permute-done | bytes 786464 | tf_op jit(solution)/shard_map/ppermute | solution.py:428
  126.7 21.3 %all_to_all.10 = bf16[32,32,128]{2,1,0:T(8,128)(2,1)S(1)} all-to-all(bf16[32,32,128]{2,1,0:T(8,128)(2,1)S(1)} %bitcast.33), channel_id=1, replica_groups=mesh['y'=4,'zh'=4,'core'=2,'zl'=2,'x'=4] {'zh','zl','x'}, dimensions={0} | all-to-all | bytes 524288 | tf_op jit(solution)/shard_map/all_to_all | solution.py:430
  148.0 5.0 %collective-permute-start.12 = (f32[16,128]{1,0:T(8,128)S(1)}, f32[16,128]{1,0:T(8,128)S(1)}, u32[]{:S(2)}, u32[]{:S(2)}) collective-permute-start(f32[16,128]{1,0:T(8,128)S(1)} %get-tuple-element.47), channel_id=1, source_target_pairs={{0,8},{8,16},{16,24},{24,32},{32,40},{40,48},{48,56},{56,64},{64,7... | collective-permute-start | bytes 24584 | tf_op jit(solution)/shard_map/ppermute | solution.py:468
  153.0 2.1 %collective-permute-start.13 = (f32[16,128]{1,0:T(8,128)S(1)}, f32[16,128]{1,0:T(8,128)S(1)}, u32[]{:S(2)}, u32[]{:S(2)}) collective-permute-start(f32[16,128]{1,0:T(8,128)S(1)} %get-tuple-element.46), channel_id=1, source_target_pairs={{8,0},{16,8},{24,16},{32,24},{40,32},{48,40},{56,48},{64,56},{72,6... | collective-permute-start | bytes 24584 | tf_op jit(solution)/shard_map/ppermute | solution.py:469
  155.2 3.6 %collective-permute-done.13.below_ref = f32[16,128]{1,0:T(8,128)S(1)} collective-permute-done((f32[16,128]{1,0:T(8,128)S(1)}, f32[16,128]{1,0:T(8,128)S(1)}, u32[]{:S(2)}, u32[]{:S(2)}) %collective-permute-start.13) | collective-permute-done | bytes 8224 | tf_op jit(solution)/shard_map/ppermute | solution.py:469
  158.9 6.7 %shard_map.167 = (f32[4,4,8,64]{3,2,1,0:T(8,128)S(1)}, bf16[4,4,12,384]{3,2,1,0:T(8,128)(2,1)S(1)}) custom-call(f32[16,128]{1,0:T(8,128)S(1)} %collective-permute-done.12.above_ref, f32[32,128]{1,0:T(8,128)S(1)} %convert_reduce_fusion.mine_ref, f32[16,128]{1,0:T(8,128)S(1)} %collective-permute-done.13.below_ref, f32[4,4,8,64]{3,2,1,0:T(8,128)S(1)} %slice.113.noisy_ref, ...), custom_call_target="tpu_custom_call" | custom-call | tf_op jit(solution)/shard_map/pallas_call | solution.py:259
  (145 shorter events, 30.6 us)
Async XLA Ops:
  0.6 71.9 %copy-start = (bf16[4096,64]{0,1:T(8,128)(2,1)S(1)}, bf16[4096,64]{0,1:T(8,128)(2,1)}, u32[]{:S(2)}) copy-start(bf16[4096,64]{0,1:T(8,128)(2,1)} %param.18) | copy-start | bytes 1572868
  3.6 21.5 %copy-start.7 = (bf16[3,3,3,16,384]{4,3,2,1,0:T(8,128)(2,1)S(1)}, bf16[3,3,3,16,384]{4,3,2,1,0:T(8,128)(2,1)}, u32[]{:S(2)}) copy-start(bf16[3,3,3,16,384]{4,3,2,1,0:T(8,128)(2,1)} %param.24) | copy-start | bytes 995332
  3.6 38.0 %collective-permute-start = (f32[90,128]{1,0:T(8,128)S(1)}, f32[90,128]{1,0:T(8,128)S(1)}, u32[]{:S(2)}, u32[]{:S(2)}) collective-permute-start(f32[90,128]{1,0:T(8,128)S(1)} %maximum_bitcast_fusion.1), channel_id=1, source_target_pairs={{0,8},{8,16},{16,24},{24,32},{32,40},{40,48},{48,56},{56,64},{64,7... | collective-permute-start | bytes 138248 | tf_op jit(solution)/shard_map/ppermute | solution.py:310
  12.3 54.9 %all-to-all-start = ((bf16[32,48,384]{2,1,0:T(8,128)(2,1)}), bf16[32,48,384]{2,1,0:T(8,128)(2,1)}, u32[]{:S(2)}, u32[]{:S(2)}) async-start(bf16[32,48,384]{2,1,0:T(8,128)(2,1)} %shard_map.161), calls=%async_computation | async-start | bytes 2359296 | tf_op jit(solution)/shard_map/all_to_all | solution.py:406
  22.4 27.3 %collective-permute-start.1 = (f32[90,128]{1,0:T(8,128)}, f32[90,128]{1,0:T(8,128)S(1)}, u32[]{:S(2)}, u32[]{:S(2)}) collective-permute-start(f32[90,128]{1,0:T(8,128)} %maximum_bitcast_fusion.2), channel_id=1, source_target_pairs={{8,0},{16,8},{24,16},{32,24},{40,32},{48,40},{56,48},{64,56},{72,6... | collective-permute-start | bytes 138248 | tf_op jit(solution)/shard_map/ppermute | solution.py:311
  42.4 18.4 %copy-start.3 = (f32[6,2,12,16]{3,1,2,0:T(2,128)}, f32[6,2,12,16]{3,1,2,0:T(2,128)S(1)}, u32[]{:S(2)}) copy-start(f32[6,2,12,16]{3,1,2,0:T(2,128)S(1)} %copy.52) | copy-start | bytes 27652
  52.5 8.4 %collective-permute-start.2 = (f32[48,128]{1,0:T(8,128)S(1)}, f32[48,128]{1,0:T(8,128)S(1)}, u32[]{:S(2)}, u32[]{:S(2)}) collective-permute-start(f32[48,128]{1,0:T(8,128)S(1)} %maximum_bitcast_fusion.3), channel_id=1, source_target_pairs={{0,1},{1,2},{2,3},{3,4},{4,5},{5,6},{6,7},{8,9},{9,10},{10,11},{11... | collective-permute-start | bytes 73736 | tf_op jit(solution)/shard_map/ppermute | solution.py:310
  55.4 6.2 %collective-permute-start.3 = (f32[48,128]{1,0:T(8,128)S(1)}, f32[48,128]{1,0:T(8,128)S(1)}, u32[]{:S(2)}, u32[]{:S(2)}) collective-permute-start(f32[48,128]{1,0:T(8,128)S(1)} %maximum_bitcast_fusion.4), channel_id=1, source_target_pairs={{1,0},{2,1},{3,2},{4,3},{5,4},{6,5},{7,6},{9,8},{10,9},{11,10},{12... | collective-permute-start | bytes 73736 | tf_op jit(solution)/shard_map/ppermute | solution.py:311
  69.4 9.8 %collective-permute-start.5 = (bf16[768,256]{1,0:T(8,128)(2,1)}, bf16[768,256]{1,0:T(8,128)(2,1)}, u32[]{:S(2)}, u32[]{:S(2)}) collective-permute-start(bf16[768,256]{1,0:T(8,128)(2,1)} %get-tuple-element.35), channel_id=1, source_target_pairs={{0,64},{64,128},{128,192},{192,0},{1,65},{65,129},{129,193},{193,1... | collective-permute-start | bytes 1179656 | tf_op jit(solution)/shard_map/ppermute | solution.py:414
  72.5 6.9 %collective-permute-start.4 = (bf16[1536,128]{1,0:T(8,128)(2,1)}, bf16[1536,128]{1,0:T(8,128)(2,1)}, u32[]{:S(2)}, u32[]{:S(2)}) collective-permute-start(bf16[1536,128]{1,0:T(8,128)(2,1)} %slice.142), channel_id=1, source_target_pairs={{0,8},{8,0},{1,9},{9,1},{2,10},{10,2},{3,11},{11,3},{4,12},{12,4},... | collective-permute-start | bytes 1179656 | tf_op jit(solution)/shard_map/ppermute | solution.py:416
  72.6 30.5 %collective-permute-start.10 = (bf16[768,256]{1,0:T(8,128)(2,1)}, bf16[768,256]{1,0:T(8,128)(2,1)S(1)}, u32[]{:S(2)}, u32[]{:S(2)}) collective-permute-start(bf16[768,256]{1,0:T(8,128)(2,1)} %get-tuple-element.35), channel_id=1, source_target_pairs={{64,0},{128,64},{192,128},{0,192},{65,1},{129,65},{193,129},{1,193... | collective-permute-start | bytes 1179656 | tf_op jit(solution)/shard_map/ppermute | solution.py:419
  74.3 17.4 %collective-permute-start.7 = (bf16[768,256]{1,0:T(8,128)(2,1)}, bf16[768,256]{1,0:T(8,128)(2,1)S(1)}, u32[]{:S(2)}, u32[]{:S(2)}) collective-permute-start(bf16[768,256]{1,0:T(8,128)(2,1)} %get-tuple-element.34), channel_id=1, source_target_pairs={{64,0},{128,64},{192,128},{0,192},{65,1},{129,65},{193,129},{1,193... | collective-permute-start | bytes 1179656 | tf_op jit(solution)/shard_map/ppermute | solution.py:415
  75.8 27.4 %collective-permute-start.9 = (bf16[768,256]{1,0:T(8,128)(2,1)}, bf16[768,256]{1,0:T(8,128)(2,1)S(1)}, u32[]{:S(2)}, u32[]{:S(2)}) collective-permute-start(bf16[768,256]{1,0:T(8,128)(2,1)} %get-tuple-element.34), channel_id=1, source_target_pairs={{0,64},{64,128},{128,192},{192,0},{1,65},{65,129},{129,193},{193,1... | collective-permute-start | bytes 1179656 | tf_op jit(solution)/shard_map/ppermute | solution.py:418
  79.2 32.8 %collective-permute-start.6 = (bf16[768,256]{1,0:T(8,128)(2,1)}, bf16[768,256]{1,0:T(8,128)(2,1)S(1)}, u32[]{:S(2)}, u32[]{:S(2)}) collective-permute-start(bf16[768,256]{1,0:T(8,128)(2,1)} %collective-permute-done.5.refs_2_), channel_id=1, source_target_pairs={{0,64},{64,128},{128,192},{192,0},{1,65},{65,129},{129,193},{193,1... | collective-permute-start | bytes 1179656 | tf_op jit(solution)/shard_map/ppermute | solution.py:421
  91.7 20.3 %collective-permute-start.8 = (bf16[768,256]{1,0:T(8,128)(2,1)S(1)}, bf16[768,256]{1,0:T(8,128)(2,1)S(1)}, u32[]{:S(2)}, u32[]{:S(2)}) collective-permute-start(bf16[768,256]{1,0:T(8,128)(2,1)S(1)} %collective-permute-done.7.refs_3_), channel_id=1, source_target_pairs={{64,0},{128,64},{192,128},{0,192},{65,1},{129,65},{193,129},{1,193... | collective-permute-start | bytes 1179656 | tf_op jit(solution)/shard_map/ppermute | solution.py:422
  103.2 55.7 %slice-start = ((s8[7962624]{0:T(1024)(128)(4,1)}), s8[3768320]{0:T(1024)(128)(4,1)S(1)}, s32[]{:S(2)}) async-start(s8[7962624]{0:T(1024)(128)(4,1)} %bitcast.30), calls=%async_computation.2 | async-start | bytes 7536640
  112.0 46.9 %slice-start.1 = ((s8[7962624]{0:T(1024)(128)(4,1)}), s8[4194304]{0:T(1024)(128)(4,1)S(1)}, s32[]{:S(2)}) async-start(s8[7962624]{0:T(1024)(128)(4,1)} %bitcast.30), calls=%async_computation.3 | async-start | bytes 8388608
  121.8 33.3 %copy-start.11 = (f32[384]{0:T(512)S(1)}, f32[384]{0:T(512)}, u32[]{:S(2)}) copy-start(f32[384]{0:T(512)} %param.25) | copy-start | bytes 4612
  121.8 33.3 %copy-start.12 = (f32[384]{0:T(512)S(1)}, f32[384]{0:T(512)}, u32[]{:S(2)}) copy-start(f32[384]{0:T(512)} %param.26) | copy-start | bytes 4612
  121.8 33.3 %copy-start.13 = (f32[384]{0:T(512)S(1)}, f32[384]{0:T(512)}, u32[]{:S(2)}) copy-start(f32[384]{0:T(512)} %param.29) | copy-start | bytes 4612
  121.8 37.0 %copy-start.1 = (f32[3,64]{1,0:T(4,128)S(1)}, f32[3,64]{1,0:T(4,128)}, u32[]{:S(2)}) copy-start(f32[3,64]{1,0:T(4,128)} %pad_maximum_fusion.9.affine_ref) | copy-start | bytes 2308
  121.8 3.7 %collective-permute-start.11 = (f32[1536,128]{1,0:T(8,128)S(1)}, f32[1536,128]{1,0:T(8,128)S(1)}, u32[]{:S(2)}, u32[]{:S(2)}) collective-permute-start(f32[1536,128]{1,0:T(8,128)S(1)} %get-tuple-element.16), channel_id=1, source_target_pairs={{0,8},{8,0},{1,9},{9,1},{2,10},{10,2},{3,11},{11,3},{4,12},{12,4},... | collective-permute-start | bytes 2359304 | tf_op jit(solution)/shard_map/ppermute | solution.py:428
  148.0 7.2 %collective-permute-start.12 = (f32[16,128]{1,0:T(8,128)S(1)}, f32[16,128]{1,0:T(8,128)S(1)}, u32[]{:S(2)}, u32[]{:S(2)}) collective-permute-start(f32[16,128]{1,0:T(8,128)S(1)} %get-tuple-element.47), channel_id=1, source_target_pairs={{0,8},{8,16},{16,24},{24,32},{32,40},{40,48},{48,56},{56,64},{64,7... | collective-permute-start | bytes 24584 | tf_op jit(solution)/shard_map/ppermute | solution.py:468
  153.0 5.9 %collective-permute-start.13 = (f32[16,128]{1,0:T(8,128)S(1)}, f32[16,128]{1,0:T(8,128)S(1)}, u32[]{:S(2)}, u32[]{:S(2)}) collective-permute-start(f32[16,128]{1,0:T(8,128)S(1)} %get-tuple-element.46), channel_id=1, source_target_pairs={{8,0},{16,8},{24,16},{32,24},{40,32},{48,40},{56,48},{64,56},{72,6... | collective-permute-start | bytes 24584 | tf_op jit(solution)/shard_map/ppermute | solution.py:469
  (9 other events, 58.7 us)

commit v4 on v3

--- a/solution.py
+++ b/solution.py
@@ -155,7 +155,7 @@
         in_specs=in_specs,
         out_specs=out_specs,
         out_shape=out_shape,
-        compiler_params=pltpu.CompilerParams(vmem_limit_bytes=40 << 20),
+        compiler_params=pltpu.CompilerParams(vmem_limit_bytes=20 << 20),
         cost_estimate=pl.CostEstimate(
             flops=2 * rows * keys * 512 * 2,
             bytes_accessed=rows * 4096,
@@ -164,15 +164,17 @@
     )(*args)
 
 
+def inside(at, low, high, before, after):
+    return ((at > low) | before) & ((at < high) | after)
+
+
 def tail_kernel(
     above_ref,
     mine_ref,
     below_ref,
-    noisy_ref,
-    cache_ref,
+    cells_ref,
     affine_ref,
-    token_ok_ref,
-    cell_ok_ref,
+    beyond_ref,
     w1_ref,
     b1_ref,
     gain_ref,
@@ -185,6 +187,7 @@
     sems,
     vel,
     lat,
+    den,
     first,
     act,
     wide,
@@ -199,11 +202,22 @@
             vel[f, at, 0:4, :] = rows[f * 4 : f * 4 + 4]
             vel[f, at, 4:8, :] = turned[f * 4 : f * 4 + 4]
     level, scale, mean = affine_ref[0:1, :], affine_ref[1:2, :], affine_ref[2:3, :]
-    denoised = noisy_ref[...] - level * vel[:, :, :, 0:64]
-    den_ref[...] = denoised
-    latent = jnp.where(token_ok_ref[...] > 0, denoised * scale + mean, 0.0)
+    denoised = cells_ref[2:6, :, :, 0:64] - level * vel[:, :, :, 0:64]
+    up, down, before, after = (beyond_ref[k] > 0 for k in range(4))
+    row = lax.broadcasted_iota(jnp.int32, denoised.shape, 1)
+    col = lax.broadcasted_iota(jnp.int32, denoised.shape, 2)
+    kept = inside(row, 0, 3, up, down) & inside(col, 0, 7, before, after)
+    latent = jnp.where(kept, denoised * scale + mean, 0.0)
+    for k in range(4):
+        part = jnp.concatenate([denoised, denoised], axis=3).reshape(F * 32, 128)
+        part = pltpu.roll(part, 128 - LAT * k, axis=1) if k else part
+        part = part.reshape(F, 4, 8, 128)
+        for f in range(F):
+            for r in range(2):
+                den[f, 2 * r + k // 2, pl.ds(k % 2, 8, stride=2), :] = part[f, r + 1]
+    den_ref[...] = den[:, :, 2:14, 0:LAT]
     lat[...] = jnp.zeros(lat.shape, jnp.float32)
-    lat[0:2, :, 0:8, 0:64] = cache_ref[...]
+    lat[0:2, :, 0:8, 0:64] = cells_ref[0:2, :, :, 0:64]
     lat[2:6, :, 0:8, 0:64] = latent.astype(jnp.bfloat16).astype(jnp.float32)
     here = lat[:, :, 0:8, :].reshape(192, 128)
     right = pltpu.roll(lat[:, :, 1:9, :].reshape(192, 128), 64, axis=1)
@@ -213,7 +227,7 @@
     window = jnp.concatenate([pair, lower], axis=3).reshape(192, 256).astype(jnp.bfloat16)
     parts = C1 // 128
     for k in range(parts):
-        act[k, 0:2, :, 0:14, :] = mid_ref[:, :, :, pl.ds(k * 128, 128)]
+        act[k, 0:2, :, 0:16, :] = mid_ref[:, :, :, pl.ds(k * 128, 128)]
     gain = gain_ref[...]
     for p in range(2):
         for q in range(2):
@@ -228,7 +242,10 @@
             power = jnp.mean(value * value, axis=1, keepdims=True)
             normed = value * lax.rsqrt(power + EPSILON) * gain
             active = (normed / (1.0 + jnp.exp(-normed))).reshape(F, 32, C1)
-            active = active * cell_ok_ref[2 * p + q, :, 0:1]
+            at = lax.broadcasted_iota(jnp.int32, (32, C1), 0)
+            kept = inside(2 * (at // 8) + p, 0, 5, up, down)
+            kept = kept & inside(2 * (at % 8) + q, 0, 13, before, after)
+            active = jnp.where(kept, active, 0.0)
             value = value.reshape(F, 4, 8, C1)
             active = active.reshape(F, 4, 8, C1)
             for r in range(3):
@@ -255,13 +272,14 @@
 
 def tail(*args):
     specs = [pl.BlockSpec(memory_space=pltpu.VMEM)] * len(args)
-    specs[12] = pl.BlockSpec(memory_space=pl.ANY)
+    specs[5] = pl.BlockSpec(memory_space=pltpu.SMEM)
+    specs[10] = pl.BlockSpec(memory_space=pl.ANY)
     return pl.pallas_call(
         tail_kernel,
         in_specs=specs,
         out_specs=[pl.BlockSpec(memory_space=pltpu.VMEM)] * 2,
         out_shape=[
-            jax.ShapeDtypeStruct((F, 4, 8, 64), jnp.float32),
+            jax.ShapeDtypeStruct((F, 4, 12, LAT), jnp.float32),
             jax.ShapeDtypeStruct((F, 4, 12, C1), jnp.bfloat16),
         ],
         scratch_shapes=[
@@ -269,6 +287,7 @@
             pltpu.SemaphoreType.DMA((9,)),
             pltpu.VMEM((F, 4, 8, 128), jnp.float32),
             pltpu.VMEM((6, 4, 16, 128), jnp.float32),
+            pltpu.VMEM((F, 4, 16, 128), jnp.float32),
             pltpu.VMEM((C1 // 128, F, 6, 24, 128), jnp.float32),
             pltpu.VMEM((C1 // 128, 6, 6, 24, 128), jnp.float32),
             pltpu.VMEM((6, 6, 16, 3 * C1), jnp.bfloat16),
@@ -277,20 +296,122 @@
     )(*args)
 
 
+def window_kernel(w_ref, out_ref):
+    out_ref[...] = jnp.zeros(out_ref.shape, out_ref.dtype)
+    for t in range(3):
+        for u in range(3):
+            for v in range(3):
+                taps = w_ref[t, u, v]
+                for p in range(2):
+                    for q in range(2):
+                        (dr, a), (dc, b) = divmod(p + u, 2), divmod(q + v, 2)
+                        at = dr * 128 + dc * 64 + a * 32 + b * 16
+                        out_ref[t, pl.ds(at, LAT), pl.ds((2 * p + q) * C1, C1)] = taps
+
+
 def window_weights(weight):
-    cells = [
-        jnp.pad(weight, ((0, 0), (p, 1 - p), (q, 1 - q), (0, 0), (0, 0)))
-        for p in range(2)
-        for q in range(2)
-    ]
-    joined = jnp.stack(cells, axis=4).reshape(3, 2, 2, 2, 2, LAT, 4, C1)
-    return joined.transpose(0, 1, 3, 2, 4, 5, 6, 7).reshape(3, 16 * LAT, 4 * C1)
-
-
-def by_token(cells):
-    frames = cells.shape[0]
-    split = cells.reshape(frames, 4, 2, 8, 2, LAT).transpose(0, 1, 3, 2, 4, 5)
-    return split.reshape(frames, 4, 8, 4 * LAT)
+    return pl.pallas_call(
+        window_kernel,
+        out_shape=jax.ShapeDtypeStruct((3, 16 * LAT, 4 * C1), jnp.bfloat16),
+        compiler_params=pltpu.CompilerParams(vmem_limit_bytes=16 << 20),
+    )(weight)
+
+
+def put_frames(ref, rows, tokens):
+    count = tokens[0].shape[0]
+    low = lax.broadcasted_iota(jnp.int32, (count, 128), 1) < 64
+    for i in range(2):
+        for h in range(2):
+            one = tokens[i + 2 * h]
+            two = pltpu.roll(tokens[i + 4], 64, axis=1) if h == 0 else jnp.zeros_like(one)
+            ref[i, pl.ds(rows + h * count, count), 384:512] = jnp.where(low, one, two)
+
+
+def get_frames(ref, rows, count):
+    out = {}
+    for i in range(2):
+        for h in range(2):
+            both = ref[i, pl.ds(rows + h * count, count), 384:512]
+            out[i + 2 * h] = both
+            if h == 0:
+                out[i + 4] = pltpu.roll(both, 64, axis=1)
+    return [out[f] for f in range(6)]
+
+
+def edge_rows_kernel(noisy_ref, cache_ref, mid_ref, tok_ref, down_ref, up_ref, cells):
+    cells[...] = jnp.zeros(cells.shape, jnp.float32)
+    cells[0:2, :, 0:12, 0:LAT] = cache_ref[...].astype(jnp.float32)
+    cells[2:6, :, 0:12, 0:LAT] = noisy_ref[...]
+    lane = lax.broadcasted_iota(jnp.int32, (8, 128), 1)
+    tokens = {}
+    for r in range(2):
+        for f in range(6):
+            token = jnp.zeros((8, 128), jnp.float32)
+            for k in range(4):
+                part = cells[f, 2 * r + k // 2, pl.ds(k % 2, 8, stride=2), :]
+                part = pltpu.roll(part, LAT * k, axis=1) if k else part
+                token = jnp.where((lane >= LAT * k) & (lane < LAT * k + LAT), part, token)
+            tok_ref[f, r] = token
+            tokens[f, r] = token
+    for ref, row, r in ((down_ref, 3, 1), (up_ref, 0, 0)):
+        ref[...] = jnp.zeros(ref.shape, jnp.float32)
+        ref[:, 0:12, 0:C1] = mid_ref[:, row].astype(jnp.float32)
+        put_frames(ref, 0, [tokens[f, r] for f in range(6)])
+
+
+def edge_cols_kernel(tok_ref, mid_ref, above_ref, below_ref, toks, mids, right_ref, left_ref):
+    above, below = get_frames(above_ref, 0, 8), get_frames(below_ref, 0, 8)
+    for f in range(6):
+        toks[f, 0] = above[f]
+        toks[f, 1] = tok_ref[f, 0]
+        toks[f, 2] = tok_ref[f, 1]
+        toks[f, 3] = below[f]
+    mids[...] = jnp.zeros(mids.shape, jnp.float32)
+    mids[:, 0, 0:12, :] = above_ref[:, 0:12, 0:C1]
+    mids[:, 1:5, 0:12, :] = mid_ref[...].astype(jnp.float32)
+    mids[:, 5, 0:12, :] = below_ref[:, 0:12, 0:C1]
+    for ref, token, col in ((right_ref, 5, 11), (left_ref, 0, 0)):
+        ref[...] = jnp.zeros(ref.shape, jnp.float32)
+        for i in range(2):
+            for row in range(6):
+                ref[i, pl.ds(row, 1), 0:C1] = mids[i, row, pl.ds(col, 1), :]
+        for r in range(4):
+            put_rows(ref, r, [toks[f, r, pl.ds(token, 1), :] for f in range(6)])
+
+
+def put_rows(ref, r, tokens):
+    low = lax.broadcasted_iota(jnp.int32, (1, 128), 1) < 64
+    for i in range(2):
+        for h in range(2):
+            one = tokens[i + 2 * h]
+            two = pltpu.roll(tokens[i + 4], 64, axis=1) if h == 0 else jnp.zeros_like(one)
+            ref[i, pl.ds(4 * h + r, 1), 384:512] = jnp.where(low, one, two)
+
+
+def place_kernel(toks, mids, left_ref, right_ref, cells_ref, cache_ref):
+    cells_ref[...] = jnp.zeros(cells_ref.shape, jnp.float32)
+    cache_ref[...] = jnp.zeros(cache_ref.shape, jnp.float32)
+    for f in range(6):
+        for r in range(4):
+            cells_ref[f, r, 1:7, :] = toks[f, r, 0:6, :]
+    cache_ref[:, :, 1:13, :] = mids[:, :, 0:12, :]
+    for ref, token, col in ((left_ref, 0, 0), (right_ref, 7, 13)):
+        frames = get_frames(ref, 0, 4)
+        for f in range(6):
+            for r in range(4):
+                cells_ref[f, r, pl.ds(token, 1), :] = frames[f][r : r + 1]
+        for i in range(2):
+            for row in range(6):
+                cache_ref[i, row, pl.ds(col, 1), :] = ref[i, pl.ds(row, 1), 0:C1]
+
+
+def small_call(kernel, shapes, scratch=()):
+    return pl.pallas_call(
+        kernel,
+        out_shape=[jax.ShapeDtypeStruct(shape, jnp.float32) for shape in shapes],
+        scratch_shapes=[pltpu.VMEM(shape, jnp.float32) for shape in scratch],
+        compiler_params=pltpu.CompilerParams(vmem_limit_bytes=8 << 20),
+    )
 
 
 def along(axis, step):
@@ -298,43 +419,20 @@
     return [(i, i + step) for i in range(count) if 0 <= i + step < count]
 
 
-def swap_edges(parts, axis, dims, widths):
-    def cut(tail):
-        flat = []
-        for part, dim, width in zip(parts, dims, widths):
-            size = part.shape[dim]
-            start = size - width if tail else 0
-            flat.append(lax.slice_in_dim(part, start, start + width, axis=dim).reshape(-1))
-        return jnp.concatenate(flat).reshape(-1, 128)
-
-    before = lax.ppermute(cut(True), axis, along(axis, 1)).reshape(-1)
-    after = lax.ppermute(cut(False), axis, along(axis, -1)).reshape(-1)
-    wider, at = [], 0
-    for part, dim, width in zip(parts, dims, widths):
-        shape = list(part.shape)
-        shape[dim] = width
-        size = math.prod(shape)
-        wider.append(
-            jnp.concatenate(
-                [
-                    before[at : at + size].reshape(shape),
-                    part,
-                    after[at : at + size].reshape(shape),
-                ],
-                axis=dim,
-            )
-        )
-        at += size
-    return wider
-
-
 def input_halos(noisy, cache_in, cache_mid):
-    both = jnp.concatenate([cache_in.astype(jnp.float32), noisy], axis=0)
-    parts = [both, cache_mid.astype(jnp.float32)]
-    parts = swap_edges(parts, SEQ, (1, 1), (2, 1))
-    both, cache_mid = swap_edges(parts, BLK, (2, 2), (2, 1))
-    both = by_token(both)
-    return both[2:], both[:2], cache_mid
+    edge = (2, 16, 512)
+    toks, down, up = small_call(
+        edge_rows_kernel, [(6, 2, 8, 128), edge, edge], [(6, 4, 16, 128)]
+    )(noisy, cache_in, cache_mid)
+    above = lax.ppermute(down, SEQ, along(SEQ, 1))
+    below = lax.ppermute(up, SEQ, along(SEQ, -1))
+    side = (2, 8, 512)
+    toks, mids, right, left = small_call(
+        edge_cols_kernel, [(6, 4, 8, 128), (2, 6, 16, C1), side, side]
+    )(toks, cache_mid, above, below)
+    before = lax.ppermute(right, BLK, along(BLK, 1))
+    after = lax.ppermute(left, BLK, along(BLK, -1))
+    return small_call(place_kernel, [(6, 4, 8, 128), (2, 6, 16, C1)])(toks, mids, before, after)
 
 
 def pack_kernel(q_ref, k_ref, v_ref, out_ref):
@@ -400,8 +498,10 @@
     )(own, oth)
 
 
-def attention(query_vectors, key_vectors, value_vectors, weight_head, work):
+def attention(query_vectors, key_vectors, value_vectors, weight_head, work, inputs):
     packed = pack(query_vectors, key_vectors, value_vectors)
+    packed, inputs = lax.optimization_barrier((packed, inputs))
+    work = work(*inputs)
     heads, tokens = packed.shape[:2]
     moved = lax.all_to_all(packed, HEAD, split_axis=0, concat_axis=0, tiled=True)
     moved, work = lax.optimization_barrier((moved, work))
@@ -417,6 +517,7 @@
     state = flash(moved, q_oth, [moved])
     left_b = lax.ppermute(b, "y", right)
     right_a = lax.ppermute(a, "y", left)
+    state, left_a, right_b = lax.optimization_barrier((state, left_a, right_b))
     state = flash(moved, q_oth, [left_a, right_b], state)
     far_a = lax.ppermute(left_a, "y", right)
     far_b = lax.ppermute(right_b, "y", left)
@@ -448,34 +549,34 @@
     weight_mid,
     bias_mid,
 ):
-    row, col = lax.axis_index(SEQ), lax.axis_index(BLK)
-    last_row, last_col = lax.axis_size(SEQ) - 1, lax.axis_size(BLK) - 1
-    row_ok, col_ok = inside(8, row, last_row), inside(16, col, last_col)
-    token_ok = (row_ok[::2, None] & col_ok[None, ::2]).astype(jnp.float32)
-    token_ok = jnp.broadcast_to(token_ok[:, :, None], (4, 8, 4 * LAT))
-    cell_ok = inside(8, row, last_row)[1:7, None] & jnp.pad(col_ok[1:15], (0, 2))[None, :]
-    cell_ok = cell_ok.reshape(3, 2, 8, 2).transpose(1, 3, 0, 2).astype(jnp.float32)
-    cell_ok = jnp.pad(cell_ok, ((0, 0), (0, 0), (0, 1), (0, 0))).reshape(4, 32, 1)
-    cell_ok = jnp.broadcast_to(cell_ok, (4, 32, 128))
-    level = jnp.broadcast_to(noise_level, (4 * LAT,))
-    affine = jnp.stack([level, jnp.tile(latent_scale, 4), jnp.tile(latent_mean, 4)])
-
-    halos = input_halos(noisy_latent, cache_in, cache_mid)
-    work = (*halos, token_ok, cell_ok, affine, window_weights(weight_in))
-    mine, work = attention(query_vectors, key_vectors, value_vectors, weight_head, work)
-    noisy, cache_first, cache_second, token_ok, cell_ok, affine, weight_first = work
+    def work(noisy, cache_first, cache_second, weight_first):
+        row, col = lax.axis_index(SEQ), lax.axis_index(BLK)
+        last_row, last_col = lax.axis_size(SEQ) - 1, lax.axis_size(BLK) - 1
+        beyond = jnp.stack([row > 0, row < last_row, col > 0, col < last_col])
+        level = jnp.broadcast_to(noise_level, (4 * LAT,))
+        affine = jnp.stack([level, jnp.tile(latent_scale, 4), jnp.tile(latent_mean, 4)])
+        halos = input_halos(noisy, cache_first, cache_second)
+        return (*halos, beyond.astype(jnp.int32), affine, window_weights(weight_first))
+
+    mine, work = attention(
+        query_vectors,
+        key_vectors,
+        value_vectors,
+        weight_head,
+        work,
+        (noisy_latent, cache_in, cache_mid, weight_in),
+    )
+    cells, cache_second, beyond, affine, weight_first = work
 
     above = lax.ppermute(mine[16:], SEQ, along(SEQ, 1))
     below = lax.ppermute(mine[:16], SEQ, along(SEQ, -1))
-    denoised, features = tail(
+    return tail(
         above,
         mine,
         below,
-        noisy,
-        cache_first,
+        cells,
         affine,
-        token_ok,
-        cell_ok,
+        beyond,
         weight_first,
         bias_in.reshape(1, C1),
         norm_gain.reshape(1, C1),
@@ -483,13 +584,6 @@
         weight_mid.reshape(9, 3 * C1, C1),
         bias_mid.reshape(1, C1),
     )
-    denoised = denoised[:, 1:3, 1:7].reshape(F, 2, 6, 2, 2, LAT).transpose(0, 1, 3, 2, 4, 5)
-    return denoised.reshape(F, 4, 12, LAT), features
-
-
-def inside(count, index, last):
-    at = jnp.arange(count)
-    return ((at >= 2) | (index > 0)) & ((at < count - 2) | (index < last))
 
 
 def solution(mesh):

time: 168 us -> 154 us (0.917)
  local copies, waits for them, and re-layouts: 25.9 us -> 4.77 us
  waiting for transfers between devices: 19.6 us -> 36.4 us
  other arithmetic: 14 us -> 0.2 us
  starting transfers between devices: 37.9 us -> 42.4 us
  Pallas kernels: 46.5 us -> 48.6 us
  blocking collectives: 21.3 us -> 19.6 us
    ppermute x4, waiting for transfers between devices: 7.33 us -> 24.1 us  [the longest x1 15.3 us: input_halos(): above = lax.ppermute(down, SEQ, along(SEQ, 1))]
    transpose x1 -> x0, other arithmetic: 7.59 us -> none  [window_weights(): return joined.transpose(0, 1, 3, 2, 4, 5, 6, 7).reshape(3, 16 * LAT, 4 * C1)]
    another operation x9 -> x5, local copies, waits for them, and re-layouts: 7.07 us -> 0.18 us  [the longest x3 0.17 us: work(): jnp.stack([level, jnp.tile(latent_scale, 4), jnp.tile(latent_mean, 4)])]
    reshape x23 -> x0, local copies, waits for them, and re-layouts: 5.94 us -> none  [the longest x1 4 us: window_weights(): return joined.transpose(0, 1, 3, 2, 4, 5, 6, 7).reshape(3, 16 * LAT, 4 * C1)]
    slice x23 -> x0, local copies, waits for them, and re-layouts: 4.75 us -> none  [the longest x4 1.96 us: input_halos(): return (both[2:], both[:2], cache_mid)]
    ppermute x1, waiting for transfers between devices: 3.4 us -> 0.01 us  [attention(): left_a = lax.ppermute(a, 'y', right)]
    ppermute x1, waiting for transfers between devices: 3.31 us -> 6.57 us  [attention(): right_b = lax.ppermute(b, 'y', left)]
    concatenate x3 -> x0, other arithmetic: 3.04 us -> none  [the longest x2 1.98 us: swap_edges(): jnp.concatenate([before[at:at + size].reshape(shape), part, after[at:at +...]
  transfers between devices with their start and end apart: 15 -> 15, of which waited for: 5 -> 6; matrix products, arithmetic and copies ran while one was open for 19% -> 1% of each run, Pallas kernels for 17% -> 18%
where the time goes in v4:
time: 154 us
  Pallas kernels  48.6 us (32%)
  starting transfers between devices  42.4 us (28%)
  waiting for transfers between devices  36.4 us (24%)
  blocking collectives  19.6 us (13%)
  local copies, waits for them, and re-layouts  4.77 us (3%)
  between operations  1.72 us (1%)
    pallas_call x4, Pallas kernels, flash(): pl.pallas_call(functools.partial(flash_kernel, first, last, len(kvs), hal...  37.1 us
    all_to_all x1, blocking collectives, attention(): lax.all_to_all(partial, HEAD, split_axis=0, concat_axis=0, tiled=True)  19.6 us
    ppermute x1, waiting for transfers between devices, input_halos(): above = lax.ppermute(down, SEQ, along(SEQ, 1))  15.3 us
    all_to_all x1, starting transfers between devices, attention(): lax.all_to_all(packed, HEAD, split_axis=0, concat_axis=0, tiled=True)  12 us
    pallas_call x1, Pallas kernels, tail(): pl.pallas_call(tail_kernel, in_specs=specs, out_specs=[pl.BlockSpec(memor...  7.29 us
    ppermute x1, waiting for transfers between devices, attention(): right_b = lax.ppermute(b, 'y', left)  6.57 us
    ppermute x1, waiting for transfers between devices, input_halos(): below = lax.ppermute(up, SEQ, along(SEQ, -1))  5.71 us
    ppermute x1, starting transfers between devices, input_halos(): above = lax.ppermute(down, SEQ, along(SEQ, 1))  5.09 us
  transfers between devices with their start and end apart: 15, of which 6 were waited for; matrix products, arithmetic and copies ran while one was open for 1% of the time, Pallas kernels for 18%

profile of v4, /device:TPU:1, one launch (start us, length us, event | category | flops | bytes accessed | tf_op | source)
XLA Modules:
  0.0 153.7 jit_solution(6652601926149185565)
XLA Ops:
  0.7 2.4 %shard_map.161 = bf16[32,48,384]{2,1,0:T(8,128)(2,1)} custom-call(bf16[48,4096]{1,0:T(8,128)(2,1)} %q_ref.1, bf16[48,4096]{1,0:T(8,128)(2,1)} %k_ref.1, bf16[48,4096]{1,0:T(8,128)(2,1)} %v_ref.1), custom_call_target="tpu_custom_call" | custom-call | tf_op jit(solution)/shard_map/pallas_call | solution.py:450
  3.1 12.0 %all-to-all-start = ((bf16[32,48,384]{2,1,0:T(8,128)(2,1)}), bf16[32,48,384]{2,1,0:T(8,128)(2,1)}, u32[]{:S(2)}, u32[]{:S(2)}) async-start(bf16[32,48,384]{2,1,0:T(8,128)(2,1)} %shard_map.161), calls=%async_computation | async-start | bytes 2359296 | tf_op jit(solution)/shard_map/all_to_all | solution.py:506
  15.4 5.1 %collective-permute-start = (f32[2,16,512]{2,1,0:T(8,128)S(1)}, f32[2,16,512]{2,1,0:T(8,128)S(1)}, u32[]{:S(2)}, u32[]{:S(2)}) collective-permute-start(f32[2,16,512]{2,1,0:T(8,128)S(1)} %get-tuple-element.32), channel_id=1, source_target_pairs={{0,8},{8,16},{16,24},{24,32},{32,40},{40,48},{48,56},{56,64},{64,7... | collective-permute-start | bytes 196616 | tf_op jit(solution)/shard_map/ppermute | solution.py:427
  20.4 1.9 %collective-permute-start.1 = (f32[2,16,512]{2,1,0:T(8,128)S(1)}, f32[2,16,512]{2,1,0:T(8,128)S(1)}, u32[]{:S(2)}, u32[]{:S(2)}) collective-permute-start(f32[2,16,512]{2,1,0:T(8,128)S(1)} %get-tuple-element.33), channel_id=1, source_target_pairs={{8,0},{16,8},{24,16},{32,24},{40,32},{48,40},{56,48},{64,56},{72,6... | collective-permute-start | bytes 196616 | tf_op jit(solution)/shard_map/ppermute | solution.py:428
  23.3 15.3 %collective-permute-done.above_ref = f32[2,16,512]{2,1,0:T(8,128)S(1)} collective-permute-done((f32[2,16,512]{2,1,0:T(8,128)S(1)}, f32[2,16,512]{2,1,0:T(8,128)S(1)}, u32[]{:S(2)}, u32[]{:S(2)}) %collective-permute-start) | collective-permute-done | bytes 65568 | tf_op jit(solution)/shard_map/ppermute | solution.py:427
  38.6 5.7 %collective-permute-done.1.below_ref = f32[2,16,512]{2,1,0:T(8,128)S(1)} collective-permute-done((f32[2,16,512]{2,1,0:T(8,128)S(1)}, f32[2,16,512]{2,1,0:T(8,128)S(1)}, u32[]{:S(2)}, u32[]{:S(2)}) %collective-permute-start.1) | collective-permute-done | bytes 65568 | tf_op jit(solution)/shard_map/ppermute | solution.py:428
  44.5 3.2 %collective-permute-start.2 = (f32[2,8,512]{2,1,0:T(8,128)S(1)}, f32[2,8,512]{2,1,0:T(8,128)S(1)}, u32[]{:S(2)}, u32[]{:S(2)}) collective-permute-start(f32[2,8,512]{2,1,0:T(8,128)S(1)} %get-tuple-element.36), channel_id=1, source_target_pairs={{0,1},{1,2},{2,3},{3,4},{4,5},{5,6},{6,7},{8,9},{9,10},{10,11},{11... | collective-permute-start | bytes 98312 | tf_op jit(solution)/shard_map/ppermute | solution.py:433
  49.4 3.0 %collective-permute-done.3.right_ref = f32[2,8,512]{2,1,0:T(8,128)S(1)} collective-permute-done((f32[2,8,512]{2,1,0:T(8,128)S(1)}, f32[2,8,512]{2,1,0:T(8,128)S(1)}, u32[]{:S(2)}, u32[]{:S(2)}) %collective-permute-start.3) | collective-permute-done | bytes 32800 | tf_op jit(solution)/shard_map/ppermute | solution.py:434
  52.5 1.8 %slice.20 = bf16[1536,128]{1,0:T(8,128)(2,1)} slice(bf16[1536,384]{1,0:T(8,128)(2,1)} %bitcast.5.refs_0_.refs_2_), slice={[0:1536], [256:384]} | slice | bytes 786432 | tf_op jit(solution)/shard_map/slice | solution.py:516
  55.6 4.2 %collective-permute-start.5 = (bf16[768,256]{1,0:T(8,128)(2,1)S(1)}, bf16[768,256]{1,0:T(8,128)(2,1)S(1)}, u32[]{:S(2)}, u32[]{:S(2)}) collective-permute-start(bf16[768,256]{1,0:T(8,128)(2,1)S(1)} %get-tuple-element.55), channel_id=1, source_target_pairs={{0,64},{64,128},{128,192},{192,0},{1,65},{65,129},{129,193},{193,1... | collective-permute-start | bytes 1179656 | tf_op jit(solution)/shard_map/ppermute | solution.py:514
  59.8 1.8 %collective-permute-start.10 = (bf16[768,256]{1,0:T(8,128)(2,1)S(1)}, bf16[768,256]{1,0:T(8,128)(2,1)S(1)}, u32[]{:S(2)}, u32[]{:S(2)}) collective-permute-start(bf16[768,256]{1,0:T(8,128)(2,1)S(1)} %get-tuple-element.55), channel_id=1, source_target_pairs={{64,0},{128,64},{192,128},{0,192},{65,1},{129,65},{193,129},{1,193... | collective-permute-start | bytes 1179656 | tf_op jit(solution)/shard_map/ppermute | solution.py:519
  61.6 1.4 collective-permute-start.6
  63.1 9.0 %shard_map.166.refs_4_ = f32[3072,256]{1,0:T(8,128)S(1)} custom-call(bf16[1536,384]{1,0:T(8,128)(2,1)} %bitcast.5.refs_0_.refs_2_, bf16[1536,128]{1,0:T(8,128)(2,1)} %collective-permute-done.4.refs_1_, bf16[1536,384]{1,0:T(8,128)(2,1)} %bitcast.5.refs_0_.refs_2_), custom_call_target="tpu_custom_call" | custom-call | flops 4831838208 | bytes 6291456 | tf_op jit(solution)/shard_map/pallas_call | solution.py:152
  72.1 6.6 %collective-permute-done.6.refs_3_ = bf16[768,256]{1,0:T(8,128)(2,1)S(1)} collective-permute-done((bf16[768,256]{1,0:T(8,128)(2,1)S(1)}, bf16[768,256]{1,0:T(8,128)(2,1)S(1)}, u32[]{:S(2)}, u32[]{:S(2)}) %collective-permute-start.6) | collective-permute-done | bytes 393248 | tf_op jit(solution)/shard_map/ppermute | solution.py:515
  80.0 2.1 %collective-permute-start.8 = (bf16[768,256]{1,0:T(8,128)(2,1)S(1)}, bf16[768,256]{1,0:T(8,128)(2,1)S(1)}, u32[]{:S(2)}, u32[]{:S(2)}) collective-permute-start(bf16[768,256]{1,0:T(8,128)(2,1)S(1)} %collective-permute-done.6.refs_3_), channel_id=1, source_target_pairs={{64,0},{128,64},{192,128},{0,192},{65,1},{129,65},{193,129},{1,193... | collective-permute-start | bytes 1179656 | tf_op jit(solution)/shard_map/ppermute | solution.py:523
  82.0 8.9 %shard_map.167.refs_4_ = f32[3072,256]{1,0:T(8,128)S(1)} custom-call(bf16[1536,384]{1,0:T(8,128)(2,1)} %bitcast.5.refs_0_.refs_2_, bf16[1536,128]{1,0:T(8,128)(2,1)} %collective-permute-done.4.refs_1_, bf16[768,256]{1,0:T(8,128)(2,1)S(1)} %collective-permute-done.5.refs_2_, bf16[768,256]{1,0:T(8,128)(2,1)S(1)} %collective-permute-done.6.refs_3_, ...), custom_call_target="tpu_custom_call" | custom-call | flops 4831838208 | bytes 6291456 | tf_op jit(solution)/shard_map/pallas_call | solution.py:152
  91.0 9.1 %shard_map.168.refs_4_ = f32[3072,256]{1,0:T(8,128)S(1)} custom-call(bf16[1536,384]{1,0:T(8,128)(2,1)} %bitcast.5.refs_0_.refs_2_, bf16[1536,128]{1,0:T(8,128)(2,1)} %collective-permute-done.4.refs_1_, bf16[768,256]{1,0:T(8,128)(2,1)S(1)} %collective-permute-done.9.refs_2_, bf16[768,256]{1,0:T(8,128)(2,1)S(1)} %collective-permute-done.10.refs_3_, ...), custom_call_target="tpu_custom_call" | custom-call | flops 4831838208 | bytes 6291456 | tf_op jit(solution)/shard_map/pallas_call | solution.py:152
  100.2 10.1 %shard_map.169 = (f32[1536,128]{1,0:T(8,128)S(1)}, f32[1536,128]{1,0:T(8,128)S(1)}) custom-call(bf16[1536,384]{1,0:T(8,128)(2,1)} %bitcast.5.refs_0_.refs_2_, bf16[1536,128]{1,0:T(8,128)(2,1)} %collective-permute-done.4.refs_1_, bf16[768,256]{1,0:T(8,128)(2,1)S(1)} %collective-permute-done.7.refs_2_, bf16[768,256]{1,0:T(8,128)(2,1)S(1)} %collective-permute-done.8.refs_3_, ...), custom_call_target="tpu_custom_call" | custom-call | flops 4831838208 | bytes 6291456 | tf_op jit(solution)/shard_map/pallas_call | solution.py:152
  111.4 1.9 %collective-permute-done.11.oth_ref = f32[1536,128]{1,0:T(8,128)S(1)} collective-permute-done((f32[1536,128]{1,0:T(8,128)S(1)}, f32[1536,128]{1,0:T(8,128)S(1)}, u32[]{:S(2)}, u32[]{:S(2)}) %collective-permute-start.11) | collective-permute-done | bytes 786464 | tf_op jit(solution)/shard_map/ppermute | solution.py:529
  114.5 19.6 %all_to_all.10 = bf16[32,32,128]{2,1,0:T(8,128)(2,1)S(1)} all-to-all(bf16[32,32,128]{2,1,0:T(8,128)(2,1)S(1)} %bitcast.11), channel_id=1, replica_groups=mesh['y'=4,'zh'=4,'core'=2,'zl'=2,'x'=4] {'zh','zl','x'}, dimensions={0} | all-to-all | bytes 524288 | tf_op jit(solution)/shard_map/all_to_all | solution.py:531
  134.1 5.0 %collective-permute-start.12 = (f32[16,128]{1,0:T(8,128)S(1)}, f32[16,128]{1,0:T(8,128)S(1)}, u32[]{:S(2)}, u32[]{:S(2)}) collective-permute-start(f32[16,128]{1,0:T(8,128)S(1)} %get-tuple-element.57), channel_id=1, source_target_pairs={{0,8},{8,16},{16,24},{24,32},{32,40},{40,48},{48,56},{56,64},{64,7... | collective-permute-start | bytes 24584 | tf_op jit(solution)/shard_map/ppermute | solution.py:571
  139.1 1.9 %collective-permute-start.13 = (f32[16,128]{1,0:T(8,128)S(1)}, f32[16,128]{1,0:T(8,128)S(1)}, u32[]{:S(2)}, u32[]{:S(2)}) collective-permute-start(f32[16,128]{1,0:T(8,128)S(1)} %get-tuple-element.56), channel_id=1, source_target_pairs={{8,0},{16,8},{24,16},{32,24},{40,32},{48,40},{56,48},{64,56},{72,6... | collective-permute-start | bytes 24584 | tf_op jit(solution)/shard_map/ppermute | solution.py:572
  141.1 3.9 %collective-permute-done.13.below_ref = f32[16,128]{1,0:T(8,128)S(1)} collective-permute-done((f32[16,128]{1,0:T(8,128)S(1)}, f32[16,128]{1,0:T(8,128)S(1)}, u32[]{:S(2)}, u32[]{:S(2)}) %collective-permute-start.13) | collective-permute-done | bytes 8224 | tf_op jit(solution)/shard_map/ppermute | solution.py:572
  145.0 7.3 %shard_map.171 = (f32[4,4,12,16]{3,2,1,0:T(8,128)S(1)}, bf16[4,4,12,384]{3,2,1,0:T(8,128)(2,1)S(1)}) custom-call(f32[16,128]{1,0:T(8,128)S(1)} %collective-permute-done.12.above_ref, f32[32,128]{1,0:T(8,128)S(1)} %convert_reduce_fusion.mine_ref, f32[16,128]{1,0:T(8,128)S(1)} %collective-permute-done.13.below_ref, ...), custom_call_target="tpu_custom_call" | custom-call | tf_op jit(solution)/shard_map/pallas_call | solution.py:277
  (65 shorter events, 8.9 us)
Async XLA Ops:
  0.6 53.6 %copy-start = (bf16[4096,64]{0,1:T(8,128)(2,1)S(1)}, bf16[4096,64]{0,1:T(8,128)(2,1)}, u32[]{:S(2)}) copy-start(bf16[4096,64]{0,1:T(8,128)(2,1)} %param.18) | copy-start | bytes 1572868
  0.7 48.4 %copy-start.1 = (bf16[3,3,3,16,384]{4,3,2,1,0:T(8,128)(2,1)S(1)}, bf16[3,3,3,16,384]{4,3,2,1,0:T(8,128)(2,1)}, u32[]{:S(2)}) copy-start(bf16[3,3,3,16,384]{4,3,2,1,0:T(8,128)(2,1)} %w_ref) | copy-start | bytes 995332
  0.7 21.7 %copy-start.8 = (f32[16]{0:T(128)S(1)}, f32[16]{0:T(128)}, u32[]{:S(2)}) copy-start(f32[16]{0:T(128)} %param.22) | copy-start | bytes 196
  0.7 21.8 %copy-start.9 = (f32[16]{0:T(128)S(1)}, f32[16]{0:T(128)}, u32[]{:S(2)}) copy-start(f32[16]{0:T(128)} %param.21) | copy-start | bytes 196
  3.1 49.4 %all-to-all-start = ((bf16[32,48,384]{2,1,0:T(8,128)(2,1)}), bf16[32,48,384]{2,1,0:T(8,128)(2,1)}, u32[]{:S(2)}, u32[]{:S(2)}) async-start(bf16[32,48,384]{2,1,0:T(8,128)(2,1)} %shard_map.161), calls=%async_computation | async-start | bytes 2359296 | tf_op jit(solution)/shard_map/all_to_all | solution.py:506
  15.4 23.3 %collective-permute-start = (f32[2,16,512]{2,1,0:T(8,128)S(1)}, f32[2,16,512]{2,1,0:T(8,128)S(1)}, u32[]{:S(2)}, u32[]{:S(2)}) collective-permute-start(f32[2,16,512]{2,1,0:T(8,128)S(1)} %get-tuple-element.32), channel_id=1, source_target_pairs={{0,8},{8,16},{16,24},{24,32},{32,40},{40,48},{48,56},{56,64},{64,7... | collective-permute-start | bytes 196616 | tf_op jit(solution)/shard_map/ppermute | solution.py:427
  20.4 23.9 %collective-permute-start.1 = (f32[2,16,512]{2,1,0:T(8,128)S(1)}, f32[2,16,512]{2,1,0:T(8,128)S(1)}, u32[]{:S(2)}, u32[]{:S(2)}) collective-permute-start(f32[2,16,512]{2,1,0:T(8,128)S(1)} %get-tuple-element.33), channel_id=1, source_target_pairs={{8,0},{16,8},{24,16},{32,24},{40,32},{48,40},{56,48},{64,56},{72,6... | collective-permute-start | bytes 196616 | tf_op jit(solution)/shard_map/ppermute | solution.py:428
  44.5 4.8 %collective-permute-start.2 = (f32[2,8,512]{2,1,0:T(8,128)S(1)}, f32[2,8,512]{2,1,0:T(8,128)S(1)}, u32[]{:S(2)}, u32[]{:S(2)}) collective-permute-start(f32[2,8,512]{2,1,0:T(8,128)S(1)} %get-tuple-element.36), channel_id=1, source_target_pairs={{0,1},{1,2},{2,3},{3,4},{4,5},{5,6},{6,7},{8,9},{9,10},{10,11},{11... | collective-permute-start | bytes 98312 | tf_op jit(solution)/shard_map/ppermute | solution.py:433
  47.7 4.7 %collective-permute-start.3 = (f32[2,8,512]{2,1,0:T(8,128)S(1)}, f32[2,8,512]{2,1,0:T(8,128)S(1)}, u32[]{:S(2)}, u32[]{:S(2)}) collective-permute-start(f32[2,8,512]{2,1,0:T(8,128)S(1)} %get-tuple-element.37), channel_id=1, source_target_pairs={{1,0},{2,1},{3,2},{4,3},{5,4},{6,5},{7,6},{9,8},{10,9},{11,10},{12... | collective-permute-start | bytes 98312 | tf_op jit(solution)/shard_map/ppermute | solution.py:434
  54.3 8.9 %collective-permute-start.4 = (bf16[1536,128]{1,0:T(8,128)(2,1)}, bf16[1536,128]{1,0:T(8,128)(2,1)}, u32[]{:S(2)}, u32[]{:S(2)}) collective-permute-start(bf16[1536,128]{1,0:T(8,128)(2,1)} %slice.20), channel_id=1, source_target_pairs={{0,8},{8,0},{1,9},{9,1},{2,10},{10,2},{3,11},{11,3},{4,12},{12,4},... | collective-permute-start | bytes 1179656 | tf_op jit(solution)/shard_map/ppermute | solution.py:516
  55.6 16.5 %collective-permute-start.5 = (bf16[768,256]{1,0:T(8,128)(2,1)S(1)}, bf16[768,256]{1,0:T(8,128)(2,1)S(1)}, u32[]{:S(2)}, u32[]{:S(2)}) collective-permute-start(bf16[768,256]{1,0:T(8,128)(2,1)S(1)} %get-tuple-element.55), channel_id=1, source_target_pairs={{0,64},{64,128},{128,192},{192,0},{1,65},{65,129},{129,193},{193,1... | collective-permute-start | bytes 1179656 | tf_op jit(solution)/shard_map/ppermute | solution.py:514
  59.8 31.1 %collective-permute-start.10 = (bf16[768,256]{1,0:T(8,128)(2,1)S(1)}, bf16[768,256]{1,0:T(8,128)(2,1)S(1)}, u32[]{:S(2)}, u32[]{:S(2)}) collective-permute-start(bf16[768,256]{1,0:T(8,128)(2,1)S(1)} %get-tuple-element.55), channel_id=1, source_target_pairs={{64,0},{128,64},{192,128},{0,192},{65,1},{129,65},{193,129},{1,193... | collective-permute-start | bytes 1179656 | tf_op jit(solution)/shard_map/ppermute | solution.py:519
  61.6 17.0 %collective-permute-start.6 = (bf16[768,256]{1,0:T(8,128)(2,1)S(1)}, bf16[768,256]{1,0:T(8,128)(2,1)S(1)}, u32[]{:S(2)}, u32[]{:S(2)}) collective-permute-start(bf16[768,256]{1,0:T(8,128)(2,1)S(1)} %get-tuple-element.54), channel_id=1, source_target_pairs={{64,0},{128,64},{192,128},{0,192},{65,1},{129,65},{193,129},{1,193... | collective-permute-start | bytes 1179656 | tf_op jit(solution)/shard_map/ppermute | solution.py:515
  63.0 28.0 %collective-permute-start.9 = (bf16[768,256]{1,0:T(8,128)(2,1)S(1)}, bf16[768,256]{1,0:T(8,128)(2,1)S(1)}, u32[]{:S(2)}, u32[]{:S(2)}) collective-permute-start(bf16[768,256]{1,0:T(8,128)(2,1)S(1)} %get-tuple-element.54), channel_id=1, source_target_pairs={{0,64},{64,128},{128,192},{192,0},{1,65},{65,129},{129,193},{193,1... | collective-permute-start | bytes 1179656 | tf_op jit(solution)/shard_map/ppermute | solution.py:518
  78.7 21.5 %collective-permute-start.7 = (bf16[768,256]{1,0:T(8,128)(2,1)S(1)}, bf16[768,256]{1,0:T(8,128)(2,1)S(1)}, u32[]{:S(2)}, u32[]{:S(2)}) collective-permute-start(bf16[768,256]{1,0:T(8,128)(2,1)S(1)} %collective-permute-done.5.refs_2_), channel_id=1, source_target_pairs={{0,64},{64,128},{128,192},{192,0},{1,65},{65,129},{129,193},{193,1... | collective-permute-start | bytes 1179656 | tf_op jit(solution)/shard_map/ppermute | solution.py:522
  80.0 20.2 %collective-permute-start.8 = (bf16[768,256]{1,0:T(8,128)(2,1)S(1)}, bf16[768,256]{1,0:T(8,128)(2,1)S(1)}, u32[]{:S(2)}, u32[]{:S(2)}) collective-permute-start(bf16[768,256]{1,0:T(8,128)(2,1)S(1)} %collective-permute-done.6.refs_3_), channel_id=1, source_target_pairs={{64,0},{128,64},{192,128},{0,192},{65,1},{129,65},{193,129},{1,193... | collective-permute-start | bytes 1179656 | tf_op jit(solution)/shard_map/ppermute | solution.py:523
  91.0 54.0 %slice-start = ((s8[7962624]{0:T(1024)(128)(4,1)}), s8[4194304]{0:T(1024)(128)(4,1)S(1)}, s32[]{:S(2)}) async-start(s8[7962624]{0:T(1024)(128)(4,1)} %bitcast.8), calls=%async_computation.2 | async-start | bytes 8388608
  100.1 41.0 %copy-start.5 = (f32[384]{0:T(512)S(1)}, f32[384]{0:T(512)}, u32[]{:S(2)}) copy-start(f32[384]{0:T(512)} %param.25) | copy-start | bytes 4612
  100.1 41.0 %copy-start.6 = (f32[384]{0:T(512)S(1)}, f32[384]{0:T(512)}, u32[]{:S(2)}) copy-start(f32[384]{0:T(512)} %param.26) | copy-start | bytes 4612
  100.1 41.0 %copy-start.7 = (f32[384]{0:T(512)S(1)}, f32[384]{0:T(512)}, u32[]{:S(2)}) copy-start(f32[384]{0:T(512)} %param.29) | copy-start | bytes 4612
  100.1 44.9 %slice-start.1 = ((s8[7962624]{0:T(1024)(128)(4,1)}), s8[3768320]{0:T(1024)(128)(4,1)S(1)}, s32[]{:S(2)}) async-start(s8[7962624]{0:T(1024)(128)(4,1)} %bitcast.8), calls=%async_computation.3 | async-start | bytes 7536640
  110.3 3.1 %collective-permute-start.11 = (f32[1536,128]{1,0:T(8,128)S(1)}, f32[1536,128]{1,0:T(8,128)S(1)}, u32[]{:S(2)}, u32[]{:S(2)}) collective-permute-start(f32[1536,128]{1,0:T(8,128)S(1)} %get-tuple-element.46), channel_id=1, source_target_pairs={{0,8},{8,0},{1,9},{9,1},{2,10},{10,2},{3,11},{11,3},{4,12},{12,4},... | collective-permute-start | bytes 2359304 | tf_op jit(solution)/shard_map/ppermute | solution.py:529
  134.1 7.0 %collective-permute-start.12 = (f32[16,128]{1,0:T(8,128)S(1)}, f32[16,128]{1,0:T(8,128)S(1)}, u32[]{:S(2)}, u32[]{:S(2)}) collective-permute-start(f32[16,128]{1,0:T(8,128)S(1)} %get-tuple-element.57), channel_id=1, source_target_pairs={{0,8},{8,16},{16,24},{24,32},{32,40},{40,48},{48,56},{56,64},{64,7... | collective-permute-start | bytes 24584 | tf_op jit(solution)/shard_map/ppermute | solution.py:571
  139.1 5.9 %collective-permute-start.13 = (f32[16,128]{1,0:T(8,128)S(1)}, f32[16,128]{1,0:T(8,128)S(1)}, u32[]{:S(2)}, u32[]{:S(2)}) collective-permute-start(f32[16,128]{1,0:T(8,128)S(1)} %get-tuple-element.56), channel_id=1, source_target_pairs={{8,0},{16,8},{24,16},{32,24},{40,32},{48,40},{56,48},{64,56},{72,6... | collective-permute-start | bytes 24584 | tf_op jit(solution)/shard_map/ppermute | solution.py:572
  (3 other events, 43.4 us)

commit v5 on v4

--- a/solution.py
+++ b/solution.py
@@ -34,18 +34,20 @@
 
 
 def flash_kernel(first, last, n_kv, half, *refs):
-    qo_ref, qx_ref = refs[:2]
-    kv_refs = refs[2 : 2 + n_kv]
-    refs = refs[2 + n_kv :]
+    q_ref, refs = refs[0], refs[1:]
+    if not last:
+        qx_ref, refs = refs[0], refs[1:]
+    kv_refs, refs = refs[:n_kv], refs[n_kv:]
     if not first:
         st_ref, refs = refs[0], refs[1:]
     if last:
-        w_ref, own_ref, oth_ref = refs
+        w_ref, u_ref = refs
+        query = q_ref[...]
     else:
         (so_ref,) = refs
-    i = pl.program_id(0)
+        query = jnp.where(pl.program_id(0) < half, q_ref[...], qx_ref[...])
     scale = math.log2(math.e) / math.sqrt(HEAD_DIM)
-    qf = jnp.where(i < half, qo_ref[...], qx_ref[...]).astype(jnp.float32) * scale
+    qf = query.astype(jnp.float32) * scale
     q_hi = qf.astype(jnp.bfloat16)
     q_lo = (qf - q_hi.astype(jnp.float32)).astype(jnp.bfloat16)
     q = jnp.concatenate([q_hi, q_lo], axis=1)
@@ -96,72 +98,67 @@
         tops[r] = top
         s = following
     lane = lax.broadcasted_iota(jnp.int32, (SUB, 128), 1)
-    outs = []
     for r in range(subs):
         if last:
             total = accs[r][:, 128:]
             mixed = (accs[r][:, :128] / total).astype(jnp.bfloat16)
             u = jnp.dot(mixed, w_ref[...], preferred_element_type=jnp.float32)
-            outs.append(jnp.where(lane < 64, u, tops[r] + jnp.log2(total)))
+            u_ref[pl.ds(r * SUB, SUB), :] = jnp.where(lane < 64, u, tops[r] + jnp.log2(total))
         else:
             so_ref[pl.ds(r * SUB, SUB), :] = jnp.concatenate(
                 [accs[r][:, :128], jnp.where(lane < 64, accs[r][:, 128:], tops[r])], axis=1
             )
-    if last:
-
-        @pl.when(i < half)
-        def _():
-            for r in range(subs):
-                own_ref[pl.ds(r * SUB, SUB), :] = outs[r]
-
-        @pl.when(i >= half)
-        def _():
-            for r in range(subs):
-                oth_ref[pl.ds(r * SUB, SUB), :] = outs[r]
-
-
-def flash(q_own, q_oth, kvs, state=None, weight=None):
-    first, last = state is None, weight is not None
-    rows = q_own.shape[0]
+
+
+def flash(q_own, q_oth, kvs, state=None):
+    rows = q_oth.shape[0]
     half = rows // TILE
     keys = sum(kv.shape[0] for kv in kvs)
-
-    def lower(i):
-        return (jnp.minimum(i, half - 1), 0)
-
-    def upper(i):
-        return (jnp.maximum(i - half, 0), 0)
-
     in_specs = [
         pl.BlockSpec((TILE, 128), lambda i: (jnp.minimum(i, half - 1), 2)),
-        pl.BlockSpec((TILE, 128), upper),
+        pl.BlockSpec((TILE, 128), lambda i: (jnp.maximum(i - half, 0), 0)),
     ]
     in_specs += [pl.BlockSpec((kv.shape[0], 256), lambda i: (0, 0)) for kv in kvs]
     args = [q_own, q_oth, *kvs]
-    if not first:
+    if state is not None:
         in_specs.append(pl.BlockSpec((TILE, 256), lambda i: (i, 0)))
         args.append(state)
-    if last:
-        in_specs.append(pl.BlockSpec(weight.shape, lambda i: (0, 0)))
-        args.append(weight)
-        out_specs = [pl.BlockSpec((TILE, 128), lower), pl.BlockSpec((TILE, 128), upper)]
-        out_shape = [jax.ShapeDtypeStruct((rows, 128), jnp.float32)] * 2
-    else:
-        out_specs = pl.BlockSpec((TILE, 256), lambda i: (i, 0))
-        out_shape = jax.ShapeDtypeStruct((2 * rows, 256), jnp.float32)
     return pl.pallas_call(
-        functools.partial(flash_kernel, first, last, len(kvs), half),
+        functools.partial(flash_kernel, state is None, False, len(kvs), half),
         grid=(2 * half,),
         in_specs=in_specs,
-        out_specs=out_specs,
-        out_shape=out_shape,
+        out_specs=pl.BlockSpec((TILE, 256), lambda i: (i, 0)),
+        out_shape=jax.ShapeDtypeStruct((2 * rows, 256), jnp.float32),
         compiler_params=pltpu.CompilerParams(vmem_limit_bytes=20 << 20),
-        cost_estimate=pl.CostEstimate(
-            flops=2 * rows * keys * 512 * 2,
-            bytes_accessed=rows * 4096,
-            transcendentals=2 * rows * keys,
-        ),
+        cost_estimate=flash_cost(2 * rows, keys),
     )(*args)
+
+
+def flash_last(query, lane_block, kvs, state, half_at, weight):
+    rows = query.shape[0]
+    half = rows // TILE
+    keys = sum(kv.shape[0] for kv in kvs)
+    in_specs = [pl.BlockSpec((TILE, 128), lambda i: (i, lane_block))]
+    in_specs += [pl.BlockSpec((kv.shape[0], 256), lambda i: (0, 0)) for kv in kvs]
+    in_specs += [
+        pl.BlockSpec((TILE, 256), lambda i: (i + half_at * half, 0)),
+        pl.BlockSpec(weight.shape, lambda i: (0, 0)),
+    ]
+    return pl.pallas_call(
+        functools.partial(flash_kernel, False, True, len(kvs), half),
+        grid=(half,),
+        in_specs=in_specs,
+        out_specs=pl.BlockSpec((TILE, 128), lambda i: (i, 0)),
+        out_shape=jax.ShapeDtypeStruct((rows, 128), jnp.float32),
+        compiler_params=pltpu.CompilerParams(vmem_limit_bytes=20 << 20),
+        cost_estimate=flash_cost(rows, keys),
+    )(query, *kvs, state, weight)
+
+
+def flash_cost(rows, keys):
+    return pl.CostEstimate(
+        flops=rows * keys * 1024, bytes_accessed=rows * 2048, transcendentals=rows * keys
+    )
 
 
 def inside(at, low, high, before, after):
@@ -169,9 +166,9 @@
 
 
 def tail_kernel(
-    above_ref,
+    near_ref,
     mine_ref,
-    below_ref,
+    apart_ref,
     cells_ref,
     affine_ref,
     beyond_ref,
@@ -183,20 +180,18 @@
     b2_ref,
     den_ref,
     out_ref,
-    w2_buf,
-    sems,
     vel,
     lat,
     den,
     first,
     act,
     wide,
+    done,
 ):
-    for tap in range(9):
-        pltpu.make_async_copy(w2_ref.at[tap], w2_buf.at[tap], sems.at[tap]).start()
-    for at, rows in enumerate(
-        (above_ref[...], mine_ref[0:16, :], mine_ref[16:32, :], below_ref[...])
-    ):
+    even = beyond_ref[4] > 0
+    above = jnp.where(even, apart_ref[...], near_ref[...])
+    below = jnp.where(even, near_ref[...], apart_ref[...])
+    for at, rows in enumerate((above, mine_ref[0:16, :], mine_ref[16:32, :], below)):
         turned = pltpu.roll(rows, 64, axis=1)
         for f in range(F):
             vel[f, at, 0:4, :] = rows[f * 4 : f * 4 + 4]
@@ -214,8 +209,9 @@
         part = part.reshape(F, 4, 8, 128)
         for f in range(F):
             for r in range(2):
-                den[f, 2 * r + k // 2, pl.ds(k % 2, 8, stride=2), :] = part[f, r + 1]
-    den_ref[...] = den[:, :, 2:14, 0:LAT]
+                rows = pl.ds(8 * (k % 2) + 2 * r + k // 2, 8, stride=16)
+                den[f, rows, :] = part[f, r + 1]
+    den_ref[...] = den[:, 16:112, :].reshape(F, 12, 8, 128)[:, :, 0:4, 0:LAT]
     lat[...] = jnp.zeros(lat.shape, jnp.float32)
     lat[0:2, :, 0:8, 0:64] = cells_ref[0:2, :, :, 0:64]
     lat[2:6, :, 0:8, 0:64] = latent.astype(jnp.bfloat16).astype(jnp.float32)
@@ -264,33 +260,36 @@
     total = jnp.concatenate(middle, axis=1) + b2_ref[...]
     for tap in range(9):
         t, u = divmod(tap, 3)
-        pltpu.make_async_copy(w2_ref.at[tap], w2_buf.at[tap], sems.at[tap]).wait()
         rows = wide[t : t + 4, u : u + 4].reshape(256, 3 * C1)
-        total = total + jnp.dot(rows, w2_buf[tap], preferred_element_type=jnp.float32)
-    out_ref[...] = total.reshape(F, 4, 16, C1)[:, :, 0:12].astype(jnp.bfloat16)
+        total = total + jnp.dot(rows, w2_ref[tap], preferred_element_type=jnp.float32)
+    for k in range(parts):
+        for f in range(F):
+            for i in range(4):
+                at = f * 64 + i * 16
+                done[k, f, pl.ds(i, 16, stride=8), :] = total[at : at + 16, k * 128 : k * 128 + 128]
+        cells = done[k, :, 0:96, :].reshape(F, 12, 8, 128)[:, :, 0:4]
+        out_ref[:, :, :, pl.ds(k * 128, 128)] = cells.astype(jnp.bfloat16)
 
 
 def tail(*args):
     specs = [pl.BlockSpec(memory_space=pltpu.VMEM)] * len(args)
     specs[5] = pl.BlockSpec(memory_space=pltpu.SMEM)
-    specs[10] = pl.BlockSpec(memory_space=pl.ANY)
     return pl.pallas_call(
         tail_kernel,
         in_specs=specs,
         out_specs=[pl.BlockSpec(memory_space=pltpu.VMEM)] * 2,
         out_shape=[
-            jax.ShapeDtypeStruct((F, 4, 12, LAT), jnp.float32),
-            jax.ShapeDtypeStruct((F, 4, 12, C1), jnp.bfloat16),
+            jax.ShapeDtypeStruct((F, 12, 4, LAT), jnp.float32),
+            jax.ShapeDtypeStruct((F, 12, 4, C1), jnp.bfloat16),
         ],
         scratch_shapes=[
-            pltpu.VMEM((9, 3 * C1, C1), jnp.bfloat16),
-            pltpu.SemaphoreType.DMA((9,)),
             pltpu.VMEM((F, 4, 8, 128), jnp.float32),
             pltpu.VMEM((6, 4, 16, 128), jnp.float32),
-            pltpu.VMEM((F, 4, 16, 128), jnp.float32),
+            pltpu.VMEM((F, 128, 128), jnp.float32),
             pltpu.VMEM((C1 // 128, F, 6, 24, 128), jnp.float32),
             pltpu.VMEM((C1 // 128, 6, 6, 24, 128), jnp.float32),
             pltpu.VMEM((6, 6, 16, 3 * C1), jnp.bfloat16),
+            pltpu.VMEM((C1 // 128, F, 128, 128), jnp.float32),
         ],
         compiler_params=pltpu.CompilerParams(vmem_limit_bytes=32 << 20),
     )(*args)
@@ -504,29 +503,31 @@
     work = work(*inputs)
     heads, tokens = packed.shape[:2]
     moved = lax.all_to_all(packed, HEAD, split_axis=0, concat_axis=0, tiled=True)
-    moved, work = lax.optimization_barrier((moved, work))
     moved = moved.reshape(heads * tokens, 3 * HEAD_DIM)
     swap = [(0, 1), (1, 0)]
     right = [(i, (i + 1) % 4) for i in range(4)]
     left = [((i + 1) % 4, i) for i in range(4)]
     mid = moved.shape[0] // 2
-    a, b = moved[:mid, :256], moved[mid:, :256]
+    a, b, q_own = moved[:mid, :256], moved[mid:, :256], moved[:, 256:]
+    (a, b, q_own), work = lax.optimization_barrier(((a, b, q_own), work))
     left_a = lax.ppermute(a, "y", right)
     right_b = lax.ppermute(b, "y", left)
-    q_oth = lax.ppermute(moved[:, 256:], "core", swap)
+    q_oth = lax.ppermute(q_own, "core", swap)
     state = flash(moved, q_oth, [moved])
+    state, a, b = lax.optimization_barrier((state, a, b))
     left_b = lax.ppermute(b, "y", right)
     right_a = lax.ppermute(a, "y", left)
+    state = flash(moved, q_oth, [left_a, right_b], state)
     state, left_a, right_b = lax.optimization_barrier((state, left_a, right_b))
-    state = flash(moved, q_oth, [left_a, right_b], state)
-    far_a = lax.ppermute(left_a, "y", right)
-    far_b = lax.ppermute(right_b, "y", left)
+    far = [lax.ppermute(left_a, "y", right), lax.ppermute(right_b, "y", left)]
     state = flash(moved, q_oth, [left_b, right_a], state)
     head = lax.axis_index(HEAD)
     weight = lax.dynamic_slice_in_dim(weight_head, head * HEAD_DIM, HEAD_DIM, axis=0)
     weight = jnp.pad(weight, ((0, 0), (0, 64)))
-    own, oth = flash(moved, q_oth, [far_a, far_b], state, weight)
+    oth = flash_last(q_oth, 0, far, state, 1, weight)
+    oth, state = lax.optimization_barrier((oth, state))
     oth = lax.ppermute(oth, "core", swap)
+    own = flash_last(moved, 2, far, state, 0, weight)
     partial = merge(own, oth).reshape(heads, 32, 128)
     parts = lax.all_to_all(partial, HEAD, split_axis=0, concat_axis=0, tiled=True)
     return jnp.sum(parts.astype(jnp.float32), axis=0), work
@@ -552,7 +553,8 @@
     def work(noisy, cache_first, cache_second, weight_first):
         row, col = lax.axis_index(SEQ), lax.axis_index(BLK)
         last_row, last_col = lax.axis_size(SEQ) - 1, lax.axis_size(BLK) - 1
-        beyond = jnp.stack([row > 0, row < last_row, col > 0, col < last_col])
+        even = lax.axis_index("core") == 0
+        beyond = jnp.stack([row > 0, row < last_row, col > 0, col < last_col, even])
         level = jnp.broadcast_to(noise_level, (4 * LAT,))
         affine = jnp.stack([level, jnp.tile(latent_scale, 4), jnp.tile(latent_mean, 4)])
         halos = input_halos(noisy, cache_first, cache_second)
@@ -568,12 +570,17 @@
     )
     cells, cache_second, beyond, affine, weight_first = work
 
-    above = lax.ppermute(mine[16:], SEQ, along(SEQ, 1))
-    below = lax.ppermute(mine[:16], SEQ, along(SEQ, -1))
-    return tail(
-        above,
+    count = lax.axis_size(SEQ)
+    even = lax.axis_index("core") == 0
+    low, high = mine[:16], mine[16:]
+    near = lax.ppermute(jnp.where(even, high, low), SEQ, [(i, i ^ 1) for i in range(count)])
+    pairs = [(i, i + 1) for i in range(1, count - 1, 2)]
+    pairs += [(j, i) for i, j in pairs]
+    apart = lax.ppermute(jnp.where(even, low, high), SEQ, pairs)
+    denoised, features = tail(
+        near,
         mine,
-        below,
+        apart,
         cells,
         affine,
         beyond,
@@ -584,6 +591,7 @@
         weight_mid.reshape(9, 3 * C1, C1),
         bias_mid.reshape(1, C1),
     )
+    return denoised.transpose(0, 2, 1, 3), features.transpose(0, 2, 1, 3)
 
 
 def solution(mesh):

time: 154 us -> 145 us (0.942)
  waiting for transfers between devices: 36.4 us -> 27.6 us
  starting transfers between devices: 42.4 us -> 40.3 us
  local copies, waits for them, and re-layouts: 4.77 us -> 6.57 us
    ppermute x1, waiting for transfers between devices: 6.57 us -> 0.01 us  [attention(): right_b = lax.ppermute(b, 'y', left)]
    ppermute x5, starting transfers between devices: 10.2 us -> 7.75 us  [the longest x2 2.93 us: attention(): far = [lax.ppermute(left_a, 'y', right), lax.ppermute(right_b, 'y', left)]]
    unnamed x25 -> x37, local copies, waits for them, and re-layouts: 0.18 us -> 2.37 us
    pallas_call x1, Pallas kernels: 7.29 us -> 5.35 us  [tail(): pl.pallas_call(tail_kernel, in_specs=specs, out_specs=[pl.BlockSpec(memor...]
    ppermute x1, waiting for transfers between devices: 1.91 us -> 0.01 us  [attention(): oth = lax.ppermute(oth, 'core', swap)]
    slice x3 -> x2, local copies, waits for them, and re-layouts: 2.94 us -> 3.85 us  [attention(): a, b, q_own = (moved[:mid, :256], moved[mid:, :256], moved[:, 256:])]
    pallas_call x4 -> x5, Pallas kernels: 37.1 us -> 37.6 us  [the longest x3 26.8 us: flash(): pl.pallas_call(functools.partial(flash_kernel, state is None, False, len(...]
  transfers between devices with their start and end apart: 15 -> 15, of which waited for: 6 -> 4; matrix products, arithmetic and copies ran while one was open for 1% -> 0% of each run, Pallas kernels for 18% -> 24%
where the time goes in v5:
time: 145 us; the launch traced here: 144 us
  Pallas kernels  48.5 us (33%)
  starting transfers between devices  40.3 us (28%)
  waiting for transfers between devices  27.6 us (19%)
  blocking collectives  19.6 us (14%)
  local copies, waits for them, and re-layouts  6.57 us (5%)
  between operations  1.72 us (1%)
    pallas_call x3, Pallas kernels, flash(): pl.pallas_call(functools.partial(flash_kernel, state is None, False, len(...  26.8 us
    all_to_all x1, blocking collectives, attention(): lax.all_to_all(partial, HEAD, split_axis=0, concat_axis=0, tiled=True)  19.6 us
    ppermute x1, waiting for transfers between devices, input_halos(): above = lax.ppermute(down, SEQ, along(SEQ, 1))  15.4 us
    all_to_all x1, starting transfers between devices, attention(): lax.all_to_all(packed, HEAD, split_axis=0, concat_axis=0, tiled=True)  12 us
    pallas_call x2, Pallas kernels, flash_last(): pl.pallas_call(functools.partial(flash_kernel, False, True, len(kvs), hal...  10.7 us
    ppermute x1, waiting for transfers between devices, input_halos(): below = lax.ppermute(up, SEQ, along(SEQ, -1))  5.71 us
    pallas_call x1, Pallas kernels, tail(): pl.pallas_call(tail_kernel, in_specs=specs, out_specs=[pl.BlockSpec(memor...  5.35 us
    ppermute x1, starting transfers between devices, input_halos(): above = lax.ppermute(down, SEQ, along(SEQ, 1))  5.09 us
  transfers between devices with their start and end apart: 15, of which 4 were waited for; matrix products, arithmetic and copies ran while one was open for 0% of the time, Pallas kernels for 24%

profile of v5, /device:TPU:1, one launch (start us, length us, event | category | flops | bytes accessed | tf_op | source)
XLA Modules:
  0.0 144.4 jit_solution(657673361874840275)
XLA Ops:
  0.7 2.4 %shard_map.161 = bf16[32,48,384]{2,1,0:T(8,128)(2,1)} custom-call(bf16[48,4096]{1,0:T(8,128)(2,1)} %q_ref.1, bf16[48,4096]{1,0:T(8,128)(2,1)} %k_ref.1, bf16[48,4096]{1,0:T(8,128)(2,1)} %v_ref.1), custom_call_target="tpu_custom_call" | custom-call | tf_op jit(solution)/shard_map/pallas_call | solution.py:449
  3.1 12.0 %all-to-all-start = ((bf16[32,48,384]{2,1,0:T(8,128)(2,1)}), bf16[32,48,384]{2,1,0:T(8,128)(2,1)}, u32[]{:S(2)}, u32[]{:S(2)}) async-start(bf16[32,48,384]{2,1,0:T(8,128)(2,1)} %shard_map.161), calls=%async_computation | async-start | bytes 2359296 | tf_op jit(solution)/shard_map/all_to_all | solution.py:505
  15.3 5.1 %collective-permute-start = (f32[2,16,512]{2,1,0:T(8,128)S(1)}, f32[2,16,512]{2,1,0:T(8,128)S(1)}, u32[]{:S(2)}, u32[]{:S(2)}) collective-permute-start(f32[2,16,512]{2,1,0:T(8,128)S(1)} %get-tuple-element.39), channel_id=1, source_target_pairs={{0,8},{8,16},{16,24},{24,32},{32,40},{40,48},{48,56},{56,64},{64,7... | collective-permute-start | bytes 196616 | tf_op jit(solution)/shard_map/ppermute | solution.py:426
  20.4 1.9 %collective-permute-start.1 = (f32[2,16,512]{2,1,0:T(8,128)S(1)}, f32[2,16,512]{2,1,0:T(8,128)S(1)}, u32[]{:S(2)}, u32[]{:S(2)}) collective-permute-start(f32[2,16,512]{2,1,0:T(8,128)S(1)} %get-tuple-element.40), channel_id=1, source_target_pairs={{8,0},{16,8},{24,16},{32,24},{40,32},{48,40},{56,48},{64,56},{72,6... | collective-permute-start | bytes 196616 | tf_op jit(solution)/shard_map/ppermute | solution.py:427
  23.2 15.4 %collective-permute-done.above_ref = f32[2,16,512]{2,1,0:T(8,128)S(1)} collective-permute-done((f32[2,16,512]{2,1,0:T(8,128)S(1)}, f32[2,16,512]{2,1,0:T(8,128)S(1)}, u32[]{:S(2)}, u32[]{:S(2)}) %collective-permute-start) | collective-permute-done | bytes 65568 | tf_op jit(solution)/shard_map/ppermute | solution.py:426
  38.6 5.7 %collective-permute-done.1.below_ref = f32[2,16,512]{2,1,0:T(8,128)S(1)} collective-permute-done((f32[2,16,512]{2,1,0:T(8,128)S(1)}, f32[2,16,512]{2,1,0:T(8,128)S(1)}, u32[]{:S(2)}, u32[]{:S(2)}) %collective-permute-start.1) | collective-permute-done | bytes 65568 | tf_op jit(solution)/shard_map/ppermute | solution.py:427
  45.7 3.2 %collective-permute-start.2 = (f32[2,8,512]{2,1,0:T(8,128)}, f32[2,8,512]{2,1,0:T(8,128)S(1)}, u32[]{:S(2)}, u32[]{:S(2)}) collective-permute-start(f32[2,8,512]{2,1,0:T(8,128)} %get-tuple-element.43), channel_id=1, source_target_pairs={{0,1},{1,2},{2,3},{3,4},{4,5},{5,6},{6,7},{8,9},{9,10},{10,11},{11... | collective-permute-start | bytes 98312 | tf_op jit(solution)/shard_map/ppermute | solution.py:432
  50.7 3.2 %collective-permute-done.3.right_ref = f32[2,8,512]{2,1,0:T(8,128)} collective-permute-done((f32[2,8,512]{2,1,0:T(8,128)}, f32[2,8,512]{2,1,0:T(8,128)}, u32[]{:S(2)}, u32[]{:S(2)}) %collective-permute-start.3) | collective-permute-done | bytes 32800 | tf_op jit(solution)/shard_map/ppermute | solution.py:433
  56.3 2.0 %fusion = (bf16[768,256]{1,0:T(8,128)(2,1)}, bf16[768,256]{1,0:T(8,128)(2,1)}) fusion(bf16[1536,384]{1,0:T(8,128)(2,1)} %bitcast.refs_0_.refs_2_), kind=kLoop, calls=%fused_computation.5 | loop fusion | bytes 1572864 | tf_op jit(solution)/shard_map/slice | solution.py:511
  58.4 1.8 %slice.22 = bf16[1536,128]{1,0:T(8,128)(2,1)} slice(bf16[1536,384]{1,0:T(8,128)(2,1)} %bitcast.refs_0_.refs_2_), slice={[0:1536], [256:384]} | slice | bytes 786432 | tf_op jit(solution)/shard_map/slice | solution.py:511
  60.4 4.2 %collective-permute-start.5 = (bf16[768,256]{1,0:T(8,128)(2,1)}, bf16[768,256]{1,0:T(8,128)(2,1)S(1)}, u32[]{:S(2)}, u32[]{:S(2)}) collective-permute-start(bf16[768,256]{1,0:T(8,128)(2,1)} %get-tuple-element.55), channel_id=1, source_target_pairs={{0,64},{64,128},{128,192},{192,0},{1,65},{65,129},{129,193},{193,1... | collective-permute-start | bytes 1179656 | tf_op jit(solution)/shard_map/ppermute | solution.py:513
  64.6 1.8 %collective-permute-start.6 = (bf16[768,256]{1,0:T(8,128)(2,1)}, bf16[768,256]{1,0:T(8,128)(2,1)S(1)}, u32[]{:S(2)}, u32[]{:S(2)}) collective-permute-start(bf16[768,256]{1,0:T(8,128)(2,1)} %get-tuple-element.54), channel_id=1, source_target_pairs={{64,0},{128,64},{192,128},{0,192},{65,1},{129,65},{193,129},{1,193... | collective-permute-start | bytes 1179656 | tf_op jit(solution)/shard_map/ppermute | solution.py:514
  66.4 9.0 %shard_map.166.refs_4_ = f32[3072,256]{1,0:T(8,128)S(1)} custom-call(bf16[1536,384]{1,0:T(8,128)(2,1)} %bitcast.refs_0_.refs_2_, bf16[1536,128]{1,0:T(8,128)(2,1)} %collective-permute-done.4.refs_1_.refs_0_, bf16[1536,384]{1,0:T(8,128)(2,1)} %bitcast.refs_0_.refs_2_), custom_call_target="tpu_custom_call" | custom-call | flops 4831838208 | bytes 6291456 | tf_op jit(solution)/shard_map/pallas_call | solution.py:126
  77.0 8.9 %shard_map.167.refs_4_ = f32[3072,256]{1,0:T(8,128)S(1)} custom-call(bf16[1536,384]{1,0:T(8,128)(2,1)} %bitcast.refs_0_.refs_2_, bf16[1536,128]{1,0:T(8,128)(2,1)} %collective-permute-done.4.refs_1_.refs_0_, bf16[768,256]{1,0:T(8,128)(2,1)S(1)} %collective-permute-done.5.refs_2_, bf16[768,256]{1,0:T(8,128)(2,1)S(1)} %collective-permute-done.6.refs_3_, ...), custom_call_target="tpu_custom_call" | custom-call | flops 4831838208 | bytes 6291456 | tf_op jit(solution)/shard_map/pallas_call | solution.py:126
  86.0 2.8 %collective-permute-start.8 = (bf16[768,256]{1,0:T(8,128)(2,1)S(1)}, bf16[768,256]{1,0:T(8,128)(2,1)S(1)}, u32[]{:S(2)}, u32[]{:S(2)}) collective-permute-start(bf16[768,256]{1,0:T(8,128)(2,1)S(1)} %collective-permute-done.6.refs_3_), channel_id=1, source_target_pairs={{64,0},{128,64},{192,128},{0,192},{65,1},{129,65},{193,129},{1,193... | collective-permute-start | bytes 1179656 | tf_op jit(solution)/shard_map/ppermute | solution.py:522
  88.8 8.9 %shard_map.168.refs_3_ = f32[3072,256]{1,0:T(8,128)S(1)} custom-call(bf16[1536,384]{1,0:T(8,128)(2,1)} %bitcast.refs_0_.refs_2_, bf16[1536,128]{1,0:T(8,128)(2,1)} %collective-permute-done.4.refs_1_.refs_0_, bf16[768,256]{1,0:T(8,128)(2,1)S(1)} %collective-permute-done.9.refs_2_, bf16[768,256]{1,0:T(8,128)(2,1)S(1)} %collective-permute-done.10.refs_3_, ...), custom_call_target="tpu_custom_call" | custom-call | flops 4831838208 | bytes 6291456 | tf_op jit(solution)/shard_map/pallas_call | solution.py:126
  97.8 5.4 %shard_map.169 = f32[1536,128]{1,0:T(8,128)S(1)} custom-call(bf16[1536,128]{1,0:T(8,128)(2,1)} %collective-permute-done.4.refs_1_.refs_0_, bf16[768,256]{1,0:T(8,128)(2,1)S(1)} %collective-permute-done.7.refs_1_, bf16[768,256]{1,0:T(8,128)(2,1)S(1)} %collective-permute-done.8.refs_2_, f32[3072,256]{1,0:T(8,128)S(1)} %shard_map.168.refs_3_, ...), custom_call_target="tpu_custom_call" | custom-call | flops 2415919104 | bytes 3145728 | tf_op jit(solution)/shard_map/pallas_call | solution.py:147
  103.3 1.5 %collective-permute-start.11 = (f32[1536,128]{1,0:T(8,128)S(1)}, f32[1536,128]{1,0:T(8,128)S(1)}, u32[]{:S(2)}, u32[]{:S(2)}) collective-permute-start(f32[1536,128]{1,0:T(8,128)S(1)} %shard_map.169), channel_id=1, source_target_pairs={{0,8},{8,0},{1,9},{9,1},{2,10},{10,2},{3,11},{11,3},{4,12},{12,4},... | collective-permute-start | bytes 2359304 | tf_op jit(solution)/shard_map/ppermute | solution.py:529
  104.8 5.3 %shard_map.170.own_ref = f32[1536,128]{1,0:T(8,128)S(1)} custom-call(bf16[1536,384]{1,0:T(8,128)(2,1)} %bitcast.refs_0_.refs_2_, bf16[768,256]{1,0:T(8,128)(2,1)S(1)} %collective-permute-done.7.refs_1_, bf16[768,256]{1,0:T(8,128)(2,1)S(1)} %collective-permute-done.8.refs_2_, f32[3072,256]{1,0:T(8,128)S(1)} %shard_map.168.refs_3_, ...), custom_call_target="tpu_custom_call" | custom-call | flops 2415919104 | bytes 3145728 | tf_op jit(solution)/shard_map/pallas_call | solution.py:147
  111.3 19.6 %all_to_all.10 = bf16[32,32,128]{2,1,0:T(8,128)(2,1)S(1)} all-to-all(bf16[32,32,128]{2,1,0:T(8,128)(2,1)S(1)} %bitcast.14), channel_id=1, replica_groups=mesh['y'=4,'zh'=4,'core'=2,'zl'=2,'x'=4] {'zh','zl','x'}, dimensions={0} | all-to-all | bytes 524288 | tf_op jit(solution)/shard_map/all_to_all | solution.py:532
  131.0 2.3 %collective-permute-start.12 = (f32[16,128]{1,0:T(8,128)S(1)}, f32[16,128]{1,0:T(8,128)S(1)}, u32[]{:S(2)}, u32[]{:S(2)}) collective-permute-start(f32[16,128]{1,0:T(8,128)S(1)} %get-tuple-element.69), channel_id=1, source_target_pairs={{0,8},{8,0},{16,24},{24,16},{32,40},{40,32},{48,56},{56,48},{64,72... | collective-permute-start | bytes 24584 | tf_op jit(solution)/shard_map/ppermute | solution.py:576
  133.2 2.6 %collective-permute-start.13 = (f32[16,128]{1,0:T(8,128)S(1)}, f32[16,128]{1,0:T(8,128)S(1)}, u32[]{:S(2)}, u32[]{:S(2)}) collective-permute-start(f32[16,128]{1,0:T(8,128)S(1)} %get-tuple-element.68), channel_id=1, source_target_pairs={{8,16},{24,32},{40,48},{56,64},{72,80},{88,96},{104,112},{120,128}... | collective-permute-start | bytes 24584 | tf_op jit(solution)/shard_map/ppermute | solution.py:579
  135.9 3.2 %collective-permute-done.13.apart_ref = f32[16,128]{1,0:T(8,128)S(1)} collective-permute-done((f32[16,128]{1,0:T(8,128)S(1)}, f32[16,128]{1,0:T(8,128)S(1)}, u32[]{:S(2)}, u32[]{:S(2)}) %collective-permute-start.13) | collective-permute-done | bytes 8224 | tf_op jit(solution)/shard_map/ppermute | solution.py:579
  139.1 5.3 %shard_map.172 = (f32[4,12,4,16]{3,2,1,0:T(4,128)}, bf16[4,12,4,384]{3,2,1,0:T(4,128)(2,1)}) custom-call(f32[16,128]{1,0:T(8,128)S(1)} %collective-permute-done.12.near_ref, f32[32,128]{1,0:T(8,128)S(1)} %convert_reduce_fusion.mine_ref, f32[16,128]{1,0:T(8,128)S(1)} %collective-permute-done.13.apart_ref, f32[6,4,8,128]{3,2,1,0:T(8,128)S(1)} %copy-done.3, ...), custom_call_target="tpu_custom_call" | custom-call | tf_op jit(solution)/shard_map/pallas_call | solution.py:277
  (77 shorter events, 9.1 us)
Async XLA Ops:
  0.6 59.6 %copy-start = (bf16[4096,64]{0,1:T(8,128)(2,1)S(1)}, bf16[4096,64]{0,1:T(8,128)(2,1)}, u32[]{:S(2)}) copy-start(bf16[4096,64]{0,1:T(8,128)(2,1)} %param.18) | copy-start | bytes 1572868
  0.7 49.7 %copy-start.1 = (bf16[3,3,3,16,384]{4,3,2,1,0:T(8,128)(2,1)S(1)}, bf16[3,3,3,16,384]{4,3,2,1,0:T(8,128)(2,1)}, u32[]{:S(2)}) copy-start(bf16[3,3,3,16,384]{4,3,2,1,0:T(8,128)(2,1)} %w_ref) | copy-start | bytes 995332
  0.7 21.8 %copy-start.15 = (f32[16]{0:T(128)S(1)}, f32[16]{0:T(128)}, u32[]{:S(2)}) copy-start(f32[16]{0:T(128)} %param.21) | copy-start | bytes 196
  3.1 53.3 %all-to-all-start = ((bf16[32,48,384]{2,1,0:T(8,128)(2,1)}), bf16[32,48,384]{2,1,0:T(8,128)(2,1)}, u32[]{:S(2)}, u32[]{:S(2)}) async-start(bf16[32,48,384]{2,1,0:T(8,128)(2,1)} %shard_map.161), calls=%async_computation | async-start | bytes 2359296 | tf_op jit(solution)/shard_map/all_to_all | solution.py:505
  15.3 23.3 %collective-permute-start = (f32[2,16,512]{2,1,0:T(8,128)S(1)}, f32[2,16,512]{2,1,0:T(8,128)S(1)}, u32[]{:S(2)}, u32[]{:S(2)}) collective-permute-start(f32[2,16,512]{2,1,0:T(8,128)S(1)} %get-tuple-element.39), channel_id=1, source_target_pairs={{0,8},{8,16},{16,24},{24,32},{32,40},{40,48},{48,56},{56,64},{64,7... | collective-permute-start | bytes 196616 | tf_op jit(solution)/shard_map/ppermute | solution.py:426
  20.4 23.9 %collective-permute-start.1 = (f32[2,16,512]{2,1,0:T(8,128)S(1)}, f32[2,16,512]{2,1,0:T(8,128)S(1)}, u32[]{:S(2)}, u32[]{:S(2)}) collective-permute-start(f32[2,16,512]{2,1,0:T(8,128)S(1)} %get-tuple-element.40), channel_id=1, source_target_pairs={{8,0},{16,8},{24,16},{32,24},{40,32},{48,40},{56,48},{64,56},{72,6... | collective-permute-start | bytes 196616 | tf_op jit(solution)/shard_map/ppermute | solution.py:427
  45.7 4.9 %collective-permute-start.2 = (f32[2,8,512]{2,1,0:T(8,128)}, f32[2,8,512]{2,1,0:T(8,128)S(1)}, u32[]{:S(2)}, u32[]{:S(2)}) collective-permute-start(f32[2,8,512]{2,1,0:T(8,128)} %get-tuple-element.43), channel_id=1, source_target_pairs={{0,1},{1,2},{2,3},{3,4},{4,5},{5,6},{6,7},{8,9},{9,10},{10,11},{11... | collective-permute-start | bytes 98312 | tf_op jit(solution)/shard_map/ppermute | solution.py:432
  48.9 5.0 %collective-permute-start.3 = (f32[2,8,512]{2,1,0:T(8,128)}, f32[2,8,512]{2,1,0:T(8,128)}, u32[]{:S(2)}, u32[]{:S(2)}) collective-permute-start(f32[2,8,512]{2,1,0:T(8,128)} %get-tuple-element.44), channel_id=1, source_target_pairs={{1,0},{2,1},{3,2},{4,3},{5,4},{6,5},{7,6},{9,8},{10,9},{11,10},{12... | collective-permute-start | bytes 98312 | tf_op jit(solution)/shard_map/ppermute | solution.py:433
  60.2 6.2 %collective-permute-start.4 = (bf16[1536,128]{1,0:T(8,128)(2,1)}, bf16[1536,128]{1,0:T(8,128)(2,1)}, u32[]{:S(2)}, u32[]{:S(2)}) collective-permute-start(bf16[1536,128]{1,0:T(8,128)(2,1)} %slice.22), channel_id=1, source_target_pairs={{0,8},{8,0},{1,9},{9,1},{2,10},{10,2},{3,11},{11,3},{4,12},{12,4},... | collective-permute-start | bytes 1179656 | tf_op jit(solution)/shard_map/ppermute | solution.py:515
  60.4 16.6 %collective-permute-start.5 = (bf16[768,256]{1,0:T(8,128)(2,1)}, bf16[768,256]{1,0:T(8,128)(2,1)S(1)}, u32[]{:S(2)}, u32[]{:S(2)}) collective-permute-start(bf16[768,256]{1,0:T(8,128)(2,1)} %get-tuple-element.55), channel_id=1, source_target_pairs={{0,64},{64,128},{128,192},{192,0},{1,65},{65,129},{129,193},{193,1... | collective-permute-start | bytes 1179656 | tf_op jit(solution)/shard_map/ppermute | solution.py:513
  64.6 12.4 %collective-permute-start.6 = (bf16[768,256]{1,0:T(8,128)(2,1)}, bf16[768,256]{1,0:T(8,128)(2,1)S(1)}, u32[]{:S(2)}, u32[]{:S(2)}) collective-permute-start(bf16[768,256]{1,0:T(8,128)(2,1)} %get-tuple-element.54), channel_id=1, source_target_pairs={{64,0},{128,64},{192,128},{0,192},{65,1},{129,65},{193,129},{1,193... | collective-permute-start | bytes 1179656 | tf_op jit(solution)/shard_map/ppermute | solution.py:514
  75.4 13.4 %collective-permute-start.10 = (bf16[768,256]{1,0:T(8,128)(2,1)S(1)}, bf16[768,256]{1,0:T(8,128)(2,1)S(1)}, u32[]{:S(2)}, u32[]{:S(2)}) collective-permute-start(bf16[768,256]{1,0:T(8,128)(2,1)S(1)} %copy-done.7), channel_id=1, source_target_pairs={{64,0},{128,64},{192,128},{0,192},{65,1},{129,65},{193,129},{1,193... | collective-permute-start | bytes 1179656 | tf_op jit(solution)/shard_map/ppermute | solution.py:519
  76.9 12.0 %collective-permute-start.9 = (bf16[768,256]{1,0:T(8,128)(2,1)S(1)}, bf16[768,256]{1,0:T(8,128)(2,1)S(1)}, u32[]{:S(2)}, u32[]{:S(2)}) collective-permute-start(bf16[768,256]{1,0:T(8,128)(2,1)S(1)} %copy-done.6), channel_id=1, source_target_pairs={{0,64},{64,128},{128,192},{192,0},{1,65},{65,129},{129,193},{193,1... | collective-permute-start | bytes 1179656 | tf_op jit(solution)/shard_map/ppermute | solution.py:518
  85.9 11.9 %collective-permute-start.7 = (bf16[768,256]{1,0:T(8,128)(2,1)S(1)}, bf16[768,256]{1,0:T(8,128)(2,1)S(1)}, u32[]{:S(2)}, u32[]{:S(2)}) collective-permute-start(bf16[768,256]{1,0:T(8,128)(2,1)S(1)} %collective-permute-done.5.refs_2_), channel_id=1, source_target_pairs={{0,64},{64,128},{128,192},{192,0},{1,65},{65,129},{129,193},{193,1... | collective-permute-start | bytes 1179656 | tf_op jit(solution)/shard_map/ppermute | solution.py:522
  86.0 11.8 %collective-permute-start.8 = (bf16[768,256]{1,0:T(8,128)(2,1)S(1)}, bf16[768,256]{1,0:T(8,128)(2,1)S(1)}, u32[]{:S(2)}, u32[]{:S(2)}) collective-permute-start(bf16[768,256]{1,0:T(8,128)(2,1)S(1)} %collective-permute-done.6.refs_3_), channel_id=1, source_target_pairs={{64,0},{128,64},{192,128},{0,192},{65,1},{129,65},{193,129},{1,193... | collective-permute-start | bytes 1179656 | tf_op jit(solution)/shard_map/ppermute | solution.py:522
  97.8 41.3 %slice-start = ((s8[7962624]{0:T(1024)(128)(4,1)}), s8[4194304]{0:T(1024)(128)(4,1)S(1)}, s32[]{:S(2)}) async-start(s8[7962624]{0:T(1024)(128)(4,1)} %bitcast.11), calls=%async_computation.2 | async-start | bytes 8388608
  103.3 32.5 %copy-start.11 = (f32[384]{0:T(512)S(1)}, f32[384]{0:T(512)}, u32[]{:S(2)}) copy-start(f32[384]{0:T(512)} %param.25) | copy-start | bytes 4612
  103.3 32.5 %copy-start.12 = (f32[384]{0:T(512)S(1)}, f32[384]{0:T(512)}, u32[]{:S(2)}) copy-start(f32[384]{0:T(512)} %param.26) | copy-start | bytes 4612
  103.3 32.5 %copy-start.13 = (f32[384]{0:T(512)S(1)}, f32[384]{0:T(512)}, u32[]{:S(2)}) copy-start(f32[384]{0:T(512)} %param.29) | copy-start | bytes 4612
  103.3 35.8 %slice-start.1 = ((s8[7962624]{0:T(1024)(128)(4,1)}), s8[3768320]{0:T(1024)(128)(4,1)S(1)}, s32[]{:S(2)}) async-start(s8[7962624]{0:T(1024)(128)(4,1)} %bitcast.11), calls=%async_computation.3 | async-start | bytes 7536640
  103.3 35.8 %copy-start.3 = (f32[6,4,8,128]{3,2,1,0:T(8,128)S(1)}, f32[6,4,8,128]{3,2,1,0:T(8,128)}, u32[]{:S(2)}) copy-start(f32[6,4,8,128]{3,2,1,0:T(8,128)} %copy-done.2) | copy-start | bytes 294916
  103.3 6.8 %collective-permute-start.11 = (f32[1536,128]{1,0:T(8,128)S(1)}, f32[1536,128]{1,0:T(8,128)S(1)}, u32[]{:S(2)}, u32[]{:S(2)}) collective-permute-start(f32[1536,128]{1,0:T(8,128)S(1)} %shard_map.169), channel_id=1, source_target_pairs={{0,8},{8,0},{1,9},{9,1},{2,10},{10,2},{3,11},{11,3},{4,12},{12,4},... | collective-permute-start | bytes 2359304 | tf_op jit(solution)/shard_map/ppermute | solution.py:529
  131.0 4.9 %collective-permute-start.12 = (f32[16,128]{1,0:T(8,128)S(1)}, f32[16,128]{1,0:T(8,128)S(1)}, u32[]{:S(2)}, u32[]{:S(2)}) collective-permute-start(f32[16,128]{1,0:T(8,128)S(1)} %get-tuple-element.69), channel_id=1, source_target_pairs={{0,8},{8,0},{16,24},{24,16},{32,40},{40,32},{48,56},{56,48},{64,72... | collective-permute-start | bytes 24584 | tf_op jit(solution)/shard_map/ppermute | solution.py:576
  133.2 5.9 %collective-permute-start.13 = (f32[16,128]{1,0:T(8,128)S(1)}, f32[16,128]{1,0:T(8,128)S(1)}, u32[]{:S(2)}, u32[]{:S(2)}) collective-permute-start(f32[16,128]{1,0:T(8,128)S(1)} %get-tuple-element.68), channel_id=1, source_target_pairs={{8,16},{24,32},{40,48},{56,64},{72,80},{88,96},{104,112},{120,128}... | collective-permute-start | bytes 24584 | tf_op jit(solution)/shard_map/ppermute | solution.py:579
  (9 other events, 98.7 us)

commit v6 on v5

--- a/solution.py
+++ b/solution.py
@@ -24,6 +24,13 @@
 SUB = 256
 CHUNK = 768
 NT = (((1,), (1,)), ((), ()))
+
+
+def mesh_index(axes):
+    index = 0
+    for axis in axes:
+        index = index * lax.axis_size(axis) + lax.axis_index(axis)
+    return index
 
 
 def lane_max(s):
@@ -43,6 +50,8 @@
     if last:
         w_ref, u_ref = refs
         query = q_ref[...]
+        own = w_ref[:, pl.ds(pl.multiple_of(mesh_index(HEAD) * HEAD_DIM, HEAD_DIM), HEAD_DIM)]
+        weight = jnp.concatenate([own, jnp.zeros_like(own)], axis=0)
     else:
         (so_ref,) = refs
         query = jnp.where(pl.program_id(0) < half, q_ref[...], qx_ref[...])
@@ -102,7 +111,7 @@
         if last:
             total = accs[r][:, 128:]
             mixed = (accs[r][:, :128] / total).astype(jnp.bfloat16)
-            u = jnp.dot(mixed, w_ref[...], preferred_element_type=jnp.float32)
+            u = lax.dot_general(mixed, weight, NT, preferred_element_type=jnp.float32)
             u_ref[pl.ds(r * SUB, SUB), :] = jnp.where(lane < 64, u, tops[r] + jnp.log2(total))
         else:
             so_ref[pl.ds(r * SUB, SUB), :] = jnp.concatenate(
@@ -170,8 +179,9 @@
     mine_ref,
     apart_ref,
     cells_ref,
-    affine_ref,
-    beyond_ref,
+    level_ref,
+    scale_ref,
+    mean_ref,
     w1_ref,
     b1_ref,
     gain_ref,
@@ -187,8 +197,12 @@
     act,
     wide,
     done,
+    vecs,
 ):
-    even = beyond_ref[4] > 0
+    even = lax.axis_index("core") == 0
+    at_row, at_col = mesh_index(SEQ), mesh_index(BLK)
+    up, down = at_row > 0, at_row < lax.axis_size(SEQ) - 1
+    before, after = at_col > 0, at_col < lax.axis_size(BLK) - 1
     above = jnp.where(even, apart_ref[...], near_ref[...])
     below = jnp.where(even, near_ref[...], apart_ref[...])
     for at, rows in enumerate((above, mine_ref[0:16, :], mine_ref[16:32, :], below)):
@@ -196,9 +210,14 @@
         for f in range(F):
             vel[f, at, 0:4, :] = rows[f * 4 : f * 4 + 4]
             vel[f, at, 4:8, :] = turned[f * 4 : f * 4 + 4]
-    level, scale, mean = affine_ref[0:1, :], affine_ref[1:2, :], affine_ref[2:3, :]
-    denoised = cells_ref[2:6, :, :, 0:64] - level * vel[:, :, :, 0:64]
-    up, down, before, after = (beyond_ref[k] > 0 for k in range(4))
+    vecs[...] = jnp.zeros(vecs.shape, jnp.float32)
+    vecs[0:1, 0:LAT] = scale_ref[...].reshape(1, LAT)
+    vecs[8:9, 0:LAT] = mean_ref[...].reshape(1, LAT)
+    base = vecs[...]
+    tiled = base + pltpu.roll(base, LAT, axis=1)
+    tiled = tiled + pltpu.roll(tiled, 2 * LAT, axis=1)
+    scale, mean = tiled[0:1, 0:64], tiled[8:9, 0:64]
+    denoised = cells_ref[2:6, :, :, 0:64] - level_ref[0] * vel[:, :, :, 0:64]
     row = lax.broadcasted_iota(jnp.int32, denoised.shape, 1)
     col = lax.broadcasted_iota(jnp.int32, denoised.shape, 2)
     kept = inside(row, 0, 3, up, down) & inside(col, 0, 7, before, after)
@@ -224,11 +243,11 @@
     parts = C1 // 128
     for k in range(parts):
         act[k, 0:2, :, 0:16, :] = mid_ref[:, :, :, pl.ds(k * 128, 128)]
-    gain = gain_ref[...]
+    gain = gain_ref[...].reshape(1, C1)
     for p in range(2):
         for q in range(2):
             lanes = pl.ds((2 * p + q) * C1, C1)
-            value = b1_ref[...]
+            value = b1_ref[...].reshape(1, C1)
             for t in range(3):
                 value = value + jnp.dot(
                     window[t * 32 : t * 32 + 128],
@@ -257,7 +276,7 @@
                 jnp.bfloat16
             )
     middle = [first[k, :, 1:5, pl.ds(1, 16), :].reshape(256, 128) for k in range(parts)]
-    total = jnp.concatenate(middle, axis=1) + b2_ref[...]
+    total = jnp.concatenate(middle, axis=1) + b2_ref[...].reshape(1, C1)
     for tap in range(9):
         t, u = divmod(tap, 3)
         rows = wide[t : t + 4, u : u + 4].reshape(256, 3 * C1)
@@ -273,7 +292,7 @@
 
 def tail(*args):
     specs = [pl.BlockSpec(memory_space=pltpu.VMEM)] * len(args)
-    specs[5] = pl.BlockSpec(memory_space=pltpu.SMEM)
+    specs[4] = pl.BlockSpec(memory_space=pltpu.SMEM)
     return pl.pallas_call(
         tail_kernel,
         in_specs=specs,
@@ -290,6 +309,7 @@
             pltpu.VMEM((C1 // 128, 6, 6, 24, 128), jnp.float32),
             pltpu.VMEM((6, 6, 16, 3 * C1), jnp.bfloat16),
             pltpu.VMEM((C1 // 128, F, 128, 128), jnp.float32),
+            pltpu.VMEM((16, 128), jnp.float32),
         ],
         compiler_params=pltpu.CompilerParams(vmem_limit_bytes=32 << 20),
     )(*args)
@@ -418,7 +438,7 @@
     return [(i, i + step) for i in range(count) if 0 <= i + step < count]
 
 
-def input_halos(noisy, cache_in, cache_mid):
+def halo_rows(noisy, cache_in, cache_mid):
     edge = (2, 16, 512)
     toks, down, up = small_call(
         edge_rows_kernel, [(6, 2, 8, 128), edge, edge], [(6, 4, 16, 128)]
@@ -426,12 +446,9 @@
     above = lax.ppermute(down, SEQ, along(SEQ, 1))
     below = lax.ppermute(up, SEQ, along(SEQ, -1))
     side = (2, 8, 512)
-    toks, mids, right, left = small_call(
-        edge_cols_kernel, [(6, 4, 8, 128), (2, 6, 16, C1), side, side]
-    )(toks, cache_mid, above, below)
-    before = lax.ppermute(right, BLK, along(BLK, 1))
-    after = lax.ppermute(left, BLK, along(BLK, -1))
-    return small_call(place_kernel, [(6, 4, 8, 128), (2, 6, 16, C1)])(toks, mids, before, after)
+    return small_call(edge_cols_kernel, [(6, 4, 8, 128), (2, 6, 16, C1), side, side])(
+        toks, cache_mid, above, below
+    )
 
 
 def pack_kernel(q_ref, k_ref, v_ref, out_ref):
@@ -497,10 +514,26 @@
     )(own, oth)
 
 
-def attention(query_vectors, key_vectors, value_vectors, weight_head, work, inputs):
+def head_sum_kernel(parts_ref, mine_ref, near_ref, apart_ref):
+    total = parts_ref[0].astype(jnp.float32)
+    for h in range(1, parts_ref.shape[0]):
+        total = total + parts_ref[h].astype(jnp.float32)
+    mine_ref[...] = total
+    even = lax.axis_index("core") == 0
+    near_ref[...] = jnp.where(even, total[16:32], total[0:16])
+    apart_ref[...] = jnp.where(even, total[0:16], total[16:32])
+
+
+def head_sum(parts):
+    return small_call(head_sum_kernel, [(32, 128), (16, 128), (16, 128)])(parts)
+
+
+def attention(query_vectors, key_vectors, value_vectors, weight_head, inputs):
     packed = pack(query_vectors, key_vectors, value_vectors)
     packed, inputs = lax.optimization_barrier((packed, inputs))
-    work = work(*inputs)
+    noisy, cache_in, cache_mid, weight_in = inputs
+    rows = halo_rows(noisy, cache_in, cache_mid)
+    weight_first = window_weights(weight_in)
     heads, tokens = packed.shape[:2]
     moved = lax.all_to_all(packed, HEAD, split_axis=0, concat_axis=0, tiled=True)
     moved = moved.reshape(heads * tokens, 3 * HEAD_DIM)
@@ -509,28 +542,34 @@
     left = [((i + 1) % 4, i) for i in range(4)]
     mid = moved.shape[0] // 2
     a, b, q_own = moved[:mid, :256], moved[mid:, :256], moved[:, 256:]
-    (a, b, q_own), work = lax.optimization_barrier(((a, b, q_own), work))
+    a, b, q_own, rows, weight_first = lax.optimization_barrier((a, b, q_own, rows, weight_first))
     left_a = lax.ppermute(a, "y", right)
     right_b = lax.ppermute(b, "y", left)
     q_oth = lax.ppermute(q_own, "core", swap)
     state = flash(moved, q_oth, [moved])
-    state, a, b = lax.optimization_barrier((state, a, b))
+    toks, mids, to_right, to_left = rows
+    state, a, b, to_right, to_left = lax.optimization_barrier((state, a, b, to_right, to_left))
     left_b = lax.ppermute(b, "y", right)
     right_a = lax.ppermute(a, "y", left)
+    before = lax.ppermute(to_right, BLK, along(BLK, 1))
+    after = lax.ppermute(to_left, BLK, along(BLK, -1))
     state = flash(moved, q_oth, [left_a, right_b], state)
-    state, left_a, right_b = lax.optimization_barrier((state, left_a, right_b))
+    state, left_a, right_b, before, after = lax.optimization_barrier(
+        (state, left_a, right_b, before, after)
+    )
+    borders = small_call(place_kernel, [(6, 4, 8, 128), (2, 6, 16, C1)])(
+        toks, mids, before, after
+    )
     far = [lax.ppermute(left_a, "y", right), lax.ppermute(right_b, "y", left)]
     state = flash(moved, q_oth, [left_b, right_a], state)
-    head = lax.axis_index(HEAD)
-    weight = lax.dynamic_slice_in_dim(weight_head, head * HEAD_DIM, HEAD_DIM, axis=0)
-    weight = jnp.pad(weight, ((0, 0), (0, 64)))
+    weight = weight_head.T
     oth = flash_last(q_oth, 0, far, state, 1, weight)
     oth, state = lax.optimization_barrier((oth, state))
     oth = lax.ppermute(oth, "core", swap)
     own = flash_last(moved, 2, far, state, 0, weight)
     partial = merge(own, oth).reshape(heads, 32, 128)
     parts = lax.all_to_all(partial, HEAD, split_axis=0, concat_axis=0, tiled=True)
-    return jnp.sum(parts.astype(jnp.float32), axis=0), work
+    return head_sum(parts), (*borders, weight_first)
 
 
 def shards(
@@ -550,46 +589,33 @@
     weight_mid,
     bias_mid,
 ):
-    def work(noisy, cache_first, cache_second, weight_first):
-        row, col = lax.axis_index(SEQ), lax.axis_index(BLK)
-        last_row, last_col = lax.axis_size(SEQ) - 1, lax.axis_size(BLK) - 1
-        even = lax.axis_index("core") == 0
-        beyond = jnp.stack([row > 0, row < last_row, col > 0, col < last_col, even])
-        level = jnp.broadcast_to(noise_level, (4 * LAT,))
-        affine = jnp.stack([level, jnp.tile(latent_scale, 4), jnp.tile(latent_mean, 4)])
-        halos = input_halos(noisy, cache_first, cache_second)
-        return (*halos, beyond.astype(jnp.int32), affine, window_weights(weight_first))
-
-    mine, work = attention(
+    (mine, near, apart), (cells, cache_second, weight_first) = attention(
         query_vectors,
         key_vectors,
         value_vectors,
         weight_head,
-        work,
         (noisy_latent, cache_in, cache_mid, weight_in),
     )
-    cells, cache_second, beyond, affine, weight_first = work
 
     count = lax.axis_size(SEQ)
-    even = lax.axis_index("core") == 0
-    low, high = mine[:16], mine[16:]
-    near = lax.ppermute(jnp.where(even, high, low), SEQ, [(i, i ^ 1) for i in range(count)])
+    near = lax.ppermute(near, SEQ, [(i, i ^ 1) for i in range(count)])
     pairs = [(i, i + 1) for i in range(1, count - 1, 2)]
     pairs += [(j, i) for i, j in pairs]
-    apart = lax.ppermute(jnp.where(even, low, high), SEQ, pairs)
+    apart = lax.ppermute(apart, SEQ, pairs)
     denoised, features = tail(
         near,
         mine,
         apart,
         cells,
-        affine,
-        beyond,
+        noise_level,
+        latent_scale,
+        latent_mean,
         weight_first,
-        bias_in.reshape(1, C1),
-        norm_gain.reshape(1, C1),
+        bias_in,
+        norm_gain,
         cache_second,
         weight_mid.reshape(9, 3 * C1, C1),
-        bias_mid.reshape(1, C1),
+        bias_mid,
     )
     return denoised.transpose(0, 2, 1, 3), features.transpose(0, 2, 1, 3)
 

time: 145 us -> 129 us (0.89)
  Pallas kernels: 48.5 us -> 40.7 us
  waiting for transfers between devices: 27.6 us -> 24.6 us
  local copies, waits for them, and re-layouts: 6.57 us -> 3.72 us
    ppermute x6, waiting for transfers between devices: 27.5 us -> 23.2 us  [the longest x1 15.1 us: halo_rows(): above = lax.ppermute(down, SEQ, along(SEQ, 1))]
    slice x2, local copies, waits for them, and re-layouts: 3.85 us -> 0.08 us  [attention(): a, b, q_own = (moved[:mid, :256], moved[mid:, :256], moved[:, 256:])]
    pallas_call x3, Pallas kernels: 26.8 us -> 23.2 us  [flash(): pl.pallas_call(functools.partial(flash_kernel, state is None, False, len(...]
    ppermute x1, starting transfers between devices: 4.24 us -> 1.41 us  [attention(): left_a = lax.ppermute(a, 'y', right)]
    pallas_call x2, Pallas kernels: 10.7 us -> 8.57 us  [flash_last(): pl.pallas_call(functools.partial(flash_kernel, False, True, len(kvs), hal...]
    ppermute x1, starting transfers between devices: 0.01 us -> 1.65 us  [attention(): q_oth = lax.ppermute(q_own, 'core', swap)]
    unnamed x37 -> x40, local copies, waits for them, and re-layouts: 2.37 us -> 3.6 us
  transfers between devices with their start and end apart: 15 -> 15, of which waited for: 4 -> 5; matrix products, arithmetic and copies ran while one was open for 0% -> 0% of each run, Pallas kernels for 24% -> 22%
where the time goes in v6:
time: 129 us
  Pallas kernels  40.7 us (32%)
  starting transfers between devices  39 us (30%)
  waiting for transfers between devices  24.6 us (19%)
  blocking collectives  19.4 us (15%)
  local copies, waits for them, and re-layouts  3.72 us (3%)
  between operations  1.71 us (1%)
    pallas_call x3, Pallas kernels, flash(): pl.pallas_call(functools.partial(flash_kernel, state is None, False, len(...  23.2 us
    all_to_all x1, blocking collectives, attention(): lax.all_to_all(partial, HEAD, split_axis=0, concat_axis=0, tiled=True)  19.4 us
    ppermute x1, waiting for transfers between devices, halo_rows(): above = lax.ppermute(down, SEQ, along(SEQ, 1))  15.1 us
    all_to_all x1, starting transfers between devices, attention(): lax.all_to_all(packed, HEAD, split_axis=0, concat_axis=0, tiled=True)  11.9 us
    pallas_call x2, Pallas kernels, flash_last(): pl.pallas_call(functools.partial(flash_kernel, False, True, len(kvs), hal...  8.57 us
    ppermute x1, waiting for transfers between devices, halo_rows(): below = lax.ppermute(up, SEQ, along(SEQ, -1))  5.63 us
    ppermute x1, starting transfers between devices, halo_rows(): above = lax.ppermute(down, SEQ, along(SEQ, 1))  5.15 us
    pallas_call x1, Pallas kernels, tail(): pl.pallas_call(tail_kernel, in_specs=specs, out_specs=[pl.BlockSpec(memor...  4.76 us
  transfers between devices with their start and end apart: 15, of which 5 were waited for; matrix products, arithmetic and copies ran while one was open for 0% of the time, Pallas kernels for 22%

profile of v6, /device:TPU:1, one launch (start us, length us, event | category | flops | bytes accessed | tf_op | source)
XLA Modules:
  0.0 129.1 jit_solution(1005354424921602481)
XLA Ops:
  0.7 2.3 %shard_map.158 = bf16[32,48,384]{2,1,0:T(8,128)(2,1)} custom-call(bf16[48,4096]{1,0:T(8,128)(2,1)} %q_ref.1, bf16[48,4096]{1,0:T(8,128)(2,1)} %k_ref.1, bf16[48,4096]{1,0:T(8,128)(2,1)} %v_ref.1), custom_call_target="tpu_custom_call" | custom-call | tf_op jit(solution)/shard_map/pallas_call | solution.py:466
  3.0 11.9 %all-to-all-start = ((bf16[32,48,384]{2,1,0:T(8,128)(2,1)}), bf16[32,48,384]{2,1,0:T(8,128)(2,1)S(1)}, u32[]{:S(2)}, u32[]{:S(2)}) async-start(bf16[32,48,384]{2,1,0:T(8,128)(2,1)} %shard_map.158), calls=%async_computation | async-start | bytes 2359296 | tf_op jit(solution)/shard_map/all_to_all | solution.py:538
  15.1 5.2 %collective-permute-start = (f32[2,16,512]{2,1,0:T(8,128)S(1)}, f32[2,16,512]{2,1,0:T(8,128)S(1)}, u32[]{:S(2)}, u32[]{:S(2)}) collective-permute-start(f32[2,16,512]{2,1,0:T(8,128)S(1)} %get-tuple-element.46), channel_id=1, source_target_pairs={{0,8},{8,16},{16,24},{24,32},{32,40},{40,48},{48,56},{56,64},{64,7... | collective-permute-start | bytes 196616 | tf_op jit(solution)/shard_map/ppermute | solution.py:446
  20.3 1.9 %collective-permute-start.1 = (f32[2,16,512]{2,1,0:T(8,128)S(1)}, f32[2,16,512]{2,1,0:T(8,128)S(1)}, u32[]{:S(2)}, u32[]{:S(2)}) collective-permute-start(f32[2,16,512]{2,1,0:T(8,128)S(1)} %get-tuple-element.47), channel_id=1, source_target_pairs={{8,0},{16,8},{24,16},{32,24},{40,32},{48,40},{56,48},{64,56},{72,6... | collective-permute-start | bytes 196616 | tf_op jit(solution)/shard_map/ppermute | solution.py:447
  23.4 15.1 %collective-permute-done.above_ref = f32[2,16,512]{2,1,0:T(8,128)S(1)} collective-permute-done((f32[2,16,512]{2,1,0:T(8,128)S(1)}, f32[2,16,512]{2,1,0:T(8,128)S(1)}, u32[]{:S(2)}, u32[]{:S(2)}) %collective-permute-start) | collective-permute-done | bytes 65568 | tf_op jit(solution)/shard_map/ppermute | solution.py:446
  38.5 5.6 %collective-permute-done.1.below_ref = f32[2,16,512]{2,1,0:T(8,128)S(1)} collective-permute-done((f32[2,16,512]{2,1,0:T(8,128)S(1)}, f32[2,16,512]{2,1,0:T(8,128)S(1)}, u32[]{:S(2)}, u32[]{:S(2)}) %collective-permute-start.1) | collective-permute-done | bytes 65568 | tf_op jit(solution)/shard_map/ppermute | solution.py:447
  47.0 1.7 %collective-permute-start.2 = (bf16[1536,128]{1,0:T(8,128)(2,1)S(1)}, bf16[1536,128]{1,0:T(8,128)(2,1)S(1)}, u32[]{:S(2)}, u32[]{:S(2)}) collective-permute-start(bf16[1536,128]{1,0:T(8,128)(2,1)S(1)} %slice.14), channel_id=1, source_target_pairs={{0,8},{8,0},{1,9},{9,1},{2,10},{10,2},{3,11},{11,3},{4,12},{12,4},... | collective-permute-start | bytes 1179656 | tf_op jit(solution)/shard_map/ppermute | solution.py:548
  48.6 1.4 %collective-permute-start.3 = (bf16[768,256]{1,0:T(8,128)(2,1)S(1)}, bf16[768,256]{1,0:T(8,128)(2,1)S(1)}, u32[]{:S(2)}, u32[]{:S(2)}) collective-permute-start(bf16[768,256]{1,0:T(8,128)(2,1)S(1)} %get-tuple-element.64), channel_id=1, source_target_pairs={{0,64},{64,128},{128,192},{192,0},{1,65},{65,129},{129,193},{193,1... | collective-permute-start | bytes 1179656 | tf_op jit(solution)/shard_map/ppermute | solution.py:546
  50.0 1.7 %collective-permute-start.4 = (bf16[768,256]{1,0:T(8,128)(2,1)S(1)}, bf16[768,256]{1,0:T(8,128)(2,1)S(1)}, u32[]{:S(2)}, u32[]{:S(2)}) collective-permute-start(bf16[768,256]{1,0:T(8,128)(2,1)S(1)} %get-tuple-element.63), channel_id=1, source_target_pairs={{64,0},{128,64},{192,128},{0,192},{65,1},{129,65},{193,129},{1,193... | collective-permute-start | bytes 1179656 | tf_op jit(solution)/shard_map/ppermute | solution.py:547
  51.8 7.8 %shard_map.162.refs_4_ = f32[3072,256]{1,0:T(8,128)S(1)} custom-call(bf16[1536,384]{1,0:T(8,128)(2,1)S(1)} %bitcast.11, bf16[1536,128]{1,0:T(8,128)(2,1)S(1)} %collective-permute-done.2.refs_1_.refs_0_, bf16[1536,384]{1,0:T(8,128)(2,1)S(1)} %bitcast.12), custom_call_target="tpu_custom_call" | custom-call | flops 4831838208 | bytes 6291456 | tf_op jit(solution)/shard_map/pallas_call | solution.py:135
  59.6 3.1 %collective-permute-start.5 = (f32[2,8,512]{2,1,0:T(8,128)S(1)}, f32[2,8,512]{2,1,0:T(8,128)S(1)}, u32[]{:S(2)}, u32[]{:S(2)}) collective-permute-start(f32[2,8,512]{2,1,0:T(8,128)S(1)} %copy-done.14), channel_id=1, source_target_pairs={{0,1},{1,2},{2,3},{3,4},{4,5},{5,6},{6,7},{8,9},{9,10},{10,11},{11... | collective-permute-start | bytes 98312 | tf_op jit(solution)/shard_map/ppermute | solution.py:554
  62.7 1.3 %collective-permute-start.6 = (f32[2,8,512]{2,1,0:T(8,128)S(1)}, f32[2,8,512]{2,1,0:T(8,128)S(1)}, u32[]{:S(2)}, u32[]{:S(2)}) collective-permute-start(f32[2,8,512]{2,1,0:T(8,128)S(1)} %copy-done.12), channel_id=1, source_target_pairs={{1,0},{2,1},{3,2},{4,3},{5,4},{6,5},{7,6},{9,8},{10,9},{11,10},{12... | collective-permute-start | bytes 98312 | tf_op jit(solution)/shard_map/ppermute | solution.py:555
  64.0 1.6 %collective-permute-start.10 = (bf16[768,256]{1,0:T(8,128)(2,1)S(1)}, bf16[768,256]{1,0:T(8,128)(2,1)S(1)}, u32[]{:S(2)}, u32[]{:S(2)}) collective-permute-start(bf16[768,256]{1,0:T(8,128)(2,1)S(1)} %get-tuple-element.64), channel_id=1, source_target_pairs={{64,0},{128,64},{192,128},{0,192},{65,1},{129,65},{193,129},{1,193... | collective-permute-start | bytes 1179656 | tf_op jit(solution)/shard_map/ppermute | solution.py:553
  65.5 7.7 %shard_map.163.refs_4_ = f32[3072,256]{1,0:T(8,128)S(1)} custom-call(bf16[1536,384]{1,0:T(8,128)(2,1)S(1)} %bitcast.13, bf16[1536,128]{1,0:T(8,128)(2,1)S(1)} %collective-permute-done.2.refs_1_.refs_0_, bf16[768,256]{1,0:T(8,128)(2,1)S(1)} %collective-permute-done.3.refs_2_, bf16[768,256]{1,0:T(8,128)(2,1)S(1)} %collective-permute-done.4.refs_3_, ...), custom_call_target="tpu_custom_call" | custom-call | flops 4831838208 | bytes 6291456 | tf_op jit(solution)/shard_map/pallas_call | solution.py:135
  73.4 2.7 %collective-permute-start.8 = (bf16[768,256]{1,0:T(8,128)(2,1)S(1)}, bf16[768,256]{1,0:T(8,128)(2,1)S(1)}, u32[]{:S(2)}, u32[]{:S(2)}) collective-permute-start(bf16[768,256]{1,0:T(8,128)(2,1)S(1)} %collective-permute-done.4.refs_3_), channel_id=1, source_target_pairs={{64,0},{128,64},{192,128},{0,192},{65,1},{129,65},{193,129},{1,193... | collective-permute-start | bytes 1179656 | tf_op jit(solution)/shard_map/ppermute | solution.py:563
  76.2 7.7 %shard_map.164.refs_3_ = f32[3072,256]{1,0:T(8,128)S(1)} custom-call(bf16[1536,384]{1,0:T(8,128)(2,1)S(1)} %bitcast.14, bf16[1536,128]{1,0:T(8,128)(2,1)S(1)} %collective-permute-done.2.refs_1_.refs_0_, bf16[768,256]{1,0:T(8,128)(2,1)S(1)} %collective-permute-done.9.refs_2_, bf16[768,256]{1,0:T(8,128)(2,1)S(1)} %collective-permute-done.10.refs_3_, ...), custom_call_target="tpu_custom_call" | custom-call | flops 4831838208 | bytes 6291456 | tf_op jit(solution)/shard_map/pallas_call | solution.py:135
  85.1 4.2 %shard_map.165 = f32[1536,128]{1,0:T(8,128)S(1)} custom-call(bf16[1536,128]{1,0:T(8,128)(2,1)S(1)} %collective-permute-done.2.refs_1_.refs_0_, bf16[768,256]{1,0:T(8,128)(2,1)S(1)} %collective-permute-done.7.refs_1_, bf16[768,256]{1,0:T(8,128)(2,1)S(1)} %collective-permute-done.8.refs_2_, f32[3072,256]{1,0:T(8,128)S(1)} %shard_map.164.refs_3_, ...), custom_call_target="tpu_custom_call" | custom-call | flops 2415919104 | bytes 3145728 | tf_op jit(solution)/shard_map/pallas_call | solution.py:156
  89.5 1.9 %collective-permute-start.11 = (f32[1536,128]{1,0:T(8,128)S(1)}, f32[1536,128]{1,0:T(8,128)S(1)}, u32[]{:S(2)}, u32[]{:S(2)}) collective-permute-start(f32[1536,128]{1,0:T(8,128)S(1)} %shard_map.165), channel_id=1, source_target_pairs={{0,8},{8,0},{1,9},{9,1},{2,10},{10,2},{3,11},{11,3},{4,12},{12,4},... | collective-permute-start | bytes 2359304 | tf_op jit(solution)/shard_map/ppermute | solution.py:568
  91.3 4.3 %shard_map.166.own_ref = f32[1536,128]{1,0:T(8,128)S(1)} custom-call(bf16[1536,384]{1,0:T(8,128)(2,1)S(1)} %bitcast.15, bf16[768,256]{1,0:T(8,128)(2,1)S(1)} %collective-permute-done.7.refs_1_, bf16[768,256]{1,0:T(8,128)(2,1)S(1)} %collective-permute-done.8.refs_2_, f32[3072,256]{1,0:T(8,128)S(1)} %shard_map.164.refs_3_, bf16[64,4096]{1,0:T(8,128)(2,1)S(1)} %bitcast.18), custom_call_target="tpu_custom_call" | custom-call | flops 2415919104 | bytes 3145728 | tf_op jit(solution)/shard_map/pallas_call | solution.py:156
  96.9 19.4 %all_to_all.10.parts_ref = bf16[32,32,128]{2,1,0:T(8,128)(2,1)S(1)} all-to-all(bf16[32,32,128]{2,1,0:T(8,128)(2,1)S(1)} %bitcast.16), channel_id=1, replica_groups=mesh['y'=4,'zh'=4,'core'=2,'zl'=2,'x'=4] {'zh','zl','x'}, dimensions={0} | all-to-all | bytes 524288 | tf_op jit(solution)/shard_map/all_to_all | solution.py:571
  116.3 2.1 %collective-permute-start.12 = (f32[16,128]{1,0:T(8,128)S(1)}, f32[16,128]{1,0:T(8,128)S(1)}, u32[]{:S(2)}, u32[]{:S(2)}) collective-permute-start(f32[16,128]{1,0:T(8,128)S(1)} %get-tuple-element.68), channel_id=1, source_target_pairs={{0,8},{8,0},{16,24},{24,16},{32,40},{40,32},{48,56},{56,48},{64,72... | collective-permute-start | bytes 24584 | tf_op jit(solution)/shard_map/ppermute | solution.py:601
  118.4 2.6 %collective-permute-start.13 = (f32[16,128]{1,0:T(8,128)S(1)}, f32[16,128]{1,0:T(8,128)S(1)}, u32[]{:S(2)}, u32[]{:S(2)}) collective-permute-start(f32[16,128]{1,0:T(8,128)S(1)} %get-tuple-element.70), channel_id=1, source_target_pairs={{8,16},{24,32},{40,48},{56,64},{72,80},{88,96},{104,112},{120,128}... | collective-permute-start | bytes 24584 | tf_op jit(solution)/shard_map/ppermute | solution.py:604
  121.7 2.5 %collective-permute-done.13.apart_ref = f32[16,128]{1,0:T(8,128)S(1)} collective-permute-done((f32[16,128]{1,0:T(8,128)S(1)}, f32[16,128]{1,0:T(8,128)S(1)}, u32[]{:S(2)}, u32[]{:S(2)}) %collective-permute-start.13) | collective-permute-done | bytes 8224 | tf_op jit(solution)/shard_map/ppermute | solution.py:604
  124.3 4.8 %shard_map.170 = (f32[4,12,4,16]{3,2,1,0:T(4,128)}, bf16[4,12,4,384]{3,2,1,0:T(4,128)(2,1)}) custom-call(f32[16,128]{1,0:T(8,128)S(1)} %collective-permute-done.12.near_ref, f32[32,128]{1,0:T(8,128)S(1)} %get-tuple-element.69.mine_ref, f32[16,128]{1,0:T(8,128)S(1)} %collective-permute-done.13.apart_ref, f32[6,4,8,128]{3,2,1,0:T(8,128)S(1)} %get-tuple-element.75.cells_ref, ...), custom_call_target="tpu_custom_call" | custom-call | tf_op jit(solution)/shard_map/pallas_call | solution.py:296
  (66 shorter events, 7.0 us)
Async XLA Ops:
  3.0 43.9 %all-to-all-start = ((bf16[32,48,384]{2,1,0:T(8,128)(2,1)}), bf16[32,48,384]{2,1,0:T(8,128)(2,1)S(1)}, u32[]{:S(2)}, u32[]{:S(2)}) async-start(bf16[32,48,384]{2,1,0:T(8,128)(2,1)} %shard_map.158), calls=%async_computation | async-start | bytes 2359296 | tf_op jit(solution)/shard_map/all_to_all | solution.py:538
  15.1 23.4 %collective-permute-start = (f32[2,16,512]{2,1,0:T(8,128)S(1)}, f32[2,16,512]{2,1,0:T(8,128)S(1)}, u32[]{:S(2)}, u32[]{:S(2)}) collective-permute-start(f32[2,16,512]{2,1,0:T(8,128)S(1)} %get-tuple-element.46), channel_id=1, source_target_pairs={{0,8},{8,16},{16,24},{24,32},{32,40},{40,48},{48,56},{56,64},{64,7... | collective-permute-start | bytes 196616 | tf_op jit(solution)/shard_map/ppermute | solution.py:446
  20.3 23.8 %collective-permute-start.1 = (f32[2,16,512]{2,1,0:T(8,128)S(1)}, f32[2,16,512]{2,1,0:T(8,128)S(1)}, u32[]{:S(2)}, u32[]{:S(2)}) collective-permute-start(f32[2,16,512]{2,1,0:T(8,128)S(1)} %get-tuple-element.47), channel_id=1, source_target_pairs={{8,0},{16,8},{24,16},{32,24},{40,32},{48,40},{56,48},{64,56},{72,6... | collective-permute-start | bytes 196616 | tf_op jit(solution)/shard_map/ppermute | solution.py:447
  47.0 4.8 %collective-permute-start.2 = (bf16[1536,128]{1,0:T(8,128)(2,1)S(1)}, bf16[1536,128]{1,0:T(8,128)(2,1)S(1)}, u32[]{:S(2)}, u32[]{:S(2)}) collective-permute-start(bf16[1536,128]{1,0:T(8,128)(2,1)S(1)} %slice.14), channel_id=1, source_target_pairs={{0,8},{8,0},{1,9},{9,1},{2,10},{10,2},{3,11},{11,3},{4,12},{12,4},... | collective-permute-start | bytes 1179656 | tf_op jit(solution)/shard_map/ppermute | solution.py:548
  48.6 16.9 %collective-permute-start.3 = (bf16[768,256]{1,0:T(8,128)(2,1)S(1)}, bf16[768,256]{1,0:T(8,128)(2,1)S(1)}, u32[]{:S(2)}, u32[]{:S(2)}) collective-permute-start(bf16[768,256]{1,0:T(8,128)(2,1)S(1)} %get-tuple-element.64), channel_id=1, source_target_pairs={{0,64},{64,128},{128,192},{192,0},{1,65},{65,129},{129,193},{193,1... | collective-permute-start | bytes 1179656 | tf_op jit(solution)/shard_map/ppermute | solution.py:546
  50.0 15.5 %collective-permute-start.4 = (bf16[768,256]{1,0:T(8,128)(2,1)S(1)}, bf16[768,256]{1,0:T(8,128)(2,1)S(1)}, u32[]{:S(2)}, u32[]{:S(2)}) collective-permute-start(bf16[768,256]{1,0:T(8,128)(2,1)S(1)} %get-tuple-element.63), channel_id=1, source_target_pairs={{64,0},{128,64},{192,128},{0,192},{65,1},{129,65},{193,129},{1,193... | collective-permute-start | bytes 1179656 | tf_op jit(solution)/shard_map/ppermute | solution.py:547
  59.6 13.7 %collective-permute-start.5 = (f32[2,8,512]{2,1,0:T(8,128)S(1)}, f32[2,8,512]{2,1,0:T(8,128)S(1)}, u32[]{:S(2)}, u32[]{:S(2)}) collective-permute-start(f32[2,8,512]{2,1,0:T(8,128)S(1)} %copy-done.14), channel_id=1, source_target_pairs={{0,1},{1,2},{2,3},{3,4},{4,5},{5,6},{6,7},{8,9},{9,10},{10,11},{11... | collective-permute-start | bytes 98312 | tf_op jit(solution)/shard_map/ppermute | solution.py:554
  62.7 10.6 %collective-permute-start.6 = (f32[2,8,512]{2,1,0:T(8,128)S(1)}, f32[2,8,512]{2,1,0:T(8,128)S(1)}, u32[]{:S(2)}, u32[]{:S(2)}) collective-permute-start(f32[2,8,512]{2,1,0:T(8,128)S(1)} %copy-done.12), channel_id=1, source_target_pairs={{1,0},{2,1},{3,2},{4,3},{5,4},{6,5},{7,6},{9,8},{10,9},{11,10},{12... | collective-permute-start | bytes 98312 | tf_op jit(solution)/shard_map/ppermute | solution.py:555
  64.0 12.1 %collective-permute-start.10 = (bf16[768,256]{1,0:T(8,128)(2,1)S(1)}, bf16[768,256]{1,0:T(8,128)(2,1)S(1)}, u32[]{:S(2)}, u32[]{:S(2)}) collective-permute-start(bf16[768,256]{1,0:T(8,128)(2,1)S(1)} %get-tuple-element.64), channel_id=1, source_target_pairs={{64,0},{128,64},{192,128},{0,192},{65,1},{129,65},{193,129},{1,193... | collective-permute-start | bytes 1179656 | tf_op jit(solution)/shard_map/ppermute | solution.py:553
  65.5 10.6 %collective-permute-start.9 = (bf16[768,256]{1,0:T(8,128)(2,1)S(1)}, bf16[768,256]{1,0:T(8,128)(2,1)S(1)}, u32[]{:S(2)}, u32[]{:S(2)}) collective-permute-start(bf16[768,256]{1,0:T(8,128)(2,1)S(1)} %get-tuple-element.63), channel_id=1, source_target_pairs={{0,64},{64,128},{128,192},{192,0},{1,65},{65,129},{129,193},{193,1... | collective-permute-start | bytes 1179656 | tf_op jit(solution)/shard_map/ppermute | solution.py:552
  73.3 11.8 %collective-permute-start.7 = (bf16[768,256]{1,0:T(8,128)(2,1)S(1)}, bf16[768,256]{1,0:T(8,128)(2,1)S(1)}, u32[]{:S(2)}, u32[]{:S(2)}) collective-permute-start(bf16[768,256]{1,0:T(8,128)(2,1)S(1)} %collective-permute-done.3.refs_2_), channel_id=1, source_target_pairs={{0,64},{64,128},{128,192},{192,0},{1,65},{65,129},{129,193},{193,1... | collective-permute-start | bytes 1179656 | tf_op jit(solution)/shard_map/ppermute | solution.py:563
  73.4 11.7 %collective-permute-start.8 = (bf16[768,256]{1,0:T(8,128)(2,1)S(1)}, bf16[768,256]{1,0:T(8,128)(2,1)S(1)}, u32[]{:S(2)}, u32[]{:S(2)}) collective-permute-start(bf16[768,256]{1,0:T(8,128)(2,1)S(1)} %collective-permute-done.4.refs_3_), channel_id=1, source_target_pairs={{64,0},{128,64},{192,128},{0,192},{65,1},{129,65},{193,129},{1,193... | collective-permute-start | bytes 1179656 | tf_op jit(solution)/shard_map/ppermute | solution.py:563
  85.1 39.1 %slice-start = ((s8[7962624]{0:T(1024)(128)(4,1)}), s8[4194304]{0:T(1024)(128)(4,1)S(1)}, s32[]{:S(2)}) async-start(s8[7962624]{0:T(1024)(128)(4,1)} %bitcast.6), calls=%async_computation.2 | async-start | bytes 8388608
  89.4 32.2 %copy-start.2 = (f32[2,6,16,384]{3,2,1,0:T(8,128)S(1)}, f32[2,6,16,384]{3,2,1,0:T(8,128)}, u32[]{:S(2)}) copy-start(f32[2,6,16,384]{3,2,1,0:T(8,128)} %copy-done.1) | copy-start | bytes 884740
  89.4 32.2 %copy-start.4 = (f32[6,4,8,128]{3,2,1,0:T(8,128)S(1)}, f32[6,4,8,128]{3,2,1,0:T(8,128)}, u32[]{:S(2)}) copy-start(f32[6,4,8,128]{3,2,1,0:T(8,128)} %copy-done.3) | copy-start | bytes 294916
  89.4 34.9 %slice-start.1 = ((s8[7962624]{0:T(1024)(128)(4,1)}), s8[3768320]{0:T(1024)(128)(4,1)S(1)}, s32[]{:S(2)}) async-start(s8[7962624]{0:T(1024)(128)(4,1)} %bitcast.6), calls=%async_computation.3 | async-start | bytes 7536640
  89.4 34.8 %copy-start.5 = (f32[384]{0:T(512)S(1)}, f32[384]{0:T(512)}, u32[]{:S(2)}) copy-start(f32[384]{0:T(512)} %b1_ref.1) | copy-start | bytes 4612
  89.4 34.8 %copy-start.6 = (f32[384]{0:T(512)S(1)}, f32[384]{0:T(512)}, u32[]{:S(2)}) copy-start(f32[384]{0:T(512)} %gain_ref.1) | copy-start | bytes 4612
  89.4 34.8 %copy-start.7 = (f32[384]{0:T(512)S(1)}, f32[384]{0:T(512)}, u32[]{:S(2)}) copy-start(f32[384]{0:T(512)} %b2_ref.1) | copy-start | bytes 4612
  89.4 34.8 %copy-start.8 = (f32[16]{0:T(128)S(1)}, f32[16]{0:T(128)}, u32[]{:S(2)}) copy-start(f32[16]{0:T(128)} %scale_ref.1) | copy-start | bytes 196
  89.5 34.8 %copy-start.9 = (f32[16]{0:T(128)S(1)}, f32[16]{0:T(128)}, u32[]{:S(2)}) copy-start(f32[16]{0:T(128)} %mean_ref.1) | copy-start | bytes 196
  89.5 6.2 %collective-permute-start.11 = (f32[1536,128]{1,0:T(8,128)S(1)}, f32[1536,128]{1,0:T(8,128)S(1)}, u32[]{:S(2)}, u32[]{:S(2)}) collective-permute-start(f32[1536,128]{1,0:T(8,128)S(1)} %shard_map.165), channel_id=1, source_target_pairs={{0,8},{8,0},{1,9},{9,1},{2,10},{10,2},{3,11},{11,3},{4,12},{12,4},... | collective-permute-start | bytes 2359304 | tf_op jit(solution)/shard_map/ppermute | solution.py:568
  116.3 5.4 %collective-permute-start.12 = (f32[16,128]{1,0:T(8,128)S(1)}, f32[16,128]{1,0:T(8,128)S(1)}, u32[]{:S(2)}, u32[]{:S(2)}) collective-permute-start(f32[16,128]{1,0:T(8,128)S(1)} %get-tuple-element.68), channel_id=1, source_target_pairs={{0,8},{8,0},{16,24},{24,16},{32,40},{40,32},{48,56},{56,48},{64,72... | collective-permute-start | bytes 24584 | tf_op jit(solution)/shard_map/ppermute | solution.py:601
  118.4 5.9 %collective-permute-start.13 = (f32[16,128]{1,0:T(8,128)S(1)}, f32[16,128]{1,0:T(8,128)S(1)}, u32[]{:S(2)}, u32[]{:S(2)}) collective-permute-start(f32[16,128]{1,0:T(8,128)S(1)} %get-tuple-element.70), channel_id=1, source_target_pairs={{8,16},{24,32},{40,48},{56,64},{72,80},{88,96},{104,112},{120,128}... | collective-permute-start | bytes 24584 | tf_op jit(solution)/shard_map/ppermute | solution.py:604
  (11 other events, 86.5 us)

commit v7 on v6

--- a/solution.py
+++ b/solution.py
@@ -20,7 +20,7 @@
 HEAD = ("zh", "zl", "x")
 SHARD = SEQ + BLK
 
-TILE = 512
+TILE = 1536
 SUB = 256
 CHUNK = 768
 NT = (((1,), (1,)), ((), ()))
@@ -78,9 +78,9 @@
             )
     items = [
         (r, b, c)
+        for r in range(subs)
         for b in range(n_kv)
         for c in range(kv_refs[b].shape[0] // CHUNK)
-        for r in range(subs)
     ]
     ones = jnp.ones((CHUNK, 128), jnp.bfloat16)
 
@@ -357,10 +357,13 @@
     return [out[f] for f in range(6)]
 
 
-def edge_rows_kernel(noisy_ref, cache_ref, mid_ref, tok_ref, down_ref, up_ref, cells):
+def edges_kernel(noisy_ref, cache_ref, mid_ref, tok_ref, *refs):
+    down_ref, up_ref, right_ref, left_ref = refs[:4]
+    corner_refs, cells, mids = refs[4:8], refs[8], refs[9]
     cells[...] = jnp.zeros(cells.shape, jnp.float32)
     cells[0:2, :, 0:12, 0:LAT] = cache_ref[...].astype(jnp.float32)
     cells[2:6, :, 0:12, 0:LAT] = noisy_ref[...]
+    mids[:, :, 0:12, :] = mid_ref[...].astype(jnp.float32)
     lane = lax.broadcasted_iota(jnp.int32, (8, 128), 1)
     tokens = {}
     for r in range(2):
@@ -374,28 +377,26 @@
             tokens[f, r] = token
     for ref, row, r in ((down_ref, 3, 1), (up_ref, 0, 0)):
         ref[...] = jnp.zeros(ref.shape, jnp.float32)
-        ref[:, 0:12, 0:C1] = mid_ref[:, row].astype(jnp.float32)
+        ref[:, 0:12, 0:C1] = mids[:, row, 0:12, :]
         put_frames(ref, 0, [tokens[f, r] for f in range(6)])
-
-
-def edge_cols_kernel(tok_ref, mid_ref, above_ref, below_ref, toks, mids, right_ref, left_ref):
-    above, below = get_frames(above_ref, 0, 8), get_frames(below_ref, 0, 8)
-    for f in range(6):
-        toks[f, 0] = above[f]
-        toks[f, 1] = tok_ref[f, 0]
-        toks[f, 2] = tok_ref[f, 1]
-        toks[f, 3] = below[f]
-    mids[...] = jnp.zeros(mids.shape, jnp.float32)
-    mids[:, 0, 0:12, :] = above_ref[:, 0:12, 0:C1]
-    mids[:, 1:5, 0:12, :] = mid_ref[...].astype(jnp.float32)
-    mids[:, 5, 0:12, :] = below_ref[:, 0:12, 0:C1]
     for ref, token, col in ((right_ref, 5, 11), (left_ref, 0, 0)):
         ref[...] = jnp.zeros(ref.shape, jnp.float32)
         for i in range(2):
-            for row in range(6):
+            for row in range(4):
                 ref[i, pl.ds(row, 1), 0:C1] = mids[i, row, pl.ds(col, 1), :]
-        for r in range(4):
-            put_rows(ref, r, [toks[f, r, pl.ds(token, 1), :] for f in range(6)])
+        for r in range(2):
+            put_rows(ref, r, [tok_ref[f, r, pl.ds(token, 1), :] for f in range(6)])
+    low = lax.broadcasted_iota(jnp.int32, (1, 128), 1) < 64
+    for ref, (row, r), (token, col) in zip(
+        corner_refs, ((3, 1), (3, 1), (0, 0), (0, 0)), ((5, 11), (0, 0), (5, 11), (0, 0))
+    ):
+        ref[...] = jnp.zeros(ref.shape, jnp.float32)
+        for i in range(2):
+            ref[pl.ds(i, 1), 0:C1] = mids[i, row, pl.ds(col, 1), :]
+        for f in range(4):
+            one = tok_ref[f, r, pl.ds(token, 1), :]
+            two = pltpu.roll(tok_ref[f % 2 + 4, r, pl.ds(token, 1), :], 64, axis=1)
+            ref[pl.ds(f, 1), 384:512] = jnp.where(low, one, two)
 
 
 def put_rows(ref, r, tokens):
@@ -407,21 +408,36 @@
             ref[i, pl.ds(4 * h + r, 1), 384:512] = jnp.where(low, one, two)
 
 
-def place_kernel(toks, mids, left_ref, right_ref, cells_ref, cache_ref):
+def place_kernel(tok_ref, mid_ref, *refs):
+    above_ref, below_ref, before_ref, after_ref = refs[:4]
+    corner_refs, cells_ref, cache_ref = refs[4:8], refs[8], refs[9]
     cells_ref[...] = jnp.zeros(cells_ref.shape, jnp.float32)
     cache_ref[...] = jnp.zeros(cache_ref.shape, jnp.float32)
     for f in range(6):
-        for r in range(4):
-            cells_ref[f, r, 1:7, :] = toks[f, r, 0:6, :]
-    cache_ref[:, :, 1:13, :] = mids[:, :, 0:12, :]
-    for ref, token, col in ((left_ref, 0, 0), (right_ref, 7, 13)):
+        for r in range(2):
+            cells_ref[f, r + 1, 1:7, :] = tok_ref[f, r, 0:6, :]
+    cache_ref[:, 1:5, 1:13, :] = mid_ref[...].astype(jnp.float32)
+    for ref, r, row in ((above_ref, 0, 0), (below_ref, 3, 5)):
+        frames = get_frames(ref, 0, 8)
+        for f in range(6):
+            cells_ref[f, r, 1:7, :] = frames[f][0:6]
+        cache_ref[:, row, 1:13, :] = ref[:, 0:12, 0:C1]
+    for ref, token, col in ((before_ref, 0, 0), (after_ref, 7, 13)):
         frames = get_frames(ref, 0, 4)
         for f in range(6):
-            for r in range(4):
-                cells_ref[f, r, pl.ds(token, 1), :] = frames[f][r : r + 1]
+            for r in range(2):
+                cells_ref[f, r + 1, pl.ds(token, 1), :] = frames[f][r : r + 1]
         for i in range(2):
-            for row in range(6):
-                cache_ref[i, row, pl.ds(col, 1), :] = ref[i, pl.ds(row, 1), 0:C1]
+            for row in range(4):
+                cache_ref[i, row + 1, pl.ds(col, 1), :] = ref[i, pl.ds(row, 1), 0:C1]
+    for ref, (r, row), (token, col) in zip(
+        corner_refs, ((0, 0), (0, 0), (3, 5), (3, 5)), ((0, 0), (7, 13), (0, 0), (7, 13))
+    ):
+        for i in range(2):
+            cache_ref[i, row, pl.ds(col, 1), :] = ref[pl.ds(i, 1), 0:C1]
+        for f in range(6):
+            both = ref[pl.ds(f % 4, 1), 384:512]
+            cells_ref[f, r, pl.ds(token, 1), :] = pltpu.roll(both, 64, axis=1) if f > 3 else both
 
 
 def small_call(kernel, shapes, scratch=()):
@@ -438,17 +454,28 @@
     return [(i, i + step) for i in range(count) if 0 <= i + step < count]
 
 
-def halo_rows(noisy, cache_in, cache_mid):
-    edge = (2, 16, 512)
-    toks, down, up = small_call(
-        edge_rows_kernel, [(6, 2, 8, 128), edge, edge], [(6, 4, 16, 128)]
+def input_borders(noisy, cache_in, cache_mid):
+    edge, side, corner = (2, 16, 512), (2, 8, 512), (8, 512)
+    toks, down, up, right, left, *corners = small_call(
+        edges_kernel,
+        [(6, 2, 8, 128), edge, edge, side, side] + [corner] * 4,
+        [(6, 4, 16, 128), (2, 4, 16, C1)],
     )(noisy, cache_in, cache_mid)
-    above = lax.ppermute(down, SEQ, along(SEQ, 1))
-    below = lax.ppermute(up, SEQ, along(SEQ, -1))
-    side = (2, 8, 512)
-    return small_call(edge_cols_kernel, [(6, 4, 8, 128), (2, 6, 16, C1), side, side])(
-        toks, cache_mid, above, below
-    )
+    around = [
+        lax.ppermute(down, SEQ, along(SEQ, 1)),
+        lax.ppermute(up, SEQ, along(SEQ, -1)),
+        lax.ppermute(right, BLK, along(BLK, 1)),
+        lax.ppermute(left, BLK, along(BLK, -1)),
+    ]
+    cols = lax.axis_size(BLK)
+    for part, (row, col) in zip(corners, ((1, 1), (1, -1), (-1, 1), (-1, -1))):
+        diagonal = [
+            (i * cols + j, m * cols + n)
+            for i, m in along(SEQ, row)
+            for j, n in along(BLK, col)
+        ]
+        around.append(lax.ppermute(part, SHARD, diagonal))
+    return small_call(place_kernel, [(6, 4, 8, 128), (2, 6, 16, C1)])(toks, cache_mid, *around)
 
 
 def pack_kernel(q_ref, k_ref, v_ref, out_ref):
@@ -462,12 +489,12 @@
 def pack(query_vectors, key_vectors, value_vectors):
     tokens, width = query_vectors.shape
     heads = width // HEAD_DIM
-    block = pl.BlockSpec((tokens, width // 2), lambda i: (0, i))
+    block = pl.BlockSpec((tokens, width), lambda i: (0, i))
     return pl.pallas_call(
         pack_kernel,
-        grid=(2,),
+        grid=(1,),
         in_specs=[block] * 3,
-        out_specs=pl.BlockSpec((heads // 2, tokens, 3 * HEAD_DIM), lambda i: (i, 0, 0)),
+        out_specs=pl.BlockSpec((heads, tokens, 3 * HEAD_DIM), lambda i: (i, 0, 0)),
         out_shape=jax.ShapeDtypeStruct((heads, tokens, 3 * HEAD_DIM), jnp.bfloat16),
     )(query_vectors, key_vectors, value_vectors)
 
@@ -532,7 +559,7 @@
     packed = pack(query_vectors, key_vectors, value_vectors)
     packed, inputs = lax.optimization_barrier((packed, inputs))
     noisy, cache_in, cache_mid, weight_in = inputs
-    rows = halo_rows(noisy, cache_in, cache_mid)
+    borders = input_borders(noisy, cache_in, cache_mid)
     weight_first = window_weights(weight_in)
     heads, tokens = packed.shape[:2]
     moved = lax.all_to_all(packed, HEAD, split_axis=0, concat_axis=0, tiled=True)
@@ -542,24 +569,18 @@
     left = [((i + 1) % 4, i) for i in range(4)]
     mid = moved.shape[0] // 2
     a, b, q_own = moved[:mid, :256], moved[mid:, :256], moved[:, 256:]
-    a, b, q_own, rows, weight_first = lax.optimization_barrier((a, b, q_own, rows, weight_first))
+    a, b, q_own, borders, weight_first = lax.optimization_barrier(
+        (a, b, q_own, borders, weight_first)
+    )
     left_a = lax.ppermute(a, "y", right)
     right_b = lax.ppermute(b, "y", left)
     q_oth = lax.ppermute(q_own, "core", swap)
     state = flash(moved, q_oth, [moved])
-    toks, mids, to_right, to_left = rows
-    state, a, b, to_right, to_left = lax.optimization_barrier((state, a, b, to_right, to_left))
+    state, a, b = lax.optimization_barrier((state, a, b))
     left_b = lax.ppermute(b, "y", right)
     right_a = lax.ppermute(a, "y", left)
-    before = lax.ppermute(to_right, BLK, along(BLK, 1))
-    after = lax.ppermute(to_left, BLK, along(BLK, -1))
     state = flash(moved, q_oth, [left_a, right_b], state)
-    state, left_a, right_b, before, after = lax.optimization_barrier(
-        (state, left_a, right_b, before, after)
-    )
-    borders = small_call(place_kernel, [(6, 4, 8, 128), (2, 6, 16, C1)])(
-        toks, mids, before, after
-    )
+    state, left_a, right_b = lax.optimization_barrier((state, left_a, right_b))
     far = [lax.ppermute(left_a, "y", right), lax.ppermute(right_b, "y", left)]
     state = flash(moved, q_oth, [left_b, right_a], state)
     weight = weight_head.T

time: 129 us -> 138 us (1.070)
  starting transfers between devices: 39 us -> 54.3 us
  Pallas kernels: 40.7 us -> 34.3 us
  blocking collectives: 19.4 us -> 24.6 us
  waiting for transfers between devices: 24.6 us -> 19.8 us
    ppermute x4 -> x8, starting transfers between devices: 11.5 us -> 24.4 us  [the longest x4 12.3 us: input_borders(): around.append(lax.ppermute(part, SHARD, diagonal))]
    ppermute x4 -> x8, waiting for transfers between devices: 20.7 us -> 13.7 us  [the longest x4 13.7 us: input_borders(): around.append(lax.ppermute(part, SHARD, diagonal))]
    all_to_all x1, blocking collectives: 19.4 us -> 24.6 us  [attention(): lax.all_to_all(partial, HEAD, split_axis=0, concat_axis=0, tiled=True)]
    pallas_call x3, Pallas kernels: 23.2 us -> 18.7 us  [flash(): pl.pallas_call(functools.partial(flash_kernel, state is None, False, len(...]
    ppermute x1, starting transfers between devices: 1.72 us -> 4.31 us  [attention(): right_b = lax.ppermute(b, 'y', left)]
    ppermute x1, waiting for transfers between devices: 0.01 us -> 2.58 us  [attention(): left_a = lax.ppermute(a, 'y', right)]
    pallas_call x2, Pallas kernels: 8.57 us -> 6.46 us  [flash_last(): pl.pallas_call(functools.partial(flash_kernel, False, True, len(kvs), hal...]
    ppermute x1, starting transfers between devices: 1.65 us -> 0.09 us  [attention(): q_oth = lax.ppermute(q_own, 'core', swap)]
  transfers between devices with their start and end apart: 15 -> 19, of which waited for: 5 -> 5; matrix products, arithmetic and copies ran while one was open for 0% -> 0% of each run, Pallas kernels for 22% -> 16%
where the time goes in v7:
time: 138 us; the launch traced here: 137 us
  starting transfers between devices  54.3 us (39%)
  Pallas kernels  34.3 us (25%)
  blocking collectives  24.6 us (18%)
  waiting for transfers between devices  19.8 us (14%)
  local copies, waits for them, and re-layouts  2.5 us (2%)
  between operations  1.7 us (1%)
    all_to_all x1, blocking collectives, attention(): lax.all_to_all(partial, HEAD, split_axis=0, concat_axis=0, tiled=True)  24.6 us
    pallas_call x3, Pallas kernels, flash(): pl.pallas_call(functools.partial(flash_kernel, state is None, False, len(...  18.7 us
    ppermute x4, waiting for transfers between devices, input_borders(): around.append(lax.ppermute(part, SHARD, diagonal))  13.7 us
    ppermute x4, starting transfers between devices, input_borders(): around.append(lax.ppermute(part, SHARD, diagonal))  12.3 us
    all_to_all x1, starting transfers between devices, attention(): lax.all_to_all(packed, HEAD, split_axis=0, concat_axis=0, tiled=True)  11.9 us
    pallas_call x2, Pallas kernels, flash_last(): pl.pallas_call(functools.partial(flash_kernel, False, True, len(kvs), hal...  6.46 us
    ppermute x1, starting transfers between devices, input_borders(): lax.ppermute(down, SEQ, along(SEQ, 1))  5.16 us
    pallas_call x1, Pallas kernels, tail(): pl.pallas_call(tail_kernel, in_specs=specs, out_specs=[pl.BlockSpec(memor...  4.77 us
  transfers between devices with their start and end apart: 19, of which 5 were waited for; matrix products, arithmetic and copies ran while one was open for 0% of the time, Pallas kernels for 16%

profile of v7, /device:TPU:1, one launch (start us, length us, event | category | flops | bytes accessed | tf_op | source)
XLA Modules:
  0.0 137.2 jit_solution(4508054292336449064)
XLA Ops:
  0.7 2.5 %shard_map.158 = bf16[32,48,384]{2,1,0:T(8,128)(2,1)} custom-call(bf16[48,4096]{1,0:T(8,128)(2,1)} %q_ref.1, bf16[48,4096]{1,0:T(8,128)(2,1)} %k_ref.1, bf16[48,4096]{1,0:T(8,128)(2,1)} %v_ref.1), custom_call_target="tpu_custom_call" | custom-call | tf_op jit(solution)/shard_map/pallas_call | solution.py:493
  3.2 11.9 %all-to-all-start = ((bf16[32,48,384]{2,1,0:T(8,128)(2,1)}), bf16[32,48,384]{2,1,0:T(8,128)(2,1)S(1)}, u32[]{:S(2)}, u32[]{:S(2)}) async-start(bf16[32,48,384]{2,1,0:T(8,128)(2,1)} %shard_map.158), calls=%async_computation | async-start | bytes 2359296 | tf_op jit(solution)/shard_map/all_to_all | solution.py:565
  15.4 5.2 %collective-permute-start = (f32[2,16,512]{2,1,0:T(8,128)S(1)}, f32[2,16,512]{2,1,0:T(8,128)S(1)}, u32[]{:S(2)}, u32[]{:S(2)}) collective-permute-start(f32[2,16,512]{2,1,0:T(8,128)S(1)} %get-tuple-element.42), channel_id=1, source_target_pairs={{0,8},{8,16},{16,24},{24,32},{32,40},{40,48},{48,56},{56,64},{64,7... | collective-permute-start | bytes 196616 | tf_op jit(solution)/shard_map/ppermute | solution.py:465
  20.5 1.9 %collective-permute-start.1 = (f32[2,16,512]{2,1,0:T(8,128)S(1)}, f32[2,16,512]{2,1,0:T(8,128)S(1)}, u32[]{:S(2)}, u32[]{:S(2)}) collective-permute-start(f32[2,16,512]{2,1,0:T(8,128)S(1)} %get-tuple-element.43), channel_id=1, source_target_pairs={{8,0},{16,8},{24,16},{32,24},{40,32},{48,40},{56,48},{64,56},{72,6... | collective-permute-start | bytes 196616 | tf_op jit(solution)/shard_map/ppermute | solution.py:466
  22.5 5.4 %collective-permute-start.4 = (f32[8,512]{1,0:T(8,128)S(1)}, f32[8,512]{1,0:T(8,128)S(1)}, u32[]{:S(2)}, u32[]{:S(2)}) collective-permute-start(f32[8,512]{1,0:T(8,128)S(1)} %get-tuple-element.46), channel_id=1, source_target_pairs={{0,9},{1,10},{2,11},{3,12},{4,13},{5,14},{6,15},{8,17},{9,18},{10,... | collective-permute-start | bytes 49160 | tf_op jit(solution)/shard_map/ppermute | solution.py:477
  29.2 4.3 %collective-permute-start.6 = (f32[8,512]{1,0:T(8,128)S(1)}, f32[8,512]{1,0:T(8,128)S(1)}, u32[]{:S(2)}, u32[]{:S(2)}) collective-permute-start(f32[8,512]{1,0:T(8,128)S(1)} %get-tuple-element.48), channel_id=1, source_target_pairs={{8,1},{9,2},{10,3},{11,4},{12,5},{13,6},{14,7},{16,9},{17,10},{18,... | collective-permute-start | bytes 49160 | tf_op jit(solution)/shard_map/ppermute | solution.py:477
  33.5 6.2 %collective-permute-done.4.refs_4_ = f32[8,512]{1,0:T(8,128)S(1)} collective-permute-done((f32[8,512]{1,0:T(8,128)S(1)}, f32[8,512]{1,0:T(8,128)S(1)}, u32[]{:S(2)}, u32[]{:S(2)}) %collective-permute-start.4) | collective-permute-done | bytes 16416 | tf_op jit(solution)/shard_map/ppermute | solution.py:477
  39.7 3.8 %collective-permute-start.2 = (f32[2,8,512]{2,1,0:T(8,128)S(1)}, f32[2,8,512]{2,1,0:T(8,128)S(1)}, u32[]{:S(2)}, u32[]{:S(2)}) collective-permute-start(f32[2,8,512]{2,1,0:T(8,128)S(1)} %get-tuple-element.44), channel_id=1, source_target_pairs={{0,1},{1,2},{2,3},{3,4},{4,5},{5,6},{6,7},{8,9},{9,10},{10,11},{11... | collective-permute-start | bytes 98312 | tf_op jit(solution)/shard_map/ppermute | solution.py:467
  47.3 7.5 %collective-permute-done.7.refs_7_ = f32[8,512]{1,0:T(8,128)S(1)} collective-permute-done((f32[8,512]{1,0:T(8,128)S(1)}, f32[8,512]{1,0:T(8,128)S(1)}, u32[]{:S(2)}, u32[]{:S(2)}) %collective-permute-start.7) | collective-permute-done | bytes 16416 | tf_op jit(solution)/shard_map/ppermute | solution.py:477
  56.5 4.3 %collective-permute-start.10 = (bf16[768,256]{1,0:T(8,128)(2,1)S(1)}, bf16[768,256]{1,0:T(8,128)(2,1)S(1)}, u32[]{:S(2)}, u32[]{:S(2)}) collective-permute-start(bf16[768,256]{1,0:T(8,128)(2,1)S(1)} %get-tuple-element.59), channel_id=1, source_target_pairs={{64,0},{128,64},{192,128},{0,192},{65,1},{129,65},{193,129},{1,193... | collective-permute-start | bytes 1179656 | tf_op jit(solution)/shard_map/ppermute | solution.py:576
  60.8 6.1 %shard_map.162.refs_4_ = f32[3072,256]{1,0:T(8,128)S(1)} custom-call(bf16[1536,384]{1,0:T(8,128)(2,1)S(1)} %bitcast.11, bf16[1536,128]{1,0:T(8,128)(2,1)S(1)} %collective-permute-done.8.refs_1_.refs_0_, bf16[1536,384]{1,0:T(8,128)(2,1)S(1)} %bitcast.12), custom_call_target="tpu_custom_call" | custom-call | flops 4831838208 | bytes 6291456 | tf_op jit(solution)/shard_map/pallas_call | solution.py:135
  67.0 2.8 %collective-permute-start.14 = (bf16[768,256]{1,0:T(8,128)(2,1)S(1)}, bf16[768,256]{1,0:T(8,128)(2,1)S(1)}, u32[]{:S(2)}, u32[]{:S(2)}) collective-permute-start(bf16[768,256]{1,0:T(8,128)(2,1)S(1)} %get-tuple-element.60), channel_id=1, source_target_pairs={{64,0},{128,64},{192,128},{0,192},{65,1},{129,65},{193,129},{1,193... | collective-permute-start | bytes 1179656 | tf_op jit(solution)/shard_map/ppermute | solution.py:581
  69.8 2.6 %collective-permute-done.9.refs_2_ = bf16[768,256]{1,0:T(8,128)(2,1)S(1)} collective-permute-done((bf16[768,256]{1,0:T(8,128)(2,1)S(1)}, bf16[768,256]{1,0:T(8,128)(2,1)S(1)}, u32[]{:S(2)}, u32[]{:S(2)}) %collective-permute-start.9) | collective-permute-done | bytes 393248 | tf_op jit(solution)/shard_map/ppermute | solution.py:575
  72.4 6.3 %shard_map.163.refs_4_ = f32[3072,256]{1,0:T(8,128)S(1)} custom-call(bf16[1536,384]{1,0:T(8,128)(2,1)S(1)} %bitcast.13, bf16[1536,128]{1,0:T(8,128)(2,1)S(1)} %collective-permute-done.8.refs_1_.refs_0_, bf16[768,256]{1,0:T(8,128)(2,1)S(1)} %collective-permute-done.9.refs_2_, bf16[768,256]{1,0:T(8,128)(2,1)S(1)} %collective-permute-done.10.refs_3_, ...), custom_call_target="tpu_custom_call" | custom-call | flops 4831838208 | bytes 6291456 | tf_op jit(solution)/shard_map/pallas_call | solution.py:135
  79.0 2.7 %collective-permute-start.12 = (bf16[768,256]{1,0:T(8,128)(2,1)S(1)}, bf16[768,256]{1,0:T(8,128)(2,1)S(1)}, u32[]{:S(2)}, u32[]{:S(2)}) collective-permute-start(bf16[768,256]{1,0:T(8,128)(2,1)S(1)} %collective-permute-done.10.refs_3_), channel_id=1, source_target_pairs={{64,0},{128,64},{192,128},{0,192},{65,1},{129,65},{193,129},{1,193... | collective-permute-start | bytes 1179656 | tf_op jit(solution)/shard_map/ppermute | solution.py:584
  81.6 6.3 %shard_map.164.refs_3_ = f32[3072,256]{1,0:T(8,128)S(1)} custom-call(bf16[1536,384]{1,0:T(8,128)(2,1)S(1)} %bitcast.14, bf16[1536,128]{1,0:T(8,128)(2,1)S(1)} %collective-permute-done.8.refs_1_.refs_0_, bf16[768,256]{1,0:T(8,128)(2,1)S(1)} %collective-permute-done.13.refs_2_, bf16[768,256]{1,0:T(8,128)(2,1)S(1)} %collective-permute-done.14.refs_3_, ...), custom_call_target="tpu_custom_call" | custom-call | flops 4831838208 | bytes 6291456 | tf_op jit(solution)/shard_map/pallas_call | solution.py:135
  88.8 3.2 %shard_map.165 = f32[1536,128]{1,0:T(8,128)S(1)} custom-call(bf16[1536,128]{1,0:T(8,128)(2,1)S(1)} %collective-permute-done.8.refs_1_.refs_0_, bf16[768,256]{1,0:T(8,128)(2,1)S(1)} %collective-permute-done.11.refs_1_, bf16[768,256]{1,0:T(8,128)(2,1)S(1)} %collective-permute-done.12.refs_2_, f32[3072,256]{1,0:T(8,128)S(1)} %shard_map.164.refs_3_, ...), custom_call_target="tpu_custom_call" | custom-call | flops 2415919104 | bytes 3145728 | tf_op jit(solution)/shard_map/pallas_call | solution.py:156
  92.1 3.2 %collective-permute-start.15 = (f32[1536,128]{1,0:T(8,128)S(1)}, f32[1536,128]{1,0:T(8,128)S(1)}, u32[]{:S(2)}, u32[]{:S(2)}) collective-permute-start(f32[1536,128]{1,0:T(8,128)S(1)} %shard_map.165), channel_id=1, source_target_pairs={{0,8},{8,0},{1,9},{9,1},{2,10},{10,2},{3,11},{11,3},{4,12},{12,4},... | collective-permute-start | bytes 2359304 | tf_op jit(solution)/shard_map/ppermute | solution.py:589
  95.4 3.2 %shard_map.166.own_ref = f32[1536,128]{1,0:T(8,128)S(1)} custom-call(bf16[1536,384]{1,0:T(8,128)(2,1)S(1)} %bitcast.15, bf16[768,256]{1,0:T(8,128)(2,1)S(1)} %collective-permute-done.11.refs_1_, bf16[768,256]{1,0:T(8,128)(2,1)S(1)} %collective-permute-done.12.refs_2_, f32[3072,256]{1,0:T(8,128)S(1)} %shard_map.164.refs_3_, bf16[64,4096]{1,0:T(8,128)(2,1)S(1)} %bitcast.18), custom_call_target="tpu_custom_call" | custom-call | flops 2415919104 | bytes 3145728 | tf_op jit(solution)/shard_map/pallas_call | solution.py:156
  99.8 24.6 %all_to_all.10.parts_ref = bf16[32,32,128]{2,1,0:T(8,128)(2,1)S(1)} all-to-all(bf16[32,32,128]{2,1,0:T(8,128)(2,1)S(1)} %bitcast.16), channel_id=1, replica_groups=mesh['y'=4,'zh'=4,'core'=2,'zl'=2,'x'=4] {'zh','zl','x'}, dimensions={0} | all-to-all | bytes 524288 | tf_op jit(solution)/shard_map/all_to_all | solution.py:592
  124.4 2.1 %collective-permute-start.16 = (f32[16,128]{1,0:T(8,128)S(1)}, f32[16,128]{1,0:T(8,128)S(1)}, u32[]{:S(2)}, u32[]{:S(2)}) collective-permute-start(f32[16,128]{1,0:T(8,128)S(1)} %get-tuple-element.64), channel_id=1, source_target_pairs={{0,8},{8,0},{16,24},{24,16},{32,40},{40,32},{48,56},{56,48},{64,72... | collective-permute-start | bytes 24584 | tf_op jit(solution)/shard_map/ppermute | solution.py:622
  126.5 2.6 %collective-permute-start.17 = (f32[16,128]{1,0:T(8,128)S(1)}, f32[16,128]{1,0:T(8,128)S(1)}, u32[]{:S(2)}, u32[]{:S(2)}) collective-permute-start(f32[16,128]{1,0:T(8,128)S(1)} %get-tuple-element.66), channel_id=1, source_target_pairs={{8,16},{24,32},{40,48},{56,64},{72,80},{88,96},{104,112},{120,128}... | collective-permute-start | bytes 24584 | tf_op jit(solution)/shard_map/ppermute | solution.py:625
  129.7 2.6 %collective-permute-done.17.apart_ref = f32[16,128]{1,0:T(8,128)S(1)} collective-permute-done((f32[16,128]{1,0:T(8,128)S(1)}, f32[16,128]{1,0:T(8,128)S(1)}, u32[]{:S(2)}, u32[]{:S(2)}) %collective-permute-start.17) | collective-permute-done | bytes 8224 | tf_op jit(solution)/shard_map/ppermute | solution.py:625
  132.4 4.8 %shard_map.169 = (f32[4,12,4,16]{3,2,1,0:T(4,128)}, bf16[4,12,4,384]{3,2,1,0:T(4,128)(2,1)}) custom-call(f32[16,128]{1,0:T(8,128)S(1)} %collective-permute-done.16.near_ref, f32[32,128]{1,0:T(8,128)S(1)} %get-tuple-element.65.mine_ref, f32[16,128]{1,0:T(8,128)S(1)} %collective-permute-done.17.apart_ref, f32[6,4,8,128]{3,2,1,0:T(8,128)S(1)} %copy-done.4, ...), custom_call_target="tpu_custom_call" | custom-call | tf_op jit(solution)/shard_map/pallas_call | solution.py:296
  (65 shorter events, 9.5 us)
Async XLA Ops:
  3.2 53.1 %all-to-all-start = ((bf16[32,48,384]{2,1,0:T(8,128)(2,1)}), bf16[32,48,384]{2,1,0:T(8,128)(2,1)S(1)}, u32[]{:S(2)}, u32[]{:S(2)}) async-start(bf16[32,48,384]{2,1,0:T(8,128)(2,1)} %shard_map.158), calls=%async_computation | async-start | bytes 2359296 | tf_op jit(solution)/shard_map/all_to_all | solution.py:565
  15.4 39.4 %collective-permute-start = (f32[2,16,512]{2,1,0:T(8,128)S(1)}, f32[2,16,512]{2,1,0:T(8,128)S(1)}, u32[]{:S(2)}, u32[]{:S(2)}) collective-permute-start(f32[2,16,512]{2,1,0:T(8,128)S(1)} %get-tuple-element.42), channel_id=1, source_target_pairs={{0,8},{8,16},{16,24},{24,32},{32,40},{40,48},{48,56},{56,64},{64,7... | collective-permute-start | bytes 196616 | tf_op jit(solution)/shard_map/ppermute | solution.py:465
  20.5 34.3 %collective-permute-start.1 = (f32[2,16,512]{2,1,0:T(8,128)S(1)}, f32[2,16,512]{2,1,0:T(8,128)S(1)}, u32[]{:S(2)}, u32[]{:S(2)}) collective-permute-start(f32[2,16,512]{2,1,0:T(8,128)S(1)} %get-tuple-element.43), channel_id=1, source_target_pairs={{8,0},{16,8},{24,16},{32,24},{40,32},{48,40},{56,48},{64,56},{72,6... | collective-permute-start | bytes 196616 | tf_op jit(solution)/shard_map/ppermute | solution.py:466
  22.5 17.3 %collective-permute-start.4 = (f32[8,512]{1,0:T(8,128)S(1)}, f32[8,512]{1,0:T(8,128)S(1)}, u32[]{:S(2)}, u32[]{:S(2)}) collective-permute-start(f32[8,512]{1,0:T(8,128)S(1)} %get-tuple-element.46), channel_id=1, source_target_pairs={{0,9},{1,10},{2,11},{3,12},{4,13},{5,14},{6,15},{8,17},{9,18},{10,... | collective-permute-start | bytes 49160 | tf_op jit(solution)/shard_map/ppermute | solution.py:477
  27.9 15.6 %collective-permute-start.5 = (f32[8,512]{1,0:T(8,128)S(1)}, f32[8,512]{1,0:T(8,128)S(1)}, u32[]{:S(2)}, u32[]{:S(2)}) collective-permute-start(f32[8,512]{1,0:T(8,128)S(1)} %get-tuple-element.47), channel_id=1, source_target_pairs={{1,8},{2,9},{3,10},{4,11},{5,12},{6,13},{7,14},{9,16},{10,17},{11,... | collective-permute-start | bytes 49160 | tf_op jit(solution)/shard_map/ppermute | solution.py:477
  29.2 15.6 %collective-permute-start.6 = (f32[8,512]{1,0:T(8,128)S(1)}, f32[8,512]{1,0:T(8,128)S(1)}, u32[]{:S(2)}, u32[]{:S(2)}) collective-permute-start(f32[8,512]{1,0:T(8,128)S(1)} %get-tuple-element.48), channel_id=1, source_target_pairs={{8,1},{9,2},{10,3},{11,4},{12,5},{13,6},{14,7},{16,9},{17,10},{18,... | collective-permute-start | bytes 49160 | tf_op jit(solution)/shard_map/ppermute | solution.py:477
  39.7 15.1 %collective-permute-start.2 = (f32[2,8,512]{2,1,0:T(8,128)S(1)}, f32[2,8,512]{2,1,0:T(8,128)S(1)}, u32[]{:S(2)}, u32[]{:S(2)}) collective-permute-start(f32[2,8,512]{2,1,0:T(8,128)S(1)} %get-tuple-element.44), channel_id=1, source_target_pairs={{0,1},{1,2},{2,3},{3,4},{4,5},{5,6},{6,7},{8,9},{9,10},{10,11},{11... | collective-permute-start | bytes 98312 | tf_op jit(solution)/shard_map/ppermute | solution.py:467
  43.5 11.3 %collective-permute-start.3 = (f32[2,8,512]{2,1,0:T(8,128)S(1)}, f32[2,8,512]{2,1,0:T(8,128)S(1)}, u32[]{:S(2)}, u32[]{:S(2)}) collective-permute-start(f32[2,8,512]{2,1,0:T(8,128)S(1)} %get-tuple-element.45), channel_id=1, source_target_pairs={{1,0},{2,1},{3,2},{4,3},{5,4},{6,5},{7,6},{9,8},{10,9},{11,10},{12... | collective-permute-start | bytes 98312 | tf_op jit(solution)/shard_map/ppermute | solution.py:468
  44.8 10.0 %collective-permute-start.7 = (f32[8,512]{1,0:T(8,128)S(1)}, f32[8,512]{1,0:T(8,128)S(1)}, u32[]{:S(2)}, u32[]{:S(2)}) collective-permute-start(f32[8,512]{1,0:T(8,128)S(1)} %get-tuple-element.49), channel_id=1, source_target_pairs={{9,0},{10,1},{11,2},{12,3},{13,4},{14,5},{15,6},{17,8},{18,9},{19,... | collective-permute-start | bytes 49160 | tf_op jit(solution)/shard_map/ppermute | solution.py:477
  56.4 4.4 %collective-permute-start.8 = (bf16[1536,128]{1,0:T(8,128)(2,1)S(1)}, bf16[1536,128]{1,0:T(8,128)(2,1)S(1)}, u32[]{:S(2)}, u32[]{:S(2)}) collective-permute-start(bf16[1536,128]{1,0:T(8,128)(2,1)S(1)} %slice.14), channel_id=1, source_target_pairs={{0,8},{8,0},{1,9},{9,1},{2,10},{10,2},{3,11},{11,3},{4,12},{12,4},... | collective-permute-start | bytes 1179656 | tf_op jit(solution)/shard_map/ppermute | solution.py:577
  56.5 13.3 %collective-permute-start.10 = (bf16[768,256]{1,0:T(8,128)(2,1)S(1)}, bf16[768,256]{1,0:T(8,128)(2,1)S(1)}, u32[]{:S(2)}, u32[]{:S(2)}) collective-permute-start(bf16[768,256]{1,0:T(8,128)(2,1)S(1)} %get-tuple-element.59), channel_id=1, source_target_pairs={{64,0},{128,64},{192,128},{0,192},{65,1},{129,65},{193,129},{1,193... | collective-permute-start | bytes 1179656 | tf_op jit(solution)/shard_map/ppermute | solution.py:576
  60.8 11.6 %collective-permute-start.9 = (bf16[768,256]{1,0:T(8,128)(2,1)S(1)}, bf16[768,256]{1,0:T(8,128)(2,1)S(1)}, u32[]{:S(2)}, u32[]{:S(2)}) collective-permute-start(bf16[768,256]{1,0:T(8,128)(2,1)S(1)} %get-tuple-element.60), channel_id=1, source_target_pairs={{0,64},{64,128},{128,192},{192,0},{1,65},{65,129},{129,193},{193,1... | collective-permute-start | bytes 1179656 | tf_op jit(solution)/shard_map/ppermute | solution.py:575
  66.9 14.7 %collective-permute-start.13 = (bf16[768,256]{1,0:T(8,128)(2,1)S(1)}, bf16[768,256]{1,0:T(8,128)(2,1)S(1)}, u32[]{:S(2)}, u32[]{:S(2)}) collective-permute-start(bf16[768,256]{1,0:T(8,128)(2,1)S(1)} %get-tuple-element.59), channel_id=1, source_target_pairs={{0,64},{64,128},{128,192},{192,0},{1,65},{65,129},{129,193},{193,1... | collective-permute-start | bytes 1179656 | tf_op jit(solution)/shard_map/ppermute | solution.py:580
  67.0 14.6 %collective-permute-start.14 = (bf16[768,256]{1,0:T(8,128)(2,1)S(1)}, bf16[768,256]{1,0:T(8,128)(2,1)S(1)}, u32[]{:S(2)}, u32[]{:S(2)}) collective-permute-start(bf16[768,256]{1,0:T(8,128)(2,1)S(1)} %get-tuple-element.60), channel_id=1, source_target_pairs={{64,0},{128,64},{192,128},{0,192},{65,1},{129,65},{193,129},{1,193... | collective-permute-start | bytes 1179656 | tf_op jit(solution)/shard_map/ppermute | solution.py:581
  78.7 10.1 %collective-permute-start.11 = (bf16[768,256]{1,0:T(8,128)(2,1)S(1)}, bf16[768,256]{1,0:T(8,128)(2,1)S(1)}, u32[]{:S(2)}, u32[]{:S(2)}) collective-permute-start(bf16[768,256]{1,0:T(8,128)(2,1)S(1)} %collective-permute-done.9.refs_2_), channel_id=1, source_target_pairs={{0,64},{64,128},{128,192},{192,0},{1,65},{65,129},{129,193},{193,1... | collective-permute-start | bytes 1179656 | tf_op jit(solution)/shard_map/ppermute | solution.py:584
  79.0 9.8 %collective-permute-start.12 = (bf16[768,256]{1,0:T(8,128)(2,1)S(1)}, bf16[768,256]{1,0:T(8,128)(2,1)S(1)}, u32[]{:S(2)}, u32[]{:S(2)}) collective-permute-start(bf16[768,256]{1,0:T(8,128)(2,1)S(1)} %collective-permute-done.10.refs_3_), channel_id=1, source_target_pairs={{64,0},{128,64},{192,128},{0,192},{65,1},{129,65},{193,129},{1,193... | collective-permute-start | bytes 1179656 | tf_op jit(solution)/shard_map/ppermute | solution.py:584
  88.8 43.6 %slice-start = ((s8[7962624]{0:T(1024)(128)(4,1)}), s8[4194304]{0:T(1024)(128)(4,1)S(1)}, s32[]{:S(2)}) async-start(s8[7962624]{0:T(1024)(128)(4,1)} %bitcast.6), calls=%async_computation.2 | async-start | bytes 8388608
  92.1 40.3 %slice-start.1 = ((s8[7962624]{0:T(1024)(128)(4,1)}), s8[3768320]{0:T(1024)(128)(4,1)S(1)}, s32[]{:S(2)}) async-start(s8[7962624]{0:T(1024)(128)(4,1)} %bitcast.6), calls=%async_computation.3 | async-start | bytes 7536640
  92.1 40.3 %copy-start.2 = (f32[2,6,16,384]{3,2,1,0:T(8,128)S(1)}, f32[2,6,16,384]{3,2,1,0:T(8,128)}, u32[]{:S(2)}) copy-start(f32[2,6,16,384]{3,2,1,0:T(8,128)} %copy-done.1) | copy-start | bytes 884740
  92.1 40.3 %copy-start.4 = (f32[6,4,8,128]{3,2,1,0:T(8,128)S(1)}, f32[6,4,8,128]{3,2,1,0:T(8,128)}, u32[]{:S(2)}) copy-start(f32[6,4,8,128]{3,2,1,0:T(8,128)} %copy-done.3) | copy-start | bytes 294916
  92.1 40.3 %copy-start.5 = (f32[384]{0:T(512)S(1)}, f32[384]{0:T(512)}, u32[]{:S(2)}) copy-start(f32[384]{0:T(512)} %b1_ref.1) | copy-start | bytes 4612
  92.1 6.4 %collective-permute-start.15 = (f32[1536,128]{1,0:T(8,128)S(1)}, f32[1536,128]{1,0:T(8,128)S(1)}, u32[]{:S(2)}, u32[]{:S(2)}) collective-permute-start(f32[1536,128]{1,0:T(8,128)S(1)} %shard_map.165), channel_id=1, source_target_pairs={{0,8},{8,0},{1,9},{9,1},{2,10},{10,2},{3,11},{11,3},{4,12},{12,4},... | collective-permute-start | bytes 2359304 | tf_op jit(solution)/shard_map/ppermute | solution.py:589
  124.4 5.3 %collective-permute-start.16 = (f32[16,128]{1,0:T(8,128)S(1)}, f32[16,128]{1,0:T(8,128)S(1)}, u32[]{:S(2)}, u32[]{:S(2)}) collective-permute-start(f32[16,128]{1,0:T(8,128)S(1)} %get-tuple-element.64), channel_id=1, source_target_pairs={{0,8},{8,0},{16,24},{24,16},{32,40},{40,32},{48,56},{56,48},{64,72... | collective-permute-start | bytes 24584 | tf_op jit(solution)/shard_map/ppermute | solution.py:622
  126.5 5.9 %collective-permute-start.17 = (f32[16,128]{1,0:T(8,128)S(1)}, f32[16,128]{1,0:T(8,128)S(1)}, u32[]{:S(2)}, u32[]{:S(2)}) collective-permute-start(f32[16,128]{1,0:T(8,128)S(1)} %get-tuple-element.66), channel_id=1, source_target_pairs={{8,16},{24,32},{40,48},{56,64},{72,80},{88,96},{104,112},{120,128}... | collective-permute-start | bytes 24584 | tf_op jit(solution)/shard_map/ppermute | solution.py:625
  (11 other events, 217.0 us)

commit v8 on v6

--- a/solution.py
+++ b/solution.py
@@ -20,7 +20,7 @@
 HEAD = ("zh", "zl", "x")
 SHARD = SEQ + BLK
 
-TILE = 512
+TILE = 1536
 SUB = 256
 CHUNK = 768
 NT = (((1,), (1,)), ((), ()))
@@ -78,9 +78,9 @@
             )
     items = [
         (r, b, c)
+        for r in range(subs)
         for b in range(n_kv)
         for c in range(kv_refs[b].shape[0] // CHUNK)
-        for r in range(subs)
     ]
     ones = jnp.ones((CHUNK, 128), jnp.bfloat16)
 
@@ -548,15 +548,13 @@
     q_oth = lax.ppermute(q_own, "core", swap)
     state = flash(moved, q_oth, [moved])
     toks, mids, to_right, to_left = rows
-    state, a, b, to_right, to_left = lax.optimization_barrier((state, a, b, to_right, to_left))
+    state, a, b, to_right = lax.optimization_barrier((state, a, b, to_right))
     left_b = lax.ppermute(b, "y", right)
     right_a = lax.ppermute(a, "y", left)
     before = lax.ppermute(to_right, BLK, along(BLK, 1))
+    state = flash(moved, q_oth, [left_a, right_b], state)
+    state, left_a, right_b, to_left = lax.optimization_barrier((state, left_a, right_b, to_left))
     after = lax.ppermute(to_left, BLK, along(BLK, -1))
-    state = flash(moved, q_oth, [left_a, right_b], state)
-    state, left_a, right_b, before, after = lax.optimization_barrier(
-        (state, left_a, right_b, before, after)
-    )
     borders = small_call(place_kernel, [(6, 4, 8, 128), (2, 6, 16, C1)])(
         toks, mids, before, after
     )

time: 129 us -> 126 us (0.977); the launches traced: 129 us -> 124 us
  blocking collectives: 19.4 us -> 0 us
  starting transfers between devices: 39 us -> 47.8 us
  waiting for transfers between devices: 24.6 us -> 30.7 us
  Pallas kernels: 40.7 us -> 34.9 us
  local copies, waits for them, and re-layouts: 3.72 us -> 9.45 us
    all_to_all x1 -> x0, blocking collectives: 19.4 us -> none  [attention(): lax.all_to_all(partial, HEAD, split_axis=0, concat_axis=0, tiled=True)]
    all_to_all x0 -> x1, waiting for transfers between devices: none -> 6.7 us  [attention(): lax.all_to_all(partial, HEAD, split_axis=0, concat_axis=0, tiled=True)]
    all_to_all x0 -> x1, starting transfers between devices: none -> 6.56 us  [attention(): lax.all_to_all(partial, HEAD, split_axis=0, concat_axis=0, tiled=True)]
    unnamed x40 -> x34, local copies, waits for them, and re-layouts: 3.6 us -> 9.34 us
    pallas_call x3, Pallas kernels: 23.2 us -> 18.7 us  [flash(): pl.pallas_call(functools.partial(flash_kernel, state is None, False, len(...]
    pallas_call x2, Pallas kernels: 8.57 us -> 6.46 us  [flash_last(): pl.pallas_call(functools.partial(flash_kernel, False, True, len(kvs), hal...]
    ppermute x1, waiting for transfers between devices: 2.52 us -> 0.66 us  [shards(): apart = lax.ppermute(apart, SEQ, pairs)]
  transfers between devices with their start and end apart: 15 -> 16, of which waited for: 5 -> 6; matrix products, arithmetic and copies ran while one was open for 0% -> 0% of each run, Pallas kernels for 22% -> 18%
where the time goes in v8:
time: 126 us; the launch traced here: 124 us
  starting transfers between devices  47.8 us (38%)
  Pallas kernels  34.9 us (28%)
  waiting for transfers between devices  30.7 us (24%)
  local copies, waits for them, and re-layouts  9.45 us (7%)
  between operations  1.59 us (1%)
    pallas_call x3, Pallas kernels, flash(): pl.pallas_call(functools.partial(flash_kernel, state is None, False, len(...  18.7 us
    ppermute x1, waiting for transfers between devices, halo_rows(): above = lax.ppermute(down, SEQ, along(SEQ, 1))  15.1 us
    all_to_all x1, starting transfers between devices, attention(): lax.all_to_all(packed, HEAD, split_axis=0, concat_axis=0, tiled=True)  11.9 us
    unnamed x34, local copies, waits for them, and re-layouts  9.34 us
    all_to_all x1, waiting for transfers between devices, attention(): lax.all_to_all(partial, HEAD, split_axis=0, concat_axis=0, tiled=True)  6.7 us
    all_to_all x1, starting transfers between devices, attention(): lax.all_to_all(partial, HEAD, split_axis=0, concat_axis=0, tiled=True)  6.56 us
    pallas_call x2, Pallas kernels, flash_last(): pl.pallas_call(functools.partial(flash_kernel, False, True, len(kvs), hal...  6.46 us
    ppermute x1, waiting for transfers between devices, halo_rows(): below = lax.ppermute(up, SEQ, along(SEQ, -1))  5.63 us
  transfers between devices with their start and end apart: 16, of which 6 were waited for; matrix products, arithmetic and copies ran while one was open for 0% of the time, Pallas kernels for 18%

profile of v8, /device:TPU:1, one launch (start us, length us, event | category | flops | bytes accessed | tf_op | source)
XLA Modules:
  0.0 124.4 jit_solution(7413921218397151257)
XLA Ops:
  0.7 2.4 %shard_map.158 = bf16[32,48,384]{2,1,0:T(8,128)(2,1)} custom-call(bf16[48,4096]{1,0:T(8,128)(2,1)} %q_ref.1, bf16[48,4096]{1,0:T(8,128)(2,1)} %k_ref.1, bf16[48,4096]{1,0:T(8,128)(2,1)} %v_ref.1), custom_call_target="tpu_custom_call" | custom-call | tf_op jit(solution)/shard_map/pallas_call | solution.py:466
  3.0 11.9 %all-to-all-start = ((bf16[32,48,384]{2,1,0:T(8,128)(2,1)}), bf16[32,48,384]{2,1,0:T(8,128)(2,1)S(1)}, u32[]{:S(2)}, u32[]{:S(2)}) async-start(bf16[32,48,384]{2,1,0:T(8,128)(2,1)} %shard_map.158), calls=%async_computation | async-start | bytes 2359296 | tf_op jit(solution)/shard_map/all_to_all | solution.py:538
  15.1 5.2 %collective-permute-start = (f32[2,16,512]{2,1,0:T(8,128)S(1)}, f32[2,16,512]{2,1,0:T(8,128)S(1)}, u32[]{:S(2)}, u32[]{:S(2)}) collective-permute-start(f32[2,16,512]{2,1,0:T(8,128)S(1)} %get-tuple-element.44), channel_id=1, source_target_pairs={{0,8},{8,16},{16,24},{24,32},{32,40},{40,48},{48,56},{56,64},{64,7... | collective-permute-start | bytes 196616 | tf_op jit(solution)/shard_map/ppermute | solution.py:446
  20.3 1.9 %collective-permute-start.1 = (f32[2,16,512]{2,1,0:T(8,128)S(1)}, f32[2,16,512]{2,1,0:T(8,128)S(1)}, u32[]{:S(2)}, u32[]{:S(2)}) collective-permute-start(f32[2,16,512]{2,1,0:T(8,128)S(1)} %get-tuple-element.45), channel_id=1, source_target_pairs={{8,0},{16,8},{24,16},{32,24},{40,32},{48,40},{56,48},{64,56},{72,6... | collective-permute-start | bytes 196616 | tf_op jit(solution)/shard_map/ppermute | solution.py:447
  23.5 15.1 %collective-permute-done.above_ref = f32[2,16,512]{2,1,0:T(8,128)S(1)} collective-permute-done((f32[2,16,512]{2,1,0:T(8,128)S(1)}, f32[2,16,512]{2,1,0:T(8,128)S(1)}, u32[]{:S(2)}, u32[]{:S(2)}) %collective-permute-start) | collective-permute-done | bytes 65568 | tf_op jit(solution)/shard_map/ppermute | solution.py:446
  38.5 5.6 %collective-permute-done.1.below_ref = f32[2,16,512]{2,1,0:T(8,128)S(1)} collective-permute-done((f32[2,16,512]{2,1,0:T(8,128)S(1)}, f32[2,16,512]{2,1,0:T(8,128)S(1)}, u32[]{:S(2)}, u32[]{:S(2)}) %collective-permute-start.1) | collective-permute-done | bytes 65568 | tf_op jit(solution)/shard_map/ppermute | solution.py:447
  50.1 1.7 %collective-permute-start.4 = (bf16[768,256]{1,0:T(8,128)(2,1)S(1)}, bf16[768,256]{1,0:T(8,128)(2,1)S(1)}, u32[]{:S(2)}, u32[]{:S(2)}) collective-permute-start(bf16[768,256]{1,0:T(8,128)(2,1)S(1)} %get-tuple-element.59), channel_id=1, source_target_pairs={{64,0},{128,64},{192,128},{0,192},{65,1},{129,65},{193,129},{1,193... | collective-permute-start | bytes 1179656 | tf_op jit(solution)/shard_map/ppermute | solution.py:547
  51.8 6.1 %shard_map.162.refs_4_ = f32[3072,256]{1,0:T(8,128)S(1)} custom-call(bf16[1536,384]{1,0:T(8,128)(2,1)S(1)} %bitcast.9, bf16[1536,128]{1,0:T(8,128)(2,1)S(1)} %collective-permute-done.2.refs_1_.refs_0_, bf16[1536,384]{1,0:T(8,128)(2,1)S(1)} %bitcast.10), custom_call_target="tpu_custom_call" | custom-call | flops 4831838208 | bytes 6291456 | tf_op jit(solution)/shard_map/pallas_call | solution.py:135
  58.0 2.7 %collective-permute-start.8 = (bf16[768,256]{1,0:T(8,128)(2,1)S(1)}, bf16[768,256]{1,0:T(8,128)(2,1)S(1)}, u32[]{:S(2)}, u32[]{:S(2)}) collective-permute-start(bf16[768,256]{1,0:T(8,128)(2,1)S(1)} %get-tuple-element.60), channel_id=1, source_target_pairs={{64,0},{128,64},{192,128},{0,192},{65,1},{129,65},{193,129},{1,193... | collective-permute-start | bytes 1179656 | tf_op jit(solution)/shard_map/ppermute | solution.py:553
  61.2 6.3 %shard_map.163.refs_4_ = f32[3072,256]{1,0:T(8,128)S(1)} custom-call(bf16[1536,384]{1,0:T(8,128)(2,1)S(1)} %bitcast.11, bf16[1536,128]{1,0:T(8,128)(2,1)S(1)} %collective-permute-done.2.refs_1_.refs_0_, bf16[768,256]{1,0:T(8,128)(2,1)S(1)} %collective-permute-done.3.refs_2_, bf16[768,256]{1,0:T(8,128)(2,1)S(1)} %collective-permute-done.4.refs_3_, ...), custom_call_target="tpu_custom_call" | custom-call | flops 4831838208 | bytes 6291456 | tf_op jit(solution)/shard_map/pallas_call | solution.py:135
  68.3 2.2 %collective-permute-start.6 = (bf16[768,256]{1,0:T(8,128)(2,1)S(1)}, bf16[768,256]{1,0:T(8,128)(2,1)S(1)}, u32[]{:S(2)}, u32[]{:S(2)}) collective-permute-start(bf16[768,256]{1,0:T(8,128)(2,1)S(1)} %collective-permute-done.4.refs_3_), channel_id=1, source_target_pairs={{64,0},{128,64},{192,128},{0,192},{65,1},{129,65},{193,129},{1,193... | collective-permute-start | bytes 1179656 | tf_op jit(solution)/shard_map/ppermute | solution.py:561
  70.4 6.3 %shard_map.164.refs_3_ = f32[3072,256]{1,0:T(8,128)S(1)} custom-call(bf16[1536,384]{1,0:T(8,128)(2,1)S(1)} %bitcast.12, bf16[1536,128]{1,0:T(8,128)(2,1)S(1)} %collective-permute-done.2.refs_1_.refs_0_, bf16[768,256]{1,0:T(8,128)(2,1)S(1)} %collective-permute-done.7.refs_2_, bf16[768,256]{1,0:T(8,128)(2,1)S(1)} %collective-permute-done.8.refs_3_, ...), custom_call_target="tpu_custom_call" | custom-call | flops 4831838208 | bytes 6291456 | tf_op jit(solution)/shard_map/pallas_call | solution.py:135
  76.8 2.1 %collective-permute-done.5.refs_1_ = bf16[768,256]{1,0:T(8,128)(2,1)S(1)} collective-permute-done((bf16[768,256]{1,0:T(8,128)(2,1)S(1)}, bf16[768,256]{1,0:T(8,128)(2,1)S(1)}, u32[]{:S(2)}, u32[]{:S(2)}) %collective-permute-start.5) | collective-permute-done | bytes 393248 | tf_op jit(solution)/shard_map/ppermute | solution.py:561
  78.9 3.2 %shard_map.165 = f32[1536,128]{1,0:T(8,128)S(1)} custom-call(bf16[1536,128]{1,0:T(8,128)(2,1)S(1)} %collective-permute-done.2.refs_1_.refs_0_, bf16[768,256]{1,0:T(8,128)(2,1)S(1)} %collective-permute-done.5.refs_1_, bf16[768,256]{1,0:T(8,128)(2,1)S(1)} %collective-permute-done.6.refs_2_, f32[3072,256]{1,0:T(8,128)S(1)} %shard_map.164.refs_3_, ...), custom_call_target="tpu_custom_call" | custom-call | flops 2415919104 | bytes 3145728 | tf_op jit(solution)/shard_map/pallas_call | solution.py:156
  82.1 1.9 %collective-permute-start.9 = (f32[1536,128]{1,0:T(8,128)S(1)}, f32[1536,128]{1,0:T(8,128)S(1)}, u32[]{:S(2)}, u32[]{:S(2)}) collective-permute-start(f32[1536,128]{1,0:T(8,128)S(1)} %shard_map.165), channel_id=1, source_target_pairs={{0,8},{8,0},{1,9},{9,1},{2,10},{10,2},{3,11},{11,3},{4,12},{12,4},... | collective-permute-start | bytes 2359304 | tf_op jit(solution)/shard_map/ppermute | solution.py:566
  84.1 3.2 %shard_map.166.own_ref = f32[1536,128]{1,0:T(8,128)S(1)} custom-call(bf16[1536,384]{1,0:T(8,128)(2,1)S(1)} %bitcast.13, bf16[768,256]{1,0:T(8,128)(2,1)S(1)} %collective-permute-done.5.refs_1_, bf16[768,256]{1,0:T(8,128)(2,1)S(1)} %collective-permute-done.6.refs_2_, f32[3072,256]{1,0:T(8,128)S(1)} %shard_map.164.refs_3_, bf16[64,4096]{1,0:T(8,128)(2,1)S(1)} %bitcast.15), custom_call_target="tpu_custom_call" | custom-call | flops 2415919104 | bytes 3145728 | tf_op jit(solution)/shard_map/pallas_call | solution.py:156
  87.3 1.9 %shard_map.167 = bf16[4,8,32,128]{3,2,1,0:T(8,128)(2,1)} custom-call(f32[1536,128]{1,0:T(8,128)S(1)} %shard_map.166.own_ref, f32[1536,128]{1,0:T(8,128)S(1)} %collective-permute-done.9.oth_ref), custom_call_target="tpu_custom_call" | custom-call | tf_op jit(solution)/shard_map/pallas_call | solution.py:504
  89.2 6.6 %all-to-all-start.1 = ((bf16[32,32,128]{2,1,0:T(8,128)(2,1)}), bf16[32,32,128]{2,1,0:T(8,128)(2,1)S(1)}, u32[]{:S(2)}, u32[]{:S(2)}) async-start(bf16[32,32,128]{2,1,0:T(8,128)(2,1)} %bitcast.2), calls=%async_computation.1 | async-start | bytes 524288 | tf_op jit(solution)/shard_map/all_to_all | solution.py:569
  97.1 4.0 %collective-permute-start.12 = (f32[2,8,512]{2,1,0:T(8,128)}, f32[2,8,512]{2,1,0:T(8,128)S(1)}, u32[]{:S(2)}, u32[]{:S(2)}) collective-permute-start(f32[2,8,512]{2,1,0:T(8,128)} %copy-done.12), channel_id=1, source_target_pairs={{0,1},{1,2},{2,3},{3,4},{4,5},{5,6},{6,7},{8,9},{9,10},{10,11},{11... | collective-permute-start | bytes 98312 | tf_op jit(solution)/shard_map/ppermute | solution.py:554
  101.1 6.7 %all-to-all-done.1.parts_ref = bf16[32,32,128]{2,1,0:T(8,128)(2,1)S(1)} async-done(((bf16[32,32,128]{2,1,0:T(8,128)(2,1)}), bf16[32,32,128]{2,1,0:T(8,128)(2,1)S(1)}, u32[]{:S(2)}, u32[]{:S(2)}) %all-to-all-start.1) | async-done | bytes 262176 | tf_op jit(solution)/shard_map/all_to_all | solution.py:569
  107.8 2.1 %collective-permute-start.10 = (f32[16,128]{1,0:T(8,128)S(1)}, f32[16,128]{1,0:T(8,128)S(1)}, u32[]{:S(2)}, u32[]{:S(2)}) collective-permute-start(f32[16,128]{1,0:T(8,128)S(1)} %get-tuple-element.64), channel_id=1, source_target_pairs={{0,8},{8,0},{16,24},{24,16},{32,40},{40,32},{48,56},{56,48},{64,72... | collective-permute-start | bytes 24584 | tf_op jit(solution)/shard_map/ppermute | solution.py:599
  109.9 2.6 %collective-permute-start.11 = (f32[16,128]{1,0:T(8,128)S(1)}, f32[16,128]{1,0:T(8,128)S(1)}, u32[]{:S(2)}, u32[]{:S(2)}) collective-permute-start(f32[16,128]{1,0:T(8,128)S(1)} %get-tuple-element.66), channel_id=1, source_target_pairs={{8,16},{24,32},{40,48},{56,64},{72,80},{88,96},{104,112},{120,128}... | collective-permute-start | bytes 24584 | tf_op jit(solution)/shard_map/ppermute | solution.py:602
  115.8 3.3 %copy-done = bf16[3,3,3,384,384]{4,3,2,1,0:T(8,128)(2,1)S(1)} copy-done((bf16[3,3,3,384,384]{4,3,2,1,0:T(8,128)(2,1)S(1)}, bf16[3,3,3,384,384]{4,3,2,1,0:T(8,128)(2,1)}, u32[]{:S(2)}) %copy-start) | copy-done | bytes 7962648
  119.7 4.7 %shard_map.170 = (f32[4,12,4,16]{3,2,1,0:T(4,128)}, bf16[4,12,4,384]{3,2,1,0:T(4,128)(2,1)}) custom-call(f32[16,128]{1,0:T(8,128)S(1)} %collective-permute-done.10.near_ref, f32[32,128]{1,0:T(8,128)S(1)} %get-tuple-element.65.mine_ref, f32[16,128]{1,0:T(8,128)S(1)} %collective-permute-done.11.apart_ref, f32[6,4,8,128]{3,2,1,0:T(8,128)S(1)} %get-tuple-element.71.cells_ref, ...), custom_call_target="tpu_custom_call" | custom-call | tf_op jit(solution)/shard_map/pallas_call | solution.py:296
  (60 shorter events, 13.3 us)
Async XLA Ops:
  0.6 14.3 %copy-start.14 = (f32[4,4,12,16]{3,1,2,0:T(4,128)S(1)}, f32[4,4,12,16]{3,1,2,0:T(4,128)}, u32[]{:S(2)}) copy-start(f32[4,4,12,16]{3,1,2,0:T(4,128)} %param.19) | copy-start | bytes 36868
  0.6 14.3 %copy-start.16 = (bf16[2,4,12,16]{3,1,2,0:T(4,128)(2,1)S(1)}, bf16[2,4,12,16]{3,1,2,0:T(4,128)(2,1)}, u32[]{:S(2)}) copy-start(bf16[2,4,12,16]{3,1,2,0:T(4,128)(2,1)} %param.23) | copy-start | bytes 9220
  0.7 14.2 %copy-start.15 = (bf16[2,4,12,384]{3,1,2,0:T(4,128)(2,1)S(1)}, bf16[2,4,12,384]{3,1,2,0:T(4,128)(2,1)}, u32[]{:S(2)}) copy-start(bf16[2,4,12,384]{3,1,2,0:T(4,128)(2,1)} %param.27) | copy-start | bytes 221188
  3.0 43.9 %all-to-all-start = ((bf16[32,48,384]{2,1,0:T(8,128)(2,1)}), bf16[32,48,384]{2,1,0:T(8,128)(2,1)S(1)}, u32[]{:S(2)}, u32[]{:S(2)}) async-start(bf16[32,48,384]{2,1,0:T(8,128)(2,1)} %shard_map.158), calls=%async_computation | async-start | bytes 2359296 | tf_op jit(solution)/shard_map/all_to_all | solution.py:538
  15.1 23.4 %collective-permute-start = (f32[2,16,512]{2,1,0:T(8,128)S(1)}, f32[2,16,512]{2,1,0:T(8,128)S(1)}, u32[]{:S(2)}, u32[]{:S(2)}) collective-permute-start(f32[2,16,512]{2,1,0:T(8,128)S(1)} %get-tuple-element.44), channel_id=1, source_target_pairs={{0,8},{8,16},{16,24},{24,32},{32,40},{40,48},{48,56},{56,64},{64,7... | collective-permute-start | bytes 196616 | tf_op jit(solution)/shard_map/ppermute | solution.py:446
  20.3 23.8 %collective-permute-start.1 = (f32[2,16,512]{2,1,0:T(8,128)S(1)}, f32[2,16,512]{2,1,0:T(8,128)S(1)}, u32[]{:S(2)}, u32[]{:S(2)}) collective-permute-start(f32[2,16,512]{2,1,0:T(8,128)S(1)} %get-tuple-element.45), channel_id=1, source_target_pairs={{8,0},{16,8},{24,16},{32,24},{40,32},{48,40},{56,48},{64,56},{72,6... | collective-permute-start | bytes 196616 | tf_op jit(solution)/shard_map/ppermute | solution.py:447
  47.0 4.8 %collective-permute-start.2 = (bf16[1536,128]{1,0:T(8,128)(2,1)S(1)}, bf16[1536,128]{1,0:T(8,128)(2,1)S(1)}, u32[]{:S(2)}, u32[]{:S(2)}) collective-permute-start(bf16[1536,128]{1,0:T(8,128)(2,1)S(1)} %slice.14), channel_id=1, source_target_pairs={{0,8},{8,0},{1,9},{9,1},{2,10},{10,2},{3,11},{11,3},{4,12},{12,4},... | collective-permute-start | bytes 1179656 | tf_op jit(solution)/shard_map/ppermute | solution.py:548
  48.6 12.5 %collective-permute-start.3 = (bf16[768,256]{1,0:T(8,128)(2,1)S(1)}, bf16[768,256]{1,0:T(8,128)(2,1)S(1)}, u32[]{:S(2)}, u32[]{:S(2)}) collective-permute-start(bf16[768,256]{1,0:T(8,128)(2,1)S(1)} %get-tuple-element.60), channel_id=1, source_target_pairs={{0,64},{64,128},{128,192},{192,0},{1,65},{65,129},{129,193},{193,1... | collective-permute-start | bytes 1179656 | tf_op jit(solution)/shard_map/ppermute | solution.py:546
  50.1 11.1 %collective-permute-start.4 = (bf16[768,256]{1,0:T(8,128)(2,1)S(1)}, bf16[768,256]{1,0:T(8,128)(2,1)S(1)}, u32[]{:S(2)}, u32[]{:S(2)}) collective-permute-start(bf16[768,256]{1,0:T(8,128)(2,1)S(1)} %get-tuple-element.59), channel_id=1, source_target_pairs={{64,0},{128,64},{192,128},{0,192},{65,1},{129,65},{193,129},{1,193... | collective-permute-start | bytes 1179656 | tf_op jit(solution)/shard_map/ppermute | solution.py:547
  57.9 12.5 %collective-permute-start.7 = (bf16[768,256]{1,0:T(8,128)(2,1)S(1)}, bf16[768,256]{1,0:T(8,128)(2,1)S(1)}, u32[]{:S(2)}, u32[]{:S(2)}) collective-permute-start(bf16[768,256]{1,0:T(8,128)(2,1)S(1)} %get-tuple-element.59), channel_id=1, source_target_pairs={{0,64},{64,128},{128,192},{192,0},{1,65},{65,129},{129,193},{193,1... | collective-permute-start | bytes 1179656 | tf_op jit(solution)/shard_map/ppermute | solution.py:552
  58.0 12.5 %collective-permute-start.8 = (bf16[768,256]{1,0:T(8,128)(2,1)S(1)}, bf16[768,256]{1,0:T(8,128)(2,1)S(1)}, u32[]{:S(2)}, u32[]{:S(2)}) collective-permute-start(bf16[768,256]{1,0:T(8,128)(2,1)S(1)} %get-tuple-element.60), channel_id=1, source_target_pairs={{64,0},{128,64},{192,128},{0,192},{65,1},{129,65},{193,129},{1,193... | collective-permute-start | bytes 1179656 | tf_op jit(solution)/shard_map/ppermute | solution.py:553
  67.5 11.4 %copy-start.11 = (bf16[4096,64]{0,1:T(8,128)(2,1)S(1)}, bf16[4096,64]{0,1:T(8,128)(2,1)}, u32[]{:S(2)}) copy-start(bf16[4096,64]{0,1:T(8,128)(2,1)} %param.18) | copy-start | bytes 1572868
  67.5 11.4 %collective-permute-start.5 = (bf16[768,256]{1,0:T(8,128)(2,1)S(1)}, bf16[768,256]{1,0:T(8,128)(2,1)S(1)}, u32[]{:S(2)}, u32[]{:S(2)}) collective-permute-start(bf16[768,256]{1,0:T(8,128)(2,1)S(1)} %collective-permute-done.3.refs_2_), channel_id=1, source_target_pairs={{0,64},{64,128},{128,192},{192,0},{1,65},{65,129},{129,193},{193,1... | collective-permute-start | bytes 1179656 | tf_op jit(solution)/shard_map/ppermute | solution.py:561
  68.3 10.6 %collective-permute-start.6 = (bf16[768,256]{1,0:T(8,128)(2,1)S(1)}, bf16[768,256]{1,0:T(8,128)(2,1)S(1)}, u32[]{:S(2)}, u32[]{:S(2)}) collective-permute-start(bf16[768,256]{1,0:T(8,128)(2,1)S(1)} %collective-permute-done.4.refs_3_), channel_id=1, source_target_pairs={{64,0},{128,64},{192,128},{0,192},{65,1},{129,65},{193,129},{1,193... | collective-permute-start | bytes 1179656 | tf_op jit(solution)/shard_map/ppermute | solution.py:561
  82.1 33.7 %copy-start.6 = (f32[384]{0:T(512)S(1)}, f32[384]{0:T(512)}, u32[]{:S(2)}) copy-start(f32[384]{0:T(512)} %b1_ref.1) | copy-start | bytes 4612
  82.1 33.7 %copy-start.7 = (f32[384]{0:T(512)S(1)}, f32[384]{0:T(512)}, u32[]{:S(2)}) copy-start(f32[384]{0:T(512)} %gain_ref.1) | copy-start | bytes 4612
  82.1 33.6 %copy-start.8 = (f32[384]{0:T(512)S(1)}, f32[384]{0:T(512)}, u32[]{:S(2)}) copy-start(f32[384]{0:T(512)} %b2_ref.1) | copy-start | bytes 4612
  82.1 33.6 %copy-start.9 = (f32[16]{0:T(128)S(1)}, f32[16]{0:T(128)}, u32[]{:S(2)}) copy-start(f32[16]{0:T(128)} %scale_ref.1) | copy-start | bytes 196
  82.1 5.2 %collective-permute-start.9 = (f32[1536,128]{1,0:T(8,128)S(1)}, f32[1536,128]{1,0:T(8,128)S(1)}, u32[]{:S(2)}, u32[]{:S(2)}) collective-permute-start(f32[1536,128]{1,0:T(8,128)S(1)} %shard_map.165), channel_id=1, source_target_pairs={{0,8},{8,0},{1,9},{9,1},{2,10},{10,2},{3,11},{11,3},{4,12},{12,4},... | collective-permute-start | bytes 2359304 | tf_op jit(solution)/shard_map/ppermute | solution.py:566
  89.2 18.6 %all-to-all-start.1 = ((bf16[32,32,128]{2,1,0:T(8,128)(2,1)}), bf16[32,32,128]{2,1,0:T(8,128)(2,1)S(1)}, u32[]{:S(2)}, u32[]{:S(2)}) async-start(bf16[32,32,128]{2,1,0:T(8,128)(2,1)} %bitcast.2), calls=%async_computation.1 | async-start | bytes 524288 | tf_op jit(solution)/shard_map/all_to_all | solution.py:569
  95.8 17.3 %collective-permute-start.13 = (f32[2,8,512]{2,1,0:T(8,128)}, f32[2,8,512]{2,1,0:T(8,128)S(1)}, u32[]{:S(2)}, u32[]{:S(2)}) collective-permute-start(f32[2,8,512]{2,1,0:T(8,128)} %copy-done.13), channel_id=1, source_target_pairs={{1,0},{2,1},{3,2},{4,3},{5,4},{6,5},{7,6},{9,8},{10,9},{11,10},{12... | collective-permute-start | bytes 98312 | tf_op jit(solution)/shard_map/ppermute | solution.py:557
  97.1 16.1 %collective-permute-start.12 = (f32[2,8,512]{2,1,0:T(8,128)}, f32[2,8,512]{2,1,0:T(8,128)S(1)}, u32[]{:S(2)}, u32[]{:S(2)}) collective-permute-start(f32[2,8,512]{2,1,0:T(8,128)} %copy-done.12), channel_id=1, source_target_pairs={{0,1},{1,2},{2,3},{3,4},{4,5},{5,6},{6,7},{8,9},{9,10},{10,11},{11... | collective-permute-start | bytes 98312 | tf_op jit(solution)/shard_map/ppermute | solution.py:554
  107.8 7.3 %collective-permute-start.10 = (f32[16,128]{1,0:T(8,128)S(1)}, f32[16,128]{1,0:T(8,128)S(1)}, u32[]{:S(2)}, u32[]{:S(2)}) collective-permute-start(f32[16,128]{1,0:T(8,128)S(1)} %get-tuple-element.64), channel_id=1, source_target_pairs={{0,8},{8,0},{16,24},{24,16},{32,40},{40,32},{48,56},{56,48},{64,72... | collective-permute-start | bytes 24584 | tf_op jit(solution)/shard_map/ppermute | solution.py:599
  109.9 5.9 %collective-permute-start.11 = (f32[16,128]{1,0:T(8,128)S(1)}, f32[16,128]{1,0:T(8,128)S(1)}, u32[]{:S(2)}, u32[]{:S(2)}) collective-permute-start(f32[16,128]{1,0:T(8,128)S(1)} %get-tuple-element.66), channel_id=1, source_target_pairs={{8,16},{24,32},{40,48},{56,64},{72,80},{88,96},{104,112},{120,128}... | collective-permute-start | bytes 24584 | tf_op jit(solution)/shard_map/ppermute | solution.py:602
  (9 other events, 9.3 us)

commit v9 on v8

--- a/solution.py
+++ b/solution.py
@@ -178,14 +178,16 @@
     near_ref,
     mine_ref,
     apart_ref,
-    cells_ref,
+    toks,
+    mids,
+    before_ref,
+    after_ref,
     level_ref,
     scale_ref,
     mean_ref,
     w1_ref,
     b1_ref,
     gain_ref,
-    mid_ref,
     w2_ref,
     b2_ref,
     den_ref,
@@ -198,7 +200,10 @@
     wide,
     done,
     vecs,
+    cells_ref,
+    mid_ref,
 ):
+    place(toks, mids, before_ref, after_ref, cells_ref, mid_ref)
     even = lax.axis_index("core") == 0
     at_row, at_col = mesh_index(SEQ), mesh_index(BLK)
     up, down = at_row > 0, at_row < lax.axis_size(SEQ) - 1
@@ -292,7 +297,7 @@
 
 def tail(*args):
     specs = [pl.BlockSpec(memory_space=pltpu.VMEM)] * len(args)
-    specs[4] = pl.BlockSpec(memory_space=pltpu.SMEM)
+    specs[7] = pl.BlockSpec(memory_space=pltpu.SMEM)
     return pl.pallas_call(
         tail_kernel,
         in_specs=specs,
@@ -310,6 +315,8 @@
             pltpu.VMEM((6, 6, 16, 3 * C1), jnp.bfloat16),
             pltpu.VMEM((C1 // 128, F, 128, 128), jnp.float32),
             pltpu.VMEM((16, 128), jnp.float32),
+            pltpu.VMEM((6, 4, 8, 128), jnp.float32),
+            pltpu.VMEM((2, 6, 16, C1), jnp.float32),
         ],
         compiler_params=pltpu.CompilerParams(vmem_limit_bytes=32 << 20),
     )(*args)
@@ -407,7 +414,7 @@
             ref[i, pl.ds(4 * h + r, 1), 384:512] = jnp.where(low, one, two)
 
 
-def place_kernel(toks, mids, left_ref, right_ref, cells_ref, cache_ref):
+def place(toks, mids, left_ref, right_ref, cells_ref, cache_ref):
     cells_ref[...] = jnp.zeros(cells_ref.shape, jnp.float32)
     cache_ref[...] = jnp.zeros(cache_ref.shape, jnp.float32)
     for f in range(6):
@@ -548,18 +555,17 @@
     q_oth = lax.ppermute(q_own, "core", swap)
     state = flash(moved, q_oth, [moved])
     toks, mids, to_right, to_left = rows
-    state, a, b, to_right = lax.optimization_barrier((state, a, b, to_right))
+    state, a, b = lax.optimization_barrier((state, a, b))
     left_b = lax.ppermute(b, "y", right)
     right_a = lax.ppermute(a, "y", left)
-    before = lax.ppermute(to_right, BLK, along(BLK, 1))
     state = flash(moved, q_oth, [left_a, right_b], state)
-    state, left_a, right_b, to_left = lax.optimization_barrier((state, left_a, right_b, to_left))
-    after = lax.ppermute(to_left, BLK, along(BLK, -1))
-    borders = small_call(place_kernel, [(6, 4, 8, 128), (2, 6, 16, C1)])(
-        toks, mids, before, after
-    )
+    state, left_a, right_b = lax.optimization_barrier((state, left_a, right_b))
     far = [lax.ppermute(left_a, "y", right), lax.ppermute(right_b, "y", left)]
     state = flash(moved, q_oth, [left_b, right_a], state)
+    state, to_right, to_left = lax.optimization_barrier((state, to_right, to_left))
+    before = lax.ppermute(to_right, BLK, along(BLK, 1))
+    after = lax.ppermute(to_left, BLK, along(BLK, -1))
+    state, before, after = lax.optimization_barrier((state, before, after))
     weight = weight_head.T
     oth = flash_last(q_oth, 0, far, state, 1, weight)
     oth, state = lax.optimization_barrier((oth, state))
@@ -567,7 +573,7 @@
     own = flash_last(moved, 2, far, state, 0, weight)
     partial = merge(own, oth).reshape(heads, 32, 128)
     parts = lax.all_to_all(partial, HEAD, split_axis=0, concat_axis=0, tiled=True)
-    return head_sum(parts), (*borders, weight_first)
+    return head_sum(parts), (toks, mids, before, after, weight_first)
 
 
 def shards(
@@ -587,7 +593,7 @@
     weight_mid,
     bias_mid,
 ):
-    (mine, near, apart), (cells, cache_second, weight_first) = attention(
+    (mine, near, apart), (toks, mids, before, after, weight_first) = attention(
         query_vectors,
         key_vectors,
         value_vectors,
@@ -604,14 +610,16 @@
         near,
         mine,
         apart,
-        cells,
+        toks,
+        mids,
+        before,
+        after,
         noise_level,
         latent_scale,
         latent_mean,
         weight_first,
         bias_in,
         norm_gain,
-        cache_second,
         weight_mid.reshape(9, 3 * C1, C1),
         bias_mid,
     )

time: 126 us -> 129 us (1.024)
  blocking collectives: 0 us -> 21.8 us
  waiting for transfers between devices: 30.7 us -> 24.8 us
  local copies, waits for them, and re-layouts: 9.45 us -> 3.74 us
  starting transfers between devices: 47.8 us -> 42.1 us
    all_to_all x0 -> x1, blocking collectives: none -> 21.8 us  [attention(): lax.all_to_all(partial, HEAD, split_axis=0, concat_axis=0, tiled=True)]
    all_to_all x1 -> x0, waiting for transfers between devices: 6.7 us -> none  [attention(): lax.all_to_all(partial, HEAD, split_axis=0, concat_axis=0, tiled=True)]
    all_to_all x1 -> x0, starting transfers between devices: 6.56 us -> none  [attention(): lax.all_to_all(partial, HEAD, split_axis=0, concat_axis=0, tiled=True)]
    unnamed x34 -> x40, local copies, waits for them, and re-layouts: 9.34 us -> 3.62 us
    ppermute x2, waiting for transfers between devices: 2.1 us -> 0.01 us  [attention(): far = [lax.ppermute(left_a, 'y', right), lax.ppermute(right_b, 'y', left)]]
    ppermute x1, waiting for transfers between devices: 0.66 us -> 2.62 us  [shards(): apart = lax.ppermute(apart, SEQ, pairs)]
  transfers between devices with their start and end apart: 16 -> 15, of which waited for: 6 -> 5; matrix products, arithmetic and copies ran while one was open for 0% -> 0% of each run, Pallas kernels for 18% -> 18%
where the time goes in v9:
time: 129 us; the launch traced here: 128 us
  starting transfers between devices  42.1 us (33%)
  Pallas kernels  34.2 us (27%)
  waiting for transfers between devices  24.8 us (19%)
  blocking collectives  21.8 us (17%)
  local copies, waits for them, and re-layouts  3.74 us (3%)
  between operations  1.68 us (1%)
    all_to_all x1, blocking collectives, attention(): lax.all_to_all(partial, HEAD, split_axis=0, concat_axis=0, tiled=True)  21.8 us
    pallas_call x3, Pallas kernels, flash(): pl.pallas_call(functools.partial(flash_kernel, state is None, False, len(...  18.7 us
    ppermute x1, waiting for transfers between devices, halo_rows(): above = lax.ppermute(down, SEQ, along(SEQ, 1))  15.1 us
    all_to_all x1, starting transfers between devices, attention(): lax.all_to_all(packed, HEAD, split_axis=0, concat_axis=0, tiled=True)  11.9 us
    pallas_call x2, Pallas kernels, flash_last(): pl.pallas_call(functools.partial(flash_kernel, False, True, len(kvs), hal...  6.46 us
    ppermute x1, waiting for transfers between devices, halo_rows(): below = lax.ppermute(up, SEQ, along(SEQ, -1))  5.63 us
    ppermute x1, starting transfers between devices, halo_rows(): above = lax.ppermute(down, SEQ, along(SEQ, 1))  5.15 us
    pallas_call x1, Pallas kernels, tail(): pl.pallas_call(tail_kernel, in_specs=specs, out_specs=[pl.BlockSpec(memor...  4.86 us
  transfers between devices with their start and end apart: 15, of which 5 were waited for; matrix products, arithmetic and copies ran while one was open for 0% of the time, Pallas kernels for 18%

profile of v9, /device:TPU:1, one launch (start us, length us, event | category | flops | bytes accessed | tf_op | source)
XLA Modules:
  0.0 128.3 jit_solution(18347368807317660248)
XLA Ops:
  0.7 2.4 %shard_map.158 = bf16[32,48,384]{2,1,0:T(8,128)(2,1)} custom-call(bf16[48,4096]{1,0:T(8,128)(2,1)} %q_ref.1, bf16[48,4096]{1,0:T(8,128)(2,1)} %k_ref.1, bf16[48,4096]{1,0:T(8,128)(2,1)} %v_ref.1), custom_call_target="tpu_custom_call" | custom-call | tf_op jit(solution)/shard_map/pallas_call | solution.py:473
  3.0 11.9 %all-to-all-start = ((bf16[32,48,384]{2,1,0:T(8,128)(2,1)}), bf16[32,48,384]{2,1,0:T(8,128)(2,1)S(1)}, u32[]{:S(2)}, u32[]{:S(2)}) async-start(bf16[32,48,384]{2,1,0:T(8,128)(2,1)} %shard_map.158), calls=%async_computation | async-start | bytes 2359296 | tf_op jit(solution)/shard_map/all_to_all | solution.py:545
  15.2 5.2 %collective-permute-start = (f32[2,16,512]{2,1,0:T(8,128)S(1)}, f32[2,16,512]{2,1,0:T(8,128)S(1)}, u32[]{:S(2)}, u32[]{:S(2)}) collective-permute-start(f32[2,16,512]{2,1,0:T(8,128)S(1)} %get-tuple-element.46), channel_id=1, source_target_pairs={{0,8},{8,16},{16,24},{24,32},{32,40},{40,48},{48,56},{56,64},{64,7... | collective-permute-start | bytes 196616 | tf_op jit(solution)/shard_map/ppermute | solution.py:453
  20.3 1.9 %collective-permute-start.1 = (f32[2,16,512]{2,1,0:T(8,128)S(1)}, f32[2,16,512]{2,1,0:T(8,128)S(1)}, u32[]{:S(2)}, u32[]{:S(2)}) collective-permute-start(f32[2,16,512]{2,1,0:T(8,128)S(1)} %get-tuple-element.47), channel_id=1, source_target_pairs={{8,0},{16,8},{24,16},{32,24},{40,32},{48,40},{56,48},{64,56},{72,6... | collective-permute-start | bytes 196616 | tf_op jit(solution)/shard_map/ppermute | solution.py:454
  23.5 15.1 %collective-permute-done.above_ref = f32[2,16,512]{2,1,0:T(8,128)S(1)} collective-permute-done((f32[2,16,512]{2,1,0:T(8,128)S(1)}, f32[2,16,512]{2,1,0:T(8,128)S(1)}, u32[]{:S(2)}, u32[]{:S(2)}) %collective-permute-start) | collective-permute-done | bytes 65568 | tf_op jit(solution)/shard_map/ppermute | solution.py:453
  38.5 5.6 %collective-permute-done.1.below_ref = f32[2,16,512]{2,1,0:T(8,128)S(1)} collective-permute-done((f32[2,16,512]{2,1,0:T(8,128)S(1)}, f32[2,16,512]{2,1,0:T(8,128)S(1)}, u32[]{:S(2)}, u32[]{:S(2)}) %collective-permute-start.1) | collective-permute-done | bytes 65568 | tf_op jit(solution)/shard_map/ppermute | solution.py:454
  47.0 1.6 %collective-permute-start.2 = (bf16[1536,128]{1,0:T(8,128)(2,1)S(1)}, bf16[1536,128]{1,0:T(8,128)(2,1)S(1)}, u32[]{:S(2)}, u32[]{:S(2)}) collective-permute-start(bf16[1536,128]{1,0:T(8,128)(2,1)S(1)} %slice.14), channel_id=1, source_target_pairs={{0,8},{8,0},{1,9},{9,1},{2,10},{10,2},{3,11},{11,3},{4,12},{12,4},... | collective-permute-start | bytes 1179656 | tf_op jit(solution)/shard_map/ppermute | solution.py:555
  48.6 1.4 %collective-permute-start.3 = (bf16[768,256]{1,0:T(8,128)(2,1)S(1)}, bf16[768,256]{1,0:T(8,128)(2,1)S(1)}, u32[]{:S(2)}, u32[]{:S(2)}) collective-permute-start(bf16[768,256]{1,0:T(8,128)(2,1)S(1)} %get-tuple-element.60), channel_id=1, source_target_pairs={{0,64},{64,128},{128,192},{192,0},{1,65},{65,129},{129,193},{193,1... | collective-permute-start | bytes 1179656 | tf_op jit(solution)/shard_map/ppermute | solution.py:553
  50.1 1.7 %collective-permute-start.4 = (bf16[768,256]{1,0:T(8,128)(2,1)S(1)}, bf16[768,256]{1,0:T(8,128)(2,1)S(1)}, u32[]{:S(2)}, u32[]{:S(2)}) collective-permute-start(bf16[768,256]{1,0:T(8,128)(2,1)S(1)} %get-tuple-element.59), channel_id=1, source_target_pairs={{64,0},{128,64},{192,128},{0,192},{65,1},{129,65},{193,129},{1,193... | collective-permute-start | bytes 1179656 | tf_op jit(solution)/shard_map/ppermute | solution.py:554
  51.8 6.1 %shard_map.162.refs_4_ = f32[3072,256]{1,0:T(8,128)S(1)} custom-call(bf16[1536,384]{1,0:T(8,128)(2,1)S(1)} %bitcast.11, bf16[1536,128]{1,0:T(8,128)(2,1)S(1)} %collective-permute-done.2.refs_1_.refs_0_, bf16[1536,384]{1,0:T(8,128)(2,1)S(1)} %bitcast.12), custom_call_target="tpu_custom_call" | custom-call | flops 4831838208 | bytes 6291456 | tf_op jit(solution)/shard_map/pallas_call | solution.py:135
  58.0 2.7 %collective-permute-start.8 = (bf16[768,256]{1,0:T(8,128)(2,1)S(1)}, bf16[768,256]{1,0:T(8,128)(2,1)S(1)}, u32[]{:S(2)}, u32[]{:S(2)}) collective-permute-start(bf16[768,256]{1,0:T(8,128)(2,1)S(1)} %get-tuple-element.60), channel_id=1, source_target_pairs={{64,0},{128,64},{192,128},{0,192},{65,1},{129,65},{193,129},{1,193... | collective-permute-start | bytes 1179656 | tf_op jit(solution)/shard_map/ppermute | solution.py:560
  61.2 6.3 %shard_map.163.refs_4_ = f32[3072,256]{1,0:T(8,128)S(1)} custom-call(bf16[1536,384]{1,0:T(8,128)(2,1)S(1)} %bitcast.13, bf16[1536,128]{1,0:T(8,128)(2,1)S(1)} %collective-permute-done.2.refs_1_.refs_0_, bf16[768,256]{1,0:T(8,128)(2,1)S(1)} %collective-permute-done.3.refs_2_, bf16[768,256]{1,0:T(8,128)(2,1)S(1)} %collective-permute-done.4.refs_3_, ...), custom_call_target="tpu_custom_call" | custom-call | flops 4831838208 | bytes 6291456 | tf_op jit(solution)/shard_map/pallas_call | solution.py:135
  68.3 2.2 %collective-permute-start.6 = (bf16[768,256]{1,0:T(8,128)(2,1)S(1)}, bf16[768,256]{1,0:T(8,128)(2,1)S(1)}, u32[]{:S(2)}, u32[]{:S(2)}) collective-permute-start(bf16[768,256]{1,0:T(8,128)(2,1)S(1)} %collective-permute-done.4.refs_3_), channel_id=1, source_target_pairs={{64,0},{128,64},{192,128},{0,192},{65,1},{129,65},{193,129},{1,193... | collective-permute-start | bytes 1179656 | tf_op jit(solution)/shard_map/ppermute | solution.py:563
  70.5 6.3 %shard_map.164.refs_3_ = f32[3072,256]{1,0:T(8,128)S(1)} custom-call(bf16[1536,384]{1,0:T(8,128)(2,1)S(1)} %bitcast.14, bf16[1536,128]{1,0:T(8,128)(2,1)S(1)} %collective-permute-done.2.refs_1_.refs_0_, bf16[768,256]{1,0:T(8,128)(2,1)S(1)} %collective-permute-done.7.refs_2_, bf16[768,256]{1,0:T(8,128)(2,1)S(1)} %collective-permute-done.8.refs_3_, ...), custom_call_target="tpu_custom_call" | custom-call | flops 4831838208 | bytes 6291456 | tf_op jit(solution)/shard_map/pallas_call | solution.py:135
  76.8 1.3 %collective-permute-start.10 = (f32[2,8,512]{2,1,0:T(8,128)S(1)}, f32[2,8,512]{2,1,0:T(8,128)S(1)}, u32[]{:S(2)}, u32[]{:S(2)}) collective-permute-start(f32[2,8,512]{2,1,0:T(8,128)S(1)} %copy-done.14), channel_id=1, source_target_pairs={{1,0},{2,1},{3,2},{4,3},{5,4},{6,5},{7,6},{9,8},{10,9},{11,10},{12... | collective-permute-start | bytes 98312 | tf_op jit(solution)/shard_map/ppermute | solution.py:567
  78.1 4.0 %collective-permute-start.9 = (f32[2,8,512]{2,1,0:T(8,128)S(1)}, f32[2,8,512]{2,1,0:T(8,128)S(1)}, u32[]{:S(2)}, u32[]{:S(2)}) collective-permute-start(f32[2,8,512]{2,1,0:T(8,128)S(1)} %copy-done.12), channel_id=1, source_target_pairs={{0,1},{1,2},{2,3},{3,4},{4,5},{5,6},{6,7},{8,9},{9,10},{10,11},{11... | collective-permute-start | bytes 98312 | tf_op jit(solution)/shard_map/ppermute | solution.py:566
  83.1 3.2 %shard_map.165 = f32[1536,128]{1,0:T(8,128)S(1)} custom-call(bf16[1536,128]{1,0:T(8,128)(2,1)S(1)} %collective-permute-done.2.refs_1_.refs_0_, bf16[768,256]{1,0:T(8,128)(2,1)S(1)} %collective-permute-done.5.refs_1_, bf16[768,256]{1,0:T(8,128)(2,1)S(1)} %collective-permute-done.6.refs_2_, f32[3072,256]{1,0:T(8,128)S(1)} %shard_map.164.refs_3_, ...), custom_call_target="tpu_custom_call" | custom-call | flops 2415919104 | bytes 3145728 | tf_op jit(solution)/shard_map/pallas_call | solution.py:156
  86.5 2.8 %collective-permute-start.11 = (f32[1536,128]{1,0:T(8,128)S(1)}, f32[1536,128]{1,0:T(8,128)S(1)}, u32[]{:S(2)}, u32[]{:S(2)}) collective-permute-start(f32[1536,128]{1,0:T(8,128)S(1)} %shard_map.165), channel_id=1, source_target_pairs={{0,8},{8,0},{1,9},{9,1},{2,10},{10,2},{3,11},{11,3},{4,12},{12,4},... | collective-permute-start | bytes 2359304 | tf_op jit(solution)/shard_map/ppermute | solution.py:572
  89.2 3.2 %shard_map.166.own_ref = f32[1536,128]{1,0:T(8,128)S(1)} custom-call(bf16[1536,384]{1,0:T(8,128)(2,1)S(1)} %bitcast.15, bf16[768,256]{1,0:T(8,128)(2,1)S(1)} %collective-permute-done.5.refs_1_, bf16[768,256]{1,0:T(8,128)(2,1)S(1)} %collective-permute-done.6.refs_2_, f32[3072,256]{1,0:T(8,128)S(1)} %shard_map.164.refs_3_, bf16[64,4096]{1,0:T(8,128)(2,1)S(1)} %bitcast.18), custom_call_target="tpu_custom_call" | custom-call | flops 2415919104 | bytes 3145728 | tf_op jit(solution)/shard_map/pallas_call | solution.py:156
  93.6 21.8 %all_to_all.10.parts_ref = bf16[32,32,128]{2,1,0:T(8,128)(2,1)S(1)} all-to-all(bf16[32,32,128]{2,1,0:T(8,128)(2,1)S(1)} %bitcast.16), channel_id=1, replica_groups=mesh['y'=4,'zh'=4,'core'=2,'zl'=2,'x'=4] {'zh','zl','x'}, dimensions={0} | all-to-all | bytes 524288 | tf_op jit(solution)/shard_map/all_to_all | solution.py:575
  115.5 2.1 %collective-permute-start.12 = (f32[16,128]{1,0:T(8,128)S(1)}, f32[16,128]{1,0:T(8,128)S(1)}, u32[]{:S(2)}, u32[]{:S(2)}) collective-permute-start(f32[16,128]{1,0:T(8,128)S(1)} %get-tuple-element.70), channel_id=1, source_target_pairs={{0,8},{8,0},{16,24},{24,16},{32,40},{40,32},{48,56},{56,48},{64,72... | collective-permute-start | bytes 24584 | tf_op jit(solution)/shard_map/ppermute | solution.py:605
  117.5 2.6 %collective-permute-start.13 = (f32[16,128]{1,0:T(8,128)S(1)}, f32[16,128]{1,0:T(8,128)S(1)}, u32[]{:S(2)}, u32[]{:S(2)}) collective-permute-start(f32[16,128]{1,0:T(8,128)S(1)} %get-tuple-element.72), channel_id=1, source_target_pairs={{8,16},{24,32},{40,48},{56,64},{72,80},{88,96},{104,112},{120,128}... | collective-permute-start | bytes 24584 | tf_op jit(solution)/shard_map/ppermute | solution.py:608
  120.7 2.6 %collective-permute-done.13.apart_ref = f32[16,128]{1,0:T(8,128)S(1)} collective-permute-done((f32[16,128]{1,0:T(8,128)S(1)}, f32[16,128]{1,0:T(8,128)S(1)}, u32[]{:S(2)}, u32[]{:S(2)}) %collective-permute-start.13) | collective-permute-done | bytes 8224 | tf_op jit(solution)/shard_map/ppermute | solution.py:608
  123.5 4.9 %shard_map.169 = (f32[4,12,4,16]{3,2,1,0:T(4,128)}, bf16[4,12,4,384]{3,2,1,0:T(4,128)(2,1)}) custom-call(f32[16,128]{1,0:T(8,128)S(1)} %collective-permute-done.12.near_ref, f32[32,128]{1,0:T(8,128)S(1)} %get-tuple-element.71.mine_ref, f32[16,128]{1,0:T(8,128)S(1)} %collective-permute-done.13.apart_ref, f32[6,4,8,128]{3,2,1,0:T(8,128)S(1)} %copy-done.4, ...), custom_call_target="tpu_custom_call" | custom-call | tf_op jit(solution)/shard_map/pallas_call | solution.py:301
  (65 shorter events, 7.9 us)
Async XLA Ops:
  3.0 43.9 %all-to-all-start = ((bf16[32,48,384]{2,1,0:T(8,128)(2,1)}), bf16[32,48,384]{2,1,0:T(8,128)(2,1)S(1)}, u32[]{:S(2)}, u32[]{:S(2)}) async-start(bf16[32,48,384]{2,1,0:T(8,128)(2,1)} %shard_map.158), calls=%async_computation | async-start | bytes 2359296 | tf_op jit(solution)/shard_map/all_to_all | solution.py:545
  15.2 23.4 %collective-permute-start = (f32[2,16,512]{2,1,0:T(8,128)S(1)}, f32[2,16,512]{2,1,0:T(8,128)S(1)}, u32[]{:S(2)}, u32[]{:S(2)}) collective-permute-start(f32[2,16,512]{2,1,0:T(8,128)S(1)} %get-tuple-element.46), channel_id=1, source_target_pairs={{0,8},{8,16},{16,24},{24,32},{32,40},{40,48},{48,56},{56,64},{64,7... | collective-permute-start | bytes 196616 | tf_op jit(solution)/shard_map/ppermute | solution.py:453
  20.3 23.8 %collective-permute-start.1 = (f32[2,16,512]{2,1,0:T(8,128)S(1)}, f32[2,16,512]{2,1,0:T(8,128)S(1)}, u32[]{:S(2)}, u32[]{:S(2)}) collective-permute-start(f32[2,16,512]{2,1,0:T(8,128)S(1)} %get-tuple-element.47), channel_id=1, source_target_pairs={{8,0},{16,8},{24,16},{32,24},{40,32},{48,40},{56,48},{64,56},{72,6... | collective-permute-start | bytes 196616 | tf_op jit(solution)/shard_map/ppermute | solution.py:454
  47.0 4.8 %collective-permute-start.2 = (bf16[1536,128]{1,0:T(8,128)(2,1)S(1)}, bf16[1536,128]{1,0:T(8,128)(2,1)S(1)}, u32[]{:S(2)}, u32[]{:S(2)}) collective-permute-start(bf16[1536,128]{1,0:T(8,128)(2,1)S(1)} %slice.14), channel_id=1, source_target_pairs={{0,8},{8,0},{1,9},{9,1},{2,10},{10,2},{3,11},{11,3},{4,12},{12,4},... | collective-permute-start | bytes 1179656 | tf_op jit(solution)/shard_map/ppermute | solution.py:555
  48.6 12.5 %collective-permute-start.3 = (bf16[768,256]{1,0:T(8,128)(2,1)S(1)}, bf16[768,256]{1,0:T(8,128)(2,1)S(1)}, u32[]{:S(2)}, u32[]{:S(2)}) collective-permute-start(bf16[768,256]{1,0:T(8,128)(2,1)S(1)} %get-tuple-element.60), channel_id=1, source_target_pairs={{0,64},{64,128},{128,192},{192,0},{1,65},{65,129},{129,193},{193,1... | collective-permute-start | bytes 1179656 | tf_op jit(solution)/shard_map/ppermute | solution.py:553
  50.1 11.1 %collective-permute-start.4 = (bf16[768,256]{1,0:T(8,128)(2,1)S(1)}, bf16[768,256]{1,0:T(8,128)(2,1)S(1)}, u32[]{:S(2)}, u32[]{:S(2)}) collective-permute-start(bf16[768,256]{1,0:T(8,128)(2,1)S(1)} %get-tuple-element.59), channel_id=1, source_target_pairs={{64,0},{128,64},{192,128},{0,192},{65,1},{129,65},{193,129},{1,193... | collective-permute-start | bytes 1179656 | tf_op jit(solution)/shard_map/ppermute | solution.py:554
  57.9 12.6 %collective-permute-start.7 = (bf16[768,256]{1,0:T(8,128)(2,1)S(1)}, bf16[768,256]{1,0:T(8,128)(2,1)S(1)}, u32[]{:S(2)}, u32[]{:S(2)}) collective-permute-start(bf16[768,256]{1,0:T(8,128)(2,1)S(1)} %get-tuple-element.59), channel_id=1, source_target_pairs={{0,64},{64,128},{128,192},{192,0},{1,65},{65,129},{129,193},{193,1... | collective-permute-start | bytes 1179656 | tf_op jit(solution)/shard_map/ppermute | solution.py:559
  58.0 12.5 %collective-permute-start.8 = (bf16[768,256]{1,0:T(8,128)(2,1)S(1)}, bf16[768,256]{1,0:T(8,128)(2,1)S(1)}, u32[]{:S(2)}, u32[]{:S(2)}) collective-permute-start(bf16[768,256]{1,0:T(8,128)(2,1)S(1)} %get-tuple-element.60), channel_id=1, source_target_pairs={{64,0},{128,64},{192,128},{0,192},{65,1},{129,65},{193,129},{1,193... | collective-permute-start | bytes 1179656 | tf_op jit(solution)/shard_map/ppermute | solution.py:560
  67.5 15.6 %collective-permute-start.5 = (bf16[768,256]{1,0:T(8,128)(2,1)S(1)}, bf16[768,256]{1,0:T(8,128)(2,1)S(1)}, u32[]{:S(2)}, u32[]{:S(2)}) collective-permute-start(bf16[768,256]{1,0:T(8,128)(2,1)S(1)} %collective-permute-done.3.refs_2_), channel_id=1, source_target_pairs={{0,64},{64,128},{128,192},{192,0},{1,65},{65,129},{129,193},{193,1... | collective-permute-start | bytes 1179656 | tf_op jit(solution)/shard_map/ppermute | solution.py:563
  68.3 14.8 %collective-permute-start.6 = (bf16[768,256]{1,0:T(8,128)(2,1)S(1)}, bf16[768,256]{1,0:T(8,128)(2,1)S(1)}, u32[]{:S(2)}, u32[]{:S(2)}) collective-permute-start(bf16[768,256]{1,0:T(8,128)(2,1)S(1)} %collective-permute-done.4.refs_3_), channel_id=1, source_target_pairs={{64,0},{128,64},{192,128},{0,192},{65,1},{129,65},{193,129},{1,193... | collective-permute-start | bytes 1179656 | tf_op jit(solution)/shard_map/ppermute | solution.py:563
  76.8 5.3 %collective-permute-start.10 = (f32[2,8,512]{2,1,0:T(8,128)S(1)}, f32[2,8,512]{2,1,0:T(8,128)S(1)}, u32[]{:S(2)}, u32[]{:S(2)}) collective-permute-start(f32[2,8,512]{2,1,0:T(8,128)S(1)} %copy-done.14), channel_id=1, source_target_pairs={{1,0},{2,1},{3,2},{4,3},{5,4},{6,5},{7,6},{9,8},{10,9},{11,10},{12... | collective-permute-start | bytes 98312 | tf_op jit(solution)/shard_map/ppermute | solution.py:567
  78.1 5.0 %collective-permute-start.9 = (f32[2,8,512]{2,1,0:T(8,128)S(1)}, f32[2,8,512]{2,1,0:T(8,128)S(1)}, u32[]{:S(2)}, u32[]{:S(2)}) collective-permute-start(f32[2,8,512]{2,1,0:T(8,128)S(1)} %copy-done.12), channel_id=1, source_target_pairs={{0,1},{1,2},{2,3},{3,4},{4,5},{5,6},{6,7},{8,9},{9,10},{10,11},{11... | collective-permute-start | bytes 98312 | tf_op jit(solution)/shard_map/ppermute | solution.py:566
  83.1 40.3 %slice-start = ((s8[7962624]{0:T(1024)(128)(4,1)}), s8[4194304]{0:T(1024)(128)(4,1)S(1)}, s32[]{:S(2)}) async-start(s8[7962624]{0:T(1024)(128)(4,1)} %bitcast.6), calls=%async_computation.2 | async-start | bytes 8388608
  86.4 37.0 %slice-start.1 = ((s8[7962624]{0:T(1024)(128)(4,1)}), s8[3768320]{0:T(1024)(128)(4,1)S(1)}, s32[]{:S(2)}) async-start(s8[7962624]{0:T(1024)(128)(4,1)} %bitcast.6), calls=%async_computation.3 | async-start | bytes 7536640
  86.4 37.0 %copy-start.2 = (f32[2,6,16,384]{3,2,1,0:T(8,128)S(1)}, f32[2,6,16,384]{3,2,1,0:T(8,128)}, u32[]{:S(2)}) copy-start(f32[2,6,16,384]{3,2,1,0:T(8,128)} %copy-done.1) | copy-start | bytes 884740
  86.4 37.0 %copy-start.4 = (f32[6,4,8,128]{3,2,1,0:T(8,128)S(1)}, f32[6,4,8,128]{3,2,1,0:T(8,128)}, u32[]{:S(2)}) copy-start(f32[6,4,8,128]{3,2,1,0:T(8,128)} %copy-done.3) | copy-start | bytes 294916
  86.4 37.0 %copy-start.5 = (f32[384]{0:T(512)S(1)}, f32[384]{0:T(512)}, u32[]{:S(2)}) copy-start(f32[384]{0:T(512)} %b1_ref.1) | copy-start | bytes 4612
  86.4 37.0 %copy-start.6 = (f32[384]{0:T(512)S(1)}, f32[384]{0:T(512)}, u32[]{:S(2)}) copy-start(f32[384]{0:T(512)} %gain_ref.1) | copy-start | bytes 4612
  86.4 37.0 %copy-start.7 = (f32[384]{0:T(512)S(1)}, f32[384]{0:T(512)}, u32[]{:S(2)}) copy-start(f32[384]{0:T(512)} %b2_ref.1) | copy-start | bytes 4612
  86.4 37.0 %copy-start.8 = (f32[16]{0:T(128)S(1)}, f32[16]{0:T(128)}, u32[]{:S(2)}) copy-start(f32[16]{0:T(128)} %scale_ref.1) | copy-start | bytes 196
  86.4 37.0 %copy-start.9 = (f32[16]{0:T(128)S(1)}, f32[16]{0:T(128)}, u32[]{:S(2)}) copy-start(f32[16]{0:T(128)} %mean_ref.1) | copy-start | bytes 196
  86.5 6.0 %collective-permute-start.11 = (f32[1536,128]{1,0:T(8,128)S(1)}, f32[1536,128]{1,0:T(8,128)S(1)}, u32[]{:S(2)}, u32[]{:S(2)}) collective-permute-start(f32[1536,128]{1,0:T(8,128)S(1)} %shard_map.165), channel_id=1, source_target_pairs={{0,8},{8,0},{1,9},{9,1},{2,10},{10,2},{3,11},{11,3},{4,12},{12,4},... | collective-permute-start | bytes 2359304 | tf_op jit(solution)/shard_map/ppermute | solution.py:572
  115.5 5.3 %collective-permute-start.12 = (f32[16,128]{1,0:T(8,128)S(1)}, f32[16,128]{1,0:T(8,128)S(1)}, u32[]{:S(2)}, u32[]{:S(2)}) collective-permute-start(f32[16,128]{1,0:T(8,128)S(1)} %get-tuple-element.70), channel_id=1, source_target_pairs={{0,8},{8,0},{16,24},{24,16},{32,40},{40,32},{48,56},{56,48},{64,72... | collective-permute-start | bytes 24584 | tf_op jit(solution)/shard_map/ppermute | solution.py:605
  117.5 5.9 %collective-permute-start.13 = (f32[16,128]{1,0:T(8,128)S(1)}, f32[16,128]{1,0:T(8,128)S(1)}, u32[]{:S(2)}, u32[]{:S(2)}) collective-permute-start(f32[16,128]{1,0:T(8,128)S(1)} %get-tuple-element.72), channel_id=1, source_target_pairs={{8,16},{24,32},{40,48},{56,64},{72,80},{88,96},{104,112},{120,128}... | collective-permute-start | bytes 24584 | tf_op jit(solution)/shard_map/ppermute | solution.py:608
  (11 other events, 81.9 us)

commit v10 on v9

--- a/solution.py
+++ b/solution.py
@@ -202,7 +202,14 @@
     vecs,
     cells_ref,
     mid_ref,
+    w1_buf,
+    w2_buf,
+    sems,
 ):
+    fetch_first = pltpu.make_async_copy(w1_ref, w1_buf, sems.at[9])
+    fetch_first.start()
+    for tap in range(9):
+        pltpu.make_async_copy(w2_ref.at[tap], w2_buf.at[tap], sems.at[tap]).start()
     place(toks, mids, before_ref, after_ref, cells_ref, mid_ref)
     even = lax.axis_index("core") == 0
     at_row, at_col = mesh_index(SEQ), mesh_index(BLK)
@@ -249,6 +256,7 @@
     for k in range(parts):
         act[k, 0:2, :, 0:16, :] = mid_ref[:, :, :, pl.ds(k * 128, 128)]
     gain = gain_ref[...].reshape(1, C1)
+    fetch_first.wait()
     for p in range(2):
         for q in range(2):
             lanes = pl.ds((2 * p + q) * C1, C1)
@@ -256,7 +264,7 @@
             for t in range(3):
                 value = value + jnp.dot(
                     window[t * 32 : t * 32 + 128],
-                    w1_ref[t, :, lanes],
+                    w1_buf[t, :, lanes],
                     preferred_element_type=jnp.float32,
                 )
             power = jnp.mean(value * value, axis=1, keepdims=True)
@@ -285,7 +293,8 @@
     for tap in range(9):
         t, u = divmod(tap, 3)
         rows = wide[t : t + 4, u : u + 4].reshape(256, 3 * C1)
-        total = total + jnp.dot(rows, w2_ref[tap], preferred_element_type=jnp.float32)
+        pltpu.make_async_copy(w2_ref.at[tap], w2_buf.at[tap], sems.at[tap]).wait()
+        total = total + jnp.dot(rows, w2_buf[tap], preferred_element_type=jnp.float32)
     for k in range(parts):
         for f in range(F):
             for i in range(4):
@@ -298,6 +307,7 @@
 def tail(*args):
     specs = [pl.BlockSpec(memory_space=pltpu.VMEM)] * len(args)
     specs[7] = pl.BlockSpec(memory_space=pltpu.SMEM)
+    specs[10] = specs[13] = pl.BlockSpec(memory_space=pl.ANY)
     return pl.pallas_call(
         tail_kernel,
         in_specs=specs,
@@ -317,8 +327,11 @@
             pltpu.VMEM((16, 128), jnp.float32),
             pltpu.VMEM((6, 4, 8, 128), jnp.float32),
             pltpu.VMEM((2, 6, 16, C1), jnp.float32),
+            pltpu.VMEM((3, 16 * LAT, 4 * C1), jnp.bfloat16),
+            pltpu.VMEM((9, 3 * C1, C1), jnp.bfloat16),
+            pltpu.SemaphoreType.DMA((10,)),
         ],
-        compiler_params=pltpu.CompilerParams(vmem_limit_bytes=32 << 20),
+        compiler_params=pltpu.CompilerParams(vmem_limit_bytes=60 << 20),
     )(*args)
 
 
@@ -562,16 +575,15 @@
     state, left_a, right_b = lax.optimization_barrier((state, left_a, right_b))
     far = [lax.ppermute(left_a, "y", right), lax.ppermute(right_b, "y", left)]
     state = flash(moved, q_oth, [left_b, right_a], state)
-    state, to_right, to_left = lax.optimization_barrier((state, to_right, to_left))
-    before = lax.ppermute(to_right, BLK, along(BLK, 1))
-    after = lax.ppermute(to_left, BLK, along(BLK, -1))
-    state, before, after = lax.optimization_barrier((state, before, after))
     weight = weight_head.T
     oth = flash_last(q_oth, 0, far, state, 1, weight)
     oth, state = lax.optimization_barrier((oth, state))
     oth = lax.ppermute(oth, "core", swap)
     own = flash_last(moved, 2, far, state, 0, weight)
     partial = merge(own, oth).reshape(heads, 32, 128)
+    partial, to_right, to_left = lax.optimization_barrier((partial, to_right, to_left))
+    before = lax.ppermute(to_right, BLK, along(BLK, 1))
+    after = lax.ppermute(to_left, BLK, along(BLK, -1))
     parts = lax.all_to_all(partial, HEAD, split_axis=0, concat_axis=0, tiled=True)
     return head_sum(parts), (toks, mids, before, after, weight_first)
 

time: 129 us -> 126 us (0.977)
  blocking collectives: 21.8 us -> 0 us
  waiting for transfers between devices: 24.8 us -> 32.4 us
  starting transfers between devices: 42.1 us -> 47.8 us
  Pallas kernels: 34.2 us -> 39 us
    all_to_all x1 -> x0, blocking collectives: 21.8 us -> none  [attention(): lax.all_to_all(partial, HEAD, split_axis=0, concat_axis=0, tiled=True)]
    all_to_all x0 -> x1, waiting for transfers between devices: none -> 7.55 us  [attention(): lax.all_to_all(partial, HEAD, split_axis=0, concat_axis=0, tiled=True)]
    all_to_all x0 -> x1, starting transfers between devices: none -> 5.85 us  [attention(): lax.all_to_all(partial, HEAD, split_axis=0, concat_axis=0, tiled=True)]
    pallas_call x1, Pallas kernels: 4.86 us -> 8.85 us  [tail(): pl.pallas_call(tail_kernel, in_specs=specs, out_specs=[pl.BlockSpec(memor...]
    ppermute x2, waiting for transfers between devices: 0.01 us -> 1.33 us  [attention(): far = [lax.ppermute(left_a, 'y', right), lax.ppermute(right_b, 'y', left)]]
    unnamed x40 -> x26, local copies, waits for them, and re-layouts: 3.62 us -> 3.93 us
  transfers between devices with their start and end apart: 15 -> 16, of which waited for: 5 -> 6; matrix products, arithmetic and copies ran while one was open for 0% -> 0% of each run, Pallas kernels for 18% -> 18%
where the time goes in v10:
time: 126 us; the launch traced here: 125 us
  starting transfers between devices  47.8 us (38%)
  Pallas kernels  39 us (31%)
  waiting for transfers between devices  32.4 us (26%)
  local copies, waits for them, and re-layouts  4.04 us (3%)
  between operations  1.75 us (1%)
    pallas_call x3, Pallas kernels, flash(): pl.pallas_call(functools.partial(flash_kernel, state is None, False, len(...  18.7 us
    ppermute x1, waiting for transfers between devices, halo_rows(): above = lax.ppermute(down, SEQ, along(SEQ, 1))  14.6 us
    all_to_all x1, starting transfers between devices, attention(): lax.all_to_all(packed, HEAD, split_axis=0, concat_axis=0, tiled=True)  11.9 us
    pallas_call x1, Pallas kernels, tail(): pl.pallas_call(tail_kernel, in_specs=specs, out_specs=[pl.BlockSpec(memor...  8.85 us
    all_to_all x1, waiting for transfers between devices, attention(): lax.all_to_all(partial, HEAD, split_axis=0, concat_axis=0, tiled=True)  7.55 us
    pallas_call x2, Pallas kernels, flash_last(): pl.pallas_call(functools.partial(flash_kernel, False, True, len(kvs), hal...  6.46 us
    all_to_all x1, starting transfers between devices, attention(): lax.all_to_all(partial, HEAD, split_axis=0, concat_axis=0, tiled=True)  5.85 us
    ppermute x1, waiting for transfers between devices, halo_rows(): below = lax.ppermute(up, SEQ, along(SEQ, -1))  5.63 us
  transfers between devices with their start and end apart: 16, of which 6 were waited for; matrix products, arithmetic and copies ran while one was open for 0% of the time, Pallas kernels for 18%

profile of v10, /device:TPU:1, one launch (start us, length us, event | category | flops | bytes accessed | tf_op | source)
XLA Modules:
  0.0 125.0 jit_solution(4814918696887548741)
XLA Ops:
  0.7 2.4 %shard_map.158 = bf16[32,48,384]{2,1,0:T(8,128)(2,1)} custom-call(bf16[48,4096]{1,0:T(8,128)(2,1)} %q_ref.1, bf16[48,4096]{1,0:T(8,128)(2,1)} %k_ref.1, bf16[48,4096]{1,0:T(8,128)(2,1)} %v_ref.1), custom_call_target="tpu_custom_call" | custom-call | tf_op jit(solution)/shard_map/pallas_call | solution.py:486
  3.1 11.9 %all-to-all-start = ((bf16[32,48,384]{2,1,0:T(8,128)(2,1)}), bf16[32,48,384]{2,1,0:T(8,128)(2,1)S(1)}, u32[]{:S(2)}, u32[]{:S(2)}) async-start(bf16[32,48,384]{2,1,0:T(8,128)(2,1)} %shard_map.158), calls=%async_computation | async-start | bytes 2359296 | tf_op jit(solution)/shard_map/all_to_all | solution.py:558
  15.2 5.2 %collective-permute-start = (f32[2,16,512]{2,1,0:T(8,128)S(1)}, f32[2,16,512]{2,1,0:T(8,128)S(1)}, u32[]{:S(2)}, u32[]{:S(2)}) collective-permute-start(f32[2,16,512]{2,1,0:T(8,128)S(1)} %get-tuple-element.43), channel_id=1, source_target_pairs={{0,8},{8,16},{16,24},{24,32},{32,40},{40,48},{48,56},{56,64},{64,7... | collective-permute-start | bytes 196616 | tf_op jit(solution)/shard_map/ppermute | solution.py:466
  20.4 1.9 %collective-permute-start.1 = (f32[2,16,512]{2,1,0:T(8,128)S(1)}, f32[2,16,512]{2,1,0:T(8,128)S(1)}, u32[]{:S(2)}, u32[]{:S(2)}) collective-permute-start(f32[2,16,512]{2,1,0:T(8,128)S(1)} %get-tuple-element.44), channel_id=1, source_target_pairs={{8,0},{16,8},{24,16},{32,24},{40,32},{48,40},{56,48},{64,56},{72,6... | collective-permute-start | bytes 196616 | tf_op jit(solution)/shard_map/ppermute | solution.py:467
  24.0 14.6 %collective-permute-done.above_ref = f32[2,16,512]{2,1,0:T(8,128)S(1)} collective-permute-done((f32[2,16,512]{2,1,0:T(8,128)S(1)}, f32[2,16,512]{2,1,0:T(8,128)S(1)}, u32[]{:S(2)}, u32[]{:S(2)}) %collective-permute-start) | collective-permute-done | bytes 65568 | tf_op jit(solution)/shard_map/ppermute | solution.py:466
  38.6 5.6 %collective-permute-done.1.below_ref = f32[2,16,512]{2,1,0:T(8,128)S(1)} collective-permute-done((f32[2,16,512]{2,1,0:T(8,128)S(1)}, f32[2,16,512]{2,1,0:T(8,128)S(1)}, u32[]{:S(2)}, u32[]{:S(2)}) %collective-permute-start.1) | collective-permute-done | bytes 65568 | tf_op jit(solution)/shard_map/ppermute | solution.py:467
  45.8 2.9 %collective-permute-start.2 = (bf16[1536,128]{1,0:T(8,128)(2,1)S(1)}, bf16[1536,128]{1,0:T(8,128)(2,1)S(1)}, u32[]{:S(2)}, u32[]{:S(2)}) collective-permute-start(bf16[1536,128]{1,0:T(8,128)(2,1)S(1)} %slice.14), channel_id=1, source_target_pairs={{0,8},{8,0},{1,9},{9,1},{2,10},{10,2},{3,11},{11,3},{4,12},{12,4},... | collective-permute-start | bytes 1179656 | tf_op jit(solution)/shard_map/ppermute | solution.py:568
  50.0 1.4 %collective-permute-start.4 = (bf16[768,256]{1,0:T(8,128)(2,1)S(1)}, bf16[768,256]{1,0:T(8,128)(2,1)S(1)}, u32[]{:S(2)}, u32[]{:S(2)}) collective-permute-start(bf16[768,256]{1,0:T(8,128)(2,1)S(1)} %get-tuple-element.56), channel_id=1, source_target_pairs={{64,0},{128,64},{192,128},{0,192},{65,1},{129,65},{193,129},{1,193... | collective-permute-start | bytes 1179656 | tf_op jit(solution)/shard_map/ppermute | solution.py:567
  51.4 6.1 %shard_map.162.refs_4_ = f32[3072,256]{1,0:T(8,128)S(1)} custom-call(bf16[1536,384]{1,0:T(8,128)(2,1)S(1)} %bitcast.8, bf16[1536,128]{1,0:T(8,128)(2,1)S(1)} %collective-permute-done.2.refs_1_.refs_0_, bf16[1536,384]{1,0:T(8,128)(2,1)S(1)} %bitcast.9), custom_call_target="tpu_custom_call" | custom-call | flops 4831838208 | bytes 6291456 | tf_op jit(solution)/shard_map/pallas_call | solution.py:135
  57.7 2.6 %collective-permute-start.8 = (bf16[768,256]{1,0:T(8,128)(2,1)S(1)}, bf16[768,256]{1,0:T(8,128)(2,1)S(1)}, u32[]{:S(2)}, u32[]{:S(2)}) collective-permute-start(bf16[768,256]{1,0:T(8,128)(2,1)S(1)} %get-tuple-element.57), channel_id=1, source_target_pairs={{64,0},{128,64},{192,128},{0,192},{65,1},{129,65},{193,129},{1,193... | collective-permute-start | bytes 1179656 | tf_op jit(solution)/shard_map/ppermute | solution.py:573
  60.7 6.3 %shard_map.163.refs_4_ = f32[3072,256]{1,0:T(8,128)S(1)} custom-call(bf16[1536,384]{1,0:T(8,128)(2,1)S(1)} %bitcast.10, bf16[1536,128]{1,0:T(8,128)(2,1)S(1)} %collective-permute-done.2.refs_1_.refs_0_, bf16[768,256]{1,0:T(8,128)(2,1)S(1)} %collective-permute-done.3.refs_2_, bf16[768,256]{1,0:T(8,128)(2,1)S(1)} %collective-permute-done.4.refs_3_, ...), custom_call_target="tpu_custom_call" | custom-call | flops 4831838208 | bytes 6291456 | tf_op jit(solution)/shard_map/pallas_call | solution.py:135
  68.2 1.7 %collective-permute-start.6 = (bf16[768,256]{1,0:T(8,128)(2,1)S(1)}, bf16[768,256]{1,0:T(8,128)(2,1)S(1)}, u32[]{:S(2)}, u32[]{:S(2)}) collective-permute-start(bf16[768,256]{1,0:T(8,128)(2,1)S(1)} %collective-permute-done.4.refs_3_), channel_id=1, source_target_pairs={{64,0},{128,64},{192,128},{0,192},{65,1},{129,65},{193,129},{1,193... | collective-permute-start | bytes 1179656 | tf_op jit(solution)/shard_map/ppermute | solution.py:576
  69.9 6.3 %shard_map.164.refs_3_ = f32[3072,256]{1,0:T(8,128)S(1)} custom-call(bf16[1536,384]{1,0:T(8,128)(2,1)S(1)} %bitcast.11, bf16[1536,128]{1,0:T(8,128)(2,1)S(1)} %collective-permute-done.2.refs_1_.refs_0_, bf16[768,256]{1,0:T(8,128)(2,1)S(1)} %collective-permute-done.7.refs_2_, bf16[768,256]{1,0:T(8,128)(2,1)S(1)} %collective-permute-done.8.refs_3_, ...), custom_call_target="tpu_custom_call" | custom-call | flops 4831838208 | bytes 6291456 | tf_op jit(solution)/shard_map/pallas_call | solution.py:135
  77.6 3.2 %shard_map.165 = f32[1536,128]{1,0:T(8,128)S(1)} custom-call(bf16[1536,128]{1,0:T(8,128)(2,1)S(1)} %collective-permute-done.2.refs_1_.refs_0_, bf16[768,256]{1,0:T(8,128)(2,1)S(1)} %collective-permute-done.5.refs_1_, bf16[768,256]{1,0:T(8,128)(2,1)S(1)} %collective-permute-done.6.refs_2_, f32[3072,256]{1,0:T(8,128)S(1)} %shard_map.164.refs_3_, ...), custom_call_target="tpu_custom_call" | custom-call | flops 2415919104 | bytes 3145728 | tf_op jit(solution)/shard_map/pallas_call | solution.py:156
  80.8 2.7 %collective-permute-start.9 = (f32[1536,128]{1,0:T(8,128)S(1)}, f32[1536,128]{1,0:T(8,128)S(1)}, u32[]{:S(2)}, u32[]{:S(2)}) collective-permute-start(f32[1536,128]{1,0:T(8,128)S(1)} %shard_map.165), channel_id=1, source_target_pairs={{0,8},{8,0},{1,9},{9,1},{2,10},{10,2},{3,11},{11,3},{4,12},{12,4},... | collective-permute-start | bytes 2359304 | tf_op jit(solution)/shard_map/ppermute | solution.py:581
  83.5 3.2 %shard_map.166.own_ref = f32[1536,128]{1,0:T(8,128)S(1)} custom-call(bf16[1536,384]{1,0:T(8,128)(2,1)S(1)} %bitcast.12, bf16[768,256]{1,0:T(8,128)(2,1)S(1)} %collective-permute-done.5.refs_1_, bf16[768,256]{1,0:T(8,128)(2,1)S(1)} %collective-permute-done.6.refs_2_, f32[3072,256]{1,0:T(8,128)S(1)} %shard_map.164.refs_3_, bf16[64,4096]{1,0:T(8,128)(2,1)S(1)} %bitcast.14), custom_call_target="tpu_custom_call" | custom-call | flops 2415919104 | bytes 3145728 | tf_op jit(solution)/shard_map/pallas_call | solution.py:156
  86.8 1.9 %shard_map.167 = bf16[4,8,32,128]{3,2,1,0:T(8,128)(2,1)} custom-call(f32[1536,128]{1,0:T(8,128)S(1)} %shard_map.166.own_ref, f32[1536,128]{1,0:T(8,128)S(1)} %collective-permute-done.9.oth_ref), custom_call_target="tpu_custom_call" | custom-call | tf_op jit(solution)/shard_map/pallas_call | solution.py:524
  88.7 5.9 %all-to-all-start.1 = ((bf16[32,32,128]{2,1,0:T(8,128)(2,1)}), bf16[32,32,128]{2,1,0:T(8,128)(2,1)S(1)}, u32[]{:S(2)}, u32[]{:S(2)}) async-start(bf16[32,32,128]{2,1,0:T(8,128)(2,1)} %bitcast.2), calls=%async_computation.1 | async-start | bytes 524288 | tf_op jit(solution)/shard_map/all_to_all | solution.py:587
  94.5 3.1 %collective-permute-start.12 = (f32[2,8,512]{2,1,0:T(8,128)S(1)}, f32[2,8,512]{2,1,0:T(8,128)S(1)}, u32[]{:S(2)}, u32[]{:S(2)}) collective-permute-start(f32[2,8,512]{2,1,0:T(8,128)S(1)} %get-tuple-element.69), channel_id=1, source_target_pairs={{0,1},{1,2},{2,3},{3,4},{4,5},{5,6},{6,7},{8,9},{9,10},{10,11},{11... | collective-permute-start | bytes 98312 | tf_op jit(solution)/shard_map/ppermute | solution.py:585
  99.0 7.6 %all-to-all-done.1.parts_ref = bf16[32,32,128]{2,1,0:T(8,128)(2,1)S(1)} async-done(((bf16[32,32,128]{2,1,0:T(8,128)(2,1)}), bf16[32,32,128]{2,1,0:T(8,128)(2,1)S(1)}, u32[]{:S(2)}, u32[]{:S(2)}) %all-to-all-start.1) | async-done | bytes 262176 | tf_op jit(solution)/shard_map/all_to_all | solution.py:587
  107.2 2.3 %collective-permute-start.10 = (f32[16,128]{1,0:T(8,128)S(1)}, f32[16,128]{1,0:T(8,128)S(1)}, u32[]{:S(2)}, u32[]{:S(2)}) collective-permute-start(f32[16,128]{1,0:T(8,128)S(1)} %get-tuple-element.64), channel_id=1, source_target_pairs={{0,8},{8,0},{16,24},{24,16},{32,40},{40,32},{48,56},{56,48},{64,72... | collective-permute-start | bytes 24584 | tf_op jit(solution)/shard_map/ppermute | solution.py:617
  109.5 2.2 %collective-permute-start.11 = (f32[16,128]{1,0:T(8,128)S(1)}, f32[16,128]{1,0:T(8,128)S(1)}, u32[]{:S(2)}, u32[]{:S(2)}) collective-permute-start(f32[16,128]{1,0:T(8,128)S(1)} %get-tuple-element.66), channel_id=1, source_target_pairs={{8,16},{24,32},{40,48},{56,64},{72,80},{88,96},{104,112},{120,128}... | collective-permute-start | bytes 24584 | tf_op jit(solution)/shard_map/ppermute | solution.py:620
  112.4 2.9 %collective-permute-done.11.apart_ref = f32[16,128]{1,0:T(8,128)S(1)} collective-permute-done((f32[16,128]{1,0:T(8,128)S(1)}, f32[16,128]{1,0:T(8,128)S(1)}, u32[]{:S(2)}, u32[]{:S(2)}) %collective-permute-start.11) | collective-permute-done | bytes 8224 | tf_op jit(solution)/shard_map/ppermute | solution.py:620
  116.0 8.8 %shard_map.169 = (f32[4,12,4,16]{3,2,1,0:T(4,128)}, bf16[4,12,4,384]{3,2,1,0:T(4,128)(2,1)}) custom-call(f32[16,128]{1,0:T(8,128)} %copy-done.11, f32[32,128]{1,0:T(8,128)} %copy-done.4, f32[16,128]{1,0:T(8,128)} %copy-done.12, f32[6,4,8,128]{3,2,1,0:T(8,128)} %copy-done.3, f32[2,6,16,384]{3,2,1,0:T(8,128)} %copy-done.2, f32[2,8,512]{2,1,0:T(8,128)} %copy-done.8, ...), custom_call_target="tpu_custom_call" | custom-call | tf_op jit(solution)/shard_map/pallas_call | solution.py:311
  (51 shorter events, 10.3 us)
Async XLA Ops:
  0.6 14.3 %copy-start.6 = (f32[4,4,12,16]{3,1,2,0:T(4,128)S(1)}, f32[4,4,12,16]{3,1,2,0:T(4,128)}, u32[]{:S(2)}) copy-start(f32[4,4,12,16]{3,1,2,0:T(4,128)} %param.19) | copy-start | bytes 36868
  0.6 14.4 %copy-start.10 = (bf16[2,4,12,16]{3,1,2,0:T(4,128)(2,1)S(1)}, bf16[2,4,12,16]{3,1,2,0:T(4,128)(2,1)}, u32[]{:S(2)}) copy-start(bf16[2,4,12,16]{3,1,2,0:T(4,128)(2,1)} %param.23) | copy-start | bytes 9220
  0.7 21.6 %copy-start.1 = (bf16[3,3,3,16,384]{4,3,2,1,0:T(8,128)(2,1)S(1)}, bf16[3,3,3,16,384]{4,3,2,1,0:T(8,128)(2,1)}, u32[]{:S(2)}) copy-start(bf16[3,3,3,16,384]{4,3,2,1,0:T(8,128)(2,1)} %w_ref) | copy-start | bytes 995332
  0.7 14.3 %copy-start.7 = (bf16[2,4,12,384]{3,1,2,0:T(4,128)(2,1)S(1)}, bf16[2,4,12,384]{3,1,2,0:T(4,128)(2,1)}, u32[]{:S(2)}) copy-start(bf16[2,4,12,384]{3,1,2,0:T(4,128)(2,1)} %param.27) | copy-start | bytes 221188
  3.1 42.6 %all-to-all-start = ((bf16[32,48,384]{2,1,0:T(8,128)(2,1)}), bf16[32,48,384]{2,1,0:T(8,128)(2,1)S(1)}, u32[]{:S(2)}, u32[]{:S(2)}) async-start(bf16[32,48,384]{2,1,0:T(8,128)(2,1)} %shard_map.158), calls=%async_computation | async-start | bytes 2359296 | tf_op jit(solution)/shard_map/all_to_all | solution.py:558
  15.2 23.4 %collective-permute-start = (f32[2,16,512]{2,1,0:T(8,128)S(1)}, f32[2,16,512]{2,1,0:T(8,128)S(1)}, u32[]{:S(2)}, u32[]{:S(2)}) collective-permute-start(f32[2,16,512]{2,1,0:T(8,128)S(1)} %get-tuple-element.43), channel_id=1, source_target_pairs={{0,8},{8,16},{16,24},{24,32},{32,40},{40,48},{48,56},{56,64},{64,7... | collective-permute-start | bytes 196616 | tf_op jit(solution)/shard_map/ppermute | solution.py:466
  20.4 23.8 %collective-permute-start.1 = (f32[2,16,512]{2,1,0:T(8,128)S(1)}, f32[2,16,512]{2,1,0:T(8,128)S(1)}, u32[]{:S(2)}, u32[]{:S(2)}) collective-permute-start(f32[2,16,512]{2,1,0:T(8,128)S(1)} %get-tuple-element.44), channel_id=1, source_target_pairs={{8,0},{16,8},{24,16},{32,24},{40,32},{48,40},{56,48},{64,56},{72,6... | collective-permute-start | bytes 196616 | tf_op jit(solution)/shard_map/ppermute | solution.py:467
  45.8 5.6 %collective-permute-start.2 = (bf16[1536,128]{1,0:T(8,128)(2,1)S(1)}, bf16[1536,128]{1,0:T(8,128)(2,1)S(1)}, u32[]{:S(2)}, u32[]{:S(2)}) collective-permute-start(bf16[1536,128]{1,0:T(8,128)(2,1)S(1)} %slice.14), channel_id=1, source_target_pairs={{0,8},{8,0},{1,9},{9,1},{2,10},{10,2},{3,11},{11,3},{4,12},{12,4},... | collective-permute-start | bytes 1179656 | tf_op jit(solution)/shard_map/ppermute | solution.py:568
  48.7 12.0 %collective-permute-start.3 = (bf16[768,256]{1,0:T(8,128)(2,1)S(1)}, bf16[768,256]{1,0:T(8,128)(2,1)S(1)}, u32[]{:S(2)}, u32[]{:S(2)}) collective-permute-start(bf16[768,256]{1,0:T(8,128)(2,1)S(1)} %get-tuple-element.57), channel_id=1, source_target_pairs={{0,64},{64,128},{128,192},{192,0},{1,65},{65,129},{129,193},{193,1... | collective-permute-start | bytes 1179656 | tf_op jit(solution)/shard_map/ppermute | solution.py:566
  50.0 10.7 %collective-permute-start.4 = (bf16[768,256]{1,0:T(8,128)(2,1)S(1)}, bf16[768,256]{1,0:T(8,128)(2,1)S(1)}, u32[]{:S(2)}, u32[]{:S(2)}) collective-permute-start(bf16[768,256]{1,0:T(8,128)(2,1)S(1)} %get-tuple-element.56), channel_id=1, source_target_pairs={{64,0},{128,64},{192,128},{0,192},{65,1},{129,65},{193,129},{1,193... | collective-permute-start | bytes 1179656 | tf_op jit(solution)/shard_map/ppermute | solution.py:567
  57.5 12.4 %collective-permute-start.7 = (bf16[768,256]{1,0:T(8,128)(2,1)S(1)}, bf16[768,256]{1,0:T(8,128)(2,1)S(1)}, u32[]{:S(2)}, u32[]{:S(2)}) collective-permute-start(bf16[768,256]{1,0:T(8,128)(2,1)S(1)} %get-tuple-element.56), channel_id=1, source_target_pairs={{0,64},{64,128},{128,192},{192,0},{1,65},{65,129},{129,193},{193,1... | collective-permute-start | bytes 1179656 | tf_op jit(solution)/shard_map/ppermute | solution.py:572
  57.7 12.3 %collective-permute-start.8 = (bf16[768,256]{1,0:T(8,128)(2,1)S(1)}, bf16[768,256]{1,0:T(8,128)(2,1)S(1)}, u32[]{:S(2)}, u32[]{:S(2)}) collective-permute-start(bf16[768,256]{1,0:T(8,128)(2,1)S(1)} %get-tuple-element.57), channel_id=1, source_target_pairs={{64,0},{128,64},{192,128},{0,192},{65,1},{129,65},{193,129},{1,193... | collective-permute-start | bytes 1179656 | tf_op jit(solution)/shard_map/ppermute | solution.py:573
  67.0 10.6 %copy-start.5 = (bf16[4096,64]{0,1:T(8,128)(2,1)S(1)}, bf16[4096,64]{0,1:T(8,128)(2,1)}, u32[]{:S(2)}) copy-start(bf16[4096,64]{0,1:T(8,128)(2,1)} %param.18) | copy-start | bytes 1572868
  67.0 10.6 %collective-permute-start.5 = (bf16[768,256]{1,0:T(8,128)(2,1)S(1)}, bf16[768,256]{1,0:T(8,128)(2,1)S(1)}, u32[]{:S(2)}, u32[]{:S(2)}) collective-permute-start(bf16[768,256]{1,0:T(8,128)(2,1)S(1)} %collective-permute-done.3.refs_2_), channel_id=1, source_target_pairs={{0,64},{64,128},{128,192},{192,0},{1,65},{65,129},{129,193},{193,1... | collective-permute-start | bytes 1179656 | tf_op jit(solution)/shard_map/ppermute | solution.py:576
  68.2 9.4 %collective-permute-start.6 = (bf16[768,256]{1,0:T(8,128)(2,1)S(1)}, bf16[768,256]{1,0:T(8,128)(2,1)S(1)}, u32[]{:S(2)}, u32[]{:S(2)}) collective-permute-start(bf16[768,256]{1,0:T(8,128)(2,1)S(1)} %collective-permute-done.4.refs_3_), channel_id=1, source_target_pairs={{64,0},{128,64},{192,128},{0,192},{65,1},{129,65},{193,129},{1,193... | collective-permute-start | bytes 1179656 | tf_op jit(solution)/shard_map/ppermute | solution.py:576
  80.8 6.0 %collective-permute-start.9 = (f32[1536,128]{1,0:T(8,128)S(1)}, f32[1536,128]{1,0:T(8,128)S(1)}, u32[]{:S(2)}, u32[]{:S(2)}) collective-permute-start(f32[1536,128]{1,0:T(8,128)S(1)} %shard_map.165), channel_id=1, source_target_pairs={{0,8},{8,0},{1,9},{9,1},{2,10},{10,2},{3,11},{11,3},{4,12},{12,4},... | collective-permute-start | bytes 2359304 | tf_op jit(solution)/shard_map/ppermute | solution.py:581
  88.7 17.9 %all-to-all-start.1 = ((bf16[32,32,128]{2,1,0:T(8,128)(2,1)}), bf16[32,32,128]{2,1,0:T(8,128)(2,1)S(1)}, u32[]{:S(2)}, u32[]{:S(2)}) async-start(bf16[32,32,128]{2,1,0:T(8,128)(2,1)} %bitcast.2), calls=%async_computation.1 | async-start | bytes 524288 | tf_op jit(solution)/shard_map/all_to_all | solution.py:587
  94.5 17.8 %collective-permute-start.12 = (f32[2,8,512]{2,1,0:T(8,128)S(1)}, f32[2,8,512]{2,1,0:T(8,128)S(1)}, u32[]{:S(2)}, u32[]{:S(2)}) collective-permute-start(f32[2,8,512]{2,1,0:T(8,128)S(1)} %get-tuple-element.69), channel_id=1, source_target_pairs={{0,1},{1,2},{2,3},{3,4},{4,5},{5,6},{6,7},{8,9},{9,10},{10,11},{11... | collective-permute-start | bytes 98312 | tf_op jit(solution)/shard_map/ppermute | solution.py:585
  97.7 14.7 %collective-permute-start.13 = (f32[2,8,512]{2,1,0:T(8,128)S(1)}, f32[2,8,512]{2,1,0:T(8,128)S(1)}, u32[]{:S(2)}, u32[]{:S(2)}) collective-permute-start(f32[2,8,512]{2,1,0:T(8,128)S(1)} %get-tuple-element.70), channel_id=1, source_target_pairs={{1,0},{2,1},{3,2},{4,3},{5,4},{6,5},{7,6},{9,8},{10,9},{11,10},{12... | collective-permute-start | bytes 98312 | tf_op jit(solution)/shard_map/ppermute | solution.py:586
  107.2 5.2 %collective-permute-start.10 = (f32[16,128]{1,0:T(8,128)S(1)}, f32[16,128]{1,0:T(8,128)S(1)}, u32[]{:S(2)}, u32[]{:S(2)}) collective-permute-start(f32[16,128]{1,0:T(8,128)S(1)} %get-tuple-element.64), channel_id=1, source_target_pairs={{0,8},{8,0},{16,24},{24,16},{32,40},{40,32},{48,56},{56,48},{64,72... | collective-permute-start | bytes 24584 | tf_op jit(solution)/shard_map/ppermute | solution.py:617
  109.5 5.9 %collective-permute-start.11 = (f32[16,128]{1,0:T(8,128)S(1)}, f32[16,128]{1,0:T(8,128)S(1)}, u32[]{:S(2)}, u32[]{:S(2)}) collective-permute-start(f32[16,128]{1,0:T(8,128)S(1)} %get-tuple-element.66), channel_id=1, source_target_pairs={{8,16},{24,32},{40,48},{56,64},{72,80},{88,96},{104,112},{120,128}... | collective-permute-start | bytes 24584 | tf_op jit(solution)/shard_map/ppermute | solution.py:620
  112.4 3.0 %copy-start.8 = (f32[2,8,512]{2,1,0:T(8,128)}, f32[2,8,512]{2,1,0:T(8,128)S(1)}, u32[]{:S(2)}) copy-start(f32[2,8,512]{2,1,0:T(8,128)S(1)} %collective-permute-done.12.before_ref) | copy-start | bytes 98308
  112.4 3.0 %copy-start.9 = (f32[2,8,512]{2,1,0:T(8,128)}, f32[2,8,512]{2,1,0:T(8,128)S(1)}, u32[]{:S(2)}) copy-start(f32[2,8,512]{2,1,0:T(8,128)S(1)} %collective-permute-done.13.after_ref) | copy-start | bytes 98308
  112.4 3.0 %copy-start.11 = (f32[16,128]{1,0:T(8,128)}, f32[16,128]{1,0:T(8,128)S(1)}, u32[]{:S(2)}) copy-start(f32[16,128]{1,0:T(8,128)S(1)} %collective-permute-done.10.near_ref) | copy-start | bytes 24580
  (5 other events, 3.9 us)

commit v11 on v10

--- a/solution.py
+++ b/solution.py
@@ -206,10 +206,9 @@
     w2_buf,
     sems,
 ):
-    fetch_first = pltpu.make_async_copy(w1_ref, w1_buf, sems.at[9])
-    fetch_first.start()
     for tap in range(9):
         pltpu.make_async_copy(w2_ref.at[tap], w2_buf.at[tap], sems.at[tap]).start()
+    window_weights(w1_ref, w1_buf)
     place(toks, mids, before_ref, after_ref, cells_ref, mid_ref)
     even = lax.axis_index("core") == 0
     at_row, at_col = mesh_index(SEQ), mesh_index(BLK)
@@ -256,7 +255,6 @@
     for k in range(parts):
         act[k, 0:2, :, 0:16, :] = mid_ref[:, :, :, pl.ds(k * 128, 128)]
     gain = gain_ref[...].reshape(1, C1)
-    fetch_first.wait()
     for p in range(2):
         for q in range(2):
             lanes = pl.ds((2 * p + q) * C1, C1)
@@ -307,7 +305,7 @@
 def tail(*args):
     specs = [pl.BlockSpec(memory_space=pltpu.VMEM)] * len(args)
     specs[7] = pl.BlockSpec(memory_space=pltpu.SMEM)
-    specs[10] = specs[13] = pl.BlockSpec(memory_space=pl.ANY)
+    specs[13] = pl.BlockSpec(memory_space=pl.ANY)
     return pl.pallas_call(
         tail_kernel,
         in_specs=specs,
@@ -329,13 +327,13 @@
             pltpu.VMEM((2, 6, 16, C1), jnp.float32),
             pltpu.VMEM((3, 16 * LAT, 4 * C1), jnp.bfloat16),
             pltpu.VMEM((9, 3 * C1, C1), jnp.bfloat16),
-            pltpu.SemaphoreType.DMA((10,)),
+            pltpu.SemaphoreType.DMA((9,)),
         ],
-        compiler_params=pltpu.CompilerParams(vmem_limit_bytes=60 << 20),
+        compiler_params=pltpu.CompilerParams(vmem_limit_bytes=53 << 20),
     )(*args)
 
 
-def window_kernel(w_ref, out_ref):
+def window_weights(w_ref, out_ref):
     out_ref[...] = jnp.zeros(out_ref.shape, out_ref.dtype)
     for t in range(3):
         for u in range(3):
@@ -346,14 +344,6 @@
                         (dr, a), (dc, b) = divmod(p + u, 2), divmod(q + v, 2)
                         at = dr * 128 + dc * 64 + a * 32 + b * 16
                         out_ref[t, pl.ds(at, LAT), pl.ds((2 * p + q) * C1, C1)] = taps
-
-
-def window_weights(weight):
-    return pl.pallas_call(
-        window_kernel,
-        out_shape=jax.ShapeDtypeStruct((3, 16 * LAT, 4 * C1), jnp.bfloat16),
-        compiler_params=pltpu.CompilerParams(vmem_limit_bytes=16 << 20),
-    )(weight)
 
 
 def put_frames(ref, rows, tokens):
@@ -551,9 +541,8 @@
 def attention(query_vectors, key_vectors, value_vectors, weight_head, inputs):
     packed = pack(query_vectors, key_vectors, value_vectors)
     packed, inputs = lax.optimization_barrier((packed, inputs))
-    noisy, cache_in, cache_mid, weight_in = inputs
+    noisy, cache_in, cache_mid = inputs
     rows = halo_rows(noisy, cache_in, cache_mid)
-    weight_first = window_weights(weight_in)
     heads, tokens = packed.shape[:2]
     moved = lax.all_to_all(packed, HEAD, split_axis=0, concat_axis=0, tiled=True)
     moved = moved.reshape(heads * tokens, 3 * HEAD_DIM)
@@ -562,7 +551,7 @@
     left = [((i + 1) % 4, i) for i in range(4)]
     mid = moved.shape[0] // 2
     a, b, q_own = moved[:mid, :256], moved[mid:, :256], moved[:, 256:]
-    a, b, q_own, rows, weight_first = lax.optimization_barrier((a, b, q_own, rows, weight_first))
+    a, b, q_own, rows = lax.optimization_barrier((a, b, q_own, rows))
     left_a = lax.ppermute(a, "y", right)
     right_b = lax.ppermute(b, "y", left)
     q_oth = lax.ppermute(q_own, "core", swap)
@@ -585,7 +574,7 @@
     before = lax.ppermute(to_right, BLK, along(BLK, 1))
     after = lax.ppermute(to_left, BLK, along(BLK, -1))
     parts = lax.all_to_all(partial, HEAD, split_axis=0, concat_axis=0, tiled=True)
-    return head_sum(parts), (toks, mids, before, after, weight_first)
+    return head_sum(parts), (toks, mids, before, after)
 
 
 def shards(
@@ -605,12 +594,12 @@
     weight_mid,
     bias_mid,
 ):
-    (mine, near, apart), (toks, mids, before, after, weight_first) = attention(
+    (mine, near, apart), (toks, mids, before, after) = attention(
         query_vectors,
         key_vectors,
         value_vectors,
         weight_head,
-        (noisy_latent, cache_in, cache_mid, weight_in),
+        (noisy_latent, cache_in, cache_mid),
     )
 
     count = lax.axis_size(SEQ)
@@ -629,7 +618,7 @@
         noise_level,
         latent_scale,
         latent_mean,
-        weight_first,
+        weight_in,
         bias_in,
         norm_gain,
         weight_mid.reshape(9, 3 * C1, C1),

time: 126 us -> 121 us (0.960)
  local copies, waits for them, and re-layouts: 4.04 us -> 0.17 us
  Pallas kernels: 39 us -> 36.6 us
  waiting for transfers between devices: 32.4 us -> 34.1 us
    unnamed x26 -> x20, local copies, waits for them, and re-layouts: 3.93 us -> 0.05 us
    pallas_call x1, Pallas kernels: 8.85 us -> 6.84 us  [tail(): pl.pallas_call(tail_kernel, in_specs=specs, out_specs=[pl.BlockSpec(memor...]
    ppermute x1, waiting for transfers between devices: 14.6 us -> 16.3 us  [halo_rows(): above = lax.ppermute(down, SEQ, along(SEQ, 1))]
    ppermute x1, starting transfers between devices: 2.89 us -> 4.2 us  [attention(): q_oth = lax.ppermute(q_own, 'core', swap)]
  transfers between devices with their start and end apart: 16 -> 16, of which waited for: 6 -> 6; matrix products, arithmetic and copies ran while one was open for 0% -> 0% of each run, Pallas kernels for 18% -> 19%
where the time goes in v11:
time: 121 us; the launch traced here: 120 us
  starting transfers between devices  47.7 us (39%)
  Pallas kernels  36.6 us (30%)
  waiting for transfers between devices  34.1 us (28%)
  between operations  1.76 us (1%)
    pallas_call x3, Pallas kernels, flash(): pl.pallas_call(functools.partial(flash_kernel, state is None, False, len(...  18.7 us
    ppermute x1, waiting for transfers between devices, halo_rows(): above = lax.ppermute(down, SEQ, along(SEQ, 1))  16.3 us
    all_to_all x1, starting transfers between devices, attention(): lax.all_to_all(packed, HEAD, split_axis=0, concat_axis=0, tiled=True)  11.9 us
    all_to_all x1, waiting for transfers between devices, attention(): lax.all_to_all(partial, HEAD, split_axis=0, concat_axis=0, tiled=True)  7.55 us
    pallas_call x1, Pallas kernels, tail(): pl.pallas_call(tail_kernel, in_specs=specs, out_specs=[pl.BlockSpec(memor...  6.84 us
    pallas_call x2, Pallas kernels, flash_last(): pl.pallas_call(functools.partial(flash_kernel, False, True, len(kvs), hal...  6.46 us
    ppermute x1, waiting for transfers between devices, halo_rows(): below = lax.ppermute(up, SEQ, along(SEQ, -1))  5.63 us
    ppermute x1, starting transfers between devices, halo_rows(): above = lax.ppermute(down, SEQ, along(SEQ, 1))  5.15 us
  transfers between devices with their start and end apart: 16, of which 6 were waited for; matrix products, arithmetic and copies ran while one was open for 0% of the time, Pallas kernels for 19%

profile of v11, /device:TPU:1, one launch (start us, length us, event | category | flops | bytes accessed | tf_op | source)
XLA Modules:
  0.0 120.4 jit_solution(4360199064817734403)
XLA Ops:
  0.7 2.3 %shard_map.158 = bf16[32,48,384]{2,1,0:T(8,128)(2,1)} custom-call(bf16[48,4096]{1,0:T(8,128)(2,1)} %q_ref.1, bf16[48,4096]{1,0:T(8,128)(2,1)} %k_ref.1, bf16[48,4096]{1,0:T(8,128)(2,1)} %v_ref.1), custom_call_target="tpu_custom_call" | custom-call | tf_op jit(solution)/shard_map/pallas_call | solution.py:476
  3.0 11.9 %all-to-all-start = ((bf16[32,48,384]{2,1,0:T(8,128)(2,1)}), bf16[32,48,384]{2,1,0:T(8,128)(2,1)S(1)}, u32[]{:S(2)}, u32[]{:S(2)}) async-start(bf16[32,48,384]{2,1,0:T(8,128)(2,1)} %shard_map.158), calls=%async_computation | async-start | bytes 2359296 | tf_op jit(solution)/shard_map/all_to_all | solution.py:547
  15.1 5.2 %collective-permute-start = (f32[2,16,512]{2,1,0:T(8,128)S(1)}, f32[2,16,512]{2,1,0:T(8,128)S(1)}, u32[]{:S(2)}, u32[]{:S(2)}) collective-permute-start(f32[2,16,512]{2,1,0:T(8,128)S(1)} %get-tuple-element.41), channel_id=1, source_target_pairs={{0,8},{8,16},{16,24},{24,32},{32,40},{40,48},{48,56},{56,64},{64,7... | collective-permute-start | bytes 196616 | tf_op jit(solution)/shard_map/ppermute | solution.py:456
  20.3 1.9 %collective-permute-start.1 = (f32[2,16,512]{2,1,0:T(8,128)S(1)}, f32[2,16,512]{2,1,0:T(8,128)S(1)}, u32[]{:S(2)}, u32[]{:S(2)}) collective-permute-start(f32[2,16,512]{2,1,0:T(8,128)S(1)} %get-tuple-element.42), channel_id=1, source_target_pairs={{8,0},{16,8},{24,16},{32,24},{40,32},{48,40},{56,48},{64,56},{72,6... | collective-permute-start | bytes 196616 | tf_op jit(solution)/shard_map/ppermute | solution.py:457
  22.2 16.3 %collective-permute-done.above_ref = f32[2,16,512]{2,1,0:T(8,128)S(1)} collective-permute-done((f32[2,16,512]{2,1,0:T(8,128)S(1)}, f32[2,16,512]{2,1,0:T(8,128)S(1)}, u32[]{:S(2)}, u32[]{:S(2)}) %collective-permute-start) | collective-permute-done | bytes 65568 | tf_op jit(solution)/shard_map/ppermute | solution.py:456
  38.5 5.6 %collective-permute-done.1.below_ref = f32[2,16,512]{2,1,0:T(8,128)S(1)} collective-permute-done((f32[2,16,512]{2,1,0:T(8,128)S(1)}, f32[2,16,512]{2,1,0:T(8,128)S(1)}, u32[]{:S(2)}, u32[]{:S(2)}) %collective-permute-start.1) | collective-permute-done | bytes 65568 | tf_op jit(solution)/shard_map/ppermute | solution.py:457
  44.4 4.2 %collective-permute-start.2 = (bf16[1536,128]{1,0:T(8,128)(2,1)S(1)}, bf16[1536,128]{1,0:T(8,128)(2,1)S(1)}, u32[]{:S(2)}, u32[]{:S(2)}) collective-permute-start(bf16[1536,128]{1,0:T(8,128)(2,1)S(1)} %slice.14), channel_id=1, source_target_pairs={{0,8},{8,0},{1,9},{9,1},{2,10},{10,2},{3,11},{11,3},{4,12},{12,4},... | collective-permute-start | bytes 1179656 | tf_op jit(solution)/shard_map/ppermute | solution.py:557
  49.9 1.4 %collective-permute-start.4 = (bf16[768,256]{1,0:T(8,128)(2,1)S(1)}, bf16[768,256]{1,0:T(8,128)(2,1)S(1)}, u32[]{:S(2)}, u32[]{:S(2)}) collective-permute-start(bf16[768,256]{1,0:T(8,128)(2,1)S(1)} %get-tuple-element.53), channel_id=1, source_target_pairs={{64,0},{128,64},{192,128},{0,192},{65,1},{129,65},{193,129},{1,193... | collective-permute-start | bytes 1179656 | tf_op jit(solution)/shard_map/ppermute | solution.py:556
  51.3 6.1 %shard_map.161.refs_4_ = f32[3072,256]{1,0:T(8,128)S(1)} custom-call(bf16[1536,384]{1,0:T(8,128)(2,1)S(1)} %bitcast.8, bf16[1536,128]{1,0:T(8,128)(2,1)S(1)} %collective-permute-done.2.refs_1_.refs_0_, bf16[1536,384]{1,0:T(8,128)(2,1)S(1)} %bitcast.9), custom_call_target="tpu_custom_call" | custom-call | flops 4831838208 | bytes 6291456 | tf_op jit(solution)/shard_map/pallas_call | solution.py:135
  57.6 2.6 %collective-permute-start.8 = (bf16[768,256]{1,0:T(8,128)(2,1)S(1)}, bf16[768,256]{1,0:T(8,128)(2,1)S(1)}, u32[]{:S(2)}, u32[]{:S(2)}) collective-permute-start(bf16[768,256]{1,0:T(8,128)(2,1)S(1)} %get-tuple-element.54), channel_id=1, source_target_pairs={{64,0},{128,64},{192,128},{0,192},{65,1},{129,65},{193,129},{1,193... | collective-permute-start | bytes 1179656 | tf_op jit(solution)/shard_map/ppermute | solution.py:562
  60.6 6.3 %shard_map.162.refs_4_ = f32[3072,256]{1,0:T(8,128)S(1)} custom-call(bf16[1536,384]{1,0:T(8,128)(2,1)S(1)} %bitcast.10, bf16[1536,128]{1,0:T(8,128)(2,1)S(1)} %collective-permute-done.2.refs_1_.refs_0_, bf16[768,256]{1,0:T(8,128)(2,1)S(1)} %collective-permute-done.3.refs_2_, bf16[768,256]{1,0:T(8,128)(2,1)S(1)} %collective-permute-done.4.refs_3_, ...), custom_call_target="tpu_custom_call" | custom-call | flops 4831838208 | bytes 6291456 | tf_op jit(solution)/shard_map/pallas_call | solution.py:135
  68.0 1.7 %collective-permute-start.6 = (bf16[768,256]{1,0:T(8,128)(2,1)S(1)}, bf16[768,256]{1,0:T(8,128)(2,1)S(1)}, u32[]{:S(2)}, u32[]{:S(2)}) collective-permute-start(bf16[768,256]{1,0:T(8,128)(2,1)S(1)} %collective-permute-done.4.refs_3_), channel_id=1, source_target_pairs={{64,0},{128,64},{192,128},{0,192},{65,1},{129,65},{193,129},{1,193... | collective-permute-start | bytes 1179656 | tf_op jit(solution)/shard_map/ppermute | solution.py:565
  69.7 6.3 %shard_map.163.refs_3_ = f32[3072,256]{1,0:T(8,128)S(1)} custom-call(bf16[1536,384]{1,0:T(8,128)(2,1)S(1)} %bitcast.11, bf16[1536,128]{1,0:T(8,128)(2,1)S(1)} %collective-permute-done.2.refs_1_.refs_0_, bf16[768,256]{1,0:T(8,128)(2,1)S(1)} %collective-permute-done.7.refs_2_, bf16[768,256]{1,0:T(8,128)(2,1)S(1)} %collective-permute-done.8.refs_3_, ...), custom_call_target="tpu_custom_call" | custom-call | flops 4831838208 | bytes 6291456 | tf_op jit(solution)/shard_map/pallas_call | solution.py:135
  77.3 3.2 %shard_map.164 = f32[1536,128]{1,0:T(8,128)S(1)} custom-call(bf16[1536,128]{1,0:T(8,128)(2,1)S(1)} %collective-permute-done.2.refs_1_.refs_0_, bf16[768,256]{1,0:T(8,128)(2,1)S(1)} %collective-permute-done.5.refs_1_, bf16[768,256]{1,0:T(8,128)(2,1)S(1)} %collective-permute-done.6.refs_2_, f32[3072,256]{1,0:T(8,128)S(1)} %shard_map.163.refs_3_, ...), custom_call_target="tpu_custom_call" | custom-call | flops 2415919104 | bytes 3145728 | tf_op jit(solution)/shard_map/pallas_call | solution.py:156
  80.6 2.5 %collective-permute-start.9 = (f32[1536,128]{1,0:T(8,128)S(1)}, f32[1536,128]{1,0:T(8,128)S(1)}, u32[]{:S(2)}, u32[]{:S(2)}) collective-permute-start(f32[1536,128]{1,0:T(8,128)S(1)} %shard_map.164), channel_id=1, source_target_pairs={{0,8},{8,0},{1,9},{9,1},{2,10},{10,2},{3,11},{11,3},{4,12},{12,4},... | collective-permute-start | bytes 2359304 | tf_op jit(solution)/shard_map/ppermute | solution.py:570
  83.1 3.2 %shard_map.165.own_ref = f32[1536,128]{1,0:T(8,128)S(1)} custom-call(bf16[1536,384]{1,0:T(8,128)(2,1)S(1)} %bitcast.12, bf16[768,256]{1,0:T(8,128)(2,1)S(1)} %collective-permute-done.5.refs_1_, bf16[768,256]{1,0:T(8,128)(2,1)S(1)} %collective-permute-done.6.refs_2_, f32[3072,256]{1,0:T(8,128)S(1)} %shard_map.163.refs_3_, bf16[64,4096]{1,0:T(8,128)(2,1)S(1)} %bitcast.14), custom_call_target="tpu_custom_call" | custom-call | flops 2415919104 | bytes 3145728 | tf_op jit(solution)/shard_map/pallas_call | solution.py:156
  86.4 1.9 %shard_map.166 = bf16[4,8,32,128]{3,2,1,0:T(8,128)(2,1)} custom-call(f32[1536,128]{1,0:T(8,128)S(1)} %shard_map.165.own_ref, f32[1536,128]{1,0:T(8,128)S(1)} %collective-permute-done.9.oth_ref), custom_call_target="tpu_custom_call" | custom-call | tf_op jit(solution)/shard_map/pallas_call | solution.py:514
  88.2 4.8 %all-to-all-start.1 = ((bf16[32,32,128]{2,1,0:T(8,128)(2,1)}), bf16[32,32,128]{2,1,0:T(8,128)(2,1)S(1)}, u32[]{:S(2)}, u32[]{:S(2)}) async-start(bf16[32,32,128]{2,1,0:T(8,128)(2,1)} %bitcast.2), calls=%async_computation.1 | async-start | bytes 524288 | tf_op jit(solution)/shard_map/all_to_all | solution.py:576
  93.0 3.1 %collective-permute-start.12 = (f32[2,8,512]{2,1,0:T(8,128)S(1)}, f32[2,8,512]{2,1,0:T(8,128)S(1)}, u32[]{:S(2)}, u32[]{:S(2)}) collective-permute-start(f32[2,8,512]{2,1,0:T(8,128)S(1)} %get-tuple-element.66), channel_id=1, source_target_pairs={{0,1},{1,2},{2,3},{3,4},{4,5},{5,6},{6,7},{8,9},{9,10},{10,11},{11... | collective-permute-start | bytes 98312 | tf_op jit(solution)/shard_map/ppermute | solution.py:574
  97.5 7.6 %all-to-all-done.1.parts_ref = bf16[32,32,128]{2,1,0:T(8,128)(2,1)S(1)} async-done(((bf16[32,32,128]{2,1,0:T(8,128)(2,1)}), bf16[32,32,128]{2,1,0:T(8,128)(2,1)S(1)}, u32[]{:S(2)}, u32[]{:S(2)}) %all-to-all-start.1) | async-done | bytes 262176 | tf_op jit(solution)/shard_map/all_to_all | solution.py:576
  105.1 2.4 %collective-permute-start.10 = (f32[16,128]{1,0:T(8,128)S(1)}, f32[16,128]{1,0:T(8,128)S(1)}, u32[]{:S(2)}, u32[]{:S(2)}) collective-permute-start(f32[16,128]{1,0:T(8,128)S(1)} %get-tuple-element.61), channel_id=1, source_target_pairs={{0,8},{8,0},{16,24},{24,16},{32,40},{40,32},{48,56},{56,48},{64,72... | collective-permute-start | bytes 24584 | tf_op jit(solution)/shard_map/ppermute | solution.py:606
  107.5 2.2 %collective-permute-start.11 = (f32[16,128]{1,0:T(8,128)S(1)}, f32[16,128]{1,0:T(8,128)S(1)}, u32[]{:S(2)}, u32[]{:S(2)}) collective-permute-start(f32[16,128]{1,0:T(8,128)S(1)} %get-tuple-element.63), channel_id=1, source_target_pairs={{8,16},{24,32},{40,48},{56,64},{72,80},{88,96},{104,112},{120,128}... | collective-permute-start | bytes 24584 | tf_op jit(solution)/shard_map/ppermute | solution.py:609
  110.4 2.9 %collective-permute-done.11.apart_ref = f32[16,128]{1,0:T(8,128)S(1)} collective-permute-done((f32[16,128]{1,0:T(8,128)S(1)}, f32[16,128]{1,0:T(8,128)S(1)}, u32[]{:S(2)}, u32[]{:S(2)}) %collective-permute-start.11) | collective-permute-done | bytes 8224 | tf_op jit(solution)/shard_map/ppermute | solution.py:609
  113.4 6.8 %shard_map.168 = (f32[4,12,4,16]{3,2,1,0:T(4,128)}, bf16[4,12,4,384]{3,2,1,0:T(4,128)(2,1)}) custom-call(f32[16,128]{1,0:T(8,128)S(1)} %collective-permute-done.10.near_ref, f32[32,128]{1,0:T(8,128)S(1)} %get-tuple-element.62.mine_ref, f32[16,128]{1,0:T(8,128)S(1)} %collective-permute-done.11.apart_ref, f32[6,4,8,128]{3,2,1,0:T(8,128)S(1)} %get-tuple-element.64.toks, ...), custom_call_target="tpu_custom_call" | custom-call | tf_op jit(solution)/shard_map/pallas_call | solution.py:309
  (44 shorter events, 6.0 us)
Async XLA Ops:
  0.6 14.3 %copy-start.7 = (f32[4,4,12,16]{3,1,2,0:T(4,128)S(1)}, f32[4,4,12,16]{3,1,2,0:T(4,128)}, u32[]{:S(2)}) copy-start(f32[4,4,12,16]{3,1,2,0:T(4,128)} %param.19) | copy-start | bytes 36868
  0.6 14.3 %copy-start.9 = (bf16[2,4,12,16]{3,1,2,0:T(4,128)(2,1)S(1)}, bf16[2,4,12,16]{3,1,2,0:T(4,128)(2,1)}, u32[]{:S(2)}) copy-start(bf16[2,4,12,16]{3,1,2,0:T(4,128)(2,1)} %param.23) | copy-start | bytes 9220
  3.0 41.3 %all-to-all-start = ((bf16[32,48,384]{2,1,0:T(8,128)(2,1)}), bf16[32,48,384]{2,1,0:T(8,128)(2,1)S(1)}, u32[]{:S(2)}, u32[]{:S(2)}) async-start(bf16[32,48,384]{2,1,0:T(8,128)(2,1)} %shard_map.158), calls=%async_computation | async-start | bytes 2359296 | tf_op jit(solution)/shard_map/all_to_all | solution.py:547
  15.1 23.4 %collective-permute-start = (f32[2,16,512]{2,1,0:T(8,128)S(1)}, f32[2,16,512]{2,1,0:T(8,128)S(1)}, u32[]{:S(2)}, u32[]{:S(2)}) collective-permute-start(f32[2,16,512]{2,1,0:T(8,128)S(1)} %get-tuple-element.41), channel_id=1, source_target_pairs={{0,8},{8,16},{16,24},{24,32},{32,40},{40,48},{48,56},{56,64},{64,7... | collective-permute-start | bytes 196616 | tf_op jit(solution)/shard_map/ppermute | solution.py:456
  20.3 23.8 %collective-permute-start.1 = (f32[2,16,512]{2,1,0:T(8,128)S(1)}, f32[2,16,512]{2,1,0:T(8,128)S(1)}, u32[]{:S(2)}, u32[]{:S(2)}) collective-permute-start(f32[2,16,512]{2,1,0:T(8,128)S(1)} %get-tuple-element.42), channel_id=1, source_target_pairs={{8,0},{16,8},{24,16},{32,24},{40,32},{48,40},{56,48},{64,56},{72,6... | collective-permute-start | bytes 196616 | tf_op jit(solution)/shard_map/ppermute | solution.py:457
  44.4 6.9 %collective-permute-start.2 = (bf16[1536,128]{1,0:T(8,128)(2,1)S(1)}, bf16[1536,128]{1,0:T(8,128)(2,1)S(1)}, u32[]{:S(2)}, u32[]{:S(2)}) collective-permute-start(bf16[1536,128]{1,0:T(8,128)(2,1)S(1)} %slice.14), channel_id=1, source_target_pairs={{0,8},{8,0},{1,9},{9,1},{2,10},{10,2},{3,11},{11,3},{4,12},{12,4},... | collective-permute-start | bytes 1179656 | tf_op jit(solution)/shard_map/ppermute | solution.py:557
  48.6 12.0 %collective-permute-start.3 = (bf16[768,256]{1,0:T(8,128)(2,1)S(1)}, bf16[768,256]{1,0:T(8,128)(2,1)S(1)}, u32[]{:S(2)}, u32[]{:S(2)}) collective-permute-start(bf16[768,256]{1,0:T(8,128)(2,1)S(1)} %get-tuple-element.54), channel_id=1, source_target_pairs={{0,64},{64,128},{128,192},{192,0},{1,65},{65,129},{129,193},{193,1... | collective-permute-start | bytes 1179656 | tf_op jit(solution)/shard_map/ppermute | solution.py:555
  49.9 10.7 %collective-permute-start.4 = (bf16[768,256]{1,0:T(8,128)(2,1)S(1)}, bf16[768,256]{1,0:T(8,128)(2,1)S(1)}, u32[]{:S(2)}, u32[]{:S(2)}) collective-permute-start(bf16[768,256]{1,0:T(8,128)(2,1)S(1)} %get-tuple-element.53), channel_id=1, source_target_pairs={{64,0},{128,64},{192,128},{0,192},{65,1},{129,65},{193,129},{1,193... | collective-permute-start | bytes 1179656 | tf_op jit(solution)/shard_map/ppermute | solution.py:556
  57.5 12.2 %collective-permute-start.7 = (bf16[768,256]{1,0:T(8,128)(2,1)S(1)}, bf16[768,256]{1,0:T(8,128)(2,1)S(1)}, u32[]{:S(2)}, u32[]{:S(2)}) collective-permute-start(bf16[768,256]{1,0:T(8,128)(2,1)S(1)} %get-tuple-element.53), channel_id=1, source_target_pairs={{0,64},{64,128},{128,192},{192,0},{1,65},{65,129},{129,193},{193,1... | collective-permute-start | bytes 1179656 | tf_op jit(solution)/shard_map/ppermute | solution.py:561
  57.6 12.1 %collective-permute-start.8 = (bf16[768,256]{1,0:T(8,128)(2,1)S(1)}, bf16[768,256]{1,0:T(8,128)(2,1)S(1)}, u32[]{:S(2)}, u32[]{:S(2)}) collective-permute-start(bf16[768,256]{1,0:T(8,128)(2,1)S(1)} %get-tuple-element.54), channel_id=1, source_target_pairs={{64,0},{128,64},{192,128},{0,192},{65,1},{129,65},{193,129},{1,193... | collective-permute-start | bytes 1179656 | tf_op jit(solution)/shard_map/ppermute | solution.py:562
  66.9 10.4 %collective-permute-start.5 = (bf16[768,256]{1,0:T(8,128)(2,1)S(1)}, bf16[768,256]{1,0:T(8,128)(2,1)S(1)}, u32[]{:S(2)}, u32[]{:S(2)}) collective-permute-start(bf16[768,256]{1,0:T(8,128)(2,1)S(1)} %collective-permute-done.3.refs_2_), channel_id=1, source_target_pairs={{0,64},{64,128},{128,192},{192,0},{1,65},{65,129},{129,193},{193,1... | collective-permute-start | bytes 1179656 | tf_op jit(solution)/shard_map/ppermute | solution.py:565
  68.0 9.4 %collective-permute-start.6 = (bf16[768,256]{1,0:T(8,128)(2,1)S(1)}, bf16[768,256]{1,0:T(8,128)(2,1)S(1)}, u32[]{:S(2)}, u32[]{:S(2)}) collective-permute-start(bf16[768,256]{1,0:T(8,128)(2,1)S(1)} %collective-permute-done.4.refs_3_), channel_id=1, source_target_pairs={{64,0},{128,64},{192,128},{0,192},{65,1},{129,65},{193,129},{1,193... | collective-permute-start | bytes 1179656 | tf_op jit(solution)/shard_map/ppermute | solution.py:565
  80.6 32.8 %copy-start = (bf16[3,3,3,16,384]{4,3,2,1,0:T(8,128)(2,1)S(1)}, bf16[3,3,3,16,384]{4,3,2,1,0:T(8,128)(2,1)}, u32[]{:S(2)}) copy-start(bf16[3,3,3,16,384]{4,3,2,1,0:T(8,128)(2,1)} %w1_ref.1) | copy-start | bytes 995332
  80.6 32.8 %copy-start.1 = (f32[384]{0:T(512)S(1)}, f32[384]{0:T(512)}, u32[]{:S(2)}) copy-start(f32[384]{0:T(512)} %b1_ref.1) | copy-start | bytes 4612
  80.6 32.8 %copy-start.2 = (f32[384]{0:T(512)S(1)}, f32[384]{0:T(512)}, u32[]{:S(2)}) copy-start(f32[384]{0:T(512)} %gain_ref.1) | copy-start | bytes 4612
  80.6 32.8 %copy-start.3 = (f32[384]{0:T(512)S(1)}, f32[384]{0:T(512)}, u32[]{:S(2)}) copy-start(f32[384]{0:T(512)} %b2_ref.1) | copy-start | bytes 4612
  80.6 32.8 %copy-start.4 = (f32[16]{0:T(128)S(1)}, f32[16]{0:T(128)}, u32[]{:S(2)}) copy-start(f32[16]{0:T(128)} %scale_ref.1) | copy-start | bytes 196
  80.6 32.7 %copy-start.5 = (f32[16]{0:T(128)S(1)}, f32[16]{0:T(128)}, u32[]{:S(2)}) copy-start(f32[16]{0:T(128)} %mean_ref.1) | copy-start | bytes 196
  80.6 5.7 %collective-permute-start.9 = (f32[1536,128]{1,0:T(8,128)S(1)}, f32[1536,128]{1,0:T(8,128)S(1)}, u32[]{:S(2)}, u32[]{:S(2)}) collective-permute-start(f32[1536,128]{1,0:T(8,128)S(1)} %shard_map.164), channel_id=1, source_target_pairs={{0,8},{8,0},{1,9},{9,1},{2,10},{10,2},{3,11},{11,3},{4,12},{12,4},... | collective-permute-start | bytes 2359304 | tf_op jit(solution)/shard_map/ppermute | solution.py:570
  88.2 16.8 %all-to-all-start.1 = ((bf16[32,32,128]{2,1,0:T(8,128)(2,1)}), bf16[32,32,128]{2,1,0:T(8,128)(2,1)S(1)}, u32[]{:S(2)}, u32[]{:S(2)}) async-start(bf16[32,32,128]{2,1,0:T(8,128)(2,1)} %bitcast.2), calls=%async_computation.1 | async-start | bytes 524288 | tf_op jit(solution)/shard_map/all_to_all | solution.py:576
  93.0 17.3 %collective-permute-start.12 = (f32[2,8,512]{2,1,0:T(8,128)S(1)}, f32[2,8,512]{2,1,0:T(8,128)S(1)}, u32[]{:S(2)}, u32[]{:S(2)}) collective-permute-start(f32[2,8,512]{2,1,0:T(8,128)S(1)} %get-tuple-element.66), channel_id=1, source_target_pairs={{0,1},{1,2},{2,3},{3,4},{4,5},{5,6},{6,7},{8,9},{9,10},{10,11},{11... | collective-permute-start | bytes 98312 | tf_op jit(solution)/shard_map/ppermute | solution.py:574
  96.2 14.2 %collective-permute-start.13 = (f32[2,8,512]{2,1,0:T(8,128)S(1)}, f32[2,8,512]{2,1,0:T(8,128)S(1)}, u32[]{:S(2)}, u32[]{:S(2)}) collective-permute-start(f32[2,8,512]{2,1,0:T(8,128)S(1)} %get-tuple-element.67), channel_id=1, source_target_pairs={{1,0},{2,1},{3,2},{4,3},{5,4},{6,5},{7,6},{9,8},{10,9},{11,10},{12... | collective-permute-start | bytes 98312 | tf_op jit(solution)/shard_map/ppermute | solution.py:575
  105.1 5.3 %collective-permute-start.10 = (f32[16,128]{1,0:T(8,128)S(1)}, f32[16,128]{1,0:T(8,128)S(1)}, u32[]{:S(2)}, u32[]{:S(2)}) collective-permute-start(f32[16,128]{1,0:T(8,128)S(1)} %get-tuple-element.61), channel_id=1, source_target_pairs={{0,8},{8,0},{16,24},{24,16},{32,40},{40,32},{48,56},{56,48},{64,72... | collective-permute-start | bytes 24584 | tf_op jit(solution)/shard_map/ppermute | solution.py:606
  107.5 5.9 %collective-permute-start.11 = (f32[16,128]{1,0:T(8,128)S(1)}, f32[16,128]{1,0:T(8,128)S(1)}, u32[]{:S(2)}, u32[]{:S(2)}) collective-permute-start(f32[16,128]{1,0:T(8,128)S(1)} %get-tuple-element.63), channel_id=1, source_target_pairs={{8,16},{24,32},{40,48},{56,64},{72,80},{88,96},{104,112},{120,128}... | collective-permute-start | bytes 24584 | tf_op jit(solution)/shard_map/ppermute | solution.py:609
  (2 other events, 24.6 us)

commit v12 on v11

--- a/solution.py
+++ b/solution.py
@@ -317,11 +317,11 @@
         scratch_shapes=[
             pltpu.VMEM((F, 4, 8, 128), jnp.float32),
             pltpu.VMEM((6, 4, 16, 128), jnp.float32),
-            pltpu.VMEM((F, 128, 128), jnp.float32),
+            pltpu.VMEM((F, 144, 128), jnp.float32),
             pltpu.VMEM((C1 // 128, F, 6, 24, 128), jnp.float32),
             pltpu.VMEM((C1 // 128, 6, 6, 24, 128), jnp.float32),
             pltpu.VMEM((6, 6, 16, 3 * C1), jnp.bfloat16),
-            pltpu.VMEM((C1 // 128, F, 128, 128), jnp.float32),
+            pltpu.VMEM((C1 // 128, F, 136, 128), jnp.float32),
             pltpu.VMEM((16, 128), jnp.float32),
             pltpu.VMEM((6, 4, 8, 128), jnp.float32),
             pltpu.VMEM((2, 6, 16, C1), jnp.float32),
@@ -451,7 +451,7 @@
 def halo_rows(noisy, cache_in, cache_mid):
     edge = (2, 16, 512)
     toks, down, up = small_call(
-        edge_rows_kernel, [(6, 2, 8, 128), edge, edge], [(6, 4, 16, 128)]
+        edge_rows_kernel, [(6, 2, 8, 128), edge, edge], [(6, 4, 24, 128)]
     )(noisy, cache_in, cache_mid)
     above = lax.ppermute(down, SEQ, along(SEQ, 1))
     below = lax.ppermute(up, SEQ, along(SEQ, -1))
@@ -488,7 +488,7 @@
     share = 1.0 / (1.0 + jnp.exp2(gap))
     vel = own * share + oth * (1.0 - share)
     lane = lax.broadcasted_iota(jnp.int32, vel.shape, 1)
-    vel_ref[...] = jnp.where(lane < 64, vel, pltpu.roll(vel, 64, axis=1))
+    vel_ref[0 : vel.shape[0], :] = jnp.where(lane < 64, vel, pltpu.roll(vel, 64, axis=1))
     low = lax.broadcasted_iota(jnp.int32, (16, 128), 1) < 64
     zero = jnp.zeros((16, 128), jnp.float32)
 
@@ -504,7 +504,7 @@
                 both = jnp.where(low, column(r, at), column(r, at + 4))
                 for y in range(4):
                     piece_ref[y, b, pl.ds(r * 16 + c, 4, stride=4), :] = both[y * 4 : y * 4 + 4]
-    out_ref[...] = piece_ref[...].astype(jnp.bfloat16)
+    out_ref[...] = piece_ref[:, :, 0:32, :].astype(jnp.bfloat16)
 
 
 def merge(own, oth):
@@ -517,8 +517,8 @@
         out_specs=pl.BlockSpec(shape, lambda: (0, 0, 0, 0)),
         out_shape=jax.ShapeDtypeStruct(shape, jnp.bfloat16),
         scratch_shapes=[
-            pltpu.VMEM((rows, 128), jnp.float32),
-            pltpu.VMEM(shape, jnp.float32),
+            pltpu.VMEM((rows + 96, 128), jnp.float32),
+            pltpu.VMEM((4, 8, 40, 128), jnp.float32),
         ],
         compiler_params=pltpu.CompilerParams(vmem_limit_bytes=24 << 20),
     )(own, oth)

time: 121 us -> 121 us (level)
  no operation moved by 1% of the time
where the time goes in v12:
time: 121 us; the launch traced here: 120 us
  starting transfers between devices  47.7 us (39%)
  Pallas kernels  36.6 us (30%)
  waiting for transfers between devices  34.1 us (28%)
  between operations  1.76 us (1%)
    pallas_call x3, Pallas kernels, flash(): pl.pallas_call(functools.partial(flash_kernel, state is None, False, len(...  18.7 us
    ppermute x1, waiting for transfers between devices, halo_rows(): above = lax.ppermute(down, SEQ, along(SEQ, 1))  16.3 us
    all_to_all x1, starting transfers between devices, attention(): lax.all_to_all(packed, HEAD, split_axis=0, concat_axis=0, tiled=True)  11.9 us
    all_to_all x1, waiting for transfers between devices, attention(): lax.all_to_all(partial, HEAD, split_axis=0, concat_axis=0, tiled=True)  7.55 us
    pallas_call x1, Pallas kernels, tail(): pl.pallas_call(tail_kernel, in_specs=specs, out_specs=[pl.BlockSpec(memor...  6.84 us
    pallas_call x2, Pallas kernels, flash_last(): pl.pallas_call(functools.partial(flash_kernel, False, True, len(kvs), hal...  6.46 us
    ppermute x1, waiting for transfers between devices, halo_rows(): below = lax.ppermute(up, SEQ, along(SEQ, -1))  5.63 us
    ppermute x1, starting transfers between devices, halo_rows(): above = lax.ppermute(down, SEQ, along(SEQ, 1))  5.16 us
  transfers between devices with their start and end apart: 16, of which 6 were waited for; matrix products, arithmetic and copies ran while one was open for 0% of the time, Pallas kernels for 19%

profile of v12, /device:TPU:1, one launch (start us, length us, event | category | flops | bytes accessed | tf_op | source)
XLA Modules:
  0.0 120.4 jit_solution(4987133134003950004)
XLA Ops:
  0.7 2.3 %shard_map.158 = bf16[32,48,384]{2,1,0:T(8,128)(2,1)} custom-call(bf16[48,4096]{1,0:T(8,128)(2,1)} %q_ref.1, bf16[48,4096]{1,0:T(8,128)(2,1)} %k_ref.1, bf16[48,4096]{1,0:T(8,128)(2,1)} %v_ref.1), custom_call_target="tpu_custom_call" | custom-call | tf_op jit(solution)/shard_map/pallas_call | solution.py:476
  3.0 11.9 %all-to-all-start = ((bf16[32,48,384]{2,1,0:T(8,128)(2,1)}), bf16[32,48,384]{2,1,0:T(8,128)(2,1)S(1)}, u32[]{:S(2)}, u32[]{:S(2)}) async-start(bf16[32,48,384]{2,1,0:T(8,128)(2,1)} %shard_map.158), calls=%async_computation | async-start | bytes 2359296 | tf_op jit(solution)/shard_map/all_to_all | solution.py:547
  15.1 5.2 %collective-permute-start = (f32[2,16,512]{2,1,0:T(8,128)S(1)}, f32[2,16,512]{2,1,0:T(8,128)S(1)}, u32[]{:S(2)}, u32[]{:S(2)}) collective-permute-start(f32[2,16,512]{2,1,0:T(8,128)S(1)} %get-tuple-element.41), channel_id=1, source_target_pairs={{0,8},{8,16},{16,24},{24,32},{32,40},{40,48},{48,56},{56,64},{64,7... | collective-permute-start | bytes 196616 | tf_op jit(solution)/shard_map/ppermute | solution.py:456
  20.3 1.9 %collective-permute-start.1 = (f32[2,16,512]{2,1,0:T(8,128)S(1)}, f32[2,16,512]{2,1,0:T(8,128)S(1)}, u32[]{:S(2)}, u32[]{:S(2)}) collective-permute-start(f32[2,16,512]{2,1,0:T(8,128)S(1)} %get-tuple-element.42), channel_id=1, source_target_pairs={{8,0},{16,8},{24,16},{32,24},{40,32},{48,40},{56,48},{64,56},{72,6... | collective-permute-start | bytes 196616 | tf_op jit(solution)/shard_map/ppermute | solution.py:457
  22.2 16.3 %collective-permute-done.above_ref = f32[2,16,512]{2,1,0:T(8,128)S(1)} collective-permute-done((f32[2,16,512]{2,1,0:T(8,128)S(1)}, f32[2,16,512]{2,1,0:T(8,128)S(1)}, u32[]{:S(2)}, u32[]{:S(2)}) %collective-permute-start) | collective-permute-done | bytes 65568 | tf_op jit(solution)/shard_map/ppermute | solution.py:456
  38.5 5.6 %collective-permute-done.1.below_ref = f32[2,16,512]{2,1,0:T(8,128)S(1)} collective-permute-done((f32[2,16,512]{2,1,0:T(8,128)S(1)}, f32[2,16,512]{2,1,0:T(8,128)S(1)}, u32[]{:S(2)}, u32[]{:S(2)}) %collective-permute-start.1) | collective-permute-done | bytes 65568 | tf_op jit(solution)/shard_map/ppermute | solution.py:457
  44.4 4.2 %collective-permute-start.2 = (bf16[1536,128]{1,0:T(8,128)(2,1)S(1)}, bf16[1536,128]{1,0:T(8,128)(2,1)S(1)}, u32[]{:S(2)}, u32[]{:S(2)}) collective-permute-start(bf16[1536,128]{1,0:T(8,128)(2,1)S(1)} %slice.14), channel_id=1, source_target_pairs={{0,8},{8,0},{1,9},{9,1},{2,10},{10,2},{3,11},{11,3},{4,12},{12,4},... | collective-permute-start | bytes 1179656 | tf_op jit(solution)/shard_map/ppermute | solution.py:557
  49.9 1.4 %collective-permute-start.4 = (bf16[768,256]{1,0:T(8,128)(2,1)S(1)}, bf16[768,256]{1,0:T(8,128)(2,1)S(1)}, u32[]{:S(2)}, u32[]{:S(2)}) collective-permute-start(bf16[768,256]{1,0:T(8,128)(2,1)S(1)} %get-tuple-element.53), channel_id=1, source_target_pairs={{64,0},{128,64},{192,128},{0,192},{65,1},{129,65},{193,129},{1,193... | collective-permute-start | bytes 1179656 | tf_op jit(solution)/shard_map/ppermute | solution.py:556
  51.3 6.1 %shard_map.161.refs_4_ = f32[3072,256]{1,0:T(8,128)S(1)} custom-call(bf16[1536,384]{1,0:T(8,128)(2,1)S(1)} %bitcast.8, bf16[1536,128]{1,0:T(8,128)(2,1)S(1)} %collective-permute-done.2.refs_1_.refs_0_, bf16[1536,384]{1,0:T(8,128)(2,1)S(1)} %bitcast.9), custom_call_target="tpu_custom_call" | custom-call | flops 4831838208 | bytes 6291456 | tf_op jit(solution)/shard_map/pallas_call | solution.py:135
  57.6 2.6 %collective-permute-start.8 = (bf16[768,256]{1,0:T(8,128)(2,1)S(1)}, bf16[768,256]{1,0:T(8,128)(2,1)S(1)}, u32[]{:S(2)}, u32[]{:S(2)}) collective-permute-start(bf16[768,256]{1,0:T(8,128)(2,1)S(1)} %get-tuple-element.54), channel_id=1, source_target_pairs={{64,0},{128,64},{192,128},{0,192},{65,1},{129,65},{193,129},{1,193... | collective-permute-start | bytes 1179656 | tf_op jit(solution)/shard_map/ppermute | solution.py:562
  60.6 6.3 %shard_map.162.refs_4_ = f32[3072,256]{1,0:T(8,128)S(1)} custom-call(bf16[1536,384]{1,0:T(8,128)(2,1)S(1)} %bitcast.10, bf16[1536,128]{1,0:T(8,128)(2,1)S(1)} %collective-permute-done.2.refs_1_.refs_0_, bf16[768,256]{1,0:T(8,128)(2,1)S(1)} %collective-permute-done.3.refs_2_, bf16[768,256]{1,0:T(8,128)(2,1)S(1)} %collective-permute-done.4.refs_3_, ...), custom_call_target="tpu_custom_call" | custom-call | flops 4831838208 | bytes 6291456 | tf_op jit(solution)/shard_map/pallas_call | solution.py:135
  68.0 1.7 %collective-permute-start.6 = (bf16[768,256]{1,0:T(8,128)(2,1)S(1)}, bf16[768,256]{1,0:T(8,128)(2,1)S(1)}, u32[]{:S(2)}, u32[]{:S(2)}) collective-permute-start(bf16[768,256]{1,0:T(8,128)(2,1)S(1)} %collective-permute-done.4.refs_3_), channel_id=1, source_target_pairs={{64,0},{128,64},{192,128},{0,192},{65,1},{129,65},{193,129},{1,193... | collective-permute-start | bytes 1179656 | tf_op jit(solution)/shard_map/ppermute | solution.py:565
  69.7 6.3 %shard_map.163.refs_3_ = f32[3072,256]{1,0:T(8,128)S(1)} custom-call(bf16[1536,384]{1,0:T(8,128)(2,1)S(1)} %bitcast.11, bf16[1536,128]{1,0:T(8,128)(2,1)S(1)} %collective-permute-done.2.refs_1_.refs_0_, bf16[768,256]{1,0:T(8,128)(2,1)S(1)} %collective-permute-done.7.refs_2_, bf16[768,256]{1,0:T(8,128)(2,1)S(1)} %collective-permute-done.8.refs_3_, ...), custom_call_target="tpu_custom_call" | custom-call | flops 4831838208 | bytes 6291456 | tf_op jit(solution)/shard_map/pallas_call | solution.py:135
  77.3 3.2 %shard_map.164 = f32[1536,128]{1,0:T(8,128)S(1)} custom-call(bf16[1536,128]{1,0:T(8,128)(2,1)S(1)} %collective-permute-done.2.refs_1_.refs_0_, bf16[768,256]{1,0:T(8,128)(2,1)S(1)} %collective-permute-done.5.refs_1_, bf16[768,256]{1,0:T(8,128)(2,1)S(1)} %collective-permute-done.6.refs_2_, f32[3072,256]{1,0:T(8,128)S(1)} %shard_map.163.refs_3_, ...), custom_call_target="tpu_custom_call" | custom-call | flops 2415919104 | bytes 3145728 | tf_op jit(solution)/shard_map/pallas_call | solution.py:156
  80.6 2.5 %collective-permute-start.9 = (f32[1536,128]{1,0:T(8,128)S(1)}, f32[1536,128]{1,0:T(8,128)S(1)}, u32[]{:S(2)}, u32[]{:S(2)}) collective-permute-start(f32[1536,128]{1,0:T(8,128)S(1)} %shard_map.164), channel_id=1, source_target_pairs={{0,8},{8,0},{1,9},{9,1},{2,10},{10,2},{3,11},{11,3},{4,12},{12,4},... | collective-permute-start | bytes 2359304 | tf_op jit(solution)/shard_map/ppermute | solution.py:570
  83.1 3.2 %shard_map.165.own_ref = f32[1536,128]{1,0:T(8,128)S(1)} custom-call(bf16[1536,384]{1,0:T(8,128)(2,1)S(1)} %bitcast.12, bf16[768,256]{1,0:T(8,128)(2,1)S(1)} %collective-permute-done.5.refs_1_, bf16[768,256]{1,0:T(8,128)(2,1)S(1)} %collective-permute-done.6.refs_2_, f32[3072,256]{1,0:T(8,128)S(1)} %shard_map.163.refs_3_, bf16[64,4096]{1,0:T(8,128)(2,1)S(1)} %bitcast.14), custom_call_target="tpu_custom_call" | custom-call | flops 2415919104 | bytes 3145728 | tf_op jit(solution)/shard_map/pallas_call | solution.py:156
  86.4 1.9 %shard_map.166 = bf16[4,8,32,128]{3,2,1,0:T(8,128)(2,1)} custom-call(f32[1536,128]{1,0:T(8,128)S(1)} %shard_map.165.own_ref, f32[1536,128]{1,0:T(8,128)S(1)} %collective-permute-done.9.oth_ref), custom_call_target="tpu_custom_call" | custom-call | tf_op jit(solution)/shard_map/pallas_call | solution.py:514
  88.2 4.8 %all-to-all-start.1 = ((bf16[32,32,128]{2,1,0:T(8,128)(2,1)}), bf16[32,32,128]{2,1,0:T(8,128)(2,1)S(1)}, u32[]{:S(2)}, u32[]{:S(2)}) async-start(bf16[32,32,128]{2,1,0:T(8,128)(2,1)} %bitcast.2), calls=%async_computation.1 | async-start | bytes 524288 | tf_op jit(solution)/shard_map/all_to_all | solution.py:576
  93.0 3.1 %collective-permute-start.12 = (f32[2,8,512]{2,1,0:T(8,128)S(1)}, f32[2,8,512]{2,1,0:T(8,128)S(1)}, u32[]{:S(2)}, u32[]{:S(2)}) collective-permute-start(f32[2,8,512]{2,1,0:T(8,128)S(1)} %get-tuple-element.66), channel_id=1, source_target_pairs={{0,1},{1,2},{2,3},{3,4},{4,5},{5,6},{6,7},{8,9},{9,10},{10,11},{11... | collective-permute-start | bytes 98312 | tf_op jit(solution)/shard_map/ppermute | solution.py:574
  97.5 7.6 %all-to-all-done.1.parts_ref = bf16[32,32,128]{2,1,0:T(8,128)(2,1)S(1)} async-done(((bf16[32,32,128]{2,1,0:T(8,128)(2,1)}), bf16[32,32,128]{2,1,0:T(8,128)(2,1)S(1)}, u32[]{:S(2)}, u32[]{:S(2)}) %all-to-all-start.1) | async-done | bytes 262176 | tf_op jit(solution)/shard_map/all_to_all | solution.py:576
  105.1 2.4 %collective-permute-start.10 = (f32[16,128]{1,0:T(8,128)S(1)}, f32[16,128]{1,0:T(8,128)S(1)}, u32[]{:S(2)}, u32[]{:S(2)}) collective-permute-start(f32[16,128]{1,0:T(8,128)S(1)} %get-tuple-element.61), channel_id=1, source_target_pairs={{0,8},{8,0},{16,24},{24,16},{32,40},{40,32},{48,56},{56,48},{64,72... | collective-permute-start | bytes 24584 | tf_op jit(solution)/shard_map/ppermute | solution.py:606
  107.5 2.2 %collective-permute-start.11 = (f32[16,128]{1,0:T(8,128)S(1)}, f32[16,128]{1,0:T(8,128)S(1)}, u32[]{:S(2)}, u32[]{:S(2)}) collective-permute-start(f32[16,128]{1,0:T(8,128)S(1)} %get-tuple-element.63), channel_id=1, source_target_pairs={{8,16},{24,32},{40,48},{56,64},{72,80},{88,96},{104,112},{120,128}... | collective-permute-start | bytes 24584 | tf_op jit(solution)/shard_map/ppermute | solution.py:609
  110.4 2.9 %collective-permute-done.11.apart_ref = f32[16,128]{1,0:T(8,128)S(1)} collective-permute-done((f32[16,128]{1,0:T(8,128)S(1)}, f32[16,128]{1,0:T(8,128)S(1)}, u32[]{:S(2)}, u32[]{:S(2)}) %collective-permute-start.11) | collective-permute-done | bytes 8224 | tf_op jit(solution)/shard_map/ppermute | solution.py:609
  113.4 6.8 %shard_map.168 = (f32[4,12,4,16]{3,2,1,0:T(4,128)}, bf16[4,12,4,384]{3,2,1,0:T(4,128)(2,1)}) custom-call(f32[16,128]{1,0:T(8,128)S(1)} %collective-permute-done.10.near_ref, f32[32,128]{1,0:T(8,128)S(1)} %get-tuple-element.62.mine_ref, f32[16,128]{1,0:T(8,128)S(1)} %collective-permute-done.11.apart_ref, f32[6,4,8,128]{3,2,1,0:T(8,128)S(1)} %get-tuple-element.64.toks, ...), custom_call_target="tpu_custom_call" | custom-call | tf_op jit(solution)/shard_map/pallas_call | solution.py:309
  (44 shorter events, 6.0 us)
Async XLA Ops:
  0.6 14.3 %copy-start.7 = (f32[4,4,12,16]{3,1,2,0:T(4,128)S(1)}, f32[4,4,12,16]{3,1,2,0:T(4,128)}, u32[]{:S(2)}) copy-start(f32[4,4,12,16]{3,1,2,0:T(4,128)} %param.19) | copy-start | bytes 36868
  0.6 14.3 %copy-start.9 = (bf16[2,4,12,16]{3,1,2,0:T(4,128)(2,1)S(1)}, bf16[2,4,12,16]{3,1,2,0:T(4,128)(2,1)}, u32[]{:S(2)}) copy-start(bf16[2,4,12,16]{3,1,2,0:T(4,128)(2,1)} %param.23) | copy-start | bytes 9220
  3.0 41.3 %all-to-all-start = ((bf16[32,48,384]{2,1,0:T(8,128)(2,1)}), bf16[32,48,384]{2,1,0:T(8,128)(2,1)S(1)}, u32[]{:S(2)}, u32[]{:S(2)}) async-start(bf16[32,48,384]{2,1,0:T(8,128)(2,1)} %shard_map.158), calls=%async_computation | async-start | bytes 2359296 | tf_op jit(solution)/shard_map/all_to_all | solution.py:547
  15.1 23.4 %collective-permute-start = (f32[2,16,512]{2,1,0:T(8,128)S(1)}, f32[2,16,512]{2,1,0:T(8,128)S(1)}, u32[]{:S(2)}, u32[]{:S(2)}) collective-permute-start(f32[2,16,512]{2,1,0:T(8,128)S(1)} %get-tuple-element.41), channel_id=1, source_target_pairs={{0,8},{8,16},{16,24},{24,32},{32,40},{40,48},{48,56},{56,64},{64,7... | collective-permute-start | bytes 196616 | tf_op jit(solution)/shard_map/ppermute | solution.py:456
  20.3 23.8 %collective-permute-start.1 = (f32[2,16,512]{2,1,0:T(8,128)S(1)}, f32[2,16,512]{2,1,0:T(8,128)S(1)}, u32[]{:S(2)}, u32[]{:S(2)}) collective-permute-start(f32[2,16,512]{2,1,0:T(8,128)S(1)} %get-tuple-element.42), channel_id=1, source_target_pairs={{8,0},{16,8},{24,16},{32,24},{40,32},{48,40},{56,48},{64,56},{72,6... | collective-permute-start | bytes 196616 | tf_op jit(solution)/shard_map/ppermute | solution.py:457
  44.4 6.9 %collective-permute-start.2 = (bf16[1536,128]{1,0:T(8,128)(2,1)S(1)}, bf16[1536,128]{1,0:T(8,128)(2,1)S(1)}, u32[]{:S(2)}, u32[]{:S(2)}) collective-permute-start(bf16[1536,128]{1,0:T(8,128)(2,1)S(1)} %slice.14), channel_id=1, source_target_pairs={{0,8},{8,0},{1,9},{9,1},{2,10},{10,2},{3,11},{11,3},{4,12},{12,4},... | collective-permute-start | bytes 1179656 | tf_op jit(solution)/shard_map/ppermute | solution.py:557
  48.6 12.0 %collective-permute-start.3 = (bf16[768,256]{1,0:T(8,128)(2,1)S(1)}, bf16[768,256]{1,0:T(8,128)(2,1)S(1)}, u32[]{:S(2)}, u32[]{:S(2)}) collective-permute-start(bf16[768,256]{1,0:T(8,128)(2,1)S(1)} %get-tuple-element.54), channel_id=1, source_target_pairs={{0,64},{64,128},{128,192},{192,0},{1,65},{65,129},{129,193},{193,1... | collective-permute-start | bytes 1179656 | tf_op jit(solution)/shard_map/ppermute | solution.py:555
  49.9 10.7 %collective-permute-start.4 = (bf16[768,256]{1,0:T(8,128)(2,1)S(1)}, bf16[768,256]{1,0:T(8,128)(2,1)S(1)}, u32[]{:S(2)}, u32[]{:S(2)}) collective-permute-start(bf16[768,256]{1,0:T(8,128)(2,1)S(1)} %get-tuple-element.53), channel_id=1, source_target_pairs={{64,0},{128,64},{192,128},{0,192},{65,1},{129,65},{193,129},{1,193... | collective-permute-start | bytes 1179656 | tf_op jit(solution)/shard_map/ppermute | solution.py:556
  57.5 12.2 %collective-permute-start.7 = (bf16[768,256]{1,0:T(8,128)(2,1)S(1)}, bf16[768,256]{1,0:T(8,128)(2,1)S(1)}, u32[]{:S(2)}, u32[]{:S(2)}) collective-permute-start(bf16[768,256]{1,0:T(8,128)(2,1)S(1)} %get-tuple-element.53), channel_id=1, source_target_pairs={{0,64},{64,128},{128,192},{192,0},{1,65},{65,129},{129,193},{193,1... | collective-permute-start | bytes 1179656 | tf_op jit(solution)/shard_map/ppermute | solution.py:561
  57.6 12.1 %collective-permute-start.8 = (bf16[768,256]{1,0:T(8,128)(2,1)S(1)}, bf16[768,256]{1,0:T(8,128)(2,1)S(1)}, u32[]{:S(2)}, u32[]{:S(2)}) collective-permute-start(bf16[768,256]{1,0:T(8,128)(2,1)S(1)} %get-tuple-element.54), channel_id=1, source_target_pairs={{64,0},{128,64},{192,128},{0,192},{65,1},{129,65},{193,129},{1,193... | collective-permute-start | bytes 1179656 | tf_op jit(solution)/shard_map/ppermute | solution.py:562
  66.9 10.4 %collective-permute-start.5 = (bf16[768,256]{1,0:T(8,128)(2,1)S(1)}, bf16[768,256]{1,0:T(8,128)(2,1)S(1)}, u32[]{:S(2)}, u32[]{:S(2)}) collective-permute-start(bf16[768,256]{1,0:T(8,128)(2,1)S(1)} %collective-permute-done.3.refs_2_), channel_id=1, source_target_pairs={{0,64},{64,128},{128,192},{192,0},{1,65},{65,129},{129,193},{193,1... | collective-permute-start | bytes 1179656 | tf_op jit(solution)/shard_map/ppermute | solution.py:565
  68.0 9.4 %collective-permute-start.6 = (bf16[768,256]{1,0:T(8,128)(2,1)S(1)}, bf16[768,256]{1,0:T(8,128)(2,1)S(1)}, u32[]{:S(2)}, u32[]{:S(2)}) collective-permute-start(bf16[768,256]{1,0:T(8,128)(2,1)S(1)} %collective-permute-done.4.refs_3_), channel_id=1, source_target_pairs={{64,0},{128,64},{192,128},{0,192},{65,1},{129,65},{193,129},{1,193... | collective-permute-start | bytes 1179656 | tf_op jit(solution)/shard_map/ppermute | solution.py:565
  80.6 32.8 %copy-start = (bf16[3,3,3,16,384]{4,3,2,1,0:T(8,128)(2,1)S(1)}, bf16[3,3,3,16,384]{4,3,2,1,0:T(8,128)(2,1)}, u32[]{:S(2)}) copy-start(bf16[3,3,3,16,384]{4,3,2,1,0:T(8,128)(2,1)} %w1_ref.1) | copy-start | bytes 995332
  80.6 32.8 %copy-start.1 = (f32[384]{0:T(512)S(1)}, f32[384]{0:T(512)}, u32[]{:S(2)}) copy-start(f32[384]{0:T(512)} %b1_ref.1) | copy-start | bytes 4612
  80.6 32.8 %copy-start.2 = (f32[384]{0:T(512)S(1)}, f32[384]{0:T(512)}, u32[]{:S(2)}) copy-start(f32[384]{0:T(512)} %gain_ref.1) | copy-start | bytes 4612
  80.6 32.7 %copy-start.3 = (f32[384]{0:T(512)S(1)}, f32[384]{0:T(512)}, u32[]{:S(2)}) copy-start(f32[384]{0:T(512)} %b2_ref.1) | copy-start | bytes 4612
  80.6 32.7 %copy-start.4 = (f32[16]{0:T(128)S(1)}, f32[16]{0:T(128)}, u32[]{:S(2)}) copy-start(f32[16]{0:T(128)} %scale_ref.1) | copy-start | bytes 196
  80.6 32.7 %copy-start.5 = (f32[16]{0:T(128)S(1)}, f32[16]{0:T(128)}, u32[]{:S(2)}) copy-start(f32[16]{0:T(128)} %mean_ref.1) | copy-start | bytes 196
  80.6 5.7 %collective-permute-start.9 = (f32[1536,128]{1,0:T(8,128)S(1)}, f32[1536,128]{1,0:T(8,128)S(1)}, u32[]{:S(2)}, u32[]{:S(2)}) collective-permute-start(f32[1536,128]{1,0:T(8,128)S(1)} %shard_map.164), channel_id=1, source_target_pairs={{0,8},{8,0},{1,9},{9,1},{2,10},{10,2},{3,11},{11,3},{4,12},{12,4},... | collective-permute-start | bytes 2359304 | tf_op jit(solution)/shard_map/ppermute | solution.py:570
  88.2 16.8 %all-to-all-start.1 = ((bf16[32,32,128]{2,1,0:T(8,128)(2,1)}), bf16[32,32,128]{2,1,0:T(8,128)(2,1)S(1)}, u32[]{:S(2)}, u32[]{:S(2)}) async-start(bf16[32,32,128]{2,1,0:T(8,128)(2,1)} %bitcast.2), calls=%async_computation.1 | async-start | bytes 524288 | tf_op jit(solution)/shard_map/all_to_all | solution.py:576
  93.0 17.3 %collective-permute-start.12 = (f32[2,8,512]{2,1,0:T(8,128)S(1)}, f32[2,8,512]{2,1,0:T(8,128)S(1)}, u32[]{:S(2)}, u32[]{:S(2)}) collective-permute-start(f32[2,8,512]{2,1,0:T(8,128)S(1)} %get-tuple-element.66), channel_id=1, source_target_pairs={{0,1},{1,2},{2,3},{3,4},{4,5},{5,6},{6,7},{8,9},{9,10},{10,11},{11... | collective-permute-start | bytes 98312 | tf_op jit(solution)/shard_map/ppermute | solution.py:574
  96.2 14.2 %collective-permute-start.13 = (f32[2,8,512]{2,1,0:T(8,128)S(1)}, f32[2,8,512]{2,1,0:T(8,128)S(1)}, u32[]{:S(2)}, u32[]{:S(2)}) collective-permute-start(f32[2,8,512]{2,1,0:T(8,128)S(1)} %get-tuple-element.67), channel_id=1, source_target_pairs={{1,0},{2,1},{3,2},{4,3},{5,4},{6,5},{7,6},{9,8},{10,9},{11,10},{12... | collective-permute-start | bytes 98312 | tf_op jit(solution)/shard_map/ppermute | solution.py:575
  105.1 5.3 %collective-permute-start.10 = (f32[16,128]{1,0:T(8,128)S(1)}, f32[16,128]{1,0:T(8,128)S(1)}, u32[]{:S(2)}, u32[]{:S(2)}) collective-permute-start(f32[16,128]{1,0:T(8,128)S(1)} %get-tuple-element.61), channel_id=1, source_target_pairs={{0,8},{8,0},{16,24},{24,16},{32,40},{40,32},{48,56},{56,48},{64,72... | collective-permute-start | bytes 24584 | tf_op jit(solution)/shard_map/ppermute | solution.py:606
  107.5 5.9 %collective-permute-start.11 = (f32[16,128]{1,0:T(8,128)S(1)}, f32[16,128]{1,0:T(8,128)S(1)}, u32[]{:S(2)}, u32[]{:S(2)}) collective-permute-start(f32[16,128]{1,0:T(8,128)S(1)} %get-tuple-element.63), channel_id=1, source_target_pairs={{8,16},{24,32},{40,48},{56,64},{72,80},{88,96},{104,112},{120,128}... | collective-permute-start | bytes 24584 | tf_op jit(solution)/shard_map/ppermute | solution.py:609
  (2 other events, 24.6 us)
